TPU v7x, 32 devices: a whole 2x2x4 slice. The times are simulated.
32 devices in a mesh: narrow: 4 (over y, x), wide: 8 (over z, core).
Axes of the slice: x: 2, y: 2, z: 4, core: 2. Of those that a mesh axis runs over, the one named last changes fastest.
Arguments:
- tokens_in: bfloat16 [16384, 2048], P(('narrow', 'wide')), may hold values from -6 to 6
- out_grad: bfloat16 [16384, 2048], P(('narrow', 'wide')), may hold values from -15 to 15
- positions: int32 [16384], P('narrow'), may hold values from 0 to 12285, as said below
- query_weight: float32 [2048, 2048], P('narrow', 'wide'), may hold values from -0.125 to 0.125
- query_first: float32 [2048, 2048], P('narrow', 'wide'), may hold values from -160 to 160
- query_second: float32 [2048, 2048], P('narrow', 'wide'), may hold values from 3440.64 to 13762.56
- key_weight: float32 [2048, 512], P('narrow'), may hold values from -0.125 to 0.125
- key_first: float32 [2048, 512], P('narrow'), may hold values from -320 to 320
- key_second: float32 [2048, 512], P('narrow'), may hold values from 13926.4 to 55705.6
- value_weight: float32 [2048, 512], P('narrow'), may hold values from -0.125 to 0.125
- value_first: float32 [2048, 512], P('narrow'), may hold values from -256 to 256
- value_second: float32 [2048, 512], P('narrow'), may hold values from 7864.32 to 31129.6
- output_weight: float32 [2048, 2048], P('wide', 'narrow'), may hold values from -0.875 to 0.875
- output_first: float32 [2048, 2048], P('wide', 'narrow'), may hold values from -32 to 32
- output_second: float32 [2048, 2048], P('wide', 'narrow'), may hold values from 139.264 to 557.056
- gate_weight: float32 [2048, 8192], P('narrow', 'wide'), may hold values from -0.125 to 0.125
- gate_first: float32 [2048, 8192], P('narrow', 'wide'), may hold values from -48 to 48
- gate_second: float32 [2048, 8192], P('narrow', 'wide'), may hold values from 311.296 to 1245.184
- up_weight: float32 [2048, 8192], P('narrow', 'wide'), may hold values from -0.125 to 0.125
- up_first: float32 [2048, 8192], P('narrow', 'wide'), may hold values from -48 to 48
- up_second: float32 [2048, 8192], P('narrow', 'wide'), may hold values from 311.296 to 1245.184
- down_weight: float32 [8192, 2048], P('wide', 'narrow'), may hold values from -0.0625 to 0.0625
- down_first: float32 [8192, 2048], P('wide', 'narrow'), may hold values from -112 to 112
- down_second: float32 [8192, 2048], P('wide', 'narrow'), may hold values from 1474.56 to 5898.24
- norm_gains: float32 [2, 2048], replicated, may hold values from 0.5 to 1.5
- norm_first: float32 [2, 2048], replicated, may hold values from -160 to 160
- norm_second: float32 [2, 2048], replicated, may hold values from 3440.64 to 13762.56
- head_gains: float32 [2, 64], replicated, may hold values from 1 to 1.8
- head_first: float32 [2, 64], replicated, may hold values from -896 to 896
- head_second: float32 [2, 64], replicated, may hold values from 86835.2 to 344064
Outputs:
- block_out: bfloat16 [16384, 2048], P(('narrow', 'wide'))
- input_grad: float32 [16384, 2048], P(('narrow', 'wide'))
- query_new: float32 [2048, 2048], P('narrow', 'wide')
- query_first_new: float32 [2048, 2048], P('narrow', 'wide')
- query_second_new: float32 [2048, 2048], P('narrow', 'wide')
- key_new: float32 [2048, 512], P('narrow')
- key_first_new: float32 [2048, 512], P('narrow')
- key_second_new: float32 [2048, 512], P('narrow')
- value_new: float32 [2048, 512], P('narrow')
- value_first_new: float32 [2048, 512], P('narrow')
- value_second_new: float32 [2048, 512], P('narrow')
- output_new: float32 [2048, 2048], P('wide', 'narrow')
- output_first_new: float32 [2048, 2048], P('wide', 'narrow')
- output_second_new: float32 [2048, 2048], P('wide', 'narrow')
- gate_new: float32 [2048, 8192], P('narrow', 'wide')
- gate_first_new: float32 [2048, 8192], P('narrow', 'wide')
- gate_second_new: float32 [2048, 8192], P('narrow', 'wide')
- up_new: float32 [2048, 8192], P('narrow', 'wide')
- up_first_new: float32 [2048, 8192], P('narrow', 'wide')
- up_second_new: float32 [2048, 8192], P('narrow', 'wide')
- down_new: float32 [8192, 2048], P('wide', 'narrow')
- down_first_new: float32 [8192, 2048], P('wide', 'narrow')
- down_second_new: float32 [8192, 2048], P('wide', 'narrow')
- norm_new: float32 [2, 2048], replicated
- norm_first_new: float32 [2, 2048], replicated
- norm_second_new: float32 [2, 2048], replicated
- head_new: float32 [2, 64], replicated
- head_first_new: float32 [2, 64], replicated
- head_second_new: float32 [2, 64], replicated
Inputs may be any that keep to these rules, and one draw needn't show every extreme that they name: `positions`: within each sequence of 4096 tokens the ids rise by 1 or 2 from token to token; the steps and each sequence's first id differ from seed to seed.
All inputs are finite; a program needn't handle non-finite values.
Results may differ from a plain program's by a relative error of at most 0.028.
Values may be sent and summed in bfloat16 or wider, within the bound.
A program may use at most 384 MiB of HBM per device.

v0:
```python
import jax
import jax.numpy as jnp
from jax import lax
from jax.sharding import PartitionSpec as P

D = 2048
FF = 8192
SEQ_LEN = 4096
STEP = 10
O_FAN = 50


EPSILON = 1e-06
BETA_ONE = 0.9
BETA_TWO = 0.95
ADAM_EPSILON = 1e-08
WEIGHT_DECAY = 0.1
GAIN_RATE = 1.0
ROTARY_BASE = 10000.0
MASKED_SCORE = -1e30


def rms_scale(inputs, gain):
    return inputs * lax.rsqrt(jnp.mean(inputs * inputs, axis=-1, keepdims=True) + EPSILON) * gain


def rotate(inputs, cosine, sine_part):
    half_width = inputs.shape[-1] // 2
    first_half = inputs[..., :half_width]
    second_half = inputs[..., half_width:]
    return jnp.concatenate(
        [
            first_half * cosine - second_half * sine_part,
            second_half * cosine + first_half * sine_part,
        ],
        axis=-1,
    )


def adam_update(weight, first_moment, second_moment, gradient, rate, decay):
    first_new = BETA_ONE * first_moment + (1.0 - BETA_ONE) * gradient
    second_new = BETA_TWO * second_moment + (1.0 - BETA_TWO) * gradient * gradient
    ratio = (
        first_new
        / (1.0 - BETA_ONE**STEP)
        / (jnp.sqrt(second_new / (1.0 - BETA_TWO**STEP)) + ADAM_EPSILON)
    )
    return (weight - rate * (ratio + decay * weight), first_new, second_new)


def dot_last(left, right):
    return jnp.dot(left, right, preferred_element_type=jnp.float32)


def dot_first(left, right):
    return lax.dot_general(
        left, right, (((0,), (0,)), ((), ())), preferred_element_type=jnp.float32
    )


def dot_back(left, right):
    return lax.dot_general(
        left, right, (((1,), (1,)), ((), ())), preferred_element_type=jnp.float32
    )


def gather_rows(shard):
    return lax.all_gather(shard, "wide", axis=0, tiled=True)


def sum_back(pairs, row_count):
    summed = jnp.zeros((row_count * lax.axis_size("wide"), pairs[0][1].shape[0]), jnp.float32)
    for gradient, weight in pairs:
        summed = summed + dot_back(gradient, weight)
    return lax.psum_scatter(
        summed.astype(jnp.bfloat16), "wide", scatter_dimension=0, tiled=True
    ).astype(jnp.float32)


def shards(
    tokens_in,
    out_grad,
    positions,
    query_weight,
    query_first,
    query_second,
    key_weight,
    key_first,
    key_second,
    value_weight,
    value_first,
    value_second,
    output_weight,
    output_first,
    output_second,
    gate_weight,
    gate_first,
    gate_second,
    up_weight,
    up_first,
    up_second,
    down_weight,
    down_first,
    down_second,
    norm_gains,
    norm_first,
    norm_second,
    head_gains,
    head_first,
    head_second,
):
    wide_count = lax.axis_size("wide")
    wide_rank = lax.axis_index("wide")
    narrow_count = lax.axis_size("narrow")
    narrow_rank = lax.axis_index("narrow")
    head_dim = head_gains.shape[1]
    key_heads = key_weight.shape[1] // head_dim
    local_heads = query_weight.shape[1] // head_dim
    shard_rows = tokens_in.shape[0]
    copies = wide_count // key_heads
    query_full, key_full, value_full, output_local, gate_local, up_local, down_local = (
        lax.all_gather(query_weight.astype(jnp.bfloat16), "narrow", axis=0, tiled=True),
        lax.all_gather(key_weight.astype(jnp.bfloat16), "narrow", axis=0, tiled=True),
        lax.all_gather(value_weight.astype(jnp.bfloat16), "narrow", axis=0, tiled=True),
        lax.all_gather(output_weight.astype(jnp.bfloat16), "narrow", axis=1, tiled=True),
        lax.all_gather(gate_weight.astype(jnp.bfloat16), "narrow", axis=0, tiled=True),
        lax.all_gather(up_weight.astype(jnp.bfloat16), "narrow", axis=0, tiled=True),
        lax.all_gather(down_weight.astype(jnp.bfloat16), "narrow", axis=1, tiled=True),
    )
    key_slot = wide_rank // copies
    key_local = lax.dynamic_slice_in_dim(key_full, key_slot * head_dim, head_dim, 1)
    value_local = lax.dynamic_slice_in_dim(value_full, key_slot * head_dim, head_dim, 1)
    inverse = jnp.power(ROTARY_BASE, -2.0 * jnp.arange(head_dim // 2, dtype=jnp.float32) / head_dim)
    angles = positions.astype(jnp.float32)[:, None] * inverse[None, :]
    cosine = jnp.cos(angles)
    sine_part = jnp.sin(angles)
    residual = tokens_in.astype(jnp.float32)
    normed_in, norm_in_back = jax.vjp(rms_scale, residual, norm_gains[0])
    rows_in = gather_rows(normed_in.astype(jnp.bfloat16))
    total_rows = rows_in.shape[0]
    model_width = rows_in.shape[1]
    query_raw = dot_last(rows_in, query_full).reshape(total_rows, local_heads, head_dim)
    key_raw = dot_last(rows_in, key_local)
    value_rows = dot_last(rows_in, value_local).astype(jnp.bfloat16)

    def query_turn(raw_heads, gain):
        return rotate(rms_scale(raw_heads, gain), cosine[:, None, :], sine_part[:, None, :])

    def key_turn(raw_heads, gain):
        return rotate(rms_scale(raw_heads, gain), cosine, sine_part)

    query_rot, query_back = jax.vjp(query_turn, query_raw, head_gains[0])
    key_rot, key_back = jax.vjp(key_turn, key_raw, head_gains[1])
    query_rot = query_rot.astype(jnp.bfloat16)
    key_rot = key_rot.astype(jnp.bfloat16)
    block_rows = min(512, SEQ_LEN)
    sequence_blocks = SEQ_LEN // block_rows
    block_count = total_rows // block_rows
    score_scale = head_dim ** (-0.5)
    offsets = jnp.arange(block_rows)

    def score_block(query_block, key_block, row_index, key_index):
        products = jnp.einsum(
            "qhd,kd->hqk", query_block, key_block, preferred_element_type=jnp.float32
        )
        allowed = (row_index * block_rows + offsets)[:, None] >= (key_index * block_rows + offsets)[
            None, :
        ]
        return jnp.where(allowed[None], products * score_scale, MASKED_SCORE)

    def attend(row_index):
        query_block = lax.dynamic_slice_in_dim(query_rot, row_index * block_rows, block_rows, 0)
        first_index = row_index // sequence_blocks * sequence_blocks

        def find_top(key_index, running):
            key_block = lax.dynamic_slice_in_dim(key_rot, key_index * block_rows, block_rows, 0)
            return jnp.maximum(
                running, jnp.max(score_block(query_block, key_block, row_index, key_index), axis=-1)
            )

        row_top = jnp.floor(
            lax.fori_loop(
                first_index,
                row_index + 1,
                find_top,
                jnp.full((local_heads, block_rows), MASKED_SCORE, jnp.float32),
            )
        )

        def accumulate(key_index, carried):
            weight_sum, summed = carried
            key_block = lax.dynamic_slice_in_dim(key_rot, key_index * block_rows, block_rows, 0)
            value_block = lax.dynamic_slice_in_dim(
                value_rows, key_index * block_rows, block_rows, 0
            )
            exponent = jnp.exp(
                score_block(query_block, key_block, row_index, key_index) - row_top[:, :, None]
            )
            summed = summed + jnp.einsum(
                "hqk,kd->qhd",
                exponent.astype(jnp.bfloat16),
                value_block,
                preferred_element_type=jnp.float32,
            )
            return (weight_sum + jnp.sum(exponent, axis=-1), summed)

        weight_sum, summed = lax.fori_loop(
            first_index,
            row_index + 1,
            accumulate,
            (
                jnp.zeros((local_heads, block_rows), jnp.float32),
                jnp.zeros((block_rows, local_heads, head_dim), jnp.float32),
            ),
        )
        return (row_top, weight_sum, summed / jnp.transpose(weight_sum)[:, :, None])

    row_tops, weight_sums, attended = lax.map(attend, jnp.arange(block_count))
    attended = attended.reshape(total_rows, local_heads * head_dim)
    attended_low = attended.astype(jnp.bfloat16)
    branch = lax.psum_scatter(
        dot_last(attended_low, output_local).astype(jnp.bfloat16),
        "wide",
        scatter_dimension=0,
        tiled=True,
    ).astype(jnp.float32)
    middle = residual + branch
    normed_mid, norm_mid_back = jax.vjp(rms_scale, middle, norm_gains[1])
    rows_mid = gather_rows(normed_mid.astype(jnp.bfloat16))
    gate_pre = dot_last(rows_mid, gate_local)
    up_pre = dot_last(rows_mid, up_local)
    hidden, hidden_back = jax.vjp(
        lambda gate_in, up_in: jax.nn.silu(gate_in) * up_in, gate_pre, up_pre
    )
    hidden_low = hidden.astype(jnp.bfloat16)
    block_out = (
        middle
        + lax.psum_scatter(
            dot_last(hidden_low, down_local).astype(jnp.bfloat16),
            "wide",
            scatter_dimension=0,
            tiled=True,
        ).astype(jnp.float32)
    ).astype(jnp.bfloat16)
    grad_rows = lax.all_gather(out_grad, "wide", axis=0, tiled=True)
    hidden_grad = dot_back(grad_rows, down_local).astype(jnp.bfloat16)
    down_grad = dot_first(hidden_low, grad_rows)
    gate_grad, up_grad = hidden_back(hidden_grad.astype(jnp.float32))
    gate_grad = gate_grad.astype(jnp.bfloat16)
    up_grad = up_grad.astype(jnp.bfloat16)
    gate_wgrad = dot_first(rows_mid, gate_grad)
    up_wgrad = dot_first(rows_mid, up_grad)
    mid_back = sum_back(((gate_grad, gate_local), (up_grad, up_local)), shard_rows)
    middle_part, mid_gain_grad = norm_mid_back(mid_back)
    middle_grad = out_grad.astype(jnp.float32) + middle_part
    branch_grad = middle_grad.astype(jnp.bfloat16)
    branch_rows = lax.all_gather(branch_grad, "wide", axis=0, tiled=True)
    attended_grad = dot_back(branch_rows, output_local).astype(jnp.bfloat16)
    output_wgrad = dot_first(attended_low, branch_rows)
    head_grad = attended_grad.astype(jnp.float32).reshape(total_rows, local_heads, head_dim)
    sums_rows = jnp.transpose(weight_sums, (0, 2, 1)).reshape(total_rows, local_heads)
    scaled_grad = (head_grad / sums_rows[:, :, None]).astype(jnp.bfloat16)
    grad_dot = (
        jnp.sum(head_grad * attended.reshape(total_rows, local_heads, head_dim), axis=-1)
        / sums_rows
    )

    def back_block(carried, row_index):
        key_sum, value_sum = carried
        query_block = lax.dynamic_slice_in_dim(query_rot, row_index * block_rows, block_rows, 0)
        grad_block = lax.dynamic_slice_in_dim(scaled_grad, row_index * block_rows, block_rows, 0)
        dot_block = jnp.transpose(
            lax.dynamic_slice_in_dim(grad_dot, row_index * block_rows, block_rows, 0)
        )
        row_top = row_tops[row_index]
        first_index = row_index // sequence_blocks * sequence_blocks

        def key_step(key_index, running):
            query_sum, key_total, value_total = running
            key_start = key_index * block_rows
            key_block = lax.dynamic_slice_in_dim(key_rot, key_start, block_rows, 0)
            value_block = lax.dynamic_slice_in_dim(value_rows, key_start, block_rows, 0)
            exponent = jnp.exp(
                score_block(query_block, key_block, row_index, key_index) - row_top[:, :, None]
            )
            prob_grad = jnp.einsum(
                "qhd,kd->hqk", grad_block, value_block, preferred_element_type=jnp.float32
            )
            score_grad = (score_scale * exponent * (prob_grad - dot_block[:, :, None])).astype(
                jnp.bfloat16
            )
            query_sum = query_sum + jnp.einsum(
                "hqk,kd->qhd", score_grad, key_block, preferred_element_type=jnp.float32
            )
            key_part = jnp.einsum(
                "hqk,qhd->kd", score_grad, query_block, preferred_element_type=jnp.float32
            )
            value_part = jnp.einsum(
                "hqk,qhd->kd",
                exponent.astype(jnp.bfloat16),
                grad_block,
                preferred_element_type=jnp.float32,
            )
            key_total = lax.dynamic_update_slice_in_dim(
                key_total,
                lax.dynamic_slice_in_dim(key_total, key_start, block_rows, 0) + key_part,
                key_start,
                0,
            )
            value_total = lax.dynamic_update_slice_in_dim(
                value_total,
                lax.dynamic_slice_in_dim(value_total, key_start, block_rows, 0) + value_part,
                key_start,
                0,
            )
            return (query_sum, key_total, value_total)

        query_sum, key_sum, value_sum = lax.fori_loop(
            first_index,
            row_index + 1,
            key_step,
            (jnp.zeros((block_rows, local_heads, head_dim), jnp.float32), key_sum, value_sum),
        )
        return ((key_sum, value_sum), query_sum)

    zero_rows = jnp.zeros((total_rows, head_dim), jnp.float32)
    (key_rot_grad, value_grad), query_blocks = lax.scan(
        back_block, (zero_rows, zero_rows), jnp.arange(block_count)
    )
    query_rot_grad = query_blocks.reshape(total_rows, local_heads, head_dim)
    query_raw_grad, query_gain_grad = query_back(query_rot_grad)
    key_raw_grad, key_gain_grad = key_back(key_rot_grad)
    query_low = query_raw_grad.reshape(total_rows, local_heads * head_dim).astype(jnp.bfloat16)
    key_low = key_raw_grad.astype(jnp.bfloat16)
    value_low = value_grad.astype(jnp.bfloat16)
    query_wgrad = dot_first(rows_in, query_low)
    key_wgrad = dot_first(rows_in, key_low)
    value_wgrad = dot_first(rows_in, value_low)
    input_back = sum_back(
        ((query_low, query_full), (key_low, key_local), (value_low, value_local)), shard_rows
    )
    input_part, in_gain_grad = norm_in_back(input_back)
    input_grad = middle_grad + input_part
    own_rows = model_width // narrow_count
    gain_stack = jnp.stack([in_gain_grad, mid_gain_grad])
    head_stack = jnp.stack([query_gain_grad, key_gain_grad])
    key_spread = lax.dynamic_update_slice_in_dim(
        jnp.zeros((model_width, key_heads * head_dim), jnp.float32),
        key_wgrad,
        key_slot * head_dim,
        1,
    )
    value_spread = lax.dynamic_update_slice_in_dim(
        jnp.zeros((model_width, key_heads * head_dim), jnp.float32),
        value_wgrad,
        key_slot * head_dim,
        1,
    )
    key_total, value_total, gain_total, head_total = lax.psum(
        (key_spread, value_spread, gain_stack, head_stack), ("narrow", "wide")
    )
    key_total = lax.dynamic_slice_in_dim(key_total, narrow_rank * own_rows, own_rows, 0)
    value_total = lax.dynamic_slice_in_dim(value_total, narrow_rank * own_rows, own_rows, 0)
    query_total, output_total, gate_total, up_total, down_total = (
        lax.psum_scatter(
            query_wgrad.astype(jnp.bfloat16), "narrow", scatter_dimension=0, tiled=True
        ).astype(jnp.float32),
        lax.psum_scatter(
            output_wgrad.astype(jnp.bfloat16), "narrow", scatter_dimension=1, tiled=True
        ).astype(jnp.float32),
        lax.psum_scatter(
            gate_wgrad.astype(jnp.bfloat16), "narrow", scatter_dimension=0, tiled=True
        ).astype(jnp.float32),
        lax.psum_scatter(
            up_wgrad.astype(jnp.bfloat16), "narrow", scatter_dimension=0, tiled=True
        ).astype(jnp.float32),
        lax.psum_scatter(
            down_grad.astype(jnp.bfloat16), "narrow", scatter_dimension=1, tiled=True
        ).astype(jnp.float32),
    )
    wide_rate = D ** (-0.5)
    query_new = adam_update(
        query_weight, query_first, query_second, query_total, wide_rate, WEIGHT_DECAY
    )
    key_new = adam_update(key_weight, key_first, key_second, key_total, wide_rate, WEIGHT_DECAY)
    value_new = adam_update(
        value_weight, value_first, value_second, value_total, wide_rate, WEIGHT_DECAY
    )
    output_new = adam_update(
        output_weight, output_first, output_second, output_total, O_FAN ** (-0.5), WEIGHT_DECAY
    )
    gate_new = adam_update(
        gate_weight, gate_first, gate_second, gate_total, wide_rate, WEIGHT_DECAY
    )
    up_new = adam_update(up_weight, up_first, up_second, up_total, wide_rate, WEIGHT_DECAY)
    down_new = adam_update(
        down_weight, down_first, down_second, down_total, FF ** (-0.5), WEIGHT_DECAY
    )
    norm_new = adam_update(norm_gains, norm_first, norm_second, gain_total, GAIN_RATE, 0.0)
    head_new = adam_update(head_gains, head_first, head_second, head_total, GAIN_RATE, 0.0)
    return (
        block_out,
        input_grad,
        query_new[0],
        query_new[1],
        query_new[2],
        key_new[0],
        key_new[1],
        key_new[2],
        value_new[0],
        value_new[1],
        value_new[2],
        output_new[0],
        output_new[1],
        output_new[2],
        gate_new[0],
        gate_new[1],
        gate_new[2],
        up_new[0],
        up_new[1],
        up_new[2],
        down_new[0],
        down_new[1],
        down_new[2],
        norm_new[0],
        norm_new[1],
        norm_new[2],
        head_new[0],
        head_new[1],
        head_new[2],
    )


def solution(mesh):
    return jax.shard_map(
        shards,
        mesh=mesh,
        in_specs=(
            P(("narrow", "wide"), None),
            P(("narrow", "wide"), None),
            P("narrow"),
            P("narrow", "wide"),
            P("narrow", "wide"),
            P("narrow", "wide"),
            P("narrow", None),
            P("narrow", None),
            P("narrow", None),
            P("narrow", None),
            P("narrow", None),
            P("narrow", None),
            P("wide", "narrow"),
            P("wide", "narrow"),
            P("wide", "narrow"),
            P("narrow", "wide"),
            P("narrow", "wide"),
            P("narrow", "wide"),
            P("narrow", "wide"),
            P("narrow", "wide"),
            P("narrow", "wide"),
            P("wide", "narrow"),
            P("wide", "narrow"),
            P("wide", "narrow"),
            P(),
            P(),
            P(),
            P(),
            P(),
            P(),
        ),
        out_specs=(
            P(("narrow", "wide"), None),
            P(("narrow", "wide"), None),
            P("narrow", "wide"),
            P("narrow", "wide"),
            P("narrow", "wide"),
            P("narrow", None),
            P("narrow", None),
            P("narrow", None),
            P("narrow", None),
            P("narrow", None),
            P("narrow", None),
            P("wide", "narrow"),
            P("wide", "narrow"),
            P("wide", "narrow"),
            P("narrow", "wide"),
            P("narrow", "wide"),
            P("narrow", "wide"),
            P("narrow", "wide"),
            P("narrow", "wide"),
            P("narrow", "wide"),
            P("wide", "narrow"),
            P("wide", "narrow"),
            P("wide", "narrow"),
            P(),
            P(),
            P(),
            P(),
            P(),
            P(),
        ),
        check_vma=False,
    )
```

profile of v0, /device:TPU:0, one launch (start us, length us, event | category | flops | bytes accessed | tf_op | source)
XLA Modules:
  0.0 2655.9 jit_solution(7042825772845878004)
XLA Ops:
  18.7 29.9 %all-gather.16.cloned.1.call-done = bf16[2048,512]{1,0:T(8,128)(2,1)} async-done(((bf16[512,512]{1,0:T(8,128)(2,1)}), bf16[2048,512]{1,0:T(8,128)(2,1)}) %all-gather.16.cloned.1.call-update) | async-done | bytes 2097168 | tf_op jit(solution)/shard_map/all_gather | solution.py:123
  48.5 153.3 %all-gather.12.cloned.1.call-done = bf16[4096,2048]{1,0:T(8,128)(2,1)} async-done(((bf16[512,2048]{1,0:T(8,128)(2,1)}), bf16[4096,2048]{1,0:T(8,128)(2,1)}) %all-gather.12.cloned.1.call-update) | async-done | bytes 16777232 | tf_op jit(solution)/shard_map/all_gather | solution.py:68
  278.6 229.5 %while.115 = (s32[]{:T(128)}, f32[8,4,512]{2,1,0:T(4,128)S(1)}, f32[8,4,512]{2,1,0:T(4,128)}, f32[8,512,4,64]{1,3,2,0:T(8,128)}, s32[8]{0:T(128)S(1)}, /*index=5...) while((s32[]{:T(128)}, f32[8,4,512]{2,1,0:T(4,128)S(1)}, ...), condition=%wide.region_10.11_spmd.clone.clone, body=%wide.region_3.10_spmd.clone.clone.sunk | while | flops 414980096 | bytes 13745191 | solution.py:218
  433.3 27.1 %while.119 = (s32[]{:T(128)}, f32[4,512]{1,0:T(4,128)S(1)}, f32[512,4,64]{0,2,1:T(8,128)S(1)}, s32[]{:T(128)}, s32[]{:T(128)}, /*index=5*/s32[512]{0:T(512)S(1)}...) while((s32[]{:T(128)}, f32[4,512]{1,0:T(4,128)S(1)}, ...), condition=%wide.region_9.9_spmd.clone, body=%wide.region_7.8_spmd.clone.sunk | while | flops 277218304 | bytes 10676419 | solution.py:207
  475.6 30.9 %while.119 = (s32[]{:T(128)}, f32[4,512]{1,0:T(4,128)S(1)}, f32[512,4,64]{0,2,1:T(8,128)S(1)}, s32[]{:T(128)}, s32[]{:T(128)}, /*index=5*/s32[512]{0:T(512)S(1)}...) while((s32[]{:T(128)}, f32[4,512]{1,0:T(4,128)S(1)}, ...), condition=%wide.region_9.9_spmd.clone, body=%wide.region_7.8_spmd.clone.sunk | while | flops 277218304 | bytes 10676419 | solution.py:207
  530.2 162.1 %reduce-scatter.10.cloned.1.call-done = bf16[512,2048]{1,0:T(8,128)(2,1)} async-done(((bf16[4096,2048]{1,0:T(8,128)(2,1)}), bf16[512,2048]{1,0:T(8,128)(2,1)}) %reduce-scatter.10.cloned.1.call-update) | async-done | bytes 2097168 | tf_op jit(solution)/shard_map/reduce_scatter | solution.py:221
  701.4 44.2 %all-gather.28.cloned.1.call-done = bf16[1024,2048]{1,0:T(8,128)(2,1)} async-done(((bf16[1024,512]{1,0:T(8,128)(2,1)}), bf16[1024,2048]{1,0:T(8,128)(2,1)}) %all-gather.28.cloned.1.call-update) | async-done | bytes 4194320 | tf_op jit(solution)/shard_map/all_gather | solution.py:128
  745.6 152.7 %all-gather.30.cloned.1.call-done = bf16[4096,2048]{1,0:T(8,128)(2,1)} async-done(((bf16[512,2048]{1,0:T(8,128)(2,1)}), bf16[4096,2048]{1,0:T(8,128)(2,1)}) %all-gather.30.cloned.1.call-update) | async-done | bytes 16777232 | tf_op jit(solution)/shard_map/all_gather | solution.py:245
  898.4 23.5 convolution_convert_fusion.2
  921.9 29.9 %all-gather.26.cloned.1.call-done = bf16[2048,1024]{1,0:T(8,128)(2,1)} async-done(((bf16[512,1024]{1,0:T(8,128)(2,1)}), bf16[2048,1024]{1,0:T(8,128)(2,1)}) %all-gather.26.cloned.1.call-update) | async-done | bytes 4194320 | tf_op jit(solution)/shard_map/all_gather | solution.py:127
  951.8 153.2 %all-gather.22.cloned.1.call-done = bf16[4096,2048]{1,0:T(8,128)(2,1)} async-done(((bf16[512,2048]{1,0:T(8,128)(2,1)}), bf16[4096,2048]{1,0:T(8,128)(2,1)}) %all-gather.22.cloned.1.call-update) | async-done | bytes 16777232 | tf_op jit(solution)/shard_map/all_gather | solution.py:68
  1128.3 30.0 %all-gather.24.cloned.1.call-done = bf16[2048,1024]{1,0:T(8,128)(2,1)} async-done(((bf16[512,1024]{1,0:T(8,128)(2,1)}), bf16[2048,1024]{1,0:T(8,128)(2,1)}) %all-gather.24.cloned.1.call-update) | async-done | bytes 4194320 | tf_op jit(solution)/shard_map/all_gather | solution.py:126
  1158.3 35.6 %fusion.65 = (bf16[4096,1024]{1,0:T(8,128)(2,1)}, bf16[4096,1024]{1,0:T(8,128)(2,1)}, bf16[4096,1024]{1,0:T(8,128)(2,1)}) fusion(f32[4096,1024]{1,0:T(8,128)} %fusion.145, bf16[4096,1024]{1,0:T(8,128)(2,1)} %convolution_convert_fusion.2, bf16[4096,2048]{1,0:T(8,128)(2,1)} %all-gather.22.cloned.1.call-done, bf16[2048,1024]{1,0:T(8,128)(2,1)} %all-gather.24.cloned.1.call-done), kind=kOutput, calls=%fused_computation.79 | convolution fusion | flops 17251172352 | bytes 71303168 | tf_op jit(solution)/shard_map/dot_general | solution.py:52
  1193.9 25.8 fusion.146
  1219.7 26.6 %add_convert_fusion.1 = bf16[4096,2048]{1,0:T(8,128)(2,1)} fusion(f32[4096,2048]{1,0:T(8,128)} %fusion.146, bf16[4096,1024]{1,0:T(8,128)(2,1)} %get-tuple-element.1083, bf16[2048,1024]{1,0:T(8,128)(2,1)S(1)} %copy-done.77), kind=kOutput, calls=%fused_computation.72 | convolution fusion | flops 17196646400 | bytes 62914560 | tf_op jit(solution)/shard_map/dot_general | solution.py:62
  1246.5 168.2 %reduce-scatter.14.cloned.1.call-done = bf16[512,2048]{1,0:T(8,128)(2,1)} async-done(((bf16[4096,2048]{1,0:T(8,128)(2,1)}), bf16[512,2048]{1,0:T(8,128)(2,1)}) %reduce-scatter.14.cloned.1.call-update) | async-done | bytes 2097168 | tf_op jit(solution)/shard_map/reduce_scatter | solution.py:75
  1423.8 23.7 convolution_convert_fusion.7
  1447.6 23.9 convolution_convert_fusion.6
  1476.5 23.8 convolution_convert_fusion.5
  1500.6 72.8 %all-gather.32.cloned.1.call-done = bf16[4096,2048]{1,0:T(8,128)(2,1)} async-done(((bf16[512,2048]{1,0:T(8,128)(2,1)}), bf16[4096,2048]{1,0:T(8,128)(2,1)}) %all-gather.32.cloned.1.call-update) | async-done | bytes 16777232 | tf_op jit(solution)/shard_map/all_gather | solution.py:257
  1593.2 433.7 %while.117 = (s32[]{:T(128)}, f32[4096,64]{0,1:T(8,128)S(1)}, f32[4096,64]{0,1:T(8,128)S(1)}, f32[8,512,4,64]{1,0,3,2:T(8,128)}, s32[8]{0:T(128)S(1)}, /*index=5...) while((s32[]{:T(128)}, f32[4096,64]{0,1:T(8,128)S(1)}, ...), condition=%wide.region_20.21_spmd.clone.clone, body=%wide.region_17.20_spmd.clone.clone.sunk | while | flops 683082752 | bytes 26219360 | solution.py:327
  1706.2 30.7 %while.120 = (s32[]{:T(128)}, f32[512,4,64]{0,2,1:T(8,128)S(1)}, f32[4096,64]{0,1:T(8,128)S(1)}, f32[4096,64]{0,1:T(8,128)S(1)}, s32[]{:T(128)}, /*index=5*/bf16...) while((s32[]{:T(128)}, f32[512,4,64]{0,2,1:T(8,128)S(1)}, ...), condition=%wide.region_19.19_spmd.clone, body=%wide.region_18.18_spmd.clone.sunk | while | flops 683082752 | bytes 22513896 | solution.py:318
  1756.6 38.3 %while.120 = (s32[]{:T(128)}, f32[512,4,64]{0,2,1:T(8,128)S(1)}, f32[4096,64]{0,1:T(8,128)S(1)}, f32[4096,64]{0,1:T(8,128)S(1)}, s32[]{:T(128)}, /*index=5*/bf16...) while((s32[]{:T(128)}, f32[512,4,64]{0,2,1:T(8,128)S(1)}, ...), condition=%wide.region_19.19_spmd.clone, body=%wide.region_18.18_spmd.clone.sunk | while | flops 683082752 | bytes 22513896 | solution.py:318
  1814.6 46.0 %while.120 = (s32[]{:T(128)}, f32[512,4,64]{0,2,1:T(8,128)S(1)}, f32[4096,64]{0,1:T(8,128)S(1)}, f32[4096,64]{0,1:T(8,128)S(1)}, s32[]{:T(128)}, /*index=5*/bf16...) while((s32[]{:T(128)}, f32[512,4,64]{0,2,1:T(8,128)S(1)}, ...), condition=%wide.region_19.19_spmd.clone, body=%wide.region_18.18_spmd.clone.sunk | while | flops 683082752 | bytes 22513896 | solution.py:318
  1880.2 53.6 %while.120 = (s32[]{:T(128)}, f32[512,4,64]{0,2,1:T(8,128)S(1)}, f32[4096,64]{0,1:T(8,128)S(1)}, f32[4096,64]{0,1:T(8,128)S(1)}, s32[]{:T(128)}, /*index=5*/bf16...) while((s32[]{:T(128)}, f32[512,4,64]{0,2,1:T(8,128)S(1)}, ...), condition=%wide.region_19.19_spmd.clone, body=%wide.region_18.18_spmd.clone.sunk | while | flops 683082752 | bytes 22513896 | solution.py:318
  1953.6 61.3 %while.120 = (s32[]{:T(128)}, f32[512,4,64]{0,2,1:T(8,128)S(1)}, f32[4096,64]{0,1:T(8,128)S(1)}, f32[4096,64]{0,1:T(8,128)S(1)}, s32[]{:T(128)}, /*index=5*/bf16...) while((s32[]{:T(128)}, f32[512,4,64]{0,2,1:T(8,128)S(1)}, ...), condition=%wide.region_19.19_spmd.clone, body=%wide.region_18.18_spmd.clone.sunk | while | flops 683082752 | bytes 22513896 | solution.py:318
  2133.8 29.7 %add_convert_fusion = bf16[4096,2048]{1,0:T(8,128)(2,1)} fusion(f32[4096,2048]{1,0:T(8,128)} %fusion.109, f32[4096,2048]{1,0:T(8,128)} %fusion.112, bf16[4096,256]{0,1:T(8,128)(2,1)S(1)} %bitcast.242, bf16[2048,256]{1,0:T(8,128)(2,1)} %all-gather.14.cloned.1.call-done), kind=kOutput, calls=%fused_computation.71 | convolution fusion | flops 4320133120 | bytes 87031808 | tf_op jit(solution)/shard_map/dot_general | solution.py:62
  2163.6 23.7 convolution_convert_fusion
  2215.1 84.7 %all-reduce.8.cloned.1.call-done = (f32[2048,512]{1,0:T(8,128)}, f32[2048,512]{1,0:T(8,128)}) async-done(((f32[2048,512]{1,0:T(8,128)}, f32[2048,512]{1,0:T(8,128)}), (f32[2048,512]{1,0:T(8,128)}, f32[2048,512]{1,0:T(8,128)})) %all-reduce.8.cloned.1.call-update) | async-done | bytes 8388624 | tf_op jit(solution)/shard_map/psum | solution.py:359
  2307.1 163.4 %reduce-scatter.16.cloned.1.call-done = bf16[512,2048]{1,0:T(8,128)(2,1)} async-done(((bf16[4096,2048]{1,0:T(8,128)(2,1)}), bf16[512,2048]{1,0:T(8,128)(2,1)}) %reduce-scatter.16.cloned.1.call-update) | async-done | bytes 2097168 | tf_op jit(solution)/shard_map/reduce_scatter | solution.py:75
  2473.8 40.0 %all-reduce.4 = (f32[2,2048]{1,0:T(2,128)S(1)}, f32[2,64]{1,0:T(2,128)S(1)}) all-reduce(f32[2,2048]{1,0:T(2,128)S(1)} %pad_maximum_fusion.2, f32[2,64]{1,0:T(2,128)S(1)} %pad_maximum_fusion.3), channel_id=1, replica_groups=mesh['narrow'=4,'wide'=8] {'narrow','wide'}, use_global_device_ids=true, to_apply=%region_34.35 | all-reduce | flops 4224 | bytes 33792 | tf_op jit(solution)/shard_map/psum | solution.py:359
  2515.2 125.5 %reduce-scatter.12.cloned.1.call-done = bf16[512,2048]{1,0:T(8,128)(2,1)} async-done(((bf16[4096,2048]{1,0:T(8,128)(2,1)}), bf16[512,2048]{1,0:T(8,128)(2,1)}) %reduce-scatter.12.cloned.1.call-update) | async-done | bytes 2097168 | tf_op jit(solution)/shard_map/reduce_scatter | solution.py:238
  (1024 shorter events, 1082.9 us)
Async XLA Ops:
  7.2 41.3 %all-gather.16.cloned.1.call-start = ((), (), s32[]{:S(2)}) async-start(), calls=%async_computation.11 | async-start | bytes 2621440 | tf_op jit(solution)/shard_map/all_gather | solution.py:123
  9.5 192.3 %all-gather.12.cloned.1.call-start = ((), (), s32[]{:S(2)}) async-start(), calls=%async_computation.9 | async-start | bytes 18874368 | tf_op jit(solution)/shard_map/all_gather | solution.py:68
  14.8 214.3 %all-gather.14.cloned.1.call-start = ((), (), s32[]{:S(2)}) async-start(), calls=%async_computation.10 | async-start | bytes 1310720 | tf_op jit(solution)/shard_map/all_gather | solution.py:122
  16.7 250.1 %all-gather.18.cloned.1.call-start = ((), (), s32[]{:S(2)}) async-start(), calls=%async_computation.12 | async-start | bytes 2621440 | tf_op jit(solution)/shard_map/all_gather | solution.py:124
  17.6 496.1 %all-gather.20.cloned.1.call-start = ((), (), s32[]{:S(2)}) async-start(), calls=%async_computation.13 | async-start | bytes 1310720 | tf_op jit(solution)/shard_map/all_gather | solution.py:125
  18.5 673.8 %reduce-scatter.10.cloned.1.call-start = ((), (), s32[]{:S(2)}) async-start(), calls=%async_computation.14 | async-start | bytes 18874368 | tf_op jit(solution)/shard_map/reduce_scatter | solution.py:221
  18.5 223.7 %copy-start.72 = (f32[32]{0:T(128)}, f32[32]{0:T(128)S(1)}, u32[]{:S(2)}) copy-start(f32[32]{0:T(128)S(1)} %multiply_power_fusion) | copy-start | bytes 388
  18.6 223.3 %copy-start.67 = (f32[64]{0:T(128)}, f32[64]{0:T(128)S(1)}, u32[]{:S(2)}) copy-start(f32[64]{0:T(128)S(1)} %get-tuple-element.1098) | copy-start | bytes 772
  18.6 226.3 %copy-start.65 = (f32[64]{0:T(128)}, f32[64]{0:T(128)S(1)}, u32[]{:S(2)}) copy-start(f32[64]{0:T(128)S(1)} %get-tuple-element.1099) | copy-start | bytes 772
  18.6 223.6 %copy-start.41 = (f32[4096]{0:T(1024)}, f32[4096]{0:T(1024)S(1)}, u32[]{:S(2)}) copy-start(f32[4096]{0:T(1024)S(1)} %convert_element_type.159) | copy-start | bytes 49156
  523.9 221.7 %all-gather.28.cloned.1.call-start = ((), (), s32[]{:S(2)}) async-start(), calls=%async_computation.18 | async-start | bytes 5242880 | tf_op jit(solution)/shard_map/all_gather | solution.py:128
  526.6 371.8 %all-gather.30.cloned.1.call-start = ((), (), s32[]{:S(2)}) async-start(), calls=%async_computation.20 | async-start | bytes 18874368 | tf_op jit(solution)/shard_map/all_gather | solution.py:245
  527.4 424.4 %all-gather.26.cloned.1.call-start = ((), (), s32[]{:S(2)}) async-start(), calls=%async_computation.17 | async-start | bytes 5242880 | tf_op jit(solution)/shard_map/all_gather | solution.py:127
  530.2 574.8 %all-gather.22.cloned.1.call-start = ((), (), s32[]{:S(2)}) async-start(), calls=%async_computation.15 | async-start | bytes 18874368 | tf_op jit(solution)/shard_map/all_gather | solution.py:68
  698.3 460.0 %all-gather.24.cloned.1.call-start = ((), (), s32[]{:S(2)}) async-start(), calls=%async_computation.16 | async-start | bytes 5242880 | tf_op jit(solution)/shard_map/all_gather | solution.py:126
  701.3 713.4 %reduce-scatter.14.cloned.1.call-start = ((), (), s32[]{:S(2)}) async-start(), calls=%async_computation.21 | async-start | bytes 18874368 | tf_op jit(solution)/shard_map/reduce_scatter | solution.py:75
  1246.3 327.0 %all-gather.32.cloned.1.call-start = ((), (), s32[]{:S(2)}) async-start(), calls=%async_computation.22 | async-start | bytes 18874368 | tf_op jit(solution)/shard_map/all_gather | solution.py:257
  1423.7 763.7 %reduce-scatter.22.cloned.1.call-start = ((), (), s32[]{:S(2)}) async-start(), calls=%async_computation.26 | async-start | bytes 5242880 | tf_op jit(solution)/shard_map/reduce_scatter | solution.py:371
  1447.5 748.0 %reduce-scatter.24.cloned.1.call-start = ((), (), s32[]{:S(2)}) async-start(), calls=%async_computation.27 | async-start | bytes 5242880 | tf_op jit(solution)/shard_map/reduce_scatter | solution.py:374
  1471.5 731.4 %reduce-scatter.26.cloned.1.call-start = ((), (), s32[]{:S(2)}) async-start(), calls=%async_computation.28 | async-start | bytes 5242880 | tf_op jit(solution)/shard_map/reduce_scatter | solution.py:377
  1500.3 709.0 %reduce-scatter.18.cloned.1.call-start = ((), (), s32[]{:S(2)}) async-start(), calls=%async_computation.24 | async-start | bytes 1310720 | tf_op jit(solution)/shard_map/reduce_scatter | solution.py:365
  2056.1 156.2 %reduce-scatter.20.cloned.1.call-start = ((), (), s32[]{:S(2)}) async-start(), calls=%async_computation.25 | async-start | bytes 1310720 | tf_op jit(solution)/shard_map/reduce_scatter | solution.py:368
  2070.1 229.7 %all-reduce.8.cloned.1.call-start = ((), (), s32[]{:S(2)}) async-start(), calls=%async_computation.29 | async-start | bytes 16777216 | tf_op jit(solution)/shard_map/psum | solution.py:359
  2103.5 367.0 %reduce-scatter.16.cloned.1.call-start = ((), (), s32[]{:S(2)}) async-start(), calls=%async_computation.23 | async-start | bytes 18874368 | tf_op jit(solution)/shard_map/reduce_scatter | solution.py:75
  2163.6 477.1 %reduce-scatter.12.cloned.1.call-start = ((), (), s32[]{:S(2)}) async-start(), calls=%async_computation.19 | async-start | bytes 18874368 | tf_op jit(solution)/shard_map/reduce_scatter | solution.py:238
  2307.0 206.9 %copy-start.75 = (f32[2,64]{1,0:T(2,128)S(1)}, f32[2,64]{1,0:T(2,128)}, u32[]{:S(2)}) copy-start(f32[2,64]{1,0:T(2,128)} %param.68) | copy-start | bytes 1540
  2307.0 207.5 %copy-start.48 = (f32[2,2048]{1,0:T(2,128)S(1)}, f32[2,2048]{1,0:T(2,128)}, u32[]{:S(2)}) copy-start(f32[2,2048]{1,0:T(2,128)} %param.64) | copy-start | bytes 49156
  2307.0 207.5 %copy-start.62 = (f32[2,2048]{1,0:T(2,128)S(1)}, f32[2,2048]{1,0:T(2,128)}, u32[]{:S(2)}) copy-start(f32[2,2048]{1,0:T(2,128)} %param.65) | copy-start | bytes 49156
  2307.0 207.5 %copy-start.63 = (f32[2,2048]{1,0:T(2,128)S(1)}, f32[2,2048]{1,0:T(2,128)}, u32[]{:S(2)}) copy-start(f32[2,2048]{1,0:T(2,128)} %param.66) | copy-start | bytes 49156
  2307.0 333.7 %copy-start.40 = (f32[1,2048]{1,0:T(1,128)S(1)}, f32[1,2048]{1,0:T(1,128)}, u32[]{:S(2)}) copy-start(f32[1,2048]{1,0:T(1,128)} %get-tuple-element.1096) | copy-start | bytes 24580
  2307.0 333.6 %copy-start.51 = (f32[512]{0:T(512)S(1)}, f32[512]{0:T(512)}, u32[]{:S(2)}) copy-start(f32[512]{0:T(512)} %copy-done.49) | copy-start | bytes 6148
  2307.0 333.6 %copy-start.61 = (f32[512]{0:T(512)S(1)}, f32[512]{0:T(512)}, u32[]{:S(2)}) copy-start(f32[512]{0:T(512)} %copy-done.60) | copy-start | bytes 6148
  (71 other events, 2822.8 us)
Sparse Core Ops, SparseCore 0:
  10.5 38.0 all-gather.15
  50.7 151.0 all-gather.11
  204.3 24.8 all-gather.13
  231.4 35.2 all-gather.17
  269.0 26.4 all-gather.19
  524.0 168.2 reduce-scatter.9
  694.7 50.8 all-gather.27
  747.2 151.1 all-gather.29
  900.8 50.9 all-gather.25
  953.8 151.0 all-gather.21
  1107.4 50.9 all-gather.23
  1246.4 168.2 reduce-scatter.13
  1423.8 149.4 all-gather.31
  1576.2 50.9 reduce-scatter.21
  1630.2 52.6 reduce-scatter.23
  1685.8 52.6 reduce-scatter.25
  2056.2 26.0 reduce-scatter.17
  2085.6 27.7 reduce-scatter.19
  2120.8 179.0 all-reduce.7
  2302.1 168.2 reduce-scatter.15
  2473.0 167.6 reduce-scatter.11
where the time goes:
time: 2670 us; the launch traced here: 2660 us
  waiting for transfers between devices  1410 us (53%)
  matrix products  814 us (30%)
  local copies, waits for them, and re-layouts  159 us (6%)
  other arithmetic  139 us (5%)
  loops' own time  79.3 us (3%)
  blocking collectives  40 us (1%)
    reduce_scatter x2, waiting for transfers between devices, sum_back(): lax.psum_scatter(summed.astype(jnp.bfloat16), 'wide', scatter_dimension=0...  332 us
    all_gather x2, waiting for transfers between devices, gather_rows(): return lax.all_gather(shard, 'wide', axis=0, tiled=True)  306 us
    reduce_scatter x1, waiting for transfers between devices, shards(): lax.psum_scatter(dot_last(attended_low, output_local).astype(jnp.bfloat16...  162 us
    dot_general x7, matrix products, dot_back(): lax.dot_general(left, right, (((1,), (1,)), ((), ())), preferred_element_...  153 us
    all_gather x1, waiting for transfers between devices, shards(): grad_rows = lax.all_gather(out_grad, 'wide', axis=0, tiled=True)  153 us
    dot_general x108, matrix products, score_block(): jnp.einsum('qhd,kd->hqk', query_block, key_block, preferred_element_type=...  139 us
    dot_general x7, matrix products, dot_last(): return jnp.dot(left, right, preferred_element_type=jnp.float32)  128 us
    reduce_scatter x1, waiting for transfers between devices, shards(): lax.psum_scatter(dot_last(hidden_low, down_local).astype(jnp.bfloat16), '...  126 us
  transfers between devices with their start and end apart: 21, of which 15 were waited for; matrix products, arithmetic and copies ran while one was open for 37% of the time, Pallas kernels for 0%

commit v1 on v0

v1 whole, which is shorter than its diff:
```python
import functools
import math

import jax
import jax.numpy as jnp
from jax import lax
from jax.experimental import pallas as pl
from jax.experimental.pallas import tpu as pltpu
from jax.sharding import PartitionSpec as P

D = 2048
FF = 8192
SEQ_LEN = 4096
STEP = 10
O_FAN = 50


EPSILON = 1e-06
BETA_ONE = 0.9
BETA_TWO = 0.95
ADAM_EPSILON = 1e-08
WEIGHT_DECAY = 0.1
GAIN_RATE = 1.0
ROTARY_BASE = 10000.0
MASKED_SCORE = -1e30


def rms_scale(inputs, gain):
    return inputs * lax.rsqrt(jnp.mean(inputs * inputs, axis=-1, keepdims=True) + EPSILON) * gain


def rotate(inputs, cosine, sine_part):
    half_width = inputs.shape[-1] // 2
    first_half = inputs[..., :half_width]
    second_half = inputs[..., half_width:]
    return jnp.concatenate(
        [
            first_half * cosine - second_half * sine_part,
            second_half * cosine + first_half * sine_part,
        ],
        axis=-1,
    )


def adam_update(weight, first_moment, second_moment, gradient, rate, decay):
    first_new = BETA_ONE * first_moment + (1.0 - BETA_ONE) * gradient
    second_new = BETA_TWO * second_moment + (1.0 - BETA_TWO) * gradient * gradient
    ratio = (
        first_new
        / (1.0 - BETA_ONE**STEP)
        / (jnp.sqrt(second_new / (1.0 - BETA_TWO**STEP)) + ADAM_EPSILON)
    )
    return (weight - rate * (ratio + decay * weight), first_new, second_new)


def dot_last(left, right):
    return jnp.dot(left, right, preferred_element_type=jnp.float32)


def dot_first(left, right):
    return lax.dot_general(
        left, right, (((0,), (0,)), ((), ())), preferred_element_type=jnp.float32
    )


def dot_back(left, right):
    return lax.dot_general(
        left, right, (((1,), (1,)), ((), ())), preferred_element_type=jnp.float32
    )


LOG2E = math.log2(math.e)

def nt(a, b):
    return lax.dot_general(a, b, (((1,), (1,)), ((), ())), preferred_element_type=jnp.float32)
def tn(a, b):
    return lax.dot_general(a, b, (((0,), (0,)), ((), ())), preferred_element_type=jnp.float32)
def nn(a, b):
    return jnp.dot(a, b, preferred_element_type=jnp.float32)

def low_lanes(rows):
    return lax.broadcasted_iota(jnp.int32, (rows, 128), 1) < 64

def attend_kernel(block, heads, q_ref, kv_ref, o_ref, s_ref, kk_ref, va_ref, vb_ref, acc_ref):
    total = q_ref.shape[0]
    low = low_lanes(block)

    @pl.loop(0, total // block)
    def _(j):
        rows = pl.ds(pl.multiple_of(j * block, block), block)
        kv = kv_ref[rows, :]
        vk = jnp.concatenate([kv[:, 64:], kv[:, :64]], axis=1)
        one = jnp.ones_like(kv)
        kk_ref[rows, :] = jnp.where(low, kv, vk)
        va_ref[rows, :] = jnp.where(low, vk, one)
        vb_ref[rows, :] = jnp.where(low, one, kv)

    causal = lax.broadcasted_iota(jnp.int32, (block, block), 0) >= lax.broadcasted_iota(
        jnp.int32, (block, block), 1
    )

    @pl.loop(0, total // block)
    def _(i):
        rows = pl.ds(pl.multiple_of(i * block, block), block)
        for pair in range(heads // 2):
            lanes = pl.ds(pair * 128, 128)
            both = q_ref[rows, lanes]
            zero = jnp.zeros_like(both)
            sides = (jnp.where(low, both, zero), jnp.where(low, zero, both))

            def step(j, diagonal):
                keys = pl.ds(pl.multiple_of(j * block, block), block)
                kk = kk_ref[keys, :]
                for side in range(2):
                    weights = jnp.exp2(nt(sides[side], kk))
                    if diagonal:
                        weights = jnp.where(causal, weights, 0.0)
                    part = nn(weights.astype(jnp.bfloat16), (va_ref, vb_ref)[side][keys, :])
                    if diagonal:
                        acc_ref[side] = part
                    else:
                        acc_ref[side] += part

            step(i, True)

            @pl.loop(0, i)
            def _(j):
                step(j, False)

            first, second = acc_ref[0], acc_ref[1]
            summed = jnp.where(low, first, second)
            sums = jnp.where(low, second, first)
            sums = jnp.concatenate([sums[:, 64:], sums[:, :64]], axis=1)
            o_ref[rows, lanes] = summed / sums
            s_ref[rows, lanes] = sums

def attend(q, kv, heads, block=512):
    total = q.shape[0]
    cost = heads * total * total // 2
    return pl.pallas_call(
        functools.partial(attend_kernel, block, heads),
        out_shape=[jax.ShapeDtypeStruct(q.shape, jnp.float32), jax.ShapeDtypeStruct(q.shape, jnp.float32)],
        in_specs=[pl.BlockSpec(memory_space=pltpu.VMEM)] * 2,
        out_specs=[pl.BlockSpec(memory_space=pltpu.VMEM)] * 2,
        scratch_shapes=[pltpu.VMEM((total, 128), jnp.bfloat16)] * 3 + [pltpu.VMEM((2, block, 128), jnp.float32)],
        compiler_params=pltpu.CompilerParams(vmem_limit_bytes=56 << 20),
        cost_estimate=pl.CostEstimate(flops=4 * cost * 256, bytes_accessed=12 * q.size, transcendentals=cost),
        name="attend",
    )(q, kv)

def back_kernel(block, heads, q_ref, g_ref, d_ref, kv_ref, dq_ref, dkv_ref, kk_ref, vv_ref, ka_ref, kb_ref):
    total = q_ref.shape[0]
    low = low_lanes(block)
    count = total // block

    @pl.loop(0, count)
    def _(j):
        rows = pl.ds(pl.multiple_of(j * block, block), block)
        kv = kv_ref[rows, :]
        vk = jnp.concatenate([kv[:, 64:], kv[:, :64]], axis=1)
        zero = jnp.zeros_like(kv)
        kk_ref[rows, :] = jnp.where(low, kv, vk)
        vv_ref[rows, :] = jnp.where(low, vk, kv)
        ka_ref[rows, :] = jnp.where(low, kv, zero)
        kb_ref[rows, :] = jnp.where(low, zero, vk)
        dkv_ref[0, rows, :] = jnp.zeros((block, 128), jnp.float32)
        dkv_ref[1, rows, :] = jnp.zeros((block, 128), jnp.float32)

    causal = lax.broadcasted_iota(jnp.int32, (block, block), 0) <= lax.broadcasted_iota(
        jnp.int32, (block, block), 1
    )

    @pl.loop(0, count)
    def _(i):
        rows = pl.ds(pl.multiple_of(i * block, block), block)
        for pair in range(heads // 2):
            lanes = pl.ds(pair * 128, 128)
            qboth = q_ref[rows, lanes]
            gboth = g_ref[rows, lanes]
            zero = jnp.zeros_like(qboth)
            qs = (jnp.where(low, qboth, zero), jnp.where(low, zero, qboth))
            gs = (jnp.where(low, gboth, zero), jnp.where(low, zero, gboth))

            def step(j, diagonal):
                keys = pl.ds(pl.multiple_of(j * block, block), block)
                kk = kk_ref[keys, :]
                vv = vv_ref[keys, :]
                for side in range(2):
                    weights = jnp.exp2(nt(kk, qs[side]))
                    if diagonal:
                        weights = jnp.where(causal, weights, 0.0)
                    dots = d_ref[pl.ds(pair * 2 + side, 1), rows]
                    grads = (weights * (nt(vv, gs[side]) - dots)).astype(jnp.bfloat16)
                    dkv_ref[1, keys, :] += nn(weights.astype(jnp.bfloat16), gs[side])
                    dkv_ref[0, keys, :] += nn(grads, qs[side])
                    part = tn(grads, (ka_ref, kb_ref)[side][keys, :])
                    if diagonal and side == 0:
                        dq_ref[rows, lanes] = part
                    else:
                        dq_ref[rows, lanes] += part

            step(i, True)

            @pl.loop(0, i)
            def _(j):
                step(j, False)

def attend_back(q, g, dots, kv, heads, block=512):
    total = q.shape[0]
    cost = heads * total * total // 2
    return pl.pallas_call(
        functools.partial(back_kernel, block, heads),
        out_shape=[jax.ShapeDtypeStruct(q.shape, jnp.float32), jax.ShapeDtypeStruct((2, total, 128), jnp.float32)],
        in_specs=[pl.BlockSpec(memory_space=pltpu.VMEM)] * 4,
        out_specs=[pl.BlockSpec(memory_space=pltpu.VMEM)] * 2,
        scratch_shapes=[pltpu.VMEM((total, 128), jnp.bfloat16)] * 4,
        compiler_params=pltpu.CompilerParams(vmem_limit_bytes=56 << 20),
        cost_estimate=pl.CostEstimate(flops=10 * cost * 256, bytes_accessed=12 * q.size, transcendentals=cost),
        name="attend_back",
    )(q, g, dots, kv)


def gather_rows(shard):
    return lax.all_gather(shard, "wide", axis=0, tiled=True)


def sum_back(pairs, row_count):
    summed = jnp.zeros((row_count * lax.axis_size("wide"), pairs[0][1].shape[0]), jnp.float32)
    for gradient, weight in pairs:
        summed = summed + dot_back(gradient, weight)
    return lax.psum_scatter(
        summed.astype(jnp.bfloat16), "wide", scatter_dimension=0, tiled=True
    ).astype(jnp.float32)


def shards(
    tokens_in,
    out_grad,
    positions,
    query_weight,
    query_first,
    query_second,
    key_weight,
    key_first,
    key_second,
    value_weight,
    value_first,
    value_second,
    output_weight,
    output_first,
    output_second,
    gate_weight,
    gate_first,
    gate_second,
    up_weight,
    up_first,
    up_second,
    down_weight,
    down_first,
    down_second,
    norm_gains,
    norm_first,
    norm_second,
    head_gains,
    head_first,
    head_second,
):
    wide_count = lax.axis_size("wide")
    wide_rank = lax.axis_index("wide")
    head_dim = head_gains.shape[1]
    key_heads = key_weight.shape[1] // head_dim
    local_heads = query_weight.shape[1] // head_dim
    shard_rows = tokens_in.shape[0]
    copies = wide_count // key_heads
    key_slot = wide_rank // copies
    key_own = lax.dynamic_slice_in_dim(key_weight, key_slot * head_dim, head_dim, 1)
    value_own = lax.dynamic_slice_in_dim(value_weight, key_slot * head_dim, head_dim, 1)
    query_columns = query_weight.shape[1]
    input_full = lax.all_gather(
        jnp.concatenate([query_weight, key_own, value_own], axis=1).astype(jnp.bfloat16),
        "narrow", axis=0, tiled=True,
    )
    output_local, gate_local, up_local, down_local = (
        lax.all_gather(output_weight.astype(jnp.bfloat16), "narrow", axis=1, tiled=True),
        lax.all_gather(gate_weight.astype(jnp.bfloat16), "narrow", axis=0, tiled=True),
        lax.all_gather(up_weight.astype(jnp.bfloat16), "narrow", axis=0, tiled=True),
        lax.all_gather(down_weight.astype(jnp.bfloat16), "narrow", axis=1, tiled=True),
    )
    inverse = jnp.power(ROTARY_BASE, -2.0 * jnp.arange(head_dim // 2, dtype=jnp.float32) / head_dim)
    angles = positions.astype(jnp.float32)[:, None] * inverse[None, :]
    cosine = jnp.cos(angles)
    sine_part = jnp.sin(angles)
    residual = tokens_in.astype(jnp.float32)
    normed_in, norm_in_back = jax.vjp(rms_scale, residual, norm_gains[0])
    rows_in = gather_rows(normed_in.astype(jnp.bfloat16))
    total_rows = rows_in.shape[0]
    model_width = rows_in.shape[1]
    input_raw = dot_last(rows_in, input_full)
    query_raw = input_raw[:, :query_columns].reshape(total_rows, local_heads, head_dim)
    key_raw = input_raw[:, query_columns : query_columns + head_dim]
    value_rows = input_raw[:, query_columns + head_dim :].astype(jnp.bfloat16)

    def query_turn(raw_heads, gain):
        return rotate(rms_scale(raw_heads, gain), cosine[:, None, :], sine_part[:, None, :])

    def key_turn(raw_heads, gain):
        return rotate(rms_scale(raw_heads, gain), cosine, sine_part)

    query_rot, query_back = jax.vjp(query_turn, query_raw, head_gains[0])
    key_rot, key_back = jax.vjp(key_turn, key_raw, head_gains[1])
    score_scale = head_dim ** (-0.5)
    query_rot = (
        (query_rot * (score_scale * LOG2E))
        .reshape(total_rows, local_heads * head_dim)
        .astype(jnp.bfloat16)
    )
    key_values = jnp.concatenate([key_rot.astype(jnp.bfloat16), value_rows], axis=1)
    attended, weight_sums = attend(query_rot, key_values, local_heads)
    attended_low = attended.astype(jnp.bfloat16)
    branch = lax.psum_scatter(
        dot_last(attended_low, output_local).astype(jnp.bfloat16),
        "wide",
        scatter_dimension=0,
        tiled=True,
    ).astype(jnp.float32)
    middle = residual + branch
    normed_mid, norm_mid_back = jax.vjp(rms_scale, middle, norm_gains[1])
    rows_mid = gather_rows(normed_mid.astype(jnp.bfloat16))
    gate_pre = dot_last(rows_mid, gate_local)
    up_pre = dot_last(rows_mid, up_local)
    hidden, hidden_back = jax.vjp(
        lambda gate_in, up_in: jax.nn.silu(gate_in) * up_in, gate_pre, up_pre
    )
    hidden_low = hidden.astype(jnp.bfloat16)
    block_out = (
        middle
        + lax.psum_scatter(
            dot_last(hidden_low, down_local).astype(jnp.bfloat16),
            "wide",
            scatter_dimension=0,
            tiled=True,
        ).astype(jnp.float32)
    ).astype(jnp.bfloat16)
    grad_rows = lax.all_gather(out_grad, "wide", axis=0, tiled=True)
    hidden_grad = dot_back(grad_rows, down_local).astype(jnp.bfloat16)
    down_grad = dot_first(hidden_low, grad_rows)
    gate_grad, up_grad = hidden_back(hidden_grad.astype(jnp.float32))
    gate_grad = gate_grad.astype(jnp.bfloat16)
    up_grad = up_grad.astype(jnp.bfloat16)
    gate_wgrad = dot_first(rows_mid, gate_grad)
    up_wgrad = dot_first(rows_mid, up_grad)
    mid_back = sum_back(((gate_grad, gate_local), (up_grad, up_local)), shard_rows)
    middle_part, mid_gain_grad = norm_mid_back(mid_back)
    middle_grad = out_grad.astype(jnp.float32) + middle_part
    branch_grad = middle_grad.astype(jnp.bfloat16)
    branch_rows = lax.all_gather(branch_grad, "wide", axis=0, tiled=True)
    attended_grad = dot_back(branch_rows, output_local).astype(jnp.bfloat16)
    output_wgrad = dot_first(attended_low, branch_rows)
    head_grad = attended_grad.astype(jnp.float32) / weight_sums
    scaled_grad = head_grad.astype(jnp.bfloat16)
    grad_dot = jnp.sum(
        (head_grad * attended).reshape(total_rows, local_heads, head_dim), axis=-1
    ).T
    query_rot_grad, key_value_grad = attend_back(
        query_rot, scaled_grad, grad_dot, key_values, local_heads
    )
    query_rot_grad = query_rot_grad.reshape(total_rows, local_heads, head_dim) * score_scale
    key_value_grad = key_value_grad[:, :, :head_dim] + key_value_grad[:, :, head_dim:]
    key_rot_grad = key_value_grad[0] * (1.0 / LOG2E)
    value_grad = key_value_grad[1]
    query_raw_grad, query_gain_grad = query_back(query_rot_grad)
    key_raw_grad, key_gain_grad = key_back(key_rot_grad)
    input_low = jnp.concatenate(
        [
            query_raw_grad.reshape(total_rows, local_heads * head_dim).astype(jnp.bfloat16),
            key_raw_grad.astype(jnp.bfloat16),
            value_grad.astype(jnp.bfloat16),
        ],
        axis=1,
    )
    input_wgrad = dot_first(rows_in, input_low)
    input_back = sum_back(((input_low, input_full),), shard_rows)
    input_part, in_gain_grad = norm_in_back(input_back)
    input_grad = middle_grad + input_part
    gain_stack = jnp.stack([in_gain_grad, mid_gain_grad])
    head_stack = jnp.stack([query_gain_grad, key_gain_grad])
    gain_total, head_total = lax.psum((gain_stack, head_stack), ("narrow", "wide"))
    input_total = lax.psum_scatter(
        input_wgrad.astype(jnp.bfloat16), "narrow", scatter_dimension=0, tiled=True
    )
    query_total = input_total[:, :query_columns].astype(jnp.float32)
    spread = lax.all_gather(input_total[:, query_columns:], "wide", axis=0)
    spread = jnp.sum(
        spread.reshape(key_heads, copies, -1, 2, head_dim).astype(jnp.float32), axis=1
    ).transpose(2, 1, 0, 3)
    key_total = spread[0].reshape(key_weight.shape)
    value_total = spread[1].reshape(value_weight.shape)
    output_total, gate_total, up_total, down_total = (
        lax.psum_scatter(
            output_wgrad.astype(jnp.bfloat16), "narrow", scatter_dimension=1, tiled=True
        ).astype(jnp.float32),
        lax.psum_scatter(
            gate_wgrad.astype(jnp.bfloat16), "narrow", scatter_dimension=0, tiled=True
        ).astype(jnp.float32),
        lax.psum_scatter(
            up_wgrad.astype(jnp.bfloat16), "narrow", scatter_dimension=0, tiled=True
        ).astype(jnp.float32),
        lax.psum_scatter(
            down_grad.astype(jnp.bfloat16), "narrow", scatter_dimension=1, tiled=True
        ).astype(jnp.float32),
    )
    wide_rate = D ** (-0.5)
    query_new = adam_update(
        query_weight, query_first, query_second, query_total, wide_rate, WEIGHT_DECAY
    )
    key_new = adam_update(key_weight, key_first, key_second, key_total, wide_rate, WEIGHT_DECAY)
    value_new = adam_update(
        value_weight, value_first, value_second, value_total, wide_rate, WEIGHT_DECAY
    )
    output_new = adam_update(
        output_weight, output_first, output_second, output_total, O_FAN ** (-0.5), WEIGHT_DECAY
    )
    gate_new = adam_update(
        gate_weight, gate_first, gate_second, gate_total, wide_rate, WEIGHT_DECAY
    )
    up_new = adam_update(up_weight, up_first, up_second, up_total, wide_rate, WEIGHT_DECAY)
    down_new = adam_update(
        down_weight, down_first, down_second, down_total, FF ** (-0.5), WEIGHT_DECAY
    )
    norm_new = adam_update(norm_gains, norm_first, norm_second, gain_total, GAIN_RATE, 0.0)
    head_new = adam_update(head_gains, head_first, head_second, head_total, GAIN_RATE, 0.0)
    return (
        block_out,
        input_grad,
        query_new[0],
        query_new[1],
        query_new[2],
        key_new[0],
        key_new[1],
        key_new[2],
        value_new[0],
        value_new[1],
        value_new[2],
        output_new[0],
        output_new[1],
        output_new[2],
        gate_new[0],
        gate_new[1],
        gate_new[2],
        up_new[0],
        up_new[1],
        up_new[2],
        down_new[0],
        down_new[1],
        down_new[2],
        norm_new[0],
        norm_new[1],
        norm_new[2],
        head_new[0],
        head_new[1],
        head_new[2],
    )


def solution(mesh):
    return jax.shard_map(
        shards,
        mesh=mesh,
        in_specs=(
            P(("narrow", "wide"), None),
            P(("narrow", "wide"), None),
            P("narrow"),
            P("narrow", "wide"),
            P("narrow", "wide"),
            P("narrow", "wide"),
            P("narrow", None),
            P("narrow", None),
            P("narrow", None),
            P("narrow", None),
            P("narrow", None),
            P("narrow", None),
            P("wide", "narrow"),
            P("wide", "narrow"),
            P("wide", "narrow"),
            P("narrow", "wide"),
            P("narrow", "wide"),
            P("narrow", "wide"),
            P("narrow", "wide"),
            P("narrow", "wide"),
            P("narrow", "wide"),
            P("wide", "narrow"),
            P("wide", "narrow"),
            P("wide", "narrow"),
            P(),
            P(),
            P(),
            P(),
            P(),
            P(),
        ),
        out_specs=(
            P(("narrow", "wide"), None),
            P(("narrow", "wide"), None),
            P("narrow", "wide"),
            P("narrow", "wide"),
            P("narrow", "wide"),
            P("narrow", None),
            P("narrow", None),
            P("narrow", None),
            P("narrow", None),
            P("narrow", None),
            P("narrow", None),
            P("wide", "narrow"),
            P("wide", "narrow"),
            P("wide", "narrow"),
            P("narrow", "wide"),
            P("narrow", "wide"),
            P("narrow", "wide"),
            P("narrow", "wide"),
            P("narrow", "wide"),
            P("narrow", "wide"),
            P("wide", "narrow"),
            P("wide", "narrow"),
            P("wide", "narrow"),
            P(),
            P(),
            P(),
            P(),
            P(),
            P(),
        ),
        check_vma=False,
    )
```

time: 2670 us -> 2180 us (0.82)
  matrix products: 814 us -> 311 us
  Pallas kernels: 0 us -> 180 us
  local copies, waits for them, and re-layouts: 159 us -> 71.3 us
  loops' own time: 79.3 us -> 0 us
    dot_general x288 -> x0, matrix products: 426 us -> none  [the longest x108 139 us: score_block(): jnp.einsum('qhd,kd->hqk', query_block, key_block, preferred_element_type=...]
    pallas_call x0 -> x2, Pallas kernels: none -> 180 us  [the longest x1 119 us: attend_back(): pl.pallas_call(functools.partial(back_kernel, block, heads), out_shape=[j...]
    dynamic_update_slice x18 -> x0, local copies, waits for them, and re-layouts: 108 us -> none  [the longest x16 96.6 us: shards(): row_tops, weight_sums, attended = lax.map(attend, jnp.arange(block_count))]
    psum x1 -> x0, waiting for transfers between devices: 84.7 us -> none  [shards(): lax.psum((key_spread, value_spread, gain_stack, head_stack), ('narrow', '...]
    another operation x26 -> x0, loops' own time: 79.3 us -> none  [the longest x1 41.9 us: shards(): lax.scan(back_block, (zero_rows, zero_rows), jnp.arange(block_count))]
    all_gather x1, waiting for transfers between devices: 72.8 us -> 150 us  [shards(): branch_rows = lax.all_gather(branch_grad, 'wide', axis=0, tiled=True)]
    dot_general x7 -> x5, matrix products: 153 us -> 106 us  [dot_back(): lax.dot_general(left, right, (((1,), (1,)), ((), ())), preferred_element_...]
    reduce_scatter x1, waiting for transfers between devices: 0.01 us -> 44.5 us  [shards(): lax.psum_scatter(down_grad.astype(jnp.bfloat16), 'narrow', scatter_dimens...]
  transfers between devices with their start and end apart: 21 -> 19, of which waited for: 15 -> 15; matrix products, arithmetic and copies ran while one was open for 37% -> 14% of each run, Pallas kernels for 0% -> 3%
where the time goes in v1:
time: 2180 us; the launch traced here: 2170 us
  waiting for transfers between devices  1430 us (66%)
  matrix products  311 us (14%)
  Pallas kernels  180 us (8%)
  other arithmetic  128 us (6%)
  local copies, waits for them, and re-layouts  71.3 us (3%)
  blocking collectives  39.7 us (2%)
    reduce_scatter x2, waiting for transfers between devices, sum_back(): lax.psum_scatter(summed.astype(jnp.bfloat16), 'wide', scatter_dimension=0...  312 us
    all_gather x2, waiting for transfers between devices, gather_rows(): return lax.all_gather(shard, 'wide', axis=0, tiled=True)  307 us
    reduce_scatter x1, waiting for transfers between devices, shards(): lax.psum_scatter(dot_last(attended_low, output_local).astype(jnp.bfloat16...  160 us
    all_gather x1, waiting for transfers between devices, shards(): grad_rows = lax.all_gather(out_grad, 'wide', axis=0, tiled=True)  153 us
    all_gather x1, waiting for transfers between devices, shards(): branch_rows = lax.all_gather(branch_grad, 'wide', axis=0, tiled=True)  150 us
    reduce_scatter x1, waiting for transfers between devices, shards(): lax.psum_scatter(dot_last(hidden_low, down_local).astype(jnp.bfloat16), '...  126 us
    pallas_call x1, Pallas kernels, attend_back(): pl.pallas_call(functools.partial(back_kernel, block, heads), out_shape=[j...  119 us
    dot_general x5, matrix products, dot_last(): return jnp.dot(left, right, preferred_element_type=jnp.float32)  107 us
  transfers between devices with their start and end apart: 19, of which 15 were waited for; matrix products, arithmetic and copies ran while one was open for 14% of the time, Pallas kernels for 3%

profile of v1, /device:TPU:0, one launch (start us, length us, event | category | flops | bytes accessed | tf_op | source)
XLA Modules:
  0.0 2174.4 jit_solution(13383513432213948914)
XLA Ops:
  16.3 28.1 %all-gather.14.cloned.1.call-done = bf16[2048,384]{1,0:T(8,128)(2,1)} async-done(((bf16[512,384]{1,0:T(8,128)(2,1)}), bf16[2048,384]{1,0:T(8,128)(2,1)}) %all-gather.14.cloned.1.call-update) | async-done | bytes 1572880 | tf_op jit(solution)/shard_map/all_gather | solution.py:279
  44.4 153.3 %all-gather.12.cloned.1.call-done = bf16[4096,2048]{1,0:T(8,128)(2,1)} async-done(((bf16[512,2048]{1,0:T(8,128)(2,1)}), bf16[4096,2048]{1,0:T(8,128)(2,1)}) %all-gather.12.cloned.1.call-update) | async-done | bytes 16777232 | tf_op jit(solution)/shard_map/all_gather | solution.py:224
  248.5 61.0 %attend.1 = (f32[4096,256]{1,0:T(8,128)}, f32[4096,256]{1,0:T(8,128)}) custom-call(bf16[4096,256]{1,0:T(8,128)(2,1)} %copy.100.q_ref, bf16[4096,128]{1,0:T(8,128)(2,1)} %pad_maximum_fusion.3.kv_ref), custom_call_target="tpu_custom_call" | custom-call | flops 34359738368 | bytes 12582912 | tf_op jit(solution)/shard_map/attend/pallas_call | solution.py:140
  309.4 12.9 convolution_convert_fusion.2
  329.1 159.8 %reduce-scatter.10.cloned.1.call-done = bf16[512,2048]{1,0:T(8,128)(2,1)} async-done(((bf16[4096,2048]{1,0:T(8,128)(2,1)}), bf16[512,2048]{1,0:T(8,128)(2,1)}) %reduce-scatter.10.cloned.1.call-update) | async-done | bytes 2097168 | tf_op jit(solution)/shard_map/reduce_scatter | solution.py:320
  496.7 45.4 %all-gather.24.cloned.1.call-done = bf16[1024,2048]{1,0:T(8,128)(2,1)} async-done(((bf16[1024,512]{1,0:T(8,128)(2,1)}), bf16[1024,2048]{1,0:T(8,128)(2,1)}) %all-gather.24.cloned.1.call-update) | async-done | bytes 4194320 | tf_op jit(solution)/shard_map/all_gather | solution.py:287
  542.1 152.6 %all-gather.26.cloned.1.call-done = bf16[4096,2048]{1,0:T(8,128)(2,1)} async-done(((bf16[512,2048]{1,0:T(8,128)(2,1)}), bf16[4096,2048]{1,0:T(8,128)(2,1)}) %all-gather.26.cloned.1.call-update) | async-done | bytes 16777232 | tf_op jit(solution)/shard_map/all_gather | solution.py:344
  694.7 23.9 %convolution_convert_fusion.3 = bf16[4096,1024]{1,0:T(8,128)(2,1)} fusion(bf16[4096,2048]{1,0:T(8,128)(2,1)} %all-gather.26.cloned.1.call-done, bf16[1024,2048]{1,0:T(8,128)(2,1)} %all-gather.24.cloned.1.call-done), kind=kOutput, calls=%fused_computation.19 | convolution fusion | flops 17184063488 | bytes 29360128 | tf_op jit(solution)/shard_map/dot_general | solution.py:67
  718.6 29.5 %all-gather.22.cloned.1.call-done = bf16[2048,1024]{1,0:T(8,128)(2,1)} async-done(((bf16[512,1024]{1,0:T(8,128)(2,1)}), bf16[2048,1024]{1,0:T(8,128)(2,1)}) %all-gather.22.cloned.1.call-update) | async-done | bytes 4194320 | tf_op jit(solution)/shard_map/all_gather | solution.py:286
  748.1 153.3 %all-gather.18.cloned.1.call-done = bf16[4096,2048]{1,0:T(8,128)(2,1)} async-done(((bf16[512,2048]{1,0:T(8,128)(2,1)}), bf16[4096,2048]{1,0:T(8,128)(2,1)}) %all-gather.18.cloned.1.call-update) | async-done | bytes 16777232 | tf_op jit(solution)/shard_map/all_gather | solution.py:224
  901.4 23.4 %fusion.83 = f32[4096,1024]{1,0:T(8,128)} fusion(bf16[4096,2048]{1,0:T(8,128)(2,1)} %all-gather.18.cloned.1.call-done, bf16[2048,1024]{1,0:T(8,128)(2,1)} %all-gather.22.cloned.1.call-done), kind=kOutput, calls=%fused_computation.166 | convolution fusion | flops 17179869184 | bytes 37748736 | tf_op jit(solution)/shard_map/dot_general | solution.py:57
  924.8 30.0 %all-gather.20.cloned.1.call-done = bf16[2048,1024]{1,0:T(8,128)(2,1)} async-done(((bf16[512,1024]{1,0:T(8,128)(2,1)}), bf16[2048,1024]{1,0:T(8,128)(2,1)}) %all-gather.20.cloned.1.call-update) | async-done | bytes 4194320 | tf_op jit(solution)/shard_map/all_gather | solution.py:285
  954.8 35.6 %fusion.3 = (bf16[4096,1024]{1,0:T(8,128)(2,1)}, bf16[4096,1024]{1,0:T(8,128)(2,1)}, bf16[4096,1024]{1,0:T(8,128)(2,1)}) fusion(f32[4096,1024]{1,0:T(8,128)} %fusion.83, bf16[4096,1024]{1,0:T(8,128)(2,1)} %convolution_convert_fusion.3, bf16[4096,2048]{1,0:T(8,128)(2,1)} %all-gather.18.cloned.1.call-done, bf16[2048,1024]{1,0:T(8,128)(2,1)} %all-gather.20.cloned.1.call-done), kind=kOutput, calls=%fused_computation.7 | convolution fusion | flops 17251172352 | bytes 71303168 | tf_op jit(solution)/shard_map/dot_general | solution.py:57
  990.4 25.6 %fusion.84 = f32[4096,2048]{1,0:T(8,128)} fusion(bf16[4096,1024]{1,0:T(8,128)(2,1)} %get-tuple-element.132, bf16[2048,1024]{1,0:T(8,128)(2,1)} %all-gather.20.cloned.1.call-done), kind=kOutput, calls=%fused_computation.167 | convolution fusion | flops 17179869184 | bytes 46137344 | tf_op jit(solution)/shard_map/dot_general | solution.py:67
  1016.0 26.6 %add_convert_fusion = bf16[4096,2048]{1,0:T(8,128)(2,1)} fusion(f32[4096,2048]{1,0:T(8,128)} %fusion.84, bf16[4096,1024]{1,0:T(8,128)(2,1)} %get-tuple-element.134, bf16[2048,1024]{1,0:T(8,128)(2,1)S(1)} %copy-done.76), kind=kOutput, calls=%fused_computation | convolution fusion | flops 17196646400 | bytes 62914560 | tf_op jit(solution)/shard_map/dot_general | solution.py:67
  1043.1 167.9 %reduce-scatter.14.cloned.1.call-done = bf16[512,2048]{1,0:T(8,128)(2,1)} async-done(((bf16[4096,2048]{1,0:T(8,128)(2,1)}), bf16[512,2048]{1,0:T(8,128)(2,1)}) %reduce-scatter.14.cloned.1.call-update) | async-done | bytes 2097168 | tf_op jit(solution)/shard_map/reduce_scatter | solution.py:231
  1220.1 149.6 %all-gather.28.cloned.1.call-done = bf16[4096,2048]{1,0:T(8,128)(2,1)} async-done(((bf16[512,2048]{1,0:T(8,128)(2,1)}), bf16[4096,2048]{1,0:T(8,128)(2,1)}) %all-gather.28.cloned.1.call-update) | async-done | bytes 16777232 | tf_op jit(solution)/shard_map/all_gather | solution.py:356
  1369.7 16.0 fusion.79
  1394.7 118.7 %attend_back.1 = (f32[4096,256]{1,0:T(8,128)}, f32[2,4096,128]{2,1,0:T(8,128)}) custom-call(bf16[4096,256]{1,0:T(8,128)(2,1)} %copy.100.q_ref, bf16[4096,256]{1,0:T(8,128)(2,1)} %get-tuple-element.142.g_ref, f32[4,4096]{1,0:T(4,128)} %bitcast.88, bf16[4096,128]{1,0:T(8,128)(2,1)} %pad_maximum_fusion.3.kv_ref), custom_call_target="tpu_custom_call" | custom-call | flops 85899345920 | bytes 12582912 | tf_op jit(solution)/shard_map/attend_back/pallas_call | solution.py:211
  1554.0 13.6 convolution_convert_fusion.8
  1567.6 23.7 %convolution_convert_fusion.7 = bf16[2048,1024]{1,0:T(8,128)(2,1)} fusion(bf16[4096,2048]{1,0:T(8,128)(2,1)} %all-gather.18.cloned.1.call-done, bf16[4096,1024]{1,0:T(8,128)(2,1)} %get-tuple-element.132), kind=kOutput, calls=%fused_computation.57 | convolution fusion | flops 17181966336 | bytes 29360128 | tf_op jit(solution)/shard_map/dot_general | solution.py:61
  1591.4 24.2 %convolution_convert_fusion.6 = bf16[2048,1024]{1,0:T(8,128)(2,1)} fusion(bf16[4096,2048]{1,0:T(8,128)(2,1)} %all-gather.18.cloned.1.call-done, bf16[4096,1024]{1,0:T(8,128)(2,1)} %get-tuple-element.134), kind=kOutput, calls=%fused_computation.56 | convolution fusion | flops 17181966336 | bytes 29360128 | tf_op jit(solution)/shard_map/dot_general | solution.py:61
  1615.7 24.1 %convolution_convert_fusion.5 = bf16[1024,2048]{1,0:T(8,128)(2,1)} fusion(bf16[4096,1024]{1,0:T(8,128)(2,1)} %get-tuple-element.133, bf16[4096,2048]{1,0:T(8,128)(2,1)} %all-gather.26.cloned.1.call-done), kind=kOutput, calls=%fused_computation.55 | convolution fusion | flops 17181966336 | bytes 29360128 | tf_op jit(solution)/shard_map/dot_general | solution.py:61
  1640.0 12.7 convolution_convert_fusion.9
  1654.4 14.0 convolution_convert_fusion.1
  1668.5 23.7 %convolution_convert_fusion = bf16[4096,2048]{1,0:T(8,128)(2,1)} fusion(bf16[4096,1024]{1,0:T(8,128)(2,1)} %get-tuple-element.133, bf16[1024,2048]{1,0:T(8,128)(2,1)} %all-gather.24.cloned.1.call-done), kind=kOutput, calls=%fused_computation.11 | convolution fusion | flops 17188257792 | bytes 29360128 | tf_op jit(solution)/shard_map/dot_general | solution.py:57
  1719.4 44.5 %reduce-scatter.26.cloned.1.call-done = bf16[1024,512]{1,0:T(8,128)(2,1)} async-done(((bf16[1024,2048]{1,0:T(8,128)(2,1)}), bf16[1024,512]{1,0:T(8,128)(2,1)}) %reduce-scatter.26.cloned.1.call-update) | async-done | bytes 1048592 | tf_op jit(solution)/shard_map/reduce_scatter | solution.py:408
  1770.3 24.9 %reduce-scatter.20.cloned.1.call-done = bf16[256,512]{1,0:T(8,128)(2,1)} async-done(((bf16[256,2048]{1,0:T(8,128)(2,1)}), bf16[256,512]{1,0:T(8,128)(2,1)}) %reduce-scatter.20.cloned.1.call-update) | async-done | bytes 262160 | tf_op jit(solution)/shard_map/reduce_scatter | solution.py:399
  1800.9 18.5 all-gather.30.cloned.1.call-done
  1845.9 143.6 %reduce-scatter.16.cloned.1.call-done = bf16[512,2048]{1,0:T(8,128)(2,1)} async-done(((bf16[4096,2048]{1,0:T(8,128)(2,1)}), bf16[512,2048]{1,0:T(8,128)(2,1)}) %reduce-scatter.16.cloned.1.call-update) | async-done | bytes 2097168 | tf_op jit(solution)/shard_map/reduce_scatter | solution.py:231
  1992.9 39.7 %all-reduce.4 = (f32[2,2048]{1,0:T(2,128)S(1)}, f32[2,64]{1,0:T(2,128)S(1)}) all-reduce(f32[2,2048]{1,0:T(2,128)S(1)} %pad_maximum_fusion.5, f32[2,64]{1,0:T(2,128)S(1)} %pad_maximum_fusion.6), channel_id=1, replica_groups=mesh['narrow'=4,'wide'=8] {'narrow','wide'}, use_global_device_ids=true, to_apply=%region_20.21 | all-reduce | flops 4224 | bytes 33792 | tf_op jit(solution)/shard_map/psum | solution.py:387
  2033.9 125.6 %reduce-scatter.12.cloned.1.call-done = bf16[512,2048]{1,0:T(8,128)(2,1)} async-done(((bf16[4096,2048]{1,0:T(8,128)(2,1)}), bf16[512,2048]{1,0:T(8,128)(2,1)}) %reduce-scatter.12.cloned.1.call-update) | async-done | bytes 2097168 | tf_op jit(solution)/shard_map/reduce_scatter | solution.py:337
  (290 shorter events, 212.9 us)
Async XLA Ops:
  7.2 37.2 %all-gather.14.cloned.1.call-start = ((), (), s32[]{:S(2)}) async-start(), calls=%async_computation.10 | async-start | bytes 1966080 | tf_op jit(solution)/shard_map/all_gather | solution.py:279
  10.6 187.1 %all-gather.12.cloned.1.call-start = ((), (), s32[]{:S(2)}) async-start(), calls=%async_computation.9 | async-start | bytes 18874368 | tf_op jit(solution)/shard_map/all_gather | solution.py:224
  13.3 195.5 %copy-start.52 = (f32[512]{0:T(512)}, f32[512]{0:T(512)S(1)}, u32[]{:S(2)}) copy-start(f32[512]{0:T(512)S(1)} %fusion.57) | copy-start | bytes 6148
  13.4 195.4 %copy-start.45 = (f32[1,2048]{1,0:T(1,128)}, f32[1,2048]{1,0:T(1,128)S(1)}, u32[]{:S(2)}) copy-start(f32[1,2048]{1,0:T(1,128)S(1)} %get-tuple-element.152) | copy-start | bytes 24580
  13.4 478.1 %copy-start.38 = (f32[1,2048]{1,0:T(1,128)}, f32[1,2048]{1,0:T(1,128)S(1)}, u32[]{:S(2)}) copy-start(f32[1,2048]{1,0:T(1,128)S(1)} %get-tuple-element.151) | copy-start | bytes 24580
  15.3 294.2 %all-gather.16.cloned.1.call-start = ((), (), s32[]{:S(2)}) async-start(), calls=%async_computation.11 | async-start | bytes 1310720 | tf_op jit(solution)/shard_map/all_gather | solution.py:284
  16.1 472.8 %reduce-scatter.10.cloned.1.call-start = ((), (), s32[]{:S(2)}) async-start(), calls=%async_computation.12 | async-start | bytes 18874368 | tf_op jit(solution)/shard_map/reduce_scatter | solution.py:320
  16.2 204.1 %copy-start.72 = (f32[32]{0:T(128)}, f32[32]{0:T(128)S(1)}, u32[]{:S(2)}) copy-start(f32[32]{0:T(128)S(1)} %multiply_power_fusion) | copy-start | bytes 388
  16.2 202.2 %copy-start.66 = (f32[64]{0:T(128)}, f32[64]{0:T(128)S(1)}, u32[]{:S(2)}) copy-start(f32[64]{0:T(128)S(1)} %get-tuple-element.153) | copy-start | bytes 772
  16.2 219.3 %copy-start.64 = (f32[64]{0:T(128)}, f32[64]{0:T(128)S(1)}, u32[]{:S(2)}) copy-start(f32[64]{0:T(128)S(1)} %get-tuple-element.154) | copy-start | bytes 772
  16.3 204.1 %copy-start.41 = (f32[4096]{0:T(1024)}, f32[4096]{0:T(1024)S(1)}, u32[]{:S(2)}) copy-start(f32[4096]{0:T(1024)S(1)} %convert_element_type.144) | copy-start | bytes 49156
  322.3 219.8 %all-gather.24.cloned.1.call-start = ((), (), s32[]{:S(2)}) async-start(), calls=%async_computation.16 | async-start | bytes 5242880 | tf_op jit(solution)/shard_map/all_gather | solution.py:287
  325.1 369.6 %all-gather.26.cloned.1.call-start = ((), (), s32[]{:S(2)}) async-start(), calls=%async_computation.18 | async-start | bytes 18874368 | tf_op jit(solution)/shard_map/all_gather | solution.py:344
  325.7 422.4 %all-gather.22.cloned.1.call-start = ((), (), s32[]{:S(2)}) async-start(), calls=%async_computation.15 | async-start | bytes 5242880 | tf_op jit(solution)/shard_map/all_gather | solution.py:286
  329.1 572.3 %all-gather.18.cloned.1.call-start = ((), (), s32[]{:S(2)}) async-start(), calls=%async_computation.13 | async-start | bytes 18874368 | tf_op jit(solution)/shard_map/all_gather | solution.py:224
  493.9 460.9 %all-gather.20.cloned.1.call-start = ((), (), s32[]{:S(2)}) async-start(), calls=%async_computation.14 | async-start | bytes 5242880 | tf_op jit(solution)/shard_map/all_gather | solution.py:285
  496.7 714.3 %reduce-scatter.14.cloned.1.call-start = ((), (), s32[]{:S(2)}) async-start(), calls=%async_computation.19 | async-start | bytes 18874368 | tf_op jit(solution)/shard_map/reduce_scatter | solution.py:231
  1042.6 327.1 %all-gather.28.cloned.1.call-start = ((), (), s32[]{:S(2)}) async-start(), calls=%async_computation.20 | async-start | bytes 18874368 | tf_op jit(solution)/shard_map/all_gather | solution.py:356
  1220.1 432.7 %reduce-scatter.18.cloned.1.call-start = ((), (), s32[]{:S(2)}) async-start(), calls=%async_computation.22 | async-start | bytes 1966080 | tf_op jit(solution)/shard_map/reduce_scatter | solution.py:388
  1567.6 138.0 %reduce-scatter.22.cloned.1.call-start = ((), (), s32[]{:S(2)}) async-start(), calls=%async_computation.24 | async-start | bytes 5242880 | tf_op jit(solution)/shard_map/reduce_scatter | solution.py:402
  1591.4 120.8 %reduce-scatter.24.cloned.1.call-start = ((), (), s32[]{:S(2)}) async-start(), calls=%async_computation.25 | async-start | bytes 5242880 | tf_op jit(solution)/shard_map/reduce_scatter | solution.py:405
  1615.7 148.2 %reduce-scatter.26.cloned.1.call-start = ((), (), s32[]{:S(2)}) async-start(), calls=%async_computation.26 | async-start | bytes 5242880 | tf_op jit(solution)/shard_map/reduce_scatter | solution.py:408
  1639.9 155.3 %reduce-scatter.20.cloned.1.call-start = ((), (), s32[]{:S(2)}) async-start(), calls=%async_computation.23 | async-start | bytes 1310720 | tf_op jit(solution)/shard_map/reduce_scatter | solution.py:399
  1652.7 166.7 %all-gather.30.cloned.1.call-start = ((), (), s32[]{:S(2)}) async-start(), calls=%async_computation.27 | async-start | bytes 1179648 | tf_op jit(solution)/shard_map/all_gather | solution.py:392
  1654.4 335.2 %reduce-scatter.16.cloned.1.call-start = ((), (), s32[]{:S(2)}) async-start(), calls=%async_computation.21 | async-start | bytes 18874368 | tf_op jit(solution)/shard_map/reduce_scatter | solution.py:231
  1668.5 491.0 %reduce-scatter.12.cloned.1.call-start = ((), (), s32[]{:S(2)}) async-start(), calls=%async_computation.17 | async-start | bytes 18874368 | tf_op jit(solution)/shard_map/reduce_scatter | solution.py:337
  1842.0 191.3 %copy-start.48 = (f32[2,2048]{1,0:T(2,128)S(1)}, f32[2,2048]{1,0:T(2,128)}, u32[]{:S(2)}) copy-start(f32[2,2048]{1,0:T(2,128)} %param.54) | copy-start | bytes 49156
  1842.0 191.3 %copy-start.61 = (f32[2,2048]{1,0:T(2,128)S(1)}, f32[2,2048]{1,0:T(2,128)}, u32[]{:S(2)}) copy-start(f32[2,2048]{1,0:T(2,128)} %param.55) | copy-start | bytes 49156
  1842.0 191.2 %copy-start.62 = (f32[2,2048]{1,0:T(2,128)S(1)}, f32[2,2048]{1,0:T(2,128)}, u32[]{:S(2)}) copy-start(f32[2,2048]{1,0:T(2,128)} %param.56) | copy-start | bytes 49156
  1842.0 317.6 %copy-start.40 = (f32[1,2048]{1,0:T(1,128)S(1)}, f32[1,2048]{1,0:T(1,128)}, u32[]{:S(2)}) copy-start(f32[1,2048]{1,0:T(1,128)} %copy-done.38) | copy-start | bytes 24580
  1842.0 317.5 %copy-start.51 = (f32[512]{0:T(512)S(1)}, f32[512]{0:T(512)}, u32[]{:S(2)}) copy-start(f32[512]{0:T(512)} %copy-done.49) | copy-start | bytes 6148
  1842.0 317.5 %copy-start.60 = (f32[512]{0:T(512)S(1)}, f32[512]{0:T(512)}, u32[]{:S(2)}) copy-start(f32[512]{0:T(512)} %copy-done.59) | copy-start | bytes 6148
  (67 other events, 2719.9 us)
Sparse Core Ops, SparseCore 0:
  10.7 33.6 all-gather.13
  46.6 151.0 all-gather.11
  200.1 24.7 all-gather.15
  322.5 166.4 reduce-scatter.9
  491.2 50.8 all-gather.23
  543.6 151.1 all-gather.25
  697.2 50.9 all-gather.21
  750.3 151.0 all-gather.17
  903.9 50.9 all-gather.19
  1042.7 168.2 reduce-scatter.13
  1220.2 149.4 all-gather.27
  1567.7 29.1 reduce-scatter.17
  1599.9 52.6 reduce-scatter.21
  1655.7 52.6 reduce-scatter.23
  1711.2 52.6 reduce-scatter.25
  1767.5 27.7 reduce-scatter.19
  1797.3 22.0 all-gather.29
  1821.6 167.8 reduce-scatter.15
  1991.9 167.6 reduce-scatter.11

commit v2 on v1

--- a/solution.py
+++ b/solution.py
@@ -81,14 +81,14 @@
 def low_lanes(rows):
     return lax.broadcasted_iota(jnp.int32, (rows, 128), 1) < 64
 
-def attend_kernel(block, heads, q_ref, kv_ref, o_ref, s_ref, kk_ref, va_ref, vb_ref, acc_ref):
+def attend_kernel(block, heads, q_ref, o_ref, s_ref, low_ref, kk_ref, va_ref, vb_ref, acc_ref):
     total = q_ref.shape[0]
     low = low_lanes(block)
 
     @pl.loop(0, total // block)
     def _(j):
         rows = pl.ds(pl.multiple_of(j * block, block), block)
-        kv = kv_ref[rows, :]
+        kv = q_ref[rows, pl.ds(heads * 64, 128)]
         vk = jnp.concatenate([kv[:, 64:], kv[:, :64]], axis=1)
         one = jnp.ones_like(kv)
         kk_ref[rows, :] = jnp.where(low, kv, vk)
@@ -131,24 +131,31 @@
             summed = jnp.where(low, first, second)
             sums = jnp.where(low, second, first)
             sums = jnp.concatenate([sums[:, 64:], sums[:, :64]], axis=1)
-            o_ref[rows, lanes] = summed / sums
+            result = summed / sums
+            o_ref[rows, lanes] = result
             s_ref[rows, lanes] = sums
-
-def attend(q, kv, heads, block=512):
-    total = q.shape[0]
+            low_ref[rows, lanes] = result.astype(jnp.bfloat16)
+
+def attend(packed, heads, block=512):
+    total = packed.shape[0]
+    shape = (total, heads * 64)
     cost = heads * total * total // 2
     return pl.pallas_call(
         functools.partial(attend_kernel, block, heads),
-        out_shape=[jax.ShapeDtypeStruct(q.shape, jnp.float32), jax.ShapeDtypeStruct(q.shape, jnp.float32)],
-        in_specs=[pl.BlockSpec(memory_space=pltpu.VMEM)] * 2,
-        out_specs=[pl.BlockSpec(memory_space=pltpu.VMEM)] * 2,
+        out_shape=[
+            jax.ShapeDtypeStruct(shape, jnp.float32),
+            jax.ShapeDtypeStruct(shape, jnp.float32),
+            jax.ShapeDtypeStruct(shape, jnp.bfloat16),
+        ],
+        in_specs=[pl.BlockSpec(memory_space=pltpu.VMEM)],
+        out_specs=[pl.BlockSpec(memory_space=pltpu.VMEM)] * 3,
         scratch_shapes=[pltpu.VMEM((total, 128), jnp.bfloat16)] * 3 + [pltpu.VMEM((2, block, 128), jnp.float32)],
         compiler_params=pltpu.CompilerParams(vmem_limit_bytes=56 << 20),
-        cost_estimate=pl.CostEstimate(flops=4 * cost * 256, bytes_accessed=12 * q.size, transcendentals=cost),
+        cost_estimate=pl.CostEstimate(flops=4 * cost * 256, bytes_accessed=12 * packed.size, transcendentals=cost),
         name="attend",
-    )(q, kv)
-
-def back_kernel(block, heads, q_ref, g_ref, d_ref, kv_ref, dq_ref, dkv_ref, kk_ref, vv_ref, ka_ref, kb_ref):
+    )(packed)
+
+def back_kernel(block, heads, q_ref, g_ref, d_ref, out_ref, dq_ref, dkv_ref, kk_ref, vv_ref, ka_ref, kb_ref):
     total = q_ref.shape[0]
     low = low_lanes(block)
     count = total // block
@@ -156,7 +163,7 @@
     @pl.loop(0, count)
     def _(j):
         rows = pl.ds(pl.multiple_of(j * block, block), block)
-        kv = kv_ref[rows, :]
+        kv = q_ref[rows, pl.ds(heads * 64, 128)]
         vk = jnp.concatenate([kv[:, 64:], kv[:, :64]], axis=1)
         zero = jnp.zeros_like(kv)
         kk_ref[rows, :] = jnp.where(low, kv, vk)
@@ -195,9 +202,9 @@
                     dkv_ref[0, keys, :] += nn(grads, qs[side])
                     part = tn(grads, (ka_ref, kb_ref)[side][keys, :])
                     if diagonal and side == 0:
-                        dq_ref[rows, lanes] = part
+                        dq_ref[:, lanes] = part
                     else:
-                        dq_ref[rows, lanes] += part
+                        dq_ref[:, lanes] += part
 
             step(i, True)
 
@@ -205,23 +212,336 @@
             def _(j):
                 step(j, False)
 
-def attend_back(q, g, dots, kv, heads, block=512):
-    total = q.shape[0]
+            out_ref[rows, lanes] = (dq_ref[:, lanes] * 0.125).astype(jnp.bfloat16)
+
+    @pl.loop(0, count)
+    def _(j):
+        rows = pl.ds(pl.multiple_of(j * block, block), block)
+        keys = dkv_ref[0, rows, :] * (1.0 / LOG2E)
+        values = dkv_ref[1, rows, :]
+        keys = keys + jnp.concatenate([keys[:, 64:], keys[:, :64]], axis=1)
+        values = values + jnp.concatenate([values[:, 64:], values[:, :64]], axis=1)
+        out_ref[rows, pl.ds(heads * 64, 128)] = jnp.where(low, keys, values).astype(jnp.bfloat16)
+
+def attend_back(packed, g, dots, heads, block=512):
+    total = packed.shape[0]
     cost = heads * total * total // 2
     return pl.pallas_call(
         functools.partial(back_kernel, block, heads),
-        out_shape=[jax.ShapeDtypeStruct(q.shape, jnp.float32), jax.ShapeDtypeStruct((2, total, 128), jnp.float32)],
-        in_specs=[pl.BlockSpec(memory_space=pltpu.VMEM)] * 4,
-        out_specs=[pl.BlockSpec(memory_space=pltpu.VMEM)] * 2,
-        scratch_shapes=[pltpu.VMEM((total, 128), jnp.bfloat16)] * 4,
+        out_shape=jax.ShapeDtypeStruct(packed.shape, jnp.bfloat16),
+        in_specs=[pl.BlockSpec(memory_space=pltpu.VMEM)] * 3,
+        out_specs=pl.BlockSpec(memory_space=pltpu.VMEM),
+        scratch_shapes=[
+            pltpu.VMEM((block, heads * 64), jnp.float32),
+            pltpu.VMEM((2, total, 128), jnp.float32),
+        ]
+        + [pltpu.VMEM((total, 128), jnp.bfloat16)] * 4,
         compiler_params=pltpu.CompilerParams(vmem_limit_bytes=56 << 20),
-        cost_estimate=pl.CostEstimate(flops=10 * cost * 256, bytes_accessed=12 * q.size, transcendentals=cost),
+        cost_estimate=pl.CostEstimate(
+            flops=10 * cost * 256, bytes_accessed=12 * packed.size, transcendentals=cost
+        ),
         name="attend_back",
-    )(q, g, dots, kv)
+    )(packed, g, dots)
+
+
+def remote(source, target, send, arrive, device):
+    return pltpu.make_async_remote_copy(
+        src_ref=source,
+        dst_ref=target,
+        send_sem=send,
+        recv_sem=arrive,
+        device_id=device,
+        device_id_type=pl.DeviceIdType.MESH,
+    )
+
+
+def place():
+    narrow = lax.axis_index("narrow")
+    wide = lax.axis_index("wide")
+    return narrow, wide, wide // 2, wide % 2
+
+
+def greet_neighbours():
+    narrow, wide, chip, core = place()
+    barrier = pltpu.get_barrier_semaphore()
+
+    def tell(device):
+        pl.semaphore_signal(
+            barrier, inc=1, device_id=device, device_id_type=pl.DeviceIdType.MESH
+        )
+
+    tell((narrow + 1 - 2 * (narrow % 2), wide))
+    tell(((narrow + 2) % 4, wide))
+    tell((narrow, 2 * chip + 1 - core))
+
+    @pl.when(chip > 0)
+    def _():
+        tell((narrow, wide - 2))
+
+    @pl.when(chip < 3)
+    def _():
+        tell((narrow, wide + 2))
+
+    pl.semaphore_wait(barrier, 3 + jnp.minimum(chip, 1) + jnp.minimum(3 - chip, 1))
+
+
+def gather_kernel(
+    gate_ref, up_ref, down_ref, att_ref, grad_ref,
+    gate_all, up_all, down_all, att_all, grad_all,
+    own_sem, ffn_send, ffn_got, line_send, line_got, side_send, side_got,
+    core_send, core_got, grad_send, grad_got, pair_send, pair_got,
+):
+    narrow, wide, chip, core = place()
+    beside = narrow + 1 - 2 * (narrow % 2)
+    across = (narrow + 2) % 4
+    corner = (beside + 2) % 4
+    rows = att_ref.shape[0]
+    half_rows = rows // 2
+    columns = down_ref.shape[1]
+    other = (narrow, 2 * chip + 1 - core)
+    left = (narrow, wide - 2)
+    right = (narrow, wide + 2)
+    sides = ((beside, wide), (across, wide))
+    near = (beside, across)
+    greet_neighbours()
+
+    def ffn_own(k, who):
+        if k == 2:
+            return down_all.at[:, pl.ds(pl.multiple_of(who * columns, columns), columns)]
+        return (gate_all, up_all)[k].at[who]
+
+    def ffn_half(k, who, half):
+        if k == 2:
+            size = down_ref.shape[0] // 2
+            return down_all.at[
+                pl.ds(half * size, size), pl.ds(pl.multiple_of(who * columns, columns), columns)
+            ]
+        return (gate_all, up_all)[k].at[who, pl.ds(half * half_rows, half_rows), :]
+
+    def att(slot, who):
+        return att_all.at[slot, pl.ds(pl.multiple_of(who * rows, rows), rows), :]
+
+    def att_half(slot, who, half):
+        return att_all.at[
+            slot, pl.ds(pl.multiple_of(who * rows + half * half_rows, half_rows), half_rows), :
+        ]
+
+    own = []
+    for k, source in enumerate((gate_ref, up_ref, down_ref)):
+        own.append(pltpu.make_async_copy(source, ffn_own(k, narrow), own_sem.at[k]))
+    own.append(pltpu.make_async_copy(att_ref, att(wide, narrow), own_sem.at[3]))
+    own.append(pltpu.make_async_copy(grad_ref, grad_all.at[wide], own_sem.at[4]))
+    for copy in own:
+        copy.start()
+
+    def att_line(at, step, source):
+        slot = 2 * at + core
+        return remote(
+            source, att(slot, narrow), line_send.at[at, (step + 1) // 2], line_got.at[at],
+            right if step > 0 else left,
+        )
+
+    def grad_line(at, step, source):
+        slot = 2 * at + core
+        return remote(
+            source, grad_all.at[slot], grad_send.at[at, (step + 1) // 2], grad_got.at[at],
+            right if step > 0 else left,
+        )
+
+    def grad_pair(at, source):
+        slot = 2 * at + core
+        return remote(source, grad_all.at[slot], pair_send.at[at], pair_got.at[at], other)
+
+    def both_ways(line, at, source_of, act):
+        @pl.when(jnp.logical_and(at <= chip, chip < 3))
+        def _():
+            act(line(at, 1, source_of(at)))
+
+        @pl.when(jnp.logical_and(at >= chip, chip > 0))
+        def _():
+            act(line(at, -1, source_of(at)))
+
+    def att_side(at, k, source):
+        slot = 2 * at + core
+        return remote(source, att(slot, narrow), side_send.at[at, k], side_got.at[at, k], sides[k])
+
+    def att_got(at, k):
+        slot = 2 * at + core
+        target = att(slot, near[k])
+        return remote(target, target, side_send.at[at, k], side_got.at[at, k], sides[k])
+
+    def att_forward(at, k):
+        slot = 2 * at + core
+        piece = att_half(slot, near[k], k)
+        return remote(piece, piece, side_send.at[at, 2 + k], side_got.at[at, 2 + k], sides[1 - k])
+
+    def att_corner(at, k):
+        slot = 2 * at + core
+        piece = att_half(slot, corner, k)
+        return remote(piece, piece, side_send.at[at, 2 + k], side_got.at[at, 2 + k], sides[1 - k])
+
+    def att_core(at, who):
+        slot = 2 * at + core
+        piece = att(slot, who)
+        return remote(piece, piece, core_send.at[at, who], core_got.at[at, who], other)
+
+    def att_core_got(at, who):
+        slot = 2 * at + 1 - core
+        piece = att(slot, who)
+        return remote(piece, piece, core_send.at[at, who], core_got.at[at, who], other)
+
+    def ffn_side(k, j):
+        source = (gate_ref, up_ref, down_ref)[k]
+        return remote(source, ffn_own(k, narrow), ffn_send.at[k, j], ffn_got.at[k, j], sides[j])
+
+    def ffn_got_copy(k, j):
+        target = ffn_own(k, near[j])
+        return remote(target, target, ffn_send.at[k, j], ffn_got.at[k, j], sides[j])
+
+    def ffn_forward(k, j):
+        piece = ffn_half(k, near[j], j)
+        return remote(piece, piece, ffn_send.at[k, 2 + j], ffn_got.at[k, 2 + j], sides[1 - j])
+
+    def ffn_corner(k, j):
+        piece = ffn_half(k, corner, j)
+        return remote(piece, piece, ffn_send.at[k, 2 + j], ffn_got.at[k, 2 + j], sides[1 - j])
+
+    start = lambda copy: copy.start()
+    sent = lambda copy: copy.wait_send()
+    got = lambda copy: copy.wait_recv()
+
+    both_ways(att_line, chip, lambda at: att_ref, start)
+    both_ways(grad_line, chip, lambda at: grad_ref, start)
+    grad_pair(chip, grad_ref).start()
+    for k in range(2):
+        att_side(chip, k, att_ref).start()
+    for k in range(3):
+        for j in range(2):
+            ffn_side(k, j).start()
+    own[3].wait()
+    att_core(chip, narrow).start()
+
+    def att_hop(hop):
+        for at, valid in ((chip - hop, chip >= hop), (chip + hop, chip + hop <= 3)):
+
+            @pl.when(valid)
+            def _():
+                slot = 2 * at + core
+                att_line(at, 1, att(slot, narrow)).wait_recv()
+                both_ways(att_line, at, lambda at: att(2 * at + core, narrow), start)
+                for k in range(2):
+                    att_side(at, k, att(slot, narrow)).start()
+                att_core(at, narrow).start()
+
+    def ffn_step(k):
+        for j in range(2):
+            ffn_got_copy(k, j).wait_recv()
+            ffn_forward(k, j).start()
+
+    def grad_step(hop):
+        for at, valid in ((chip - hop, chip >= hop), (chip + hop, chip + hop <= 3)):
+
+            @pl.when(valid)
+            def _():
+                slot = 2 * at + core
+                grad_line(at, 1, grad_all.at[slot]).wait_recv()
+                both_ways(grad_line, at, lambda at: grad_all.at[2 * at + core], start)
+                grad_pair(at, grad_all.at[slot]).start()
+
+    def att_step(at):
+        for k in range(2):
+            att_got(at, k).wait_recv()
+            att_forward(at, k).start()
+            att_core(at, near[k]).start()
+
+    att_hop(1)
+    att_hop(2)
+    grad_step(1)
+    for k in range(3):
+        ffn_step(k)
+    att_hop(3)
+    att_step(chip)
+    att_step((chip + 1) % 4)
+    grad_step(2)
+    att_step((chip + 3) % 4)
+    att_step((chip + 2) % 4)
+    for at in range(4):
+        for k in range(2):
+            att_corner(at, k).wait_recv()
+        att_core(at, corner).start()
+    grad_step(3)
+
+    for k in range(3):
+        for j in range(2):
+            ffn_corner(k, j).wait_recv()
+            ffn_side(k, j).wait_send()
+            ffn_forward(k, j).wait_send()
+    for at in range(4):
+        slot = 2 * at + 1 - core
+        remote(
+            grad_all.at[slot], grad_all.at[slot], pair_send.at[at], pair_got.at[at], other
+        ).wait_recv()
+        grad_pair(at, grad_ref).wait_send()
+        both_ways(att_line, at, lambda at: att_ref, sent)
+        both_ways(grad_line, at, lambda at: grad_ref, sent)
+        for who in range(4):
+            att_core_got(at, who).wait_recv()
+            att_core(at, who).wait_send()
+        for k in range(2):
+            att_side(at, k, att_ref).wait_send()
+            att_forward(at, k).wait_send()
+    for k in (0, 1, 2, 4):
+        own[k].wait()
+
+
+def gather_all(gate, up, down, att, grad):
+    narrow_count = lax.axis_size("narrow")
+    wide_count = lax.axis_size("wide")
+    rows = att.shape[0]
+    if narrow_count != 4 or wide_count != 8:
+        att = lax.all_gather(lax.all_gather(att, "wide", axis=0), "narrow", axis=1, tiled=True)
+        return (
+            lax.all_gather(gate, "narrow", axis=0, tiled=True),
+            lax.all_gather(up, "narrow", axis=0, tiled=True),
+            lax.all_gather(down, "narrow", axis=1, tiled=True),
+            att,
+            lax.all_gather(grad, "wide", axis=0, tiled=True),
+        )
+    low = jnp.bfloat16
+    dma = pltpu.SemaphoreType.DMA
+    gate_all, up_all, down_all, att_all, grad_all = pl.pallas_call(
+        gather_kernel,
+        out_shape=[
+            jax.ShapeDtypeStruct((narrow_count,) + gate.shape, low),
+            jax.ShapeDtypeStruct((narrow_count,) + up.shape, low),
+            jax.ShapeDtypeStruct((down.shape[0], narrow_count * down.shape[1]), low),
+            jax.ShapeDtypeStruct((wide_count, narrow_count * rows, att.shape[1]), low),
+            jax.ShapeDtypeStruct((wide_count,) + grad.shape, low),
+        ],
+        in_specs=[pl.BlockSpec(memory_space=pl.ANY)] * 5,
+        out_specs=[pl.BlockSpec(memory_space=pl.ANY)] * 5,
+        scratch_shapes=[
+            dma((5,)), dma((3, 4)), dma((3, 4)), dma((4, 2)), dma((4,)), dma((4, 4)), dma((4, 4)),
+            dma((4, 4)), dma((4, 4)), dma((4, 2)), dma((4,)), dma((4,)), dma((4,)),
+        ],
+        compiler_params=pltpu.CompilerParams(collective_id=1, has_side_effects=True),
+        name="gather_all",
+    )(gate, up, down, att, grad)
+    return (
+        gate_all.reshape(-1, gate.shape[1]),
+        up_all.reshape(-1, up.shape[1]),
+        down_all,
+        att_all,
+        grad_all.reshape(-1, grad.shape[1]),
+    )
 
 
 def gather_rows(shard):
     return lax.all_gather(shard, "wide", axis=0, tiled=True)
+
+
+def swap(blocks):
+    return lax.all_to_all(blocks, "wide", 0, 0)
 
 
 def sum_back(pairs, row_count):
@@ -267,62 +587,63 @@
 ):
     wide_count = lax.axis_size("wide")
     wide_rank = lax.axis_index("wide")
+    narrow_count = lax.axis_size("narrow")
     head_dim = head_gains.shape[1]
     key_heads = key_weight.shape[1] // head_dim
     local_heads = query_weight.shape[1] // head_dim
-    shard_rows = tokens_in.shape[0]
+    shard_rows, model_width = tokens_in.shape
     copies = wide_count // key_heads
     key_slot = wide_rank // copies
     key_own = lax.dynamic_slice_in_dim(key_weight, key_slot * head_dim, head_dim, 1)
     value_own = lax.dynamic_slice_in_dim(value_weight, key_slot * head_dim, head_dim, 1)
     query_columns = query_weight.shape[1]
-    input_full = lax.all_gather(
-        jnp.concatenate([query_weight, key_own, value_own], axis=1).astype(jnp.bfloat16),
-        "narrow", axis=0, tiled=True,
-    )
-    output_local, gate_local, up_local, down_local = (
-        lax.all_gather(output_weight.astype(jnp.bfloat16), "narrow", axis=1, tiled=True),
-        lax.all_gather(gate_weight.astype(jnp.bfloat16), "narrow", axis=0, tiled=True),
-        lax.all_gather(up_weight.astype(jnp.bfloat16), "narrow", axis=0, tiled=True),
-        lax.all_gather(down_weight.astype(jnp.bfloat16), "narrow", axis=1, tiled=True),
-    )
+    att_own = jnp.concatenate([query_weight, key_own, value_own, output_weight.T], axis=1)
+    gate_local, up_local, down_local, att_full, grad_rows = gather_all(
+        gate_weight.astype(jnp.bfloat16),
+        up_weight.astype(jnp.bfloat16),
+        down_weight.astype(jnp.bfloat16),
+        att_own.astype(jnp.bfloat16),
+        out_grad,
+    )
+    group_columns = query_columns + 2 * head_dim
+    input_full = att_full[:, :, :group_columns]
+    output_full = att_full[:, :, group_columns:]
     inverse = jnp.power(ROTARY_BASE, -2.0 * jnp.arange(head_dim // 2, dtype=jnp.float32) / head_dim)
-    angles = positions.astype(jnp.float32)[:, None] * inverse[None, :]
+    own_positions = lax.dynamic_slice_in_dim(positions, wide_rank * shard_rows, shard_rows, 0)
+    angles = own_positions.astype(jnp.float32)[:, None] * inverse[None, :]
     cosine = jnp.cos(angles)
     sine_part = jnp.sin(angles)
     residual = tokens_in.astype(jnp.float32)
     normed_in, norm_in_back = jax.vjp(rms_scale, residual, norm_gains[0])
-    rows_in = gather_rows(normed_in.astype(jnp.bfloat16))
-    total_rows = rows_in.shape[0]
-    model_width = rows_in.shape[1]
-    input_raw = dot_last(rows_in, input_full)
-    query_raw = input_raw[:, :query_columns].reshape(total_rows, local_heads, head_dim)
-    key_raw = input_raw[:, query_columns : query_columns + head_dim]
-    value_rows = input_raw[:, query_columns + head_dim :].astype(jnp.bfloat16)
+    rows_in = normed_in.astype(jnp.bfloat16)
+    input_raw = jnp.einsum("td,gdc->gtc", rows_in, input_full, preferred_element_type=jnp.float32)
+    query_raw = input_raw[:, :, :query_columns].reshape(
+        wide_count, shard_rows, local_heads, head_dim
+    )
+    key_raw = input_raw[:, :, query_columns : query_columns + head_dim]
+    value_rows = input_raw[:, :, query_columns + head_dim :].astype(jnp.bfloat16)
 
     def query_turn(raw_heads, gain):
-        return rotate(rms_scale(raw_heads, gain), cosine[:, None, :], sine_part[:, None, :])
+        return rotate(
+            rms_scale(raw_heads, gain), cosine[None, :, None, :], sine_part[None, :, None, :]
+        )
 
     def key_turn(raw_heads, gain):
-        return rotate(rms_scale(raw_heads, gain), cosine, sine_part)
+        return rotate(rms_scale(raw_heads, gain), cosine[None], sine_part[None])
 
     query_rot, query_back = jax.vjp(query_turn, query_raw, head_gains[0])
     key_rot, key_back = jax.vjp(key_turn, key_raw, head_gains[1])
     score_scale = head_dim ** (-0.5)
     query_rot = (
         (query_rot * (score_scale * LOG2E))
-        .reshape(total_rows, local_heads * head_dim)
+        .reshape(wide_count, shard_rows, query_columns)
         .astype(jnp.bfloat16)
     )
-    key_values = jnp.concatenate([key_rot.astype(jnp.bfloat16), value_rows], axis=1)
-    attended, weight_sums = attend(query_rot, key_values, local_heads)
-    attended_low = attended.astype(jnp.bfloat16)
-    branch = lax.psum_scatter(
-        dot_last(attended_low, output_local).astype(jnp.bfloat16),
-        "wide",
-        scatter_dimension=0,
-        tiled=True,
-    ).astype(jnp.float32)
+    packed = swap(jnp.concatenate([query_rot, key_rot.astype(jnp.bfloat16), value_rows], axis=2))
+    packed = packed.reshape(wide_count * shard_rows, group_columns)
+    attended, weight_sums, attended_low = attend(packed, local_heads)
+    attended_low = swap(attended_low.reshape(wide_count, shard_rows, query_columns))
+    branch = jnp.einsum("gth,gdh->td", attended_low, output_full, preferred_element_type=jnp.float32)
     middle = residual + branch
     normed_mid, norm_mid_back = jax.vjp(rms_scale, middle, norm_gains[1])
     rows_mid = gather_rows(normed_mid.astype(jnp.bfloat16))
@@ -341,7 +662,6 @@
             tiled=True,
         ).astype(jnp.float32)
     ).astype(jnp.bfloat16)
-    grad_rows = lax.all_gather(out_grad, "wide", axis=0, tiled=True)
     hidden_grad = dot_back(grad_rows, down_local).astype(jnp.bfloat16)
     down_grad = dot_first(hidden_low, grad_rows)
     gate_grad, up_grad = hidden_back(hidden_grad.astype(jnp.float32))
@@ -353,52 +673,51 @@
     middle_part, mid_gain_grad = norm_mid_back(mid_back)
     middle_grad = out_grad.astype(jnp.float32) + middle_part
     branch_grad = middle_grad.astype(jnp.bfloat16)
-    branch_rows = lax.all_gather(branch_grad, "wide", axis=0, tiled=True)
-    attended_grad = dot_back(branch_rows, output_local).astype(jnp.bfloat16)
-    output_wgrad = dot_first(attended_low, branch_rows)
-    head_grad = attended_grad.astype(jnp.float32) / weight_sums
+    attended_grad = jnp.einsum(
+        "td,gdh->gth", branch_grad, output_full, preferred_element_type=jnp.float32
+    ).astype(jnp.bfloat16)
+    output_wgrad = jnp.einsum(
+        "td,gth->gdh", branch_grad, attended_low, preferred_element_type=jnp.float32
+    )
+    head_grad = swap(attended_grad).reshape(wide_count * shard_rows, query_columns)
+    head_grad = head_grad.astype(jnp.float32) / weight_sums
     scaled_grad = head_grad.astype(jnp.bfloat16)
-    grad_dot = jnp.sum(
-        (head_grad * attended).reshape(total_rows, local_heads, head_dim), axis=-1
-    ).T
-    query_rot_grad, key_value_grad = attend_back(
-        query_rot, scaled_grad, grad_dot, key_values, local_heads
-    )
-    query_rot_grad = query_rot_grad.reshape(total_rows, local_heads, head_dim) * score_scale
-    key_value_grad = key_value_grad[:, :, :head_dim] + key_value_grad[:, :, head_dim:]
-    key_rot_grad = key_value_grad[0] * (1.0 / LOG2E)
-    value_grad = key_value_grad[1]
+    grad_dot = jnp.sum((head_grad * attended).reshape(-1, local_heads, head_dim), axis=-1).T
+    packed_grad = attend_back(packed, scaled_grad, grad_dot, local_heads)
+    packed_grad = swap(packed_grad.reshape(wide_count, shard_rows, group_columns))
+    query_rot_grad = packed_grad[:, :, :query_columns].astype(jnp.float32).reshape(
+        wide_count, shard_rows, local_heads, head_dim
+    )
+    key_rot_grad = packed_grad[:, :, query_columns : query_columns + head_dim]
     query_raw_grad, query_gain_grad = query_back(query_rot_grad)
-    key_raw_grad, key_gain_grad = key_back(key_rot_grad)
+    key_raw_grad, key_gain_grad = key_back(key_rot_grad.astype(jnp.float32))
     input_low = jnp.concatenate(
         [
-            query_raw_grad.reshape(total_rows, local_heads * head_dim).astype(jnp.bfloat16),
+            query_raw_grad.reshape(wide_count, shard_rows, query_columns).astype(jnp.bfloat16),
             key_raw_grad.astype(jnp.bfloat16),
-            value_grad.astype(jnp.bfloat16),
+            packed_grad[:, :, query_columns + head_dim :],
         ],
-        axis=1,
-    )
-    input_wgrad = dot_first(rows_in, input_low)
-    input_back = sum_back(((input_low, input_full),), shard_rows)
+        axis=2,
+    )
+    input_wgrad = jnp.einsum("td,gtc->gdc", rows_in, input_low, preferred_element_type=jnp.float32)
+    input_back = jnp.einsum("gtc,gdc->td", input_low, input_full, preferred_element_type=jnp.float32)
     input_part, in_gain_grad = norm_in_back(input_back)
     input_grad = middle_grad + input_part
     gain_stack = jnp.stack([in_gain_grad, mid_gain_grad])
     head_stack = jnp.stack([query_gain_grad, key_gain_grad])
     gain_total, head_total = lax.psum((gain_stack, head_stack), ("narrow", "wide"))
-    input_total = lax.psum_scatter(
-        input_wgrad.astype(jnp.bfloat16), "narrow", scatter_dimension=0, tiled=True
-    )
+    att_wgrad = jnp.concatenate([input_wgrad, output_wgrad], axis=2).astype(jnp.bfloat16)
+    att_total = lax.psum_scatter(att_wgrad, "narrow", scatter_dimension=1, tiled=True)
+    input_total = lax.psum_scatter(att_total, "wide", scatter_dimension=0)
+    output_total = input_total[:, group_columns:].astype(jnp.float32).T
     query_total = input_total[:, :query_columns].astype(jnp.float32)
-    spread = lax.all_gather(input_total[:, query_columns:], "wide", axis=0)
+    spread = lax.all_gather(input_total[:, query_columns:group_columns], "wide", axis=0)
     spread = jnp.sum(
         spread.reshape(key_heads, copies, -1, 2, head_dim).astype(jnp.float32), axis=1
     ).transpose(2, 1, 0, 3)
     key_total = spread[0].reshape(key_weight.shape)
     value_total = spread[1].reshape(value_weight.shape)
-    output_total, gate_total, up_total, down_total = (
-        lax.psum_scatter(
-            output_wgrad.astype(jnp.bfloat16), "narrow", scatter_dimension=1, tiled=True
-        ).astype(jnp.float32),
+    gate_total, up_total, down_total = (
         lax.psum_scatter(
             gate_wgrad.astype(jnp.bfloat16), "narrow", scatter_dimension=0, tiled=True
         ).astype(jnp.float32),

time: 2180 us -> 1900 us (0.87)
  waiting for transfers between devices: 1430 us -> 754 us
  Pallas kernels: 180 us -> 427 us
  blocking collectives: 39.7 us -> 220 us
  matrix products: 311 us -> 288 us
    all_gather x8 -> x1, waiting for transfers between devices: 454 us -> 6.62 us  [shards(): lax.all_gather(input_total[:, query_columns:group_columns], 'wide', axis=0)]
    pallas_call x1 -> x2, Pallas kernels: 119 us -> 366 us  [the longest x1 247 us: gather_all(): pl.pallas_call(gather_kernel, out_shape=[jax.ShapeDtypeStruct((narrow_cou...]
    all_gather x2 -> x1, waiting for transfers between devices: 307 us -> 126 us  [gather_rows(): return lax.all_gather(shard, 'wide', axis=0, tiled=True)]
    all_to_all x0 -> x3, blocking collectives: none -> 179 us  [swap(): return lax.all_to_all(blocks, 'wide', 0, 0)]
    reduce_scatter x2 -> x1, waiting for transfers between devices: 312 us -> 143 us  [sum_back(): lax.psum_scatter(summed.astype(jnp.bfloat16), 'wide', scatter_dimension=0...]
    reduce_scatter x3 -> x2, waiting for transfers between devices: 185 us -> 117 us  [the longest x1 114 us: shards(): lax.psum_scatter(att_wgrad, 'narrow', scatter_dimension=1, tiled=True)]
    all_to_all x0 -> x1, waiting for transfers between devices: none -> 61.5 us  [swap(): return lax.all_to_all(blocks, 'wide', 0, 0)]
    dot_general x0 -> x6, matrix products: none -> 57 us  [the longest x1 12.3 us: shards(): jnp.einsum('gtc,gdc->td', input_low, input_full, preferred_element_type=j...]
  transfers between devices with their start and end apart: 19 -> 10, of which waited for: 15 -> 10; matrix products, arithmetic and copies ran while one was open for 14% -> 10% of each run, Pallas kernels for 3% -> 0%
where the time goes in v2:
time: 1900 us; the launch traced here: 1890 us
  waiting for transfers between devices  754 us (40%)
  Pallas kernels  427 us (22%)
  matrix products  288 us (15%)
  blocking collectives  220 us (12%)
  other arithmetic  108 us (6%)
  local copies, waits for them, and re-layouts  77.3 us (4%)
    pallas_call x1, Pallas kernels, gather_all(): pl.pallas_call(gather_kernel, out_shape=[jax.ShapeDtypeStruct((narrow_cou...  247 us
    all_to_all x3, blocking collectives, swap(): return lax.all_to_all(blocks, 'wide', 0, 0)  179 us
    reduce_scatter x1, waiting for transfers between devices, shards(): lax.psum_scatter(dot_last(hidden_low, down_local).astype(jnp.bfloat16), '...  164 us
    reduce_scatter x1, waiting for transfers between devices, sum_back(): lax.psum_scatter(summed.astype(jnp.bfloat16), 'wide', scatter_dimension=0...  143 us
    all_gather x1, waiting for transfers between devices, gather_rows(): return lax.all_gather(shard, 'wide', axis=0, tiled=True)  126 us
    pallas_call x1, Pallas kernels, attend_back(): pl.pallas_call(functools.partial(back_kernel, block, heads), out_shape=ja...  119 us
    reduce_scatter x1, waiting for transfers between devices, shards(): lax.psum_scatter(att_wgrad, 'narrow', scatter_dimension=1, tiled=True)  114 us
    dot_general x3, matrix products, dot_last(): return jnp.dot(left, right, preferred_element_type=jnp.float32)  82.7 us
  transfers between devices with their start and end apart: 10, of which 10 were waited for; matrix products, arithmetic and copies ran while one was open for 10% of the time, Pallas kernels for 0%

profile of v2, /device:TPU:0, one launch (start us, length us, event | category | flops | bytes accessed | tf_op | source)
XLA Modules:
  0.0 1894.9 jit_solution(10232969116338252186)
XLA Ops:
  19.2 246.5 %gather_all.1 = (bf16[4,512,1024]{2,1,0:T(8,128)(2,1)}, bf16[4,512,1024]{2,1,0:T(8,128)(2,1)}, bf16[1024,2048]{1,0:T(8,128)(2,1)}, bf16[8,2048,640]{2,1,0:T(8,128)(2,1)}, bf16[8,512,2048]{2,1,0:T(8,128)(2,1)}) custom-call(bf16[512,1024]{1,0:T(8,128)(2,1)} %convert_element_type.125.gate_ref, bf16[512,1024]{1,0:T(8,128)(2,1)} %convert_element_type.126.up_ref, ...), custom_call_target="tpu_custom_call" | custom-call | tf_op jit(solution)/shard_map/gather_all/pallas_call | solution.py:512
  265.7 9.6 fusion.29
  287.8 74.3 %all_to_all.20 = bf16[8,512,384]{1,2,0:T(8,128)(2,1)S(1)} all-to-all(bf16[8,512,384]{1,2,0:T(8,128)(2,1)S(1)} %pad_maximum_fusion.1), channel_id=1, replica_groups=mesh['narrow'=4,'wide'=8] {'wide'}, dimensions={0} | all-to-all | bytes 6291456 | tf_op jit(solution)/shard_map/all_to_all | solution.py:544
  365.0 61.4 %attend.1 = (f32[4096,256]{1,0:T(8,128)}, f32[4096,256]{1,0:T(8,128)}, bf16[4096,256]{1,0:T(8,128)(2,1)}) custom-call(bf16[4096,384]{1,0:T(8,128)(2,1)} %bitcast.124), custom_call_target="tpu_custom_call" | custom-call | flops 34359738368 | bytes 18874368 | tf_op jit(solution)/shard_map/attend/pallas_call | solution.py:143
  426.4 52.7 %all_to_all.21 = bf16[8,512,256]{2,1,0:T(8,128)(2,1)S(1)} all-to-all(bf16[8,512,256]{2,1,0:T(8,128)(2,1)} %bitcast.127), channel_id=1, replica_groups=mesh['narrow'=4,'wide'=8] {'wide'}, dimensions={0} | all-to-all | bytes 4194304 | tf_op jit(solution)/shard_map/all_to_all | solution.py:544
  479.1 7.9 multiply_reduce_fusion.2
  491.4 23.6 %convolution_convert_fusion.1 = bf16[4096,1024]{1,0:T(8,128)(2,1)} fusion(bf16[4096,2048]{1,0:T(8,128)(2,1)} %bitcast.144, bf16[1024,2048]{1,0:T(8,128)(2,1)} %get-tuple-element.41), kind=kOutput, calls=%fused_computation.24 | convolution fusion | flops 17184063488 | bytes 29360128 | tf_op jit(solution)/shard_map/dot_general | solution.py:67
  515.0 126.0 %all-gather.4.cloned.1.call-done = bf16[4096,2048]{1,0:T(8,128)(2,1)} async-done(((bf16[512,2048]{1,0:T(8,128)(2,1)}), bf16[4096,2048]{1,0:T(8,128)(2,1)}) %all-gather.4.cloned.1.call-update) | async-done | bytes 16777232 | tf_op jit(solution)/shard_map/all_gather | solution.py:540
  641.0 23.4 %fusion.86 = f32[4096,1024]{1,0:T(8,128)} fusion(bf16[4096,2048]{1,0:T(8,128)(2,1)} %all-gather.4.cloned.1.call-done, bf16[2048,1024]{1,0:T(8,128)(2,1)} %bitcast.146), kind=kOutput, calls=%fused_computation.163 | convolution fusion | flops 17179869184 | bytes 37748736 | tf_op jit(solution)/shard_map/dot_general | solution.py:57
  664.4 35.5 %fusion.3 = (bf16[4096,1024]{1,0:T(8,128)(2,1)}, bf16[4096,1024]{1,0:T(8,128)(2,1)}, bf16[4096,1024]{1,0:T(8,128)(2,1)}) fusion(f32[4096,1024]{1,0:T(8,128)} %fusion.86, bf16[4096,1024]{1,0:T(8,128)(2,1)} %convolution_convert_fusion.1, bf16[4096,2048]{1,0:T(8,128)(2,1)} %all-gather.4.cloned.1.call-done, bf16[2048,1024]{1,0:T(8,128)(2,1)} %bitcast.148), kind=kOutput, calls=%fused_computation.8 | convolution fusion | flops 17251172352 | bytes 71303168 | tf_op jit(solution)/shard_map/dot_general | solution.py:57
  699.9 25.6 %fusion.87 = f32[4096,2048]{1,0:T(8,128)} fusion(bf16[4096,1024]{1,0:T(8,128)(2,1)} %get-tuple-element.140, bf16[2048,1024]{1,0:T(8,128)(2,1)} %bitcast.149), kind=kOutput, calls=%fused_computation.164 | convolution fusion | flops 17179869184 | bytes 46137344 | tf_op jit(solution)/shard_map/dot_general | solution.py:67
  725.5 26.7 %add_convert_fusion = bf16[4096,2048]{1,0:T(8,128)(2,1)} fusion(f32[4096,2048]{1,0:T(8,128)} %fusion.87, bf16[4096,1024]{1,0:T(8,128)(2,1)} %get-tuple-element.142, bf16[2048,1024]{1,0:T(8,128)(2,1)S(1)} %bitcast.147), kind=kOutput, calls=%fused_computation | convolution fusion | flops 17196646400 | bytes 62914560 | tf_op jit(solution)/shard_map/dot_general | solution.py:67
  752.3 23.7 %convolution_convert_fusion = bf16[4096,2048]{1,0:T(8,128)(2,1)} fusion(bf16[4096,1024]{1,0:T(8,128)(2,1)} %get-tuple-element.141, bf16[1024,2048]{1,0:T(8,128)(2,1)} %get-tuple-element.41), kind=kOutput, calls=%fused_computation.12 | convolution fusion | flops 17188257792 | bytes 29360128 | tf_op jit(solution)/shard_map/dot_general | solution.py:57
  776.0 142.8 %reduce-scatter.10.cloned.1.call-done = bf16[512,2048]{1,0:T(8,128)(2,1)} async-done(((bf16[4096,2048]{1,0:T(8,128)(2,1)}), bf16[512,2048]{1,0:T(8,128)(2,1)}) %reduce-scatter.10.cloned.1.call-update) | async-done | bytes 2097168 | tf_op jit(solution)/shard_map/reduce_scatter | solution.py:551
  923.6 164.2 %reduce-scatter.8.cloned.1.call-done = bf16[512,2048]{1,0:T(8,128)(2,1)} async-done(((bf16[4096,2048]{1,0:T(8,128)(2,1)}), bf16[512,2048]{1,0:T(8,128)(2,1)}) %reduce-scatter.8.cloned.1.call-update) | async-done | bytes 2097168 | tf_op jit(solution)/shard_map/reduce_scatter | solution.py:658
  1093.1 9.7 convert_bitcast_fusion.2
  1102.9 52.0 %all_to_all.22 = bf16[8,512,256]{1,2,0:T(8,128)(2,1)S(1)} all-to-all(bf16[8,512,256]{1,2,0:T(8,128)(2,1)S(1)} %convert_bitcast_fusion.2), channel_id=1, replica_groups=mesh['narrow'=4,'wide'=8] {'wide'}, dimensions={0} | all-to-all | bytes 4194304 | tf_op jit(solution)/shard_map/all_to_all | solution.py:544
  1157.7 8.2 fusion.66
  1174.8 119.2 %attend_back.1 = bf16[4096,384]{1,0:T(8,128)(2,1)} custom-call(bf16[4096,384]{1,0:T(8,128)(2,1)} %bitcast.125, bf16[4096,256]{1,0:T(8,128)(2,1)} %get-tuple-element.144.g_ref, f32[4,4096]{1,0:T(4,128)} %bitcast.135), custom_call_target="tpu_custom_call" | custom-call | flops 85899345920 | bytes 18874368 | tf_op jit(solution)/shard_map/attend_back/pallas_call | solution.py:229
  1312.3 61.5 %all-to-all-done.3 = bf16[8,512,384]{1,2,0:T(8,128)(2,1)S(1)} async-done(((bf16[8,512,384]{1,2,0:T(8,128)(2,1)}), bf16[8,512,384]{1,2,0:T(8,128)(2,1)S(1)}, u32[]{:S(2)}, u32[]{:S(2)}) %all-to-all-start.3) | async-done | bytes 3145760 | tf_op jit(solution)/shard_map/all_to_all | solution.py:544
  1398.0 10.6 convert_bitcast_fusion
  1408.6 16.0 pad_maximum_fusion
  1424.7 23.7 %convolution_convert_fusion.4 = bf16[2048,1024]{1,0:T(8,128)(2,1)} fusion(bf16[4096,2048]{1,0:T(8,128)(2,1)} %all-gather.4.cloned.1.call-done, bf16[4096,1024]{1,0:T(8,128)(2,1)} %get-tuple-element.140), kind=kOutput, calls=%fused_computation.62 | convolution fusion | flops 17181966336 | bytes 29360128 | tf_op jit(solution)/shard_map/dot_general | solution.py:61
  1448.4 24.1 %convolution_convert_fusion.3 = bf16[2048,1024]{1,0:T(8,128)(2,1)} fusion(bf16[4096,2048]{1,0:T(8,128)(2,1)} %all-gather.4.cloned.1.call-done, bf16[4096,1024]{1,0:T(8,128)(2,1)} %get-tuple-element.142), kind=kOutput, calls=%fused_computation.61 | convolution fusion | flops 17181966336 | bytes 29360128 | tf_op jit(solution)/shard_map/dot_general | solution.py:61
  1472.7 24.3 %convolution_convert_fusion.2 = bf16[1024,2048]{1,0:T(8,128)(2,1)} fusion(bf16[4096,1024]{1,0:T(8,128)(2,1)} %get-tuple-element.141, bf16[4096,2048]{1,0:T(8,128)(2,1)} %bitcast.145), kind=kOutput, calls=%fused_computation.60 | convolution fusion | flops 17181966336 | bytes 29360128 | tf_op jit(solution)/shard_map/dot_general | solution.py:61
  1497.0 114.4 %reduce-scatter.12.cloned.1.call-done = bf16[8,512,640]{1,2,0:T(8,128)(2,1)} async-done(((bf16[8,2048,640]{1,2,0:T(8,128)(2,1)}), bf16[8,512,640]{1,2,0:T(8,128)(2,1)}) %reduce-scatter.12.cloned.1.call-update) | async-done | bytes 5242896 | tf_op jit(solution)/shard_map/reduce_scatter | solution.py:710
  1629.2 38.6 %reduce-scatter.16.cloned.1.call-done = bf16[512,1024]{1,0:T(8,128)(2,1)} async-done(((bf16[2048,1024]{1,0:T(8,128)(2,1)}), bf16[512,1024]{1,0:T(8,128)(2,1)}) %reduce-scatter.16.cloned.1.call-update) | async-done | bytes 1048592 | tf_op jit(solution)/shard_map/reduce_scatter | solution.py:721
  1674.3 49.0 %reduce-scatter.18.cloned.1.call-done = bf16[512,1024]{1,0:T(8,128)(2,1)} async-done(((bf16[2048,1024]{1,0:T(8,128)(2,1)}), bf16[512,1024]{1,0:T(8,128)(2,1)}) %reduce-scatter.18.cloned.1.call-update) | async-done | bytes 1048592 | tf_op jit(solution)/shard_map/reduce_scatter | solution.py:724
  1723.4 7.2 multiply_subtract_fusion.1
  1730.5 48.7 %reduce-scatter.20.cloned.1.call-done = bf16[1024,512]{1,0:T(8,128)(2,1)} async-done(((bf16[1024,2048]{1,0:T(8,128)(2,1)}), bf16[1024,512]{1,0:T(8,128)(2,1)}) %reduce-scatter.20.cloned.1.call-update) | async-done | bytes 1048592 | tf_op jit(solution)/shard_map/reduce_scatter | solution.py:727
  1785.9 12.3 fusion.18
  1798.2 41.5 %all-reduce.4 = (f32[2,2048]{1,0:T(2,128)S(1)}, f32[2,64]{1,0:T(2,128)S(1)}) all-reduce(f32[2,2048]{1,0:T(2,128)S(1)} %pad_maximum_fusion.6, f32[2,64]{1,0:T(2,128)S(1)} %pad_maximum_fusion.7), channel_id=1, replica_groups=mesh['narrow'=4,'wide'=8] {'narrow','wide'}, use_global_device_ids=true, to_apply=%region_18.19 | all-reduce | flops 4224 | bytes 33792 | tf_op jit(solution)/shard_map/psum | solution.py:708
  (262 shorter events, 174.9 us)
Async XLA Ops:
  7.2 633.8 %all-gather.4.cloned.1.call-start = ((), (), s32[]{:S(2)}) async-start(), calls=%async_computation.11 | async-start | bytes 18874368 | tf_op jit(solution)/shard_map/all_gather | solution.py:540
  9.5 256.2 %copy-start.67 = (f32[512]{0:T(512)}, f32[512]{0:T(512)S(1)}, u32[]{:S(2)}) copy-start(f32[512]{0:T(512)S(1)} %fusion.61) | copy-start | bytes 6148
  10.3 255.4 %copy-start.54 = (f32[1,2048]{1,0:T(1,128)}, f32[1,2048]{1,0:T(1,128)S(1)}, u32[]{:S(2)}) copy-start(f32[1,2048]{1,0:T(1,128)S(1)} %get-tuple-element.160) | copy-start | bytes 24580
  10.4 477.2 %copy-start.49 = (f32[1,2048]{1,0:T(1,128)}, f32[1,2048]{1,0:T(1,128)S(1)}, u32[]{:S(2)}) copy-start(f32[1,2048]{1,0:T(1,128)S(1)} %get-tuple-element.159) | copy-start | bytes 24580
  16.8 248.9 %copy-start.11 = (bf16[512,2048]{1,0:T(8,128)(2,1)S(1)}, bf16[512,2048]{1,0:T(8,128)(2,1)}, u32[]{:S(2)}) copy-start(bf16[512,2048]{1,0:T(8,128)(2,1)} %param.30) | copy-start | bytes 6291460
  490.8 428.1 %reduce-scatter.10.cloned.1.call-start = ((), (), s32[]{:S(2)}) async-start(), calls=%async_computation.13 | async-start | bytes 18874368 | tf_op jit(solution)/shard_map/reduce_scatter | solution.py:551
  752.2 335.6 %reduce-scatter.8.cloned.1.call-start = ((), (), s32[]{:S(2)}) async-start(), calls=%async_computation.12 | async-start | bytes 18874368 | tf_op jit(solution)/shard_map/reduce_scatter | solution.py:658
  776.0 142.9 %copy-start.50 = (f32[1,2048]{1,0:T(1,128)S(1)}, f32[1,2048]{1,0:T(1,128)}, u32[]{:S(2)}) copy-start(f32[1,2048]{1,0:T(1,128)} %copy-done.49) | copy-start | bytes 24580
  776.0 142.9 %copy-start.53 = (f32[512]{0:T(512)S(1)}, f32[512]{0:T(512)}, u32[]{:S(2)}) copy-start(f32[512]{0:T(512)} %copy-done.52) | copy-start | bytes 6148
  776.0 147.6 %copy-start.64 = (f32[512]{0:T(512)S(1)}, f32[512]{0:T(512)}, u32[]{:S(2)}) copy-start(f32[512]{0:T(512)} %copy-done.63) | copy-start | bytes 6148
  776.0 311.8 %copy-start.5 = (bf16[512,2048]{1,0:T(8,128)(2,1)S(1)}, bf16[512,2048]{1,0:T(8,128)(2,1)}, u32[]{:S(2)}) copy-start(bf16[512,2048]{1,0:T(8,128)(2,1)} %grad_ref.1) | copy-start | bytes 6291460
  1298.7 75.1 %all-to-all-start.3 = ((bf16[8,512,384]{1,2,0:T(8,128)(2,1)}), bf16[8,512,384]{1,2,0:T(8,128)(2,1)S(1)}, u32[]{:S(2)}, u32[]{:S(2)}) async-start(bf16[8,512,384]{1,2,0:T(8,128)(2,1)} %copy.88), calls=%async_computation.5 | async-start | bytes 6291456 | tf_op jit(solution)/shard_map/all_to_all | solution.py:544
  1302.4 309.0 %reduce-scatter.12.cloned.1.call-start = ((), (), s32[]{:S(2)}) async-start(), calls=%async_computation.14 | async-start | bytes 26214400 | tf_op jit(solution)/shard_map/reduce_scatter | solution.py:710
  1305.3 69.7 %copy-start.33 = (f32[512,32]{0,1:T(8,128)S(1)}, f32[512,32]{0,1:T(8,128)}, u32[]{:S(2)}) copy-start(f32[512,32]{0,1:T(8,128)} %copy-done.32) | copy-start | bytes 196612
  1305.3 69.7 %copy-start.35 = (f32[512,32]{0,1:T(8,128)S(1)}, f32[512,32]{0,1:T(8,128)}, u32[]{:S(2)}) copy-start(f32[512,32]{0,1:T(8,128)} %copy-done.34) | copy-start | bytes 196612
  1312.3 62.8 %copy-start.46 = (f32[8,512]{1,0:T(8,128)S(1)}, f32[8,512]{1,0:T(8,128)}, u32[]{:S(2)}) copy-start(f32[8,512]{1,0:T(8,128)} %copy-done.45) | copy-start | bytes 49156
  1312.3 62.8 %copy-start.66 = (f32[64]{0:T(128)S(1)}, f32[64]{0:T(128)}, u32[]{:S(2)}) copy-start(f32[64]{0:T(128)} %copy-done.65) | copy-start | bytes 772
  1312.3 64.5 %copy-start.48 = (f32[8,512]{1,0:T(8,128)S(1)}, f32[8,512]{1,0:T(8,128)}, u32[]{:S(2)}) copy-start(f32[8,512]{1,0:T(8,128)} %copy-done.47) | copy-start | bytes 49156
  1424.6 243.2 %reduce-scatter.16.cloned.1.call-start = ((), (), s32[]{:S(2)}) async-start(), calls=%async_computation.16 | async-start | bytes 5242880 | tf_op jit(solution)/shard_map/reduce_scatter | solution.py:721
  1448.4 275.0 %reduce-scatter.18.cloned.1.call-start = ((), (), s32[]{:S(2)}) async-start(), calls=%async_computation.17 | async-start | bytes 5242880 | tf_op jit(solution)/shard_map/reduce_scatter | solution.py:724
  1472.6 306.6 %reduce-scatter.20.cloned.1.call-start = ((), (), s32[]{:S(2)}) async-start(), calls=%async_computation.18 | async-start | bytes 5242880 | tf_op jit(solution)/shard_map/reduce_scatter | solution.py:727
  1496.9 115.0 %copy-start.27 = (f32[512,256]{1,0:T(8,128)S(1)}, f32[512,256]{1,0:T(8,128)}, u32[]{:S(2)}) copy-start(f32[512,256]{1,0:T(8,128)} %param.33) | copy-start | bytes 1572868
  1496.9 115.9 %copy-start.36 = (f32[512,512]{1,0:T(8,128)S(1)}, f32[512,512]{1,0:T(8,128)}, u32[]{:S(2)}) copy-start(f32[512,512]{1,0:T(8,128)} %param.36) | copy-start | bytes 3145732
  1496.9 345.6 %reduce-scatter.14.cloned.1.call-start = ((), (), s32[]{:S(2)}) async-start(), calls=%async_computation.15 | async-start | bytes 5898240 | tf_op jit(solution)/shard_map/reduce_scatter | solution.py:711
  1611.4 253.8 %all-gather.6.cloned.1.call-start = ((), (), s32[]{:S(2)}) async-start(), calls=%async_computation.19 | async-start | bytes 1179648 | tf_op jit(solution)/shard_map/all_gather | solution.py:714
  1674.3 104.9 %copy-start.10 = (f32[1024,512]{1,0:T(8,128)S(1)}, f32[1024,512]{1,0:T(8,128)}, u32[]{:S(2)}) copy-start(f32[1024,512]{1,0:T(8,128)} %param.51) | copy-start | bytes 6291460
  1785.9 53.9 %copy-start.70 = (f32[2,64]{1,0:T(2,128)S(1)}, f32[2,64]{1,0:T(2,128)}, u32[]{:S(2)}) copy-start(f32[2,64]{1,0:T(2,128)} %param.57) | copy-start | bytes 1540
  1785.9 53.9 %copy-start.71 = (f32[2,64]{1,0:T(2,128)S(1)}, f32[2,64]{1,0:T(2,128)}, u32[]{:S(2)}) copy-start(f32[2,64]{1,0:T(2,128)} %param.58) | copy-start | bytes 1540
  1785.9 58.2 %copy-start.51 = (f32[2,2048]{1,0:T(2,128)S(1)}, f32[2,2048]{1,0:T(2,128)}, u32[]{:S(2)}) copy-start(f32[2,2048]{1,0:T(2,128)} %param.54) | copy-start | bytes 49156
  1785.9 58.2 %copy-start.59 = (f32[2,2048]{1,0:T(2,128)S(1)}, f32[2,2048]{1,0:T(2,128)}, u32[]{:S(2)}) copy-start(f32[2,2048]{1,0:T(2,128)} %param.55) | copy-start | bytes 49156
  1785.9 58.2 %copy-start.60 = (f32[2,2048]{1,0:T(2,128)S(1)}, f32[2,2048]{1,0:T(2,128)}, u32[]{:S(2)}) copy-start(f32[2,2048]{1,0:T(2,128)} %param.56) | copy-start | bytes 49156
  1785.9 58.9 %copy-start.15 = (bf16[512,2048]{1,0:T(8,128)(2,1)S(1)}, bf16[512,2048]{1,0:T(8,128)(2,1)}, u32[]{:S(2)}) copy-start(bf16[512,2048]{1,0:T(8,128)(2,1)} %param.30) | copy-start | bytes 6291460
  (56 other events, 465.8 us)
Sparse Core Ops, SparseCore 0:
  490.9 150.0 all-gather.3
  752.3 166.4 reduce-scatter.9
  921.2 166.5 reduce-scatter.7
  1424.7 186.6 reduce-scatter.11
  1615.0 52.6 reduce-scatter.15
  1670.6 52.6 reduce-scatter.17
  1726.6 52.6 reduce-scatter.19
  1781.5 60.9 reduce-scatter.13
  1844.7 20.4 all-gather.5

commit v3 on v2

--- a/solution.py
+++ b/solution.py
@@ -286,10 +286,7 @@
 
 
 def gather_kernel(
-    gate_ref, up_ref, down_ref, att_ref, grad_ref,
-    gate_all, up_all, down_all, att_all, grad_all,
-    own_sem, ffn_send, ffn_got, line_send, line_got, side_send, side_got,
-    core_send, core_got, grad_send, grad_got, pair_send, pair_got,
+    att_ref, att_all, own_sem, line_send, line_got, side_send, side_got, core_send, core_got
 ):
     narrow, wide, chip, core = place()
     beside = narrow + 1 - 2 * (narrow % 2)
@@ -297,26 +294,11 @@
     corner = (beside + 2) % 4
     rows = att_ref.shape[0]
     half_rows = rows // 2
-    columns = down_ref.shape[1]
     other = (narrow, 2 * chip + 1 - core)
     left = (narrow, wide - 2)
     right = (narrow, wide + 2)
     sides = ((beside, wide), (across, wide))
     near = (beside, across)
-    greet_neighbours()
-
-    def ffn_own(k, who):
-        if k == 2:
-            return down_all.at[:, pl.ds(pl.multiple_of(who * columns, columns), columns)]
-        return (gate_all, up_all)[k].at[who]
-
-    def ffn_half(k, who, half):
-        if k == 2:
-            size = down_ref.shape[0] // 2
-            return down_all.at[
-                pl.ds(half * size, size), pl.ds(pl.multiple_of(who * columns, columns), columns)
-            ]
-        return (gate_all, up_all)[k].at[who, pl.ds(half * half_rows, half_rows), :]
 
     def att(slot, who):
         return att_all.at[slot, pl.ds(pl.multiple_of(who * rows, rows), rows), :]
@@ -326,214 +308,113 @@
             slot, pl.ds(pl.multiple_of(who * rows + half * half_rows, half_rows), half_rows), :
         ]
 
-    own = []
-    for k, source in enumerate((gate_ref, up_ref, down_ref)):
-        own.append(pltpu.make_async_copy(source, ffn_own(k, narrow), own_sem.at[k]))
-    own.append(pltpu.make_async_copy(att_ref, att(wide, narrow), own_sem.at[3]))
-    own.append(pltpu.make_async_copy(grad_ref, grad_all.at[wide], own_sem.at[4]))
-    for copy in own:
-        copy.start()
-
-    def att_line(at, step, source):
-        slot = 2 * at + core
+    def line(at, step, source):
         return remote(
-            source, att(slot, narrow), line_send.at[at, (step + 1) // 2], line_got.at[at],
-            right if step > 0 else left,
+            source, att(2 * at + core, narrow), line_send.at[at, (step + 1) // 2],
+            line_got.at[at], right if step > 0 else left,
         )
 
-    def grad_line(at, step, source):
-        slot = 2 * at + core
-        return remote(
-            source, grad_all.at[slot], grad_send.at[at, (step + 1) // 2], grad_got.at[at],
-            right if step > 0 else left,
-        )
-
-    def grad_pair(at, source):
-        slot = 2 * at + core
-        return remote(source, grad_all.at[slot], pair_send.at[at], pair_got.at[at], other)
-
-    def both_ways(line, at, source_of, act):
+    def both_ways(at, source, act):
         @pl.when(jnp.logical_and(at <= chip, chip < 3))
         def _():
-            act(line(at, 1, source_of(at)))
+            act(line(at, 1, source))
 
         @pl.when(jnp.logical_and(at >= chip, chip > 0))
         def _():
-            act(line(at, -1, source_of(at)))
-
-    def att_side(at, k, source):
-        slot = 2 * at + core
-        return remote(source, att(slot, narrow), side_send.at[at, k], side_got.at[at, k], sides[k])
-
-    def att_got(at, k):
-        slot = 2 * at + core
-        target = att(slot, near[k])
+            act(line(at, -1, source))
+
+    def side(at, k, source):
+        return remote(
+            source, att(2 * at + core, narrow), side_send.at[at, k], side_got.at[at, k], sides[k]
+        )
+
+    def side_arrival(at, k):
+        target = att(2 * at + core, near[k])
         return remote(target, target, side_send.at[at, k], side_got.at[at, k], sides[k])
 
-    def att_forward(at, k):
-        slot = 2 * at + core
-        piece = att_half(slot, near[k], k)
+    def forward(at, k):
+        piece = att_half(2 * at + core, near[k], k)
         return remote(piece, piece, side_send.at[at, 2 + k], side_got.at[at, 2 + k], sides[1 - k])
 
-    def att_corner(at, k):
-        slot = 2 * at + core
-        piece = att_half(slot, corner, k)
+    def corner_arrival(at, k):
+        piece = att_half(2 * at + core, corner, k)
         return remote(piece, piece, side_send.at[at, 2 + k], side_got.at[at, 2 + k], sides[1 - k])
 
-    def att_core(at, who):
-        slot = 2 * at + core
-        piece = att(slot, who)
+    def pair(at, who, half_of):
+        piece = att(2 * at + half_of, who)
         return remote(piece, piece, core_send.at[at, who], core_got.at[at, who], other)
 
-    def att_core_got(at, who):
-        slot = 2 * at + 1 - core
-        piece = att(slot, who)
-        return remote(piece, piece, core_send.at[at, who], core_got.at[at, who], other)
-
-    def ffn_side(k, j):
-        source = (gate_ref, up_ref, down_ref)[k]
-        return remote(source, ffn_own(k, narrow), ffn_send.at[k, j], ffn_got.at[k, j], sides[j])
-
-    def ffn_got_copy(k, j):
-        target = ffn_own(k, near[j])
-        return remote(target, target, ffn_send.at[k, j], ffn_got.at[k, j], sides[j])
-
-    def ffn_forward(k, j):
-        piece = ffn_half(k, near[j], j)
-        return remote(piece, piece, ffn_send.at[k, 2 + j], ffn_got.at[k, 2 + j], sides[1 - j])
-
-    def ffn_corner(k, j):
-        piece = ffn_half(k, corner, j)
-        return remote(piece, piece, ffn_send.at[k, 2 + j], ffn_got.at[k, 2 + j], sides[1 - j])
-
     start = lambda copy: copy.start()
-    sent = lambda copy: copy.wait_send()
-    got = lambda copy: copy.wait_recv()
-
-    both_ways(att_line, chip, lambda at: att_ref, start)
-    both_ways(grad_line, chip, lambda at: grad_ref, start)
-    grad_pair(chip, grad_ref).start()
+    greet_neighbours()
+    both_ways(chip, att_ref, start)
     for k in range(2):
-        att_side(chip, k, att_ref).start()
-    for k in range(3):
-        for j in range(2):
-            ffn_side(k, j).start()
-    own[3].wait()
-    att_core(chip, narrow).start()
-
-    def att_hop(hop):
-        for at, valid in ((chip - hop, chip >= hop), (chip + hop, chip + hop <= 3)):
+        side(chip, k, att_ref).start()
+    own = pltpu.make_async_copy(att_ref, att(wide, narrow), own_sem)
+    own.start()
+    own.wait()
+    pair(chip, narrow, core).start()
+
+    def hop(distance):
+        for at, valid in (
+            (chip - distance, chip >= distance), (chip + distance, chip + distance <= 3)
+        ):
 
             @pl.when(valid)
             def _():
-                slot = 2 * at + core
-                att_line(at, 1, att(slot, narrow)).wait_recv()
-                both_ways(att_line, at, lambda at: att(2 * at + core, narrow), start)
+                piece = att(2 * at + core, narrow)
+                line(at, 1, piece).wait_recv()
+                both_ways(at, piece, start)
                 for k in range(2):
-                    att_side(at, k, att(slot, narrow)).start()
-                att_core(at, narrow).start()
-
-    def ffn_step(k):
-        for j in range(2):
-            ffn_got_copy(k, j).wait_recv()
-            ffn_forward(k, j).start()
-
-    def grad_step(hop):
-        for at, valid in ((chip - hop, chip >= hop), (chip + hop, chip + hop <= 3)):
-
-            @pl.when(valid)
-            def _():
-                slot = 2 * at + core
-                grad_line(at, 1, grad_all.at[slot]).wait_recv()
-                both_ways(grad_line, at, lambda at: grad_all.at[2 * at + core], start)
-                grad_pair(at, grad_all.at[slot]).start()
-
-    def att_step(at):
+                    side(at, k, piece).start()
+                pair(at, narrow, core).start()
+
+    def around(at):
         for k in range(2):
-            att_got(at, k).wait_recv()
-            att_forward(at, k).start()
-            att_core(at, near[k]).start()
-
-    att_hop(1)
-    att_hop(2)
-    grad_step(1)
-    for k in range(3):
-        ffn_step(k)
-    att_hop(3)
-    att_step(chip)
-    att_step((chip + 1) % 4)
-    grad_step(2)
-    att_step((chip + 3) % 4)
-    att_step((chip + 2) % 4)
+            side_arrival(at, k).wait_recv()
+            forward(at, k).start()
+            pair(at, near[k], core).start()
+
+    upper = chip // 2
+    second = chip + 1 - 2 * upper
+    last = 3 - 3 * upper
+    order = (chip, second, 6 - chip - second - last, last)
+    for step in range(4):
+        if step < 3:
+            hop(step + 1)
+        around(order[step])
+    for at in order:
+        for k in range(2):
+            corner_arrival(at, k).wait_recv()
+        pair(at, corner, core).start()
+
     for at in range(4):
+        both_ways(at, att_ref, lambda copy: copy.wait_send())
+        for who in range(4):
+            pair(at, who, 1 - core).wait_recv()
+            pair(at, who, core).wait_send()
         for k in range(2):
-            att_corner(at, k).wait_recv()
-        att_core(at, corner).start()
-    grad_step(3)
-
-    for k in range(3):
-        for j in range(2):
-            ffn_corner(k, j).wait_recv()
-            ffn_side(k, j).wait_send()
-            ffn_forward(k, j).wait_send()
-    for at in range(4):
-        slot = 2 * at + 1 - core
-        remote(
-            grad_all.at[slot], grad_all.at[slot], pair_send.at[at], pair_got.at[at], other
-        ).wait_recv()
-        grad_pair(at, grad_ref).wait_send()
-        both_ways(att_line, at, lambda at: att_ref, sent)
-        both_ways(grad_line, at, lambda at: grad_ref, sent)
-        for who in range(4):
-            att_core_got(at, who).wait_recv()
-            att_core(at, who).wait_send()
-        for k in range(2):
-            att_side(at, k, att_ref).wait_send()
-            att_forward(at, k).wait_send()
-    for k in (0, 1, 2, 4):
-        own[k].wait()
-
-
-def gather_all(gate, up, down, att, grad):
+            side(at, k, att_ref).wait_send()
+            forward(at, k).wait_send()
+
+
+def gather_weights(att):
     narrow_count = lax.axis_size("narrow")
     wide_count = lax.axis_size("wide")
-    rows = att.shape[0]
     if narrow_count != 4 or wide_count != 8:
-        att = lax.all_gather(lax.all_gather(att, "wide", axis=0), "narrow", axis=1, tiled=True)
-        return (
-            lax.all_gather(gate, "narrow", axis=0, tiled=True),
-            lax.all_gather(up, "narrow", axis=0, tiled=True),
-            lax.all_gather(down, "narrow", axis=1, tiled=True),
-            att,
-            lax.all_gather(grad, "wide", axis=0, tiled=True),
-        )
-    low = jnp.bfloat16
+        return lax.all_gather(lax.all_gather(att, "wide", axis=0), "narrow", axis=1, tiled=True)
     dma = pltpu.SemaphoreType.DMA
-    gate_all, up_all, down_all, att_all, grad_all = pl.pallas_call(
+    return pl.pallas_call(
         gather_kernel,
-        out_shape=[
-            jax.ShapeDtypeStruct((narrow_count,) + gate.shape, low),
-            jax.ShapeDtypeStruct((narrow_count,) + up.shape, low),
-            jax.ShapeDtypeStruct((down.shape[0], narrow_count * down.shape[1]), low),
-            jax.ShapeDtypeStruct((wide_count, narrow_count * rows, att.shape[1]), low),
-            jax.ShapeDtypeStruct((wide_count,) + grad.shape, low),
-        ],
-        in_specs=[pl.BlockSpec(memory_space=pl.ANY)] * 5,
-        out_specs=[pl.BlockSpec(memory_space=pl.ANY)] * 5,
+        out_shape=jax.ShapeDtypeStruct((8, 4 * att.shape[0], att.shape[1]), jnp.bfloat16),
+        in_specs=[pl.BlockSpec(memory_space=pl.ANY)],
+        out_specs=pl.BlockSpec(memory_space=pl.ANY),
         scratch_shapes=[
-            dma((5,)), dma((3, 4)), dma((3, 4)), dma((4, 2)), dma((4,)), dma((4, 4)), dma((4, 4)),
-            dma((4, 4)), dma((4, 4)), dma((4, 2)), dma((4,)), dma((4,)), dma((4,)),
+            dma, dma((4, 2)), dma((4,)), dma((4, 4)), dma((4, 4)), dma((4, 4)), dma((4, 4)),
         ],
         compiler_params=pltpu.CompilerParams(collective_id=1, has_side_effects=True),
-        name="gather_all",
-    )(gate, up, down, att, grad)
-    return (
-        gate_all.reshape(-1, gate.shape[1]),
-        up_all.reshape(-1, up.shape[1]),
-        down_all,
-        att_all,
-        grad_all.reshape(-1, grad.shape[1]),
-    )
+        cost_estimate=pl.CostEstimate(flops=0, bytes_accessed=300 << 20, transcendentals=0),
+        name="gather_weights",
+    )(att)
 
 
 def gather_rows(shard):
@@ -598,13 +479,11 @@
     value_own = lax.dynamic_slice_in_dim(value_weight, key_slot * head_dim, head_dim, 1)
     query_columns = query_weight.shape[1]
     att_own = jnp.concatenate([query_weight, key_own, value_own, output_weight.T], axis=1)
-    gate_local, up_local, down_local, att_full, grad_rows = gather_all(
-        gate_weight.astype(jnp.bfloat16),
-        up_weight.astype(jnp.bfloat16),
-        down_weight.astype(jnp.bfloat16),
-        att_own.astype(jnp.bfloat16),
-        out_grad,
-    )
+    att_full = gather_weights(att_own.astype(jnp.bfloat16))
+    gate_local = lax.all_gather(gate_weight.astype(jnp.bfloat16), "narrow", axis=0, tiled=True)
+    up_local = lax.all_gather(up_weight.astype(jnp.bfloat16), "narrow", axis=0, tiled=True)
+    down_local = lax.all_gather(down_weight.astype(jnp.bfloat16), "narrow", axis=1, tiled=True)
+    grad_rows = lax.all_gather(out_grad, "wide", axis=0, tiled=True)
     group_columns = query_columns + 2 * head_dim
     input_full = att_full[:, :, :group_columns]
     output_full = att_full[:, :, group_columns:]
@@ -641,8 +520,12 @@
     )
     packed = swap(jnp.concatenate([query_rot, key_rot.astype(jnp.bfloat16), value_rows], axis=2))
     packed = packed.reshape(wide_count * shard_rows, group_columns)
+    packed, down_local, gate_local = lax.optimization_barrier((packed, down_local, gate_local))
     attended, weight_sums, attended_low = attend(packed, local_heads)
     attended_low = swap(attended_low.reshape(wide_count, shard_rows, query_columns))
+    attended_low, up_local, grad_rows = lax.optimization_barrier(
+        (attended_low, up_local, grad_rows)
+    )
     branch = jnp.einsum("gth,gdh->td", attended_low, output_full, preferred_element_type=jnp.float32)
     middle = residual + branch
     normed_mid, norm_mid_back = jax.vjp(rms_scale, middle, norm_gains[1])
@@ -653,22 +536,11 @@
         lambda gate_in, up_in: jax.nn.silu(gate_in) * up_in, gate_pre, up_pre
     )
     hidden_low = hidden.astype(jnp.bfloat16)
-    block_out = (
-        middle
-        + lax.psum_scatter(
-            dot_last(hidden_low, down_local).astype(jnp.bfloat16),
-            "wide",
-            scatter_dimension=0,
-            tiled=True,
-        ).astype(jnp.float32)
-    ).astype(jnp.bfloat16)
+    block_part = dot_last(hidden_low, down_local).astype(jnp.bfloat16)
     hidden_grad = dot_back(grad_rows, down_local).astype(jnp.bfloat16)
-    down_grad = dot_first(hidden_low, grad_rows)
     gate_grad, up_grad = hidden_back(hidden_grad.astype(jnp.float32))
     gate_grad = gate_grad.astype(jnp.bfloat16)
     up_grad = up_grad.astype(jnp.bfloat16)
-    gate_wgrad = dot_first(rows_mid, gate_grad)
-    up_wgrad = dot_first(rows_mid, up_grad)
     mid_back = sum_back(((gate_grad, gate_local), (up_grad, up_local)), shard_rows)
     middle_part, mid_gain_grad = norm_mid_back(mid_back)
     middle_grad = out_grad.astype(jnp.float32) + middle_part
@@ -680,11 +552,29 @@
         "td,gth->gdh", branch_grad, attended_low, preferred_element_type=jnp.float32
     )
     head_grad = swap(attended_grad).reshape(wide_count * shard_rows, query_columns)
+    head_grad, block_part, hidden_low, gate_grad, up_grad = lax.optimization_barrier(
+        (head_grad, block_part, hidden_low, gate_grad, up_grad)
+    )
+    block_sum = lax.psum_scatter(block_part, "wide", scatter_dimension=0, tiled=True)
+    down_total = lax.psum_scatter(
+        dot_first(hidden_low, grad_rows).astype(jnp.bfloat16),
+        "narrow", scatter_dimension=1, tiled=True,
+    )
+    gate_total = lax.psum_scatter(
+        dot_first(rows_mid, gate_grad).astype(jnp.bfloat16),
+        "narrow", scatter_dimension=0, tiled=True,
+    )
+    up_total = lax.psum_scatter(
+        dot_first(rows_mid, up_grad).astype(jnp.bfloat16),
+        "narrow", scatter_dimension=0, tiled=True,
+    )
     head_grad = head_grad.astype(jnp.float32) / weight_sums
     scaled_grad = head_grad.astype(jnp.bfloat16)
     grad_dot = jnp.sum((head_grad * attended).reshape(-1, local_heads, head_dim), axis=-1).T
     packed_grad = attend_back(packed, scaled_grad, grad_dot, local_heads)
     packed_grad = swap(packed_grad.reshape(wide_count, shard_rows, group_columns))
+    packed_grad, block_sum = lax.optimization_barrier((packed_grad, block_sum))
+    block_out = (middle + block_sum.astype(jnp.float32)).astype(jnp.bfloat16)
     query_rot_grad = packed_grad[:, :, :query_columns].astype(jnp.float32).reshape(
         wide_count, shard_rows, local_heads, head_dim
     )
@@ -705,7 +595,10 @@
     input_grad = middle_grad + input_part
     gain_stack = jnp.stack([in_gain_grad, mid_gain_grad])
     head_stack = jnp.stack([query_gain_grad, key_gain_grad])
-    gain_total, head_total = lax.psum((gain_stack, head_stack), ("narrow", "wide"))
+    gains = jnp.concatenate([gain_stack, head_stack], axis=1)
+    gains = jnp.sum(lax.all_gather(gains, ("narrow", "wide"), axis=0), axis=0)
+    gain_total = gains[:, :model_width]
+    head_total = gains[:, model_width:]
     att_wgrad = jnp.concatenate([input_wgrad, output_wgrad], axis=2).astype(jnp.bfloat16)
     att_total = lax.psum_scatter(att_wgrad, "narrow", scatter_dimension=1, tiled=True)
     input_total = lax.psum_scatter(att_total, "wide", scatter_dimension=0)
@@ -718,15 +611,9 @@
     key_total = spread[0].reshape(key_weight.shape)
     value_total = spread[1].reshape(value_weight.shape)
     gate_total, up_total, down_total = (
-        lax.psum_scatter(
-            gate_wgrad.astype(jnp.bfloat16), "narrow", scatter_dimension=0, tiled=True
-        ).astype(jnp.float32),
-        lax.psum_scatter(
-            up_wgrad.astype(jnp.bfloat16), "narrow", scatter_dimension=0, tiled=True
-        ).astype(jnp.float32),
-        lax.psum_scatter(
-            down_grad.astype(jnp.bfloat16), "narrow", scatter_dimension=1, tiled=True
-        ).astype(jnp.float32),
+        gate_total.astype(jnp.float32),
+        up_total.astype(jnp.float32),
+        down_total.astype(jnp.float32),
     )
     wide_rate = D ** (-0.5)
     query_new = adam_update(

time: 1900 us -> 1740 us (0.916)
  Pallas kernels: 427 us -> 328 us
  waiting for transfers between devices: 754 us -> 701 us
  blocking collectives: 220 us -> 178 us
    reduce_scatter x4, waiting for transfers between devices: 301 us -> 136 us  [the longest x1 49 us: shards(): lax.psum_scatter(dot_first(rows_mid, up_grad).astype(jnp.bfloat16), 'narr...]
    pallas_call x1, Pallas kernels: 247 us -> 147 us  [gather_weights(): pl.pallas_call(gather_kernel, out_shape=jax.ShapeDtypeStruct((8, 4 * att....]
    all_to_all x1 -> x3, waiting for transfers between devices: 61.5 us -> 152 us  [swap(): return lax.all_to_all(blocks, 'wide', 0, 0)]
    all_to_all x3 -> x1, blocking collectives: 179 us -> 129 us  [swap(): return lax.all_to_all(blocks, 'wide', 0, 0)]
    all_gather x0 -> x1, blocking collectives: none -> 49 us  [shards(): gains = jnp.sum(lax.all_gather(gains, ('narrow', 'wide'), axis=0), axis=0)]
    psum x1 -> x0, blocking collectives: 41.5 us -> none  [shards(): lax.psum((gain_stack, head_stack), ('narrow', 'wide'))]
    reduce_scatter x1, waiting for transfers between devices: 143 us -> 167 us  [sum_back(): lax.psum_scatter(summed.astype(jnp.bfloat16), 'wide', scatter_dimension=0...]
  transfers between devices with their start and end apart: 10 -> 16, of which waited for: 10 -> 10; matrix products, arithmetic and copies ran while one was open for 10% -> 15% of each run, Pallas kernels for 0% -> 19%
where the time goes in v3:
time: 1740 us; the launch traced here: 1730 us
  waiting for transfers between devices  701 us (40%)
  Pallas kernels  328 us (19%)
  matrix products  289 us (17%)
  blocking collectives  178 us (10%)
  other arithmetic  116 us (7%)
  local copies, waits for them, and re-layouts  84.1 us (5%)
  starting transfers between devices  17.6 us (1%)
    reduce_scatter x1, waiting for transfers between devices, sum_back(): lax.psum_scatter(summed.astype(jnp.bfloat16), 'wide', scatter_dimension=0...  167 us
    all_to_all x3, waiting for transfers between devices, swap(): return lax.all_to_all(blocks, 'wide', 0, 0)  152 us
    pallas_call x1, Pallas kernels, gather_weights(): pl.pallas_call(gather_kernel, out_shape=jax.ShapeDtypeStruct((8, 4 * att....  147 us
    all_to_all x1, blocking collectives, swap(): return lax.all_to_all(blocks, 'wide', 0, 0)  129 us
    all_gather x1, waiting for transfers between devices, gather_rows(): return lax.all_gather(shard, 'wide', axis=0, tiled=True)  125 us
    pallas_call x1, Pallas kernels, attend_back(): pl.pallas_call(functools.partial(back_kernel, block, heads), out_shape=ja...  120 us
    reduce_scatter x1, waiting for transfers between devices, shards(): lax.psum_scatter(att_wgrad, 'narrow', scatter_dimension=1, tiled=True)  114 us
    dot_general x3, matrix products, dot_last(): return jnp.dot(left, right, preferred_element_type=jnp.float32)  82.7 us
  transfers between devices with their start and end apart: 16, of which 10 were waited for; matrix products, arithmetic and copies ran while one was open for 15% of the time, Pallas kernels for 19%

profile of v3, /device:TPU:0, one launch (start us, length us, event | category | flops | bytes accessed | tf_op | source)
XLA Modules:
  0.0 1727.5 jit_solution(3105655537219215763)
XLA Ops:
  17.2 146.6 %gather_weights.1 = bf16[8,2048,640]{2,1,0:T(8,128)(2,1)} custom-call(bf16[512,640]{1,0:T(8,128)(2,1)} %pad_maximum_fusion.5.att_ref), custom_call_target="tpu_custom_call" | custom-call | bytes 314572800 | tf_op jit(solution)/shard_map/gather_weights/pallas_call | solution.py:406
  164.8 9.6 fusion.29
  192.1 128.8 %all_to_all.20 = bf16[8,512,384]{1,2,0:T(8,128)(2,1)S(1)} all-to-all(bf16[8,512,384]{1,2,0:T(8,128)(2,1)S(1)} %pad_maximum_fusion.1), channel_id=1, replica_groups=mesh['narrow'=4,'wide'=8] {'wide'}, dimensions={0} | all-to-all | bytes 6291456 | tf_op jit(solution)/shard_map/all_to_all | solution.py:425
  323.7 61.4 %attend.1 = (f32[4096,256]{1,0:T(8,128)}, f32[4096,256]{1,0:T(8,128)}, bf16[4096,256]{1,0:T(8,128)(2,1)}) custom-call(bf16[4096,384]{1,0:T(8,128)(2,1)} %bitcast.121), custom_call_target="tpu_custom_call" | custom-call | flops 34359738368 | bytes 18874368 | tf_op jit(solution)/shard_map/attend/pallas_call | solution.py:143
  389.2 8.9 all-to-all-start.1
  398.2 50.7 %all-to-all-done.1 = bf16[8,512,256]{1,2,0:T(8,128)(2,1)} async-done(((bf16[8,512,256]{1,2,0:T(8,128)(2,1)}), bf16[8,512,256]{1,2,0:T(8,128)(2,1)}, u32[]{:S(2)}, u32[]{:S(2)}) %all-to-all-start.1) | async-done | bytes 2097184 | tf_op jit(solution)/shard_map/all_to_all | solution.py:425
  448.8 7.8 multiply_reduce_fusion.2
  461.0 23.6 %convolution_convert_fusion.1 = bf16[4096,1024]{1,0:T(8,128)(2,1)} fusion(bf16[4096,2048]{1,0:T(8,128)(2,1)} %all-gather.16.cloned.1.call-done, bf16[1024,2048]{1,0:T(8,128)(2,1)} %all-gather.10.cloned.1.call-done), kind=kOutput, calls=%fused_computation.24 | convolution fusion | flops 17184063488 | bytes 29360128 | tf_op jit(solution)/shard_map/dot_general | solution.py:67
  484.6 125.1 %all-gather.18.cloned.1.call-done = bf16[4096,2048]{1,0:T(8,128)(2,1)} async-done(((bf16[512,2048]{1,0:T(8,128)(2,1)}), bf16[4096,2048]{1,0:T(8,128)(2,1)}) %all-gather.18.cloned.1.call-update) | async-done | bytes 16777232 | tf_op jit(solution)/shard_map/all_gather | solution.py:421
  609.7 23.4 %fusion.86 = f32[4096,1024]{1,0:T(8,128)} fusion(bf16[4096,2048]{1,0:T(8,128)(2,1)} %all-gather.18.cloned.1.call-done, bf16[2048,1024]{1,0:T(8,128)(2,1)} %all-gather.12.cloned.1.call-done), kind=kOutput, calls=%fused_computation.162 | convolution fusion | flops 17179869184 | bytes 37748736 | tf_op jit(solution)/shard_map/dot_general | solution.py:57
  633.1 35.5 %multiply_convert_fusion = (bf16[4096,1024]{1,0:T(8,128)(2,1)}, bf16[4096,1024]{1,0:T(8,128)(2,1)}, bf16[4096,1024]{1,0:T(8,128)(2,1)}) fusion(f32[4096,1024]{1,0:T(8,128)} %fusion.86, bf16[4096,1024]{1,0:T(8,128)(2,1)} %convolution_convert_fusion.1, bf16[4096,2048]{1,0:T(8,128)(2,1)} %all-gather.18.cloned.1.call-done, ...), kind=kOutput, calls=%fused_computation.9 | convolution fusion | flops 17251172352 | bytes 71303168 | tf_op jit(solution)/shard_map/dot_general | solution.py:57
  668.6 25.6 %fusion.87 = f32[4096,2048]{1,0:T(8,128)} fusion(bf16[4096,1024]{1,0:T(8,128)(2,1)} %get-tuple-element.58, bf16[2048,1024]{1,0:T(8,128)(2,1)} %all-gather.12.cloned.1.call-done), kind=kOutput, calls=%fused_computation.163 | convolution fusion | flops 17179869184 | bytes 46137344 | tf_op jit(solution)/shard_map/dot_general | solution.py:67
  694.2 26.9 %add_convert_fusion = bf16[4096,2048]{1,0:T(8,128)(2,1)} fusion(f32[4096,2048]{1,0:T(8,128)} %fusion.87, bf16[4096,1024]{1,0:T(8,128)(2,1)} %get-tuple-element.59, bf16[2048,1024]{1,0:T(8,128)(2,1)S(1)} %copy-done.71), kind=kOutput, calls=%fused_computation | convolution fusion | flops 17196646400 | bytes 62914560 | tf_op jit(solution)/shard_map/dot_general | solution.py:67
  721.2 166.6 %reduce-scatter.8.cloned.1.call-done = bf16[512,2048]{1,0:T(8,128)(2,1)} async-done(((bf16[4096,2048]{1,0:T(8,128)(2,1)}), bf16[512,2048]{1,0:T(8,128)(2,1)}) %reduce-scatter.8.cloned.1.call-update) | async-done | bytes 2097168 | tf_op jit(solution)/shard_map/reduce_scatter | solution.py:432
  897.5 9.1 convert_bitcast_fusion.2
  910.3 23.7 %convolution_convert_fusion = bf16[4096,2048]{1,0:T(8,128)(2,1)} fusion(bf16[4096,1024]{1,0:T(8,128)(2,1)} %get-tuple-element.60, bf16[1024,2048]{1,0:T(8,128)(2,1)} %all-gather.10.cloned.1.call-done), kind=kOutput, calls=%fused_computation.12 | convolution fusion | flops 17188257792 | bytes 29360128 | tf_op jit(solution)/shard_map/dot_general | solution.py:57
  934.1 25.2 %all-to-all-done.2 = bf16[8,512,256]{1,2,0:T(8,128)(2,1)S(1)} async-done(((bf16[8,512,256]{1,2,0:T(8,128)(2,1)}), bf16[8,512,256]{1,2,0:T(8,128)(2,1)S(1)}, u32[]{:S(2)}, u32[]{:S(2)}) %all-to-all-start.2) | async-done | bytes 2097184 | tf_op jit(solution)/shard_map/all_to_all | solution.py:425
  979.2 119.8 %attend_back.1 = bf16[4096,384]{1,0:T(8,128)(2,1)} custom-call(bf16[4096,384]{1,0:T(8,128)(2,1)} %bitcast.122, bf16[4096,256]{1,0:T(8,128)(2,1)} %get-tuple-element.187.g_ref, f32[4,4096]{1,0:T(4,128)} %bitcast.132), custom_call_target="tpu_custom_call" | custom-call | flops 85899345920 | bytes 18874368 | tf_op jit(solution)/shard_map/attend_back/pallas_call | solution.py:229
  1109.5 8.6 convert_bitcast_fusion.1
  1118.1 76.5 %all-to-all-done.3 = bf16[8,512,384]{1,2,0:T(8,128)(2,1)S(1)} async-done(((bf16[8,512,384]{1,2,0:T(8,128)(2,1)}), bf16[8,512,384]{1,2,0:T(8,128)(2,1)S(1)}, u32[]{:S(2)}, u32[]{:S(2)}) %all-to-all-start.3) | async-done | bytes 3145760 | tf_op jit(solution)/shard_map/all_to_all | solution.py:425
  1219.3 10.6 convert_bitcast_fusion
  1229.9 15.8 pad_maximum_fusion
  1245.7 23.7 %convolution_convert_fusion.4 = bf16[2048,1024]{1,0:T(8,128)(2,1)} fusion(bf16[4096,2048]{1,0:T(8,128)(2,1)} %all-gather.18.cloned.1.call-done, bf16[4096,1024]{1,0:T(8,128)(2,1)} %get-tuple-element.58), kind=kOutput, calls=%fused_computation.62 | convolution fusion | flops 17181966336 | bytes 29360128 | tf_op jit(solution)/shard_map/dot_general | solution.py:61
  1269.5 24.1 %convolution_convert_fusion.3 = bf16[2048,1024]{1,0:T(8,128)(2,1)} fusion(bf16[4096,2048]{1,0:T(8,128)(2,1)} %all-gather.18.cloned.1.call-done, bf16[4096,1024]{1,0:T(8,128)(2,1)} %get-tuple-element.59), kind=kOutput, calls=%fused_computation.61 | convolution fusion | flops 17181966336 | bytes 29360128 | tf_op jit(solution)/shard_map/dot_general | solution.py:61
  1293.7 24.2 %convolution_convert_fusion.2 = bf16[1024,2048]{1,0:T(8,128)(2,1)} fusion(bf16[4096,1024]{1,0:T(8,128)(2,1)} %get-tuple-element.60, bf16[4096,2048]{1,0:T(8,128)(2,1)} %all-gather.16.cloned.1.call-done), kind=kOutput, calls=%fused_computation.60 | convolution fusion | flops 17181966336 | bytes 29360128 | tf_op jit(solution)/shard_map/dot_general | solution.py:61
  1317.9 114.3 %reduce-scatter.12.cloned.1.call-done = bf16[8,512,640]{1,2,0:T(8,128)(2,1)} async-done(((bf16[8,2048,640]{1,2,0:T(8,128)(2,1)}), bf16[8,512,640]{1,2,0:T(8,128)(2,1)}) %reduce-scatter.12.cloned.1.call-update) | async-done | bytes 5242896 | tf_op jit(solution)/shard_map/reduce_scatter | solution.py:603
  1450.2 38.7 %reduce-scatter.16.cloned.1.call-done = bf16[512,1024]{1,0:T(8,128)(2,1)} async-done(((bf16[2048,1024]{1,0:T(8,128)(2,1)}), bf16[512,1024]{1,0:T(8,128)(2,1)}) %reduce-scatter.16.cloned.1.call-update) | async-done | bytes 1048592 | tf_op jit(solution)/shard_map/reduce_scatter | solution.py:563
  1495.4 49.0 %reduce-scatter.18.cloned.1.call-done = bf16[512,1024]{1,0:T(8,128)(2,1)} async-done(((bf16[2048,1024]{1,0:T(8,128)(2,1)}), bf16[512,1024]{1,0:T(8,128)(2,1)}) %reduce-scatter.18.cloned.1.call-update) | async-done | bytes 1048592 | tf_op jit(solution)/shard_map/reduce_scatter | solution.py:567
  1544.4 7.2 multiply_subtract_fusion.1
  1551.5 48.8 %reduce-scatter.20.cloned.1.call-done = bf16[1024,512]{1,0:T(8,128)(2,1)} async-done(((bf16[1024,2048]{1,0:T(8,128)(2,1)}), bf16[1024,512]{1,0:T(8,128)(2,1)}) %reduce-scatter.20.cloned.1.call-update) | async-done | bytes 1048592 | tf_op jit(solution)/shard_map/reduce_scatter | solution.py:559
  1606.9 12.1 fusion.18
  1619.1 49.0 %all-gather.2 = f32[32,2,2112]{2,1,0:T(2,128)S(1)} all-gather(f32[1,2,2112]{2,1,0:T(2,128)S(1)} %maximum_bitcast_fusion), channel_id=3, replica_groups=mesh['narrow'=4,'wide'=8] {'narrow','wide'}, dimensions={0}, use_global_device_ids=true | all-gather | bytes 557568 | tf_op jit(solution)/shard_map/all_gather | solution.py:599
  (278 shorter events, 191.6 us)
Async XLA Ops:
  7.2 316.5 %all-gather.10.cloned.1.call-start = ((), (), s32[]{:S(2)}) async-start(), calls=%async_computation.11 | async-start | bytes 5242880 | tf_op jit(solution)/shard_map/all_gather | solution.py:485
  10.1 313.6 %all-gather.12.cloned.1.call-start = ((), (), s32[]{:S(2)}) async-start(), calls=%async_computation.12 | async-start | bytes 5242880 | tf_op jit(solution)/shard_map/all_gather | solution.py:483
  11.3 386.8 %all-gather.14.cloned.1.call-start = ((), (), s32[]{:S(2)}) async-start(), calls=%async_computation.13 | async-start | bytes 5242880 | tf_op jit(solution)/shard_map/all_gather | solution.py:484
  14.2 434.6 %all-gather.16.cloned.1.call-start = ((), (), s32[]{:S(2)}) async-start(), calls=%async_computation.14 | async-start | bytes 18874368 | tf_op jit(solution)/shard_map/all_gather | solution.py:486
  17.2 146.6 %copy-start.9 = (bf16[512,2048]{1,0:T(8,128)(2,1)S(1)}, bf16[512,2048]{1,0:T(8,128)(2,1)}, u32[]{:S(2)}) copy-start(bf16[512,2048]{1,0:T(8,128)(2,1)} %param.30) | copy-start | bytes 6291460
  17.2 147.1 %copy-start.48 = (f32[2,2048]{1,0:T(2,128)S(1)}, f32[2,2048]{1,0:T(2,128)}, u32[]{:S(2)}) copy-start(f32[2,2048]{1,0:T(2,128)} %param.54) | copy-start | bytes 49156
  164.3 292.4 %copy-start.46 = (f32[1,2048]{1,0:T(1,128)}, f32[1,2048]{1,0:T(1,128)S(1)}, u32[]{:S(2)}) copy-start(f32[1,2048]{1,0:T(1,128)S(1)} %get-tuple-element.200) | copy-start | bytes 24580
  385.1 63.7 %copy-start.10 = (bf16[512,2048]{1,0:T(8,128)(2,1)S(1)}, bf16[512,2048]{1,0:T(8,128)(2,1)}, u32[]{:S(2)}) copy-start(bf16[512,2048]{1,0:T(8,128)(2,1)} %param.30) | copy-start | bytes 6291460
  389.2 59.6 %all-to-all-start.1 = ((bf16[8,512,256]{1,2,0:T(8,128)(2,1)}), bf16[8,512,256]{1,2,0:T(8,128)(2,1)}, u32[]{:S(2)}, u32[]{:S(2)}) async-start(bf16[8,512,256]{1,2,0:T(8,128)(2,1)} %copy.121), calls=%async_computation.1 | async-start | bytes 4194304 | tf_op jit(solution)/shard_map/all_to_all | solution.py:425
  398.1 211.6 %all-gather.18.cloned.1.call-start = ((), (), s32[]{:S(2)}) async-start(), calls=%async_computation.15 | async-start | bytes 18874368 | tf_op jit(solution)/shard_map/all_gather | solution.py:421
  460.4 427.4 %reduce-scatter.8.cloned.1.call-start = ((), (), s32[]{:S(2)}) async-start(), calls=%async_computation.16 | async-start | bytes 18874368 | tf_op jit(solution)/shard_map/reduce_scatter | solution.py:432
  721.1 166.7 %copy-start.47 = (f32[1,2048]{1,0:T(1,128)S(1)}, f32[1,2048]{1,0:T(1,128)}, u32[]{:S(2)}) copy-start(f32[1,2048]{1,0:T(1,128)} %copy-done.46) | copy-start | bytes 24580
  721.2 166.7 %copy-start.51 = (f32[512]{0:T(512)S(1)}, f32[512]{0:T(512)}, u32[]{:S(2)}) copy-start(f32[512]{0:T(512)} %copy-done.50) | copy-start | bytes 6148
  721.2 171.5 %copy-start.62 = (f32[512]{0:T(512)S(1)}, f32[512]{0:T(512)}, u32[]{:S(2)}) copy-start(f32[512]{0:T(512)} %copy-done.61) | copy-start | bytes 6148
  721.2 171.5 %copy-start.5 = (bf16[512,2048]{1,0:T(8,128)(2,1)S(1)}, bf16[512,2048]{1,0:T(8,128)(2,1)}, u32[]{:S(2)}) copy-start(bf16[512,2048]{1,0:T(8,128)(2,1)} %param.31) | copy-start | bytes 6291460
  906.7 52.6 %all-to-all-start.2 = ((bf16[8,512,256]{1,2,0:T(8,128)(2,1)}), bf16[8,512,256]{1,2,0:T(8,128)(2,1)S(1)}, u32[]{:S(2)}, u32[]{:S(2)}) async-start(bf16[8,512,256]{1,2,0:T(8,128)(2,1)} %convert_bitcast_fusion.2), calls=%async_computation.3 | async-start | bytes 4194304 | tf_op jit(solution)/shard_map/all_to_all | solution.py:425
  910.3 284.4 %reduce-scatter.10.cloned.1.call-start = ((), (), s32[]{:S(2)}) async-start(), calls=%async_computation.17 | async-start | bytes 18874368 | tf_op jit(solution)/shard_map/reduce_scatter | solution.py:558
  1103.6 91.0 %all-to-all-start.3 = ((bf16[8,512,384]{1,2,0:T(8,128)(2,1)}), bf16[8,512,384]{1,2,0:T(8,128)(2,1)S(1)}, u32[]{:S(2)}, u32[]{:S(2)}) async-start(bf16[8,512,384]{1,2,0:T(8,128)(2,1)} %copy.126), calls=%async_computation.4 | async-start | bytes 6291456 | tf_op jit(solution)/shard_map/all_to_all | solution.py:425
  1107.3 325.0 %reduce-scatter.12.cloned.1.call-start = ((), (), s32[]{:S(2)}) async-start(), calls=%async_computation.18 | async-start | bytes 26214400 | tf_op jit(solution)/shard_map/reduce_scatter | solution.py:603
  1118.1 81.8 %copy-start.30 = (f32[512,32]{0,1:T(8,128)S(1)}, f32[512,32]{0,1:T(8,128)}, u32[]{:S(2)}) copy-start(f32[512,32]{0,1:T(8,128)} %copy-done.29) | copy-start | bytes 196612
  1118.1 81.8 %copy-start.32 = (f32[512,32]{0,1:T(8,128)S(1)}, f32[512,32]{0,1:T(8,128)}, u32[]{:S(2)}) copy-start(f32[512,32]{0,1:T(8,128)} %copy-done.31) | copy-start | bytes 196612
  1245.7 243.2 %reduce-scatter.16.cloned.1.call-start = ((), (), s32[]{:S(2)}) async-start(), calls=%async_computation.20 | async-start | bytes 5242880 | tf_op jit(solution)/shard_map/reduce_scatter | solution.py:563
  1269.5 274.9 %reduce-scatter.18.cloned.1.call-start = ((), (), s32[]{:S(2)}) async-start(), calls=%async_computation.21 | async-start | bytes 5242880 | tf_op jit(solution)/shard_map/reduce_scatter | solution.py:567
  1293.6 306.7 %reduce-scatter.20.cloned.1.call-start = ((), (), s32[]{:S(2)}) async-start(), calls=%async_computation.22 | async-start | bytes 5242880 | tf_op jit(solution)/shard_map/reduce_scatter | solution.py:559
  1317.9 114.9 %copy-start.23 = (f32[512,256]{1,0:T(8,128)S(1)}, f32[512,256]{1,0:T(8,128)}, u32[]{:S(2)}) copy-start(f32[512,256]{1,0:T(8,128)} %param.33) | copy-start | bytes 1572868
  1317.9 115.9 %copy-start.33 = (f32[512,512]{1,0:T(8,128)S(1)}, f32[512,512]{1,0:T(8,128)}, u32[]{:S(2)}) copy-start(f32[512,512]{1,0:T(8,128)} %param.36) | copy-start | bytes 3145732
  1317.9 356.0 %reduce-scatter.14.cloned.1.call-start = ((), (), s32[]{:S(2)}) async-start(), calls=%async_computation.19 | async-start | bytes 5898240 | tf_op jit(solution)/shard_map/reduce_scatter | solution.py:604
  1432.3 263.0 %all-gather.20.cloned.1.call-start = ((), (), s32[]{:S(2)}) async-start(), calls=%async_computation.23 | async-start | bytes 1179648 | tf_op jit(solution)/shard_map/all_gather | solution.py:607
  1495.4 104.9 %copy-start.8 = (f32[1024,512]{1,0:T(8,128)S(1)}, f32[1024,512]{1,0:T(8,128)}, u32[]{:S(2)}) copy-start(f32[1024,512]{1,0:T(8,128)} %param.51) | copy-start | bytes 6291460
  1606.9 61.4 %copy-start.68 = (f32[2,64]{1,0:T(2,128)S(1)}, f32[2,64]{1,0:T(2,128)}, u32[]{:S(2)}) copy-start(f32[2,64]{1,0:T(2,128)} %param.57) | copy-start | bytes 1540
  1606.9 61.4 %copy-start.69 = (f32[2,64]{1,0:T(2,128)S(1)}, f32[2,64]{1,0:T(2,128)}, u32[]{:S(2)}) copy-start(f32[2,64]{1,0:T(2,128)} %param.58) | copy-start | bytes 1540
  1606.9 61.4 %copy-start.70 = (f32[2,64]{1,0:T(2,128)S(1)}, f32[2,64]{1,0:T(2,128)}, u32[]{:S(2)}) copy-start(f32[2,64]{1,0:T(2,128)} %param.59) | copy-start | bytes 1540
  (61 other events, 427.2 us)
Sparse Core Ops, SparseCore 0:
  10.4 89.1 all-gather.9
  102.1 72.2 all-gather.11
  176.9 52.8 all-gather.13
  231.2 178.2 all-gather.15
  460.5 149.1 all-gather.17
  721.3 166.4 reduce-scatter.7
  961.8 182.0 reduce-scatter.9
  1245.8 186.4 reduce-scatter.11
  1436.1 52.6 reduce-scatter.15
  1491.7 52.6 reduce-scatter.17
  1547.6 52.6 reduce-scatter.19
  1602.5 65.4 reduce-scatter.13
  1675.7 19.6 all-gather.19

commit v4 on v3

--- a/solution.py
+++ b/solution.py
@@ -425,13 +425,78 @@
     return lax.all_to_all(blocks, "wide", 0, 0)
 
 
-def sum_back(pairs, row_count):
-    summed = jnp.zeros((row_count * lax.axis_size("wide"), pairs[0][1].shape[0]), jnp.float32)
+def sum_back(pairs):
+    summed = 0.0
     for gradient, weight in pairs:
         summed = summed + dot_back(gradient, weight)
     return lax.psum_scatter(
         summed.astype(jnp.bfloat16), "wide", scatter_dimension=0, tiled=True
     ).astype(jnp.float32)
+
+
+def gain_kernel(own_ref, out_ref, first_ref, middle_ref, second_ref, send, got, send_two, got_two):
+    narrow = lax.axis_index("narrow")
+    wide = lax.axis_index("wide")
+    narrow_count = second_ref.shape[0]
+    wide_count = first_ref.shape[0]
+    barrier = pltpu.get_barrier_semaphore()
+    wides = [(narrow, (wide + step) % wide_count) for step in range(1, wide_count)]
+    narrows = [((narrow + step) % narrow_count, wide) for step in range(1, narrow_count)]
+    for device in wides + narrows:
+        pl.semaphore_signal(
+            barrier, inc=1, device_id=device, device_id_type=pl.DeviceIdType.MESH
+        )
+    pl.semaphore_wait(barrier, len(wides) + len(narrows))
+    copies = [
+        remote(own_ref, first_ref.at[step + 1], send.at[step], got.at[step], device)
+        for step, device in enumerate(wides)
+    ]
+    for copy in copies:
+        copy.start()
+    for copy in copies:
+        copy.wait()
+    total = own_ref[...]
+    for step in range(1, wide_count):
+        total = total + first_ref[step]
+    middle_ref[...] = total
+    copies = [
+        remote(middle_ref, second_ref.at[step + 1], send_two.at[step], got_two.at[step], device)
+        for step, device in enumerate(narrows)
+    ]
+    for copy in copies:
+        copy.start()
+    for copy in copies:
+        copy.wait()
+    for step in range(1, narrow_count):
+        total = total + second_ref[step]
+    out_ref[...] = total
+
+
+def sum_gains(gains):
+    narrow_count = lax.axis_size("narrow")
+    wide_count = lax.axis_size("wide")
+    size = gains.size
+    rows = -(-size // 1024) * 8
+    flat = jnp.pad(gains.reshape(-1), (0, rows * 128 - size)).reshape(rows, 128)
+    dma = pltpu.SemaphoreType.DMA
+    total = pl.pallas_call(
+        gain_kernel,
+        out_shape=jax.ShapeDtypeStruct(flat.shape, jnp.float32),
+        in_specs=[pl.BlockSpec(memory_space=pltpu.VMEM)],
+        out_specs=pl.BlockSpec(memory_space=pltpu.VMEM),
+        scratch_shapes=[
+            pltpu.VMEM((wide_count, rows, 128), jnp.float32),
+            pltpu.VMEM((rows, 128), jnp.float32),
+            pltpu.VMEM((narrow_count, rows, 128), jnp.float32),
+            dma((wide_count - 1,)),
+            dma((wide_count - 1,)),
+            dma((narrow_count - 1,)),
+            dma((narrow_count - 1,)),
+        ],
+        compiler_params=pltpu.CompilerParams(collective_id=2, has_side_effects=True),
+        name="sum_gains",
+    )(flat)
+    return total.reshape(-1)[:size].reshape(gains.shape)
 
 
 def shards(
@@ -479,11 +544,22 @@
     value_own = lax.dynamic_slice_in_dim(value_weight, key_slot * head_dim, head_dim, 1)
     query_columns = query_weight.shape[1]
     att_own = jnp.concatenate([query_weight, key_own, value_own, output_weight.T], axis=1)
-    att_full = gather_weights(att_own.astype(jnp.bfloat16))
-    gate_local = lax.all_gather(gate_weight.astype(jnp.bfloat16), "narrow", axis=0, tiled=True)
-    up_local = lax.all_gather(up_weight.astype(jnp.bfloat16), "narrow", axis=0, tiled=True)
-    down_local = lax.all_gather(down_weight.astype(jnp.bfloat16), "narrow", axis=1, tiled=True)
-    grad_rows = lax.all_gather(out_grad, "wide", axis=0, tiled=True)
+    half_rows = shard_rows // 2
+    grad_halves = [
+        lax.all_gather(out_grad[:half_rows], "wide", axis=0, tiled=True),
+        lax.all_gather(out_grad[half_rows:], "wide", axis=0, tiled=True),
+    ]
+    att_full, gate_own, up_own, down_own = lax.optimization_barrier(
+        (
+            gather_weights(att_own.astype(jnp.bfloat16)),
+            gate_weight.astype(jnp.bfloat16),
+            up_weight.astype(jnp.bfloat16),
+            down_weight.astype(jnp.bfloat16),
+        )
+    )
+    gate_local = lax.all_gather(gate_own, "narrow", axis=0, tiled=True)
+    up_local = lax.all_gather(up_own, "narrow", axis=0, tiled=True)
+    down_local = lax.all_gather(down_own, "narrow", axis=1, tiled=True)
     group_columns = query_columns + 2 * head_dim
     input_full = att_full[:, :, :group_columns]
     output_full = att_full[:, :, group_columns:]
@@ -518,30 +594,43 @@
         .reshape(wide_count, shard_rows, query_columns)
         .astype(jnp.bfloat16)
     )
-    packed = swap(jnp.concatenate([query_rot, key_rot.astype(jnp.bfloat16), value_rows], axis=2))
+    packed = jnp.concatenate([query_rot, key_rot.astype(jnp.bfloat16), value_rows], axis=2)
+    packed, grad_halves = lax.optimization_barrier((packed, grad_halves))
+    packed = swap(packed)
     packed = packed.reshape(wide_count * shard_rows, group_columns)
-    packed, down_local, gate_local = lax.optimization_barrier((packed, down_local, gate_local))
     attended, weight_sums, attended_low = attend(packed, local_heads)
     attended_low = swap(attended_low.reshape(wide_count, shard_rows, query_columns))
-    attended_low, up_local, grad_rows = lax.optimization_barrier(
-        (attended_low, up_local, grad_rows)
+    attended_low, gate_local, up_local, down_local = lax.optimization_barrier(
+        (attended_low, gate_local, up_local, down_local)
     )
     branch = jnp.einsum("gth,gdh->td", attended_low, output_full, preferred_element_type=jnp.float32)
     middle = residual + branch
     normed_mid, norm_mid_back = jax.vjp(rms_scale, middle, norm_gains[1])
-    rows_mid = gather_rows(normed_mid.astype(jnp.bfloat16))
-    gate_pre = dot_last(rows_mid, gate_local)
-    up_pre = dot_last(rows_mid, up_local)
-    hidden, hidden_back = jax.vjp(
-        lambda gate_in, up_in: jax.nn.silu(gate_in) * up_in, gate_pre, up_pre
-    )
-    hidden_low = hidden.astype(jnp.bfloat16)
-    block_part = dot_last(hidden_low, down_local).astype(jnp.bfloat16)
-    hidden_grad = dot_back(grad_rows, down_local).astype(jnp.bfloat16)
-    gate_grad, up_grad = hidden_back(hidden_grad.astype(jnp.float32))
-    gate_grad = gate_grad.astype(jnp.bfloat16)
-    up_grad = up_grad.astype(jnp.bfloat16)
-    mid_back = sum_back(((gate_grad, gate_local), (up_grad, up_local)), shard_rows)
+    mid_low = normed_mid.astype(jnp.bfloat16)
+    down_wgrad = gate_wgrad = up_wgrad = 0.0
+    block_parts = []
+    mid_sums = []
+    rows_halves = [gather_rows(mid_low[:half_rows]), gather_rows(mid_low[half_rows:])]
+    for rows_mid, grad_rows in zip(rows_halves, grad_halves):
+        hidden_grad = dot_back(grad_rows, down_local).astype(jnp.bfloat16)
+        gate_pre = dot_last(rows_mid, gate_local)
+        up_pre = dot_last(rows_mid, up_local)
+        hidden, hidden_back = jax.vjp(
+            lambda gate_in, up_in: jax.nn.silu(gate_in) * up_in, gate_pre, up_pre
+        )
+        hidden_low = hidden.astype(jnp.bfloat16)
+        gate_grad, up_grad = hidden_back(hidden_grad.astype(jnp.float32))
+        gate_grad = gate_grad.astype(jnp.bfloat16)
+        up_grad = up_grad.astype(jnp.bfloat16)
+        mid_sums.append(sum_back(((gate_grad, gate_local), (up_grad, up_local))))
+        block_parts.append(dot_last(hidden_low, down_local).astype(jnp.bfloat16))
+        down_wgrad = down_wgrad + dot_first(hidden_low, grad_rows)
+        gate_wgrad = gate_wgrad + dot_first(rows_mid, gate_grad)
+        up_wgrad = up_wgrad + dot_first(rows_mid, up_grad)
+    down_wgrad = down_wgrad.astype(jnp.bfloat16)
+    gate_wgrad = gate_wgrad.astype(jnp.bfloat16)
+    up_wgrad = up_wgrad.astype(jnp.bfloat16)
+    mid_back = jnp.concatenate(mid_sums, axis=0)
     middle_part, mid_gain_grad = norm_mid_back(mid_back)
     middle_grad = out_grad.astype(jnp.float32) + middle_part
     branch_grad = middle_grad.astype(jnp.bfloat16)
@@ -551,30 +640,28 @@
     output_wgrad = jnp.einsum(
         "td,gth->gdh", branch_grad, attended_low, preferred_element_type=jnp.float32
     )
+    attended_grad, down_wgrad = lax.optimization_barrier((attended_grad, down_wgrad))
+    down_total = lax.psum_scatter(down_wgrad, "narrow", scatter_dimension=1, tiled=True)
     head_grad = swap(attended_grad).reshape(wide_count * shard_rows, query_columns)
-    head_grad, block_part, hidden_low, gate_grad, up_grad = lax.optimization_barrier(
-        (head_grad, block_part, hidden_low, gate_grad, up_grad)
-    )
-    block_sum = lax.psum_scatter(block_part, "wide", scatter_dimension=0, tiled=True)
-    down_total = lax.psum_scatter(
-        dot_first(hidden_low, grad_rows).astype(jnp.bfloat16),
-        "narrow", scatter_dimension=1, tiled=True,
-    )
-    gate_total = lax.psum_scatter(
-        dot_first(rows_mid, gate_grad).astype(jnp.bfloat16),
-        "narrow", scatter_dimension=0, tiled=True,
-    )
-    up_total = lax.psum_scatter(
-        dot_first(rows_mid, up_grad).astype(jnp.bfloat16),
-        "narrow", scatter_dimension=0, tiled=True,
-    )
+    head_grad, block_parts, gate_wgrad, up_wgrad = lax.optimization_barrier(
+        (head_grad, block_parts, gate_wgrad, up_wgrad)
+    )
+    block_sums = [
+        lax.psum_scatter(part, "wide", scatter_dimension=0, tiled=True) for part in block_parts
+    ]
+    gate_total = lax.psum_scatter(gate_wgrad, "narrow", scatter_dimension=0, tiled=True)
+    up_total = lax.psum_scatter(up_wgrad, "narrow", scatter_dimension=0, tiled=True)
     head_grad = head_grad.astype(jnp.float32) / weight_sums
     scaled_grad = head_grad.astype(jnp.bfloat16)
     grad_dot = jnp.sum((head_grad * attended).reshape(-1, local_heads, head_dim), axis=-1).T
     packed_grad = attend_back(packed, scaled_grad, grad_dot, local_heads)
     packed_grad = swap(packed_grad.reshape(wide_count, shard_rows, group_columns))
-    packed_grad, block_sum = lax.optimization_barrier((packed_grad, block_sum))
-    block_out = (middle + block_sum.astype(jnp.float32)).astype(jnp.bfloat16)
+    packed_grad, block_sums, gate_total, up_total, down_total = lax.optimization_barrier(
+        (packed_grad, block_sums, gate_total, up_total, down_total)
+    )
+    block_out = (middle + jnp.concatenate(block_sums, axis=0).astype(jnp.float32)).astype(
+        jnp.bfloat16
+    )
     query_rot_grad = packed_grad[:, :, :query_columns].astype(jnp.float32).reshape(
         wide_count, shard_rows, local_heads, head_dim
     )
@@ -595,8 +682,7 @@
     input_grad = middle_grad + input_part
     gain_stack = jnp.stack([in_gain_grad, mid_gain_grad])
     head_stack = jnp.stack([query_gain_grad, key_gain_grad])
-    gains = jnp.concatenate([gain_stack, head_stack], axis=1)
-    gains = jnp.sum(lax.all_gather(gains, ("narrow", "wide"), axis=0), axis=0)
+    gains = sum_gains(jnp.concatenate([gain_stack, head_stack], axis=1))
     gain_total = gains[:, :model_width]
     head_total = gains[:, model_width:]
     att_wgrad = jnp.concatenate([input_wgrad, output_wgrad], axis=2).astype(jnp.bfloat16)

time: 1740 us -> 1580 us (0.908)
  blocking collectives: 178 us -> 0 us
  matrix products: 289 us -> 328 us
  waiting for transfers between devices: 701 us -> 671 us
    all_to_all x1 -> x0, blocking collectives: 129 us -> none  [swap(): return lax.all_to_all(blocks, 'wide', 0, 0)]
    reduce_scatter x1 -> x2, waiting for transfers between devices: 167 us -> 58.8 us  [sum_back(): lax.psum_scatter(summed.astype(jnp.bfloat16), 'wide', scatter_dimension=0...]
    reduce_scatter x1, waiting for transfers between devices: 114 us -> 186 us  [shards(): lax.psum_scatter(att_wgrad, 'narrow', scatter_dimension=1, tiled=True)]
    all_to_all x3 -> x4, waiting for transfers between devices: 152 us -> 224 us  [swap(): return lax.all_to_all(blocks, 'wide', 0, 0)]
    all_gather x1 -> x2, waiting for transfers between devices: 125 us -> 71 us  [gather_rows(): return lax.all_gather(shard, 'wide', axis=0, tiled=True)]
    all_gather x1 -> x0, blocking collectives: 49 us -> none  [shards(): gains = jnp.sum(lax.all_gather(gains, ('narrow', 'wide'), axis=0), axis=0)]
    reduce_scatter x4 -> x5, waiting for transfers between devices: 136 us -> 96.8 us  [the longest x2 96.8 us: shards(): lax.psum_scatter(part, 'wide', scatter_dimension=0, tiled=True)]
    all_gather x4 -> x5, waiting for transfers between devices: 0.02 us -> 21 us  [the longest x1 15.8 us: shards(): down_local = lax.all_gather(down_own, 'narrow', axis=1, tiled=True)]
  transfers between devices with their start and end apart: 16 -> 21, of which waited for: 10 -> 12; matrix products, arithmetic and copies ran while one was open for 15% -> 26% of each run, Pallas kernels for 19% -> 22%
where the time goes in v4:
time: 1580 us; the launch traced here: 1570 us
  waiting for transfers between devices  671 us (42%)
  Pallas kernels  343 us (22%)
  matrix products  328 us (21%)
  other arithmetic  106 us (7%)
  local copies, waits for them, and re-layouts  88.8 us (6%)
  starting transfers between devices  16.4 us (1%)
    all_to_all x4, waiting for transfers between devices, swap(): return lax.all_to_all(blocks, 'wide', 0, 0)  224 us
    reduce_scatter x1, waiting for transfers between devices, shards(): lax.psum_scatter(att_wgrad, 'narrow', scatter_dimension=1, tiled=True)  186 us
    pallas_call x1, Pallas kernels, gather_weights(): pl.pallas_call(gather_kernel, out_shape=jax.ShapeDtypeStruct((8, 4 * att....  147 us
    pallas_call x1, Pallas kernels, attend_back(): pl.pallas_call(functools.partial(back_kernel, block, heads), out_shape=ja...  119 us
    reduce_scatter x2, waiting for transfers between devices, shards(): lax.psum_scatter(part, 'wide', scatter_dimension=0, tiled=True)  96.8 us
    dot_general x6, matrix products, dot_last(): return jnp.dot(left, right, preferred_element_type=jnp.float32)  93.6 us
    dot_general x6, matrix products, dot_back(): lax.dot_general(left, right, (((1,), (1,)), ((), ())), preferred_element_...  93.4 us
    dot_general x6, matrix products, dot_first(): lax.dot_general(left, right, (((0,), (0,)), ((), ())), preferred_element_...  81.7 us
  transfers between devices with their start and end apart: 21, of which 12 were waited for; matrix products, arithmetic and copies ran while one was open for 26% of the time, Pallas kernels for 22%

profile of v4, /device:TPU:0, one launch (start us, length us, event | category | flops | bytes accessed | tf_op | source)
XLA Modules:
  0.0 1567.3 jit_solution(5255219732351310589)
XLA Ops:
  13.7 147.5 %gather_weights.1 = bf16[8,2048,640]{2,1,0:T(8,128)(2,1)} custom-call(bf16[512,640]{1,0:T(8,128)(2,1)} %pad_maximum_fusion.6.att_ref), custom_call_target="tpu_custom_call" | custom-call | bytes 314572800 | tf_op jit(solution)/shard_map/gather_weights/pallas_call | solution.py:406
  207.2 70.9 %all-to-all-done = bf16[8,512,384]{1,2,0:T(8,128)(2,1)S(1)} async-done(((bf16[8,512,384]{1,2,0:T(8,128)(2,1)}), bf16[8,512,384]{1,2,0:T(8,128)(2,1)S(1)}, u32[]{:S(2)}, u32[]{:S(2)}) %all-to-all-start) | async-done | bytes 3145760 | tf_op jit(solution)/shard_map/all_to_all | solution.py:425
  280.9 61.4 %attend.1 = (f32[4096,256]{1,0:T(8,128)}, f32[4096,256]{1,0:T(8,128)}, bf16[4096,256]{1,0:T(8,128)(2,1)}) custom-call(bf16[4096,384]{1,0:T(8,128)(2,1)} %bitcast.138), custom_call_target="tpu_custom_call" | custom-call | flops 34359738368 | bytes 18874368 | tf_op jit(solution)/shard_map/attend/pallas_call | solution.py:143
  350.9 15.8 %all-gather.18.cloned.1.call-done = bf16[1024,2048]{1,0:T(8,128)(2,1)} async-done(((bf16[1024,512]{1,0:T(8,128)(2,1)}), bf16[1024,2048]{1,0:T(8,128)(2,1)}) %all-gather.18.cloned.1.call-update) | async-done | bytes 4194320 | tf_op jit(solution)/shard_map/all_gather | solution.py:562
  366.6 33.2 %all-to-all-done.1 = bf16[8,512,256]{1,2,0:T(8,128)(2,1)} async-done(((bf16[8,512,256]{1,2,0:T(8,128)(2,1)}), bf16[8,512,256]{1,2,0:T(8,128)(2,1)}, u32[]{:S(2)}, u32[]{:S(2)}) %all-to-all-start.1) | async-done | bytes 2097184 | tf_op jit(solution)/shard_map/all_to_all | solution.py:425
  411.4 13.8 convolution_convert_fusion.3
  425.2 66.2 %all-gather.20.cloned.1.call-done = bf16[2048,2048]{1,0:T(8,128)(2,1)} async-done(((bf16[256,2048]{1,0:T(8,128)(2,1)}), bf16[2048,2048]{1,0:T(8,128)(2,1)}) %all-gather.20.cloned.1.call-update) | async-done | bytes 8388624 | tf_op jit(solution)/shard_map/all_gather | solution.py:421
  491.4 14.7 fusion.95
  506.1 18.4 %multiply_convert_fusion.1 = (bf16[2048,1024]{1,0:T(8,128)(2,1)}, bf16[2048,1024]{1,0:T(8,128)(2,1)}, bf16[2048,1024]{1,0:T(8,128)(2,1)}) fusion(f32[2048,1024]{1,0:T(8,128)} %fusion.95, bf16[2048,1024]{1,0:T(8,128)(2,1)} %convolution_convert_fusion.3, bf16[2048,2048]{1,0:T(8,128)(2,1)S(1)} %copy-done.75, bf16[2048,1024]{1,0:T(8,128)(2,1)} %all-gather.16.cloned.1.call-done), kind=kOutput, calls=%fused_computation.27 | convolution fusion | flops 8625586176 | bytes 37748736 | tf_op jit(solution)/shard_map/dot_general | solution.py:57
  524.5 14.7 fusion.96
  539.2 16.1 %add_convert_fusion.1 = bf16[2048,2048]{1,0:T(8,128)(2,1)} fusion(f32[2048,2048]{1,0:T(8,128)} %fusion.96, bf16[2048,1024]{1,0:T(8,128)(2,1)} %get-tuple-element.180, bf16[2048,1024]{1,0:T(8,128)(2,1)S(1)} %copy-done.79), kind=kOutput, calls=%fused_computation.2 | convolution fusion | flops 8598323200 | bytes 33554432 | tf_op jit(solution)/shard_map/dot_general | solution.py:67
  555.3 14.1 convolution_convert_fusion.2
  574.2 14.7 fusion.97
  588.9 17.3 %multiply_convert_fusion = (bf16[2048,1024]{1,0:T(8,128)(2,1)}, bf16[2048,1024]{1,0:T(8,128)(2,1)}) fusion(f32[2048,1024]{1,0:T(8,128)} %fusion.97, bf16[2048,1024]{1,0:T(8,128)(2,1)} %convolution_convert_fusion.2, bf16[2048,2048]{1,0:T(8,128)(2,1)S(1)} %copy-done.76, bf16[2048,1024]{1,0:T(8,128)(2,1)} %all-gather.16.cloned.1.call-done), kind=kOutput, calls=%fused_computation.26 | convolution fusion | flops 8621391872 | bytes 33554432 | tf_op jit(solution)/shard_map/dot_general | solution.py:57
  606.3 14.2 fusion.98
  620.5 20.5 %add_convert_fusion = bf16[2048,2048]{1,0:T(8,128)(2,1)} fusion(f32[2048,2048]{1,0:T(8,128)} %fusion.98, bf16[2048,1024]{1,0:T(8,128)(2,1)} %all-gather.16.cloned.1.call-done, bf16[2048,1024]{1,0:T(8,128)(2,1)} %convolution_convert_fusion.2, f32[2048,1024]{1,0:T(8,128)} %fusion.97), kind=kOutput, calls=%fused_computation.1 | convolution fusion | flops 8613003264 | bytes 41943040 | tf_op jit(solution)/shard_map/dot_general | solution.py:67
  641.1 14.4 convolution_convert_fusion.1
  655.5 14.0 convolution_convert_fusion
  669.5 13.7 fusion.99
  683.3 12.9 add_convert_fusion.4
  696.2 58.8 %reduce-scatter.12.cloned.1.call-done = bf16[256,2048]{1,0:T(8,128)(2,1)} async-done(((bf16[2048,2048]{1,0:T(8,128)(2,1)}), bf16[256,2048]{1,0:T(8,128)(2,1)}) %reduce-scatter.12.cloned.1.call-update) | async-done | bytes 1048592 | tf_op jit(solution)/shard_map/reduce_scatter | solution.py:432
  786.8 13.0 add_convert_fusion.3
  803.5 13.1 fusion.101
  816.7 16.2 %add_convert_fusion.2 = bf16[2048,1024]{1,0:T(8,128)(2,1)} fusion(f32[2048,1024]{1,0:T(8,128)S(1)} %fusion.101, bf16[2048,2048]{1,0:T(8,128)(2,1)} %all-gather.22.cloned.1.call-done, bf16[2048,1024]{1,0:T(8,128)(2,1)} %convolution_convert_fusion.2, f32[2048,1024]{1,0:T(8,128)} %fusion.97), kind=kOutput, calls=%fused_computation.23 | convolution fusion | flops 8608808960 | bytes 33554432 | tf_op jit(solution)/shard_map/dot_general | solution.py:61
  832.8 19.6 %all-to-all-done.2 = bf16[8,512,256]{1,2,0:T(8,128)(2,1)S(1)} async-done(((bf16[8,512,256]{1,2,0:T(8,128)(2,1)}), bf16[8,512,256]{1,2,0:T(8,128)(2,1)S(1)}, u32[]{:S(2)}, u32[]{:S(2)}) %all-to-all-start.2) | async-done | bytes 2097184 | tf_op jit(solution)/shard_map/all_to_all | solution.py:425
  874.8 119.4 %attend_back.1 = bf16[4096,384]{1,0:T(8,128)(2,1)} custom-call(bf16[4096,384]{1,0:T(8,128)(2,1)} %bitcast.139, bf16[4096,256]{1,0:T(8,128)(2,1)} %get-tuple-element.182.g_ref, f32[4,4096]{1,0:T(4,128)} %bitcast.150), custom_call_target="tpu_custom_call" | custom-call | flops 85899345920 | bytes 18874368 | tf_op jit(solution)/shard_map/attend_back/pallas_call | solution.py:229
  1013.5 100.5 %all-to-all-done.3 = bf16[8,512,384]{1,2,0:T(8,128)(2,1)S(1)} async-done(((bf16[8,512,384]{1,2,0:T(8,128)(2,1)}), bf16[8,512,384]{1,2,0:T(8,128)(2,1)S(1)}, u32[]{:S(2)}, u32[]{:S(2)}) %all-to-all-start.3) | async-done | bytes 3145760 | tf_op jit(solution)/shard_map/all_to_all | solution.py:425
  1114.1 96.8 %reduce-scatter.16.cloned.1.call-done = bf16[256,2048]{1,0:T(8,128)(2,1)} async-done(((bf16[2048,2048]{1,0:T(8,128)(2,1)}), bf16[256,2048]{1,0:T(8,128)(2,1)}) %reduce-scatter.16.cloned.1.call-update) | async-done | bytes 1048592 | tf_op jit(solution)/shard_map/reduce_scatter | solution.py:650
  1238.5 15.9 %pad_maximum_fusion = bf16[8,2048,640]{1,2,0:T(8,128)(2,1)} fusion(bf16[8,2048,256]{1,2,0:T(8,128)(2,1)} %convert_bitcast_fusion.1, bf16[8,2048,384]{1,2,0:T(8,128)(2,1)S(1)} %convert_bitcast_fusion), kind=kLoop, calls=%fused_computation | loop fusion | flops 41943040 | bytes 41943040 | tf_op jit(solution)/shard_map/concatenate | solution.py:688
  1254.6 186.3 %reduce-scatter.24.cloned.1.call-done = bf16[8,512,640]{1,2,0:T(8,128)(2,1)} async-done(((bf16[8,2048,640]{1,2,0:T(8,128)(2,1)}), bf16[8,512,640]{1,2,0:T(8,128)(2,1)}) %reduce-scatter.24.cloned.1.call-update) | async-done | bytes 5242896 | tf_op jit(solution)/shard_map/reduce_scatter | solution.py:689
  1460.3 12.8 fusion.23
  1473.8 14.4 sum_gains.1
  (324 shorter events, 276.7 us)
Async XLA Ops:
  7.2 190.5 %all-gather.10.cloned.1.call-start = ((), (), s32[]{:S(2)}) async-start(), calls=%async_computation.13 | async-start | bytes 9437184 | tf_op jit(solution)/shard_map/all_gather | solution.py:549
  10.5 192.5 %all-gather.12.cloned.1.call-start = ((), (), s32[]{:S(2)}) async-start(), calls=%async_computation.14 | async-start | bytes 9437184 | tf_op jit(solution)/shard_map/all_gather | solution.py:550
  11.2 339.6 %all-gather.14.cloned.1.call-start = ((), (), s32[]{:S(2)}) async-start(), calls=%async_computation.15 | async-start | bytes 5242880 | tf_op jit(solution)/shard_map/all_gather | solution.py:560
  167.9 182.9 %all-gather.16.cloned.1.call-start = ((), (), s32[]{:S(2)}) async-start(), calls=%async_computation.16 | async-start | bytes 5242880 | tf_op jit(solution)/shard_map/all_gather | solution.py:561
  168.6 239.1 %copy-start.50 = (f32[1,2048]{1,0:T(1,128)}, f32[1,2048]{1,0:T(1,128)S(1)}, u32[]{:S(2)}) copy-start(f32[1,2048]{1,0:T(1,128)S(1)} %get-tuple-element.199) | copy-start | bytes 24580
  203.0 75.1 %all-to-all-start = ((bf16[8,512,384]{1,2,0:T(8,128)(2,1)}), bf16[8,512,384]{1,2,0:T(8,128)(2,1)S(1)}, u32[]{:S(2)}, u32[]{:S(2)}) async-start(bf16[8,512,384]{1,2,0:T(8,128)(2,1)} %pad_maximum_fusion.1), calls=%async_computation | async-start | bytes 6291456 | tf_op jit(solution)/shard_map/all_to_all | solution.py:425
  206.6 160.0 %all-gather.18.cloned.1.call-start = ((), (), s32[]{:S(2)}) async-start(), calls=%async_computation.17 | async-start | bytes 5242880 | tf_op jit(solution)/shard_map/all_gather | solution.py:562
  342.3 57.5 %copy-start.11 = (bf16[512,2048]{1,0:T(8,128)(2,1)S(1)}, bf16[512,2048]{1,0:T(8,128)(2,1)}, u32[]{:S(2)}) copy-start(bf16[512,2048]{1,0:T(8,128)(2,1)} %param.30) | copy-start | bytes 6291460
  346.4 53.4 %all-to-all-start.1 = ((bf16[8,512,256]{1,2,0:T(8,128)(2,1)}), bf16[8,512,256]{1,2,0:T(8,128)(2,1)}, u32[]{:S(2)}, u32[]{:S(2)}) async-start(bf16[8,512,256]{1,2,0:T(8,128)(2,1)} %copy.86), calls=%async_computation.1 | async-start | bytes 4194304 | tf_op jit(solution)/shard_map/all_to_all | solution.py:425
  350.8 140.6 %all-gather.20.cloned.1.call-start = ((), (), s32[]{:S(2)}) async-start(), calls=%async_computation.18 | async-start | bytes 9437184 | tf_op jit(solution)/shard_map/all_gather | solution.py:421
  410.3 163.9 %all-gather.22.cloned.1.call-start = ((), (), s32[]{:S(2)}) async-start(), calls=%async_computation.20 | async-start | bytes 9437184 | tf_op jit(solution)/shard_map/all_gather | solution.py:421
  411.1 285.1 %reduce-scatter.10.cloned.1.call-start = ((), (), s32[]{:S(2)}) async-start(), calls=%async_computation.19 | async-start | bytes 9437184 | tf_op jit(solution)/shard_map/reduce_scatter | solution.py:432
  555.3 199.7 %reduce-scatter.12.cloned.1.call-start = ((), (), s32[]{:S(2)}) async-start(), calls=%async_computation.21 | async-start | bytes 9437184 | tf_op jit(solution)/shard_map/reduce_scatter | solution.py:432
  641.0 372.5 %reduce-scatter.22.cloned.1.call-start = ((), (), s32[]{:S(2)}) async-start(), calls=%async_computation.26 | async-start | bytes 5242880 | tf_op jit(solution)/shard_map/reduce_scatter | solution.py:644
  683.2 71.7 %copy-start.51 = (f32[1,2048]{1,0:T(1,128)S(1)}, f32[1,2048]{1,0:T(1,128)}, u32[]{:S(2)}) copy-start(f32[1,2048]{1,0:T(1,128)} %copy-done.50) | copy-start | bytes 24580
  683.2 71.7 %copy-start.55 = (f32[512]{0:T(512)S(1)}, f32[512]{0:T(512)}, u32[]{:S(2)}) copy-start(f32[512]{0:T(512)} %copy-done.54) | copy-start | bytes 6148
  696.2 63.7 %copy-start.66 = (f32[512]{0:T(512)S(1)}, f32[512]{0:T(512)}, u32[]{:S(2)}) copy-start(f32[512]{0:T(512)} %copy-done.65) | copy-start | bytes 6148
  696.2 63.7 %copy-start.5 = (bf16[512,2048]{1,0:T(8,128)(2,1)S(1)}, bf16[512,2048]{1,0:T(8,128)(2,1)}, u32[]{:S(2)}) copy-start(bf16[512,2048]{1,0:T(8,128)(2,1)} %param.31) | copy-start | bytes 6291460
  799.8 52.6 %all-to-all-start.2 = ((bf16[8,512,256]{1,2,0:T(8,128)(2,1)}), bf16[8,512,256]{1,2,0:T(8,128)(2,1)S(1)}, u32[]{:S(2)}, u32[]{:S(2)}) async-start(bf16[8,512,256]{1,2,0:T(8,128)(2,1)} %convert_bitcast_fusion.2), calls=%async_computation.4 | async-start | bytes 4194304 | tf_op jit(solution)/shard_map/all_to_all | solution.py:425
  803.5 310.6 %reduce-scatter.18.cloned.1.call-start = ((), (), s32[]{:S(2)}) async-start(), calls=%async_computation.24 | async-start | bytes 5242880 | tf_op jit(solution)/shard_map/reduce_scatter | solution.py:652
  854.8 259.2 %reduce-scatter.20.cloned.1.call-start = ((), (), s32[]{:S(2)}) async-start(), calls=%async_computation.25 | async-start | bytes 5242880 | tf_op jit(solution)/shard_map/reduce_scatter | solution.py:653
  855.4 258.6 %reduce-scatter.14.cloned.1.call-start = ((), (), s32[]{:S(2)}) async-start(), calls=%async_computation.22 | async-start | bytes 9437184 | tf_op jit(solution)/shard_map/reduce_scatter | solution.py:650
  856.2 354.6 %reduce-scatter.16.cloned.1.call-start = ((), (), s32[]{:S(2)}) async-start(), calls=%async_computation.23 | async-start | bytes 9437184 | tf_op jit(solution)/shard_map/reduce_scatter | solution.py:650
  998.8 115.2 %all-to-all-start.3 = ((bf16[8,512,384]{1,2,0:T(8,128)(2,1)}), bf16[8,512,384]{1,2,0:T(8,128)(2,1)S(1)}, u32[]{:S(2)}, u32[]{:S(2)}) async-start(bf16[8,512,384]{1,2,0:T(8,128)(2,1)} %copy.91), calls=%async_computation.5 | async-start | bytes 6291456 | tf_op jit(solution)/shard_map/all_to_all | solution.py:425
  1002.5 438.4 %reduce-scatter.24.cloned.1.call-start = ((), (), s32[]{:S(2)}) async-start(), calls=%async_computation.27 | async-start | bytes 26214400 | tf_op jit(solution)/shard_map/reduce_scatter | solution.py:689
  1254.5 186.4 %copy-start.38 = (f32[512,512]{1,0:T(8,128)S(1)}, f32[512,512]{1,0:T(8,128)}, u32[]{:S(2)}) copy-start(f32[512,512]{1,0:T(8,128)} %param.36) | copy-start | bytes 3145732
  1254.5 255.8 %reduce-scatter.26.cloned.1.call-start = ((), (), s32[]{:S(2)}) async-start(), calls=%async_computation.28 | async-start | bytes 5898240 | tf_op jit(solution)/shard_map/reduce_scatter | solution.py:690
  1440.9 94.0 %all-gather.24.cloned.1.call-start = ((), (), s32[]{:S(2)}) async-start(), calls=%async_computation.29 | async-start | bytes 1179648 | tf_op jit(solution)/shard_map/all_gather | solution.py:693
  1460.2 28.8 %copy-start.60 = (f32[512]{0:T(512)S(1)}, f32[512]{0:T(512)}, u32[]{:S(2)}) copy-start(f32[512]{0:T(512)} %copy-done.59) | copy-start | bytes 6148
  1460.2 28.9 %copy-start.72 = (f32[2,64]{1,0:T(2,128)S(1)}, f32[2,64]{1,0:T(2,128)}, u32[]{:S(2)}) copy-start(f32[2,64]{1,0:T(2,128)} %param.57) | copy-start | bytes 1540
  1460.3 28.9 %copy-start.73 = (f32[2,64]{1,0:T(2,128)S(1)}, f32[2,64]{1,0:T(2,128)}, u32[]{:S(2)}) copy-start(f32[2,64]{1,0:T(2,128)} %param.58) | copy-start | bytes 1540
  1460.3 28.9 %copy-start.74 = (f32[2,64]{1,0:T(2,128)S(1)}, f32[2,64]{1,0:T(2,128)}, u32[]{:S(2)}) copy-start(f32[2,64]{1,0:T(2,128)} %param.59) | copy-start | bytes 1540
  (76 other events, 432.4 us)
Sparse Core Ops, SparseCore 0:
  10.6 106.8 all-gather.9
  119.7 83.2 all-gather.11
  205.4 51.2 all-gather.13
  258.9 52.7 all-gather.15
  313.9 52.6 all-gather.17
  410.4 80.9 all-gather.19
  493.6 80.5 all-gather.21
  576.5 88.1 reduce-scatter.9
  667.0 87.9 reduce-scatter.11
  774.1 51.0 reduce-scatter.21
  854.9 51.5 reduce-scatter.17
  909.3 52.6 reduce-scatter.19
  964.4 130.6 reduce-scatter.13
  1097.3 113.4 reduce-scatter.15
  1254.6 186.1 reduce-scatter.23
  1443.0 62.5 reduce-scatter.25
  1512.1 22.7 all-gather.23

commit v5 on v4

--- a/solution.py
+++ b/solution.py
@@ -434,69 +434,297 @@
     ).astype(jnp.float32)
 
 
-def gain_kernel(own_ref, out_ref, first_ref, middle_ref, second_ref, send, got, send_two, got_two):
-    narrow = lax.axis_index("narrow")
-    wide = lax.axis_index("wide")
-    narrow_count = second_ref.shape[0]
-    wide_count = first_ref.shape[0]
+def scatter_kernel(
+    in_ref, out_ref, gain_ref, sum_ref, spread_ref, gain_sum_ref,
+    own, other, halves, wholes, from_left, from_right, low, wide_gains, mid_gain, narrow_gains,
+    load_sem, core_send, core_got, half_send, half_got, whole_send, whole_got,
+    line_send, left_got, right_got, spread_send, spread_got, pass_send, pass_got,
+    wide_send, wide_got, narrow_send, narrow_got,
+):
+    narrow, wide, chip, core = place()
+    beside = narrow + 1 - 2 * (narrow % 2)
+    across = (narrow + 2) % 4
+    corner = (beside + 2) % 4
+    rows = sum_ref.shape[0]
+    half_rows = rows // 2
+    split = in_ref.shape[2]
+    twin = (narrow, 2 * chip + 1 - core)
+    sides = ((beside, wide), (across, wide))
+    near = (beside, across)
+    wides = [(narrow, (wide + step) % 8) for step in range(1, 8)]
+    narrows = [((narrow + step) % 4, wide) for step in range(1, 4)]
+    upper = chip // 2
+    last = 3 - 3 * upper
+    second = chip + 1 - 2 * upper
+    order = (last, 6 - chip - second - last, second, chip)
+    f32 = jnp.float32
+
     barrier = pltpu.get_barrier_semaphore()
-    wides = [(narrow, (wide + step) % wide_count) for step in range(1, wide_count)]
-    narrows = [((narrow + step) % narrow_count, wide) for step in range(1, narrow_count)]
     for device in wides + narrows:
         pl.semaphore_signal(
             barrier, inc=1, device_id=device, device_id_type=pl.DeviceIdType.MESH
         )
-    pl.semaphore_wait(barrier, len(wides) + len(narrows))
-    copies = [
-        remote(own_ref, first_ref.at[step + 1], send.at[step], got.at[step], device)
+    pl.semaphore_wait(barrier, 10)
+
+    parts = ((in_ref, pl.ds(0, split)), (out_ref, pl.ds(split, out_ref.shape[2])))
+
+    def load(at, k):
+        source, lanes = parts[k]
+        return pltpu.make_async_copy(
+            source.at[2 * at + core], own.at[at, :, lanes], load_sem.at[at, k]
+        )
+
+    def exchange(at, k):
+        source, lanes = parts[k]
+        return remote(
+            source.at[2 * at + 1 - core], other.at[at, :, lanes], core_send.at[at, k],
+            core_got.at[at, k], twin,
+        )
+
+    def block(at, who):
+        return own.at[at, pl.ds(pl.multiple_of(who * rows, rows), rows), :]
+
+    def half_block(at, who, half):
+        return own.at[
+            at, pl.ds(pl.multiple_of(who * rows + half * half_rows, half_rows), half_rows), :
+        ]
+
+    def half(at, k):
+        return remote(
+            half_block(at, corner, k), halves.at[at, k], half_send.at[at, k], half_got.at[at, k],
+            sides[k],
+        )
+
+    def whole(at, k):
+        return remote(
+            block(at, near[k]), wholes.at[at, k], whole_send.at[at, k], whole_got.at[at, k],
+            sides[k],
+        )
+
+    def to_right(at):
+        return remote(
+            block(at, narrow), from_left.at[at], line_send.at[at], left_got.at[at],
+            (narrow, wide + 2),
+        )
+
+    def to_left(at):
+        return remote(
+            block(at, narrow), from_right.at[at], line_send.at[at], right_got.at[at],
+            (narrow, wide - 2),
+        )
+
+    def add(target, source, count, step=64):
+        @pl.loop(0, count // step)
+        def _(i):
+            piece = pl.ds(pl.multiple_of(i * step, step), step)
+            target[piece, :] = (
+                target[piece, :].astype(f32) + source[piece, :].astype(f32)
+            ).astype(jnp.bfloat16)
+
+    for at in order:
+        for k in range(2):
+            load(at, k).start()
+            exchange(at, k).start()
+    gains = [
+        remote(gain_ref, wide_gains.at[step], wide_send.at[step], wide_got.at[step], device)
         for step, device in enumerate(wides)
     ]
-    for copy in copies:
+    for copy in gains:
         copy.start()
-    for copy in copies:
+
+    def pair_up(at):
+        for k in range(2):
+            load(at, k).wait()
+            exchange(at, k).wait_recv()
+        add(own.at[at], other.at[at], 4 * rows)
+        for k in range(2):
+            half(at, k).start()
+
+    def turn(at):
+        for k in range(2):
+            half(at, k).wait_recv()
+            add(half_block(at, near[1 - k], k), halves.at[at, k], half_rows)
+        for k in range(2):
+            whole(at, k).start()
+
+    def settle(at):
+        for k in range(2):
+            whole(at, k).wait_recv()
+        target = block(at, narrow)
+
+        @pl.loop(0, rows // 64)
+        def _(i):
+            piece = pl.ds(pl.multiple_of(i * 64, 64), 64)
+            target[piece, :] = (
+                target[piece, :].astype(f32)
+                + wholes[at, 0, piece, :].astype(f32)
+                + wholes[at, 1, piece, :].astype(f32)
+            ).astype(jnp.bfloat16)
+
+        @pl.when(at > chip)
+        def _():
+            @pl.when(chip > 0)
+            def _():
+                to_right(at).wait_recv()
+                add(target, from_left.at[at], rows)
+
+            to_right(at).start()
+
+        @pl.when(at < chip)
+        def _():
+            @pl.when(chip < 3)
+            def _():
+                to_left(at).wait_recv()
+                add(target, from_right.at[at], rows)
+
+            to_left(at).start()
+
+    pair_up(order[0])
+    pair_up(order[1])
+    turn(order[0])
+    pair_up(order[2])
+    turn(order[1])
+    settle(order[0])
+    pair_up(order[3])
+    turn(order[2])
+    settle(order[1])
+    for copy in gains:
         copy.wait()
-    total = own_ref[...]
-    for step in range(1, wide_count):
-        total = total + first_ref[step]
-    middle_ref[...] = total
-    copies = [
-        remote(middle_ref, second_ref.at[step + 1], send_two.at[step], got_two.at[step], device)
+    total = gain_ref[...]
+    for step in range(7):
+        total = total + wide_gains[step]
+    mid_gain[...] = total
+    gains = [
+        remote(mid_gain, narrow_gains.at[step], narrow_send.at[step], narrow_got.at[step], device)
         for step, device in enumerate(narrows)
     ]
-    for copy in copies:
+    for copy in gains:
         copy.start()
-    for copy in copies:
+    turn(order[3])
+    settle(order[2])
+    settle(order[3])
+    target = block(chip, narrow)
+
+    @pl.when(chip > 0)
+    def _():
+        to_right(chip).wait_recv()
+        add(target, from_left.at[chip], rows)
+
+    @pl.when(chip < 3)
+    def _():
+        to_left(chip).wait_recv()
+        add(target, from_right.at[chip], rows)
+
+    lanes = pl.ds(split - 128, 128)
+
+    @pl.loop(0, rows // 64)
+    def _(i):
+        piece = pl.ds(pl.multiple_of(i * 64, 64), 64)
+        value = target[piece, :]
+        sum_ref[piece, :] = value.astype(f32)
+        low[piece, :] = target[piece, lanes]
+
+    spread_ref[wide] = low[...]
+
+    def spread(step):
+        return remote(
+            low, spread_ref.at[wide], spread_send.at[step - 1], spread_got.at[step - 1],
+            (narrow, (wide + 2 * step) % 8),
+        )
+
+    def arrival(step):
+        target = spread_ref.at[(wide + 8 - 2 * step) % 8]
+        return remote(target, target, spread_send.at[step - 1], spread_got.at[step - 1], twin)
+
+    def pass_on(step):
+        piece = spread_ref.at[(wide + 8 - 2 * step) % 8]
+        return remote(piece, piece, pass_send.at[step], pass_got.at[step], twin)
+
+    def passed(step):
+        piece = spread_ref.at[(2 * chip + 1 - core + 8 - 2 * step) % 8]
+        return remote(piece, piece, pass_send.at[step], pass_got.at[step], twin)
+
+    for step in (1, 2, 3):
+        spread(step).start()
+    pass_on(0).start()
+    for copy in gains:
         copy.wait()
-    for step in range(1, narrow_count):
-        total = total + second_ref[step]
-    out_ref[...] = total
-
-
-def sum_gains(gains):
+    for step in range(3):
+        total = total + narrow_gains[step]
+    gain_sum_ref[...] = total
+    for step in (1, 2, 3):
+        arrival(step).wait_recv()
+        pass_on(step).start()
+    for step in range(4):
+        passed(step).wait_recv()
+        pass_on(step).wait_send()
+    for step in (1, 2, 3):
+        spread(step).wait_send()
+    for at in range(4):
+        for k in range(2):
+            exchange(at, k).wait_send()
+            half(at, k).wait_send()
+            whole(at, k).wait_send()
+
+        @pl.when(at != chip)
+        def _():
+            to_right(at).wait_send()
+
+
+def sum_weights(input_wgrad, output_wgrad, gains):
     narrow_count = lax.axis_size("narrow")
     wide_count = lax.axis_size("wide")
+    split = input_wgrad.shape[2]
+    if narrow_count != 4 or wide_count != 8:
+        total = jnp.concatenate([input_wgrad, output_wgrad], axis=2)
+        total = lax.psum_scatter(total, "narrow", scatter_dimension=1, tiled=True)
+        total = lax.psum_scatter(total, "wide", scatter_dimension=0)
+        spread = lax.all_gather(total[:, split - 128 : split], "wide", axis=0)
+        gains = jnp.sum(lax.all_gather(gains, ("narrow", "wide"), axis=0), axis=0)
+        return total.astype(jnp.float32), spread, gains
+    low = jnp.bfloat16
+    rows = input_wgrad.shape[1] // 4
+    columns = split + output_wgrad.shape[2]
     size = gains.size
-    rows = -(-size // 1024) * 8
-    flat = jnp.pad(gains.reshape(-1), (0, rows * 128 - size)).reshape(rows, 128)
+    gain_rows = -(-size // 1024) * 8
+    flat = jnp.pad(gains.reshape(-1), (0, gain_rows * 128 - size)).reshape(gain_rows, 128)
     dma = pltpu.SemaphoreType.DMA
-    total = pl.pallas_call(
-        gain_kernel,
-        out_shape=jax.ShapeDtypeStruct(flat.shape, jnp.float32),
-        in_specs=[pl.BlockSpec(memory_space=pltpu.VMEM)],
-        out_specs=pl.BlockSpec(memory_space=pltpu.VMEM),
+    vmem = pltpu.VMEM
+    total, spread, flat = pl.pallas_call(
+        scatter_kernel,
+        out_shape=[
+            jax.ShapeDtypeStruct((rows, columns), jnp.float32),
+            jax.ShapeDtypeStruct((8, rows, 128), low),
+            jax.ShapeDtypeStruct(flat.shape, jnp.float32),
+        ],
+        in_specs=[
+            pl.BlockSpec(memory_space=pl.ANY),
+            pl.BlockSpec(memory_space=pl.ANY),
+            pl.BlockSpec(memory_space=vmem),
+        ],
+        out_specs=[pl.BlockSpec(memory_space=vmem)] * 3,
         scratch_shapes=[
-            pltpu.VMEM((wide_count, rows, 128), jnp.float32),
-            pltpu.VMEM((rows, 128), jnp.float32),
-            pltpu.VMEM((narrow_count, rows, 128), jnp.float32),
-            dma((wide_count - 1,)),
-            dma((wide_count - 1,)),
-            dma((narrow_count - 1,)),
-            dma((narrow_count - 1,)),
+            vmem((4, 4 * rows, columns), low),
+            vmem((4, 4 * rows, columns), low),
+            vmem((4, 2, rows // 2, columns), low),
+            vmem((4, 2, rows, columns), low),
+            vmem((4, rows, columns), low),
+            vmem((4, rows, columns), low),
+            vmem((rows, 128), low),
+            vmem((7, gain_rows, 128), jnp.float32),
+            vmem((gain_rows, 128), jnp.float32),
+            vmem((3, gain_rows, 128), jnp.float32),
+            dma((4, 2)), dma((4, 2)), dma((4, 2)), dma((4, 2)), dma((4, 2)), dma((4, 2)),
+            dma((4, 2)), dma((4,)), dma((4,)), dma((4,)), dma((3,)), dma((3,)), dma((4,)),
+            dma((4,)), dma((7,)), dma((7,)), dma((3,)), dma((3,)),
         ],
-        compiler_params=pltpu.CompilerParams(collective_id=2, has_side_effects=True),
-        name="sum_gains",
-    )(flat)
-    return total.reshape(-1)[:size].reshape(gains.shape)
+        compiler_params=pltpu.CompilerParams(
+            collective_id=3, has_side_effects=True, vmem_limit_bytes=52 << 20
+        ),
+        cost_estimate=pl.CostEstimate(flops=0, bytes_accessed=300 << 20, transcendentals=0),
+        name="sum_weights",
+    )(input_wgrad, output_wgrad, flat)
+    return total, spread, flat.reshape(-1)[:size].reshape(gains.shape)
 
 
 def shards(
@@ -630,6 +858,9 @@
     down_wgrad = down_wgrad.astype(jnp.bfloat16)
     gate_wgrad = gate_wgrad.astype(jnp.bfloat16)
     up_wgrad = up_wgrad.astype(jnp.bfloat16)
+    mid_sums, gate_wgrad, up_wgrad, down_wgrad, block_parts = lax.optimization_barrier(
+        (mid_sums, gate_wgrad, up_wgrad, down_wgrad, block_parts)
+    )
     mid_back = jnp.concatenate(mid_sums, axis=0)
     middle_part, mid_gain_grad = norm_mid_back(mid_back)
     middle_grad = out_grad.astype(jnp.float32) + middle_part
@@ -643,25 +874,22 @@
     attended_grad, down_wgrad = lax.optimization_barrier((attended_grad, down_wgrad))
     down_total = lax.psum_scatter(down_wgrad, "narrow", scatter_dimension=1, tiled=True)
     head_grad = swap(attended_grad).reshape(wide_count * shard_rows, query_columns)
-    head_grad, block_parts, gate_wgrad, up_wgrad = lax.optimization_barrier(
-        (head_grad, block_parts, gate_wgrad, up_wgrad)
-    )
-    block_sums = [
-        lax.psum_scatter(part, "wide", scatter_dimension=0, tiled=True) for part in block_parts
-    ]
+    head_grad, down_total, first_part, gate_wgrad = lax.optimization_barrier(
+        (head_grad, down_total, block_parts[0], gate_wgrad)
+    )
+    first_sum = lax.psum_scatter(first_part, "wide", scatter_dimension=0, tiled=True)
     gate_total = lax.psum_scatter(gate_wgrad, "narrow", scatter_dimension=0, tiled=True)
-    up_total = lax.psum_scatter(up_wgrad, "narrow", scatter_dimension=0, tiled=True)
     head_grad = head_grad.astype(jnp.float32) / weight_sums
     scaled_grad = head_grad.astype(jnp.bfloat16)
     grad_dot = jnp.sum((head_grad * attended).reshape(-1, local_heads, head_dim), axis=-1).T
     packed_grad = attend_back(packed, scaled_grad, grad_dot, local_heads)
+    packed_grad, up_wgrad, first_sum = lax.optimization_barrier((packed_grad, up_wgrad, first_sum))
+    up_total = lax.psum_scatter(up_wgrad, "narrow", scatter_dimension=0, tiled=True)
     packed_grad = swap(packed_grad.reshape(wide_count, shard_rows, group_columns))
-    packed_grad, block_sums, gate_total, up_total, down_total = lax.optimization_barrier(
-        (packed_grad, block_sums, gate_total, up_total, down_total)
-    )
-    block_out = (middle + jnp.concatenate(block_sums, axis=0).astype(jnp.float32)).astype(
-        jnp.bfloat16
-    )
+    packed_grad, gate_total, second_part = lax.optimization_barrier(
+        (packed_grad, gate_total, block_parts[1])
+    )
+    second_sum = lax.psum_scatter(second_part, "wide", scatter_dimension=0, tiled=True)
     query_rot_grad = packed_grad[:, :, :query_columns].astype(jnp.float32).reshape(
         wide_count, shard_rows, local_heads, head_dim
     )
@@ -676,21 +904,27 @@
         ],
         axis=2,
     )
-    input_wgrad = jnp.einsum("td,gtc->gdc", rows_in, input_low, preferred_element_type=jnp.float32)
+    input_wgrad = jnp.einsum(
+        "td,gtc->gdc", rows_in, input_low, preferred_element_type=jnp.float32
+    ).astype(jnp.bfloat16)
     input_back = jnp.einsum("gtc,gdc->td", input_low, input_full, preferred_element_type=jnp.float32)
     input_part, in_gain_grad = norm_in_back(input_back)
     input_grad = middle_grad + input_part
     gain_stack = jnp.stack([in_gain_grad, mid_gain_grad])
     head_stack = jnp.stack([query_gain_grad, key_gain_grad])
-    gains = sum_gains(jnp.concatenate([gain_stack, head_stack], axis=1))
+    input_wgrad, up_total = lax.optimization_barrier((input_wgrad, up_total))
+    input_total, spread, gains = sum_weights(
+        input_wgrad,
+        output_wgrad.astype(jnp.bfloat16),
+        jnp.concatenate([gain_stack, head_stack], axis=1),
+    )
+    input_total, second_sum = lax.optimization_barrier((input_total, second_sum))
+    block_sum = jnp.concatenate([first_sum, second_sum], axis=0).astype(jnp.float32)
+    block_out = (middle + block_sum).astype(jnp.bfloat16)
     gain_total = gains[:, :model_width]
     head_total = gains[:, model_width:]
-    att_wgrad = jnp.concatenate([input_wgrad, output_wgrad], axis=2).astype(jnp.bfloat16)
-    att_total = lax.psum_scatter(att_wgrad, "narrow", scatter_dimension=1, tiled=True)
-    input_total = lax.psum_scatter(att_total, "wide", scatter_dimension=0)
-    output_total = input_total[:, group_columns:].astype(jnp.float32).T
-    query_total = input_total[:, :query_columns].astype(jnp.float32)
-    spread = lax.all_gather(input_total[:, query_columns:group_columns], "wide", axis=0)
+    output_total = input_total[:, group_columns:].T
+    query_total = input_total[:, :query_columns]
     spread = jnp.sum(
         spread.reshape(key_heads, copies, -1, 2, head_dim).astype(jnp.float32), axis=1
     ).transpose(2, 1, 0, 3)

time: 1580 us -> 1290 us (0.82)
  waiting for transfers between devices: 671 us -> 269 us
  Pallas kernels: 343 us -> 438 us
  blocking collectives: 0 us -> 52.6 us
  other arithmetic: 106 us -> 83.6 us
    reduce_scatter x4 -> x2, waiting for transfers between devices: 283 us -> 0.01 us  [the longest x1 0.01 us: shards(): lax.psum_scatter(first_part, 'wide', scatter_dimension=0, tiled=True)]
    pallas_call x1, Pallas kernels: 14.4 us -> 110 us  [sum_weights(): pl.pallas_call(scatter_kernel, out_shape=[jax.ShapeDtypeStruct((rows, col...]
    reduce_scatter x2, waiting for transfers between devices: 58.8 us -> 1.48 us  [sum_back(): lax.psum_scatter(summed.astype(jnp.bfloat16), 'wide', scatter_dimension=0...]
    all_to_all x0 -> x1, blocking collectives: none -> 52.6 us  [swap(): return lax.all_to_all(blocks, 'wide', 0, 0)]
    all_to_all x4 -> x3, waiting for transfers between devices: 224 us -> 175 us  [swap(): return lax.all_to_all(blocks, 'wide', 0, 0)]
    concatenate x2 -> x1, other arithmetic: 16 us -> 0.02 us  [shards(): jnp.concatenate([gain_stack, head_stack], axis=1)]
    unnamed x192 -> x207, local copies, waits for them, and re-layouts: 50.6 us -> 50.7 us
  transfers between devices with their start and end apart: 21 -> 17, of which waited for: 12 -> 8; matrix products, arithmetic and copies ran while one was open for 26% -> 34% of each run, Pallas kernels for 22% -> 34%
where the time goes in v5:
time: 1290 us; the launch traced here: 1280 us
  Pallas kernels  438 us (34%)
  matrix products  334 us (26%)
  waiting for transfers between devices  269 us (21%)
  other arithmetic  83.6 us (6%)
  local copies, waits for them, and re-layouts  78.9 us (6%)
  blocking collectives  52.6 us (4%)
  between operations  15.3 us (1%)
  starting transfers between devices  12.9 us (1%)
    all_to_all x3, waiting for transfers between devices, swap(): return lax.all_to_all(blocks, 'wide', 0, 0)  175 us
    pallas_call x1, Pallas kernels, gather_weights(): pl.pallas_call(gather_kernel, out_shape=jax.ShapeDtypeStruct((8, 4 * att....  147 us
    pallas_call x1, Pallas kernels, attend_back(): pl.pallas_call(functools.partial(back_kernel, block, heads), out_shape=ja...  119 us
    pallas_call x1, Pallas kernels, sum_weights(): pl.pallas_call(scatter_kernel, out_shape=[jax.ShapeDtypeStruct((rows, col...  110 us
    dot_general x6, matrix products, dot_back(): lax.dot_general(left, right, (((1,), (1,)), ((), ())), preferred_element_...  93.3 us
    dot_general x6, matrix products, dot_last(): return jnp.dot(left, right, preferred_element_type=jnp.float32)  90.2 us
    dot_general x6, matrix products, dot_first(): lax.dot_general(left, right, (((0,), (0,)), ((), ())), preferred_element_...  89 us
    all_gather x2, waiting for transfers between devices, gather_rows(): return lax.all_gather(shard, 'wide', axis=0, tiled=True)  67.9 us
  transfers between devices with their start and end apart: 17, of which 8 were waited for; matrix products, arithmetic and copies ran while one was open for 34% of the time, Pallas kernels for 34%

profile of v5, /device:TPU:0, one launch (start us, length us, event | category | flops | bytes accessed | tf_op | source)
XLA Modules:
  0.0 1284.4 jit_solution(13806000401654060471)
XLA Ops:
  13.9 147.5 %gather_weights.1 = bf16[8,2048,640]{2,1,0:T(8,128)(2,1)} custom-call(bf16[512,640]{1,0:T(8,128)(2,1)} %pad_maximum_fusion.4.att_ref), custom_call_target="tpu_custom_call" | custom-call | bytes 314572800 | tf_op jit(solution)/shard_map/gather_weights/pallas_call | solution.py:406
  171.0 9.6 fusion.30
  207.5 70.9 %all-to-all-done = bf16[8,512,384]{1,2,0:T(8,128)(2,1)S(1)} async-done(((bf16[8,512,384]{1,2,0:T(8,128)(2,1)}), bf16[8,512,384]{1,2,0:T(8,128)(2,1)S(1)}, u32[]{:S(2)}, u32[]{:S(2)}) %all-to-all-start) | async-done | bytes 3145760 | tf_op jit(solution)/shard_map/all_to_all | solution.py:425
  281.1 61.4 %attend.1 = (f32[4096,256]{1,0:T(8,128)}, f32[4096,256]{1,0:T(8,128)}, bf16[4096,256]{1,0:T(8,128)(2,1)}) custom-call(bf16[4096,384]{1,0:T(8,128)(2,1)} %bitcast.131), custom_call_target="tpu_custom_call" | custom-call | flops 34359738368 | bytes 18874368 | tf_op jit(solution)/shard_map/attend/pallas_call | solution.py:143
  351.1 15.7 %all-gather.16.cloned.1.call-done = bf16[1024,2048]{1,0:T(8,128)(2,1)} async-done(((bf16[1024,512]{1,0:T(8,128)(2,1)}), bf16[1024,2048]{1,0:T(8,128)(2,1)}) %all-gather.16.cloned.1.call-update) | async-done | bytes 4194320 | tf_op jit(solution)/shard_map/all_gather | solution.py:790
  366.8 33.3 %all-to-all-done.1 = bf16[8,512,256]{1,2,0:T(8,128)(2,1)} async-done(((bf16[8,512,256]{1,2,0:T(8,128)(2,1)}), bf16[8,512,256]{1,2,0:T(8,128)(2,1)}, u32[]{:S(2)}, u32[]{:S(2)}) %all-to-all-start.1) | async-done | bytes 2097184 | tf_op jit(solution)/shard_map/all_to_all | solution.py:425
  411.6 13.8 %convolution_convert_fusion.2 = bf16[2048,1024]{1,0:T(8,128)(2,1)} fusion(bf16[2048,2048]{1,0:T(8,128)(2,1)} %all-gather.10.cloned.1.call-done, bf16[1024,2048]{1,0:T(8,128)(2,1)} %all-gather.16.cloned.1.call-done), kind=kOutput, calls=%fused_computation.69 | convolution fusion | flops 8592031744 | bytes 16777216 | tf_op jit(solution)/shard_map/dot_general | solution.py:67
  425.5 66.2 %all-gather.20.cloned.1.call-done = bf16[2048,2048]{1,0:T(8,128)(2,1)} async-done(((bf16[256,2048]{1,0:T(8,128)(2,1)}), bf16[2048,2048]{1,0:T(8,128)(2,1)}) %all-gather.20.cloned.1.call-update) | async-done | bytes 8388624 | tf_op jit(solution)/shard_map/all_gather | solution.py:421
  491.7 14.6 %fusion.91 = f32[2048,1024]{1,0:T(8,128)} fusion(bf16[2048,2048]{1,0:T(8,128)(2,1)} %all-gather.20.cloned.1.call-done, bf16[2048,1024]{1,0:T(8,128)(2,1)} %all-gather.12.cloned.1.call-done), kind=kOutput, calls=%fused_computation.175 | convolution fusion | flops 8589934592 | bytes 20971520 | tf_op jit(solution)/shard_map/dot_general | solution.py:57
  506.3 17.3 %multiply_convert_fusion = (bf16[2048,1024]{1,0:T(8,128)(2,1)}, bf16[2048,1024]{1,0:T(8,128)(2,1)}) fusion(f32[2048,1024]{1,0:T(8,128)} %fusion.91, bf16[2048,1024]{1,0:T(8,128)(2,1)} %convolution_convert_fusion.2, bf16[2048,2048]{1,0:T(8,128)(2,1)S(1)} %copy-done.79, bf16[2048,1024]{1,0:T(8,128)(2,1)} %all-gather.14.cloned.1.call-done), kind=kOutput, calls=%fused_computation.23 | convolution fusion | flops 8621391872 | bytes 33554432 | tf_op jit(solution)/shard_map/dot_general | solution.py:57
  523.6 14.5 %fusion.92 = f32[2048,2048]{1,0:T(8,128)} fusion(bf16[2048,1024]{1,0:T(8,128)(2,1)} %get-tuple-element.203, bf16[2048,1024]{1,0:T(8,128)(2,1)S(1)} %copy-done.81), kind=kOutput, calls=%fused_computation.176 | convolution fusion | flops 8589934592 | bytes 25165824 | tf_op jit(solution)/shard_map/dot_general | solution.py:67
  538.1 20.5 %add_convert_fusion = bf16[2048,2048]{1,0:T(8,128)(2,1)} fusion(f32[2048,2048]{1,0:T(8,128)} %fusion.92, bf16[2048,1024]{1,0:T(8,128)(2,1)} %all-gather.14.cloned.1.call-done, bf16[2048,1024]{1,0:T(8,128)(2,1)} %convolution_convert_fusion.2, f32[2048,1024]{1,0:T(8,128)} %fusion.91), kind=kOutput, calls=%fused_computation | convolution fusion | flops 8613003264 | bytes 41943040 | tf_op jit(solution)/shard_map/dot_general | solution.py:67
  558.7 14.1 %convolution_convert_fusion.3 = bf16[2048,1024]{1,0:T(8,128)(2,1)} fusion(bf16[2048,2048]{1,0:T(8,128)(2,1)} %all-gather.8.cloned.1.call-done, bf16[1024,2048]{1,0:T(8,128)(2,1)} %all-gather.16.cloned.1.call-done), kind=kOutput, calls=%fused_computation.70 | convolution fusion | flops 8592031744 | bytes 16777216 | tf_op jit(solution)/shard_map/dot_general | solution.py:67
  574.5 14.6 %fusion.89 = f32[2048,1024]{1,0:T(8,128)} fusion(bf16[2048,2048]{1,0:T(8,128)(2,1)} %all-gather.18.cloned.1.call-done, bf16[2048,1024]{1,0:T(8,128)(2,1)} %all-gather.12.cloned.1.call-done), kind=kOutput, calls=%fused_computation.173 | convolution fusion | flops 8589934592 | bytes 20971520 | tf_op jit(solution)/shard_map/dot_general | solution.py:57
  589.1 18.4 %multiply_convert_fusion.1 = (bf16[2048,1024]{1,0:T(8,128)(2,1)}, bf16[2048,1024]{1,0:T(8,128)(2,1)}, bf16[2048,1024]{1,0:T(8,128)(2,1)}) fusion(f32[2048,1024]{1,0:T(8,128)} %fusion.89, bf16[2048,1024]{1,0:T(8,128)(2,1)} %convolution_convert_fusion.3, bf16[2048,2048]{1,0:T(8,128)(2,1)S(1)} %copy-done.80, bf16[2048,1024]{1,0:T(8,128)(2,1)} %all-gather.14.cloned.1.call-done), kind=kOutput, calls=%fused_computation.24 | convolution fusion | flops 8625586176 | bytes 37748736 | tf_op jit(solution)/shard_map/dot_general | solution.py:57
  607.5 14.4 %fusion.90 = f32[2048,2048]{1,0:T(8,128)} fusion(bf16[2048,1024]{1,0:T(8,128)(2,1)} %get-tuple-element.205, bf16[2048,1024]{1,0:T(8,128)(2,1)S(1)} %copy-done.82), kind=kOutput, calls=%fused_computation.174 | convolution fusion | flops 8589934592 | bytes 25165824 | tf_op jit(solution)/shard_map/dot_general | solution.py:67
  621.9 16.0 %add_convert_fusion.1 = bf16[2048,2048]{1,0:T(8,128)(2,1)} fusion(f32[2048,2048]{1,0:T(8,128)} %fusion.90, bf16[2048,1024]{1,0:T(8,128)(2,1)} %get-tuple-element.206, bf16[2048,1024]{1,0:T(8,128)(2,1)S(1)} %copy-done.83), kind=kOutput, calls=%fused_computation.1 | convolution fusion | flops 8598323200 | bytes 33554432 | tf_op jit(solution)/shard_map/dot_general | solution.py:67
  638.0 15.3 %fusion.94 = f32[2048,1024]{1,0:T(8,128)} fusion(bf16[2048,2048]{1,0:T(8,128)(2,1)} %all-gather.18.cloned.1.call-done, bf16[2048,1024]{1,0:T(8,128)(2,1)} %get-tuple-element.206), kind=kOutput, calls=%fused_computation.178 | convolution fusion | flops 8589934592 | bytes 20971520 | tf_op jit(solution)/shard_map/dot_general | solution.py:61
  653.3 13.7 %fusion.93 = f32[2048,1024]{1,0:T(8,128)} fusion(bf16[2048,2048]{1,0:T(8,128)(2,1)} %all-gather.18.cloned.1.call-done, bf16[2048,1024]{1,0:T(8,128)(2,1)S(1)} %copy-done.87), kind=kOutput, calls=%fused_computation.177 | convolution fusion | flops 8589934592 | bytes 20971520 | tf_op jit(solution)/shard_map/dot_general | solution.py:61
  667.0 11.0 convolution_convert_fusion
  678.0 14.2 %convolution_convert_fusion.1 = bf16[2048,2048]{1,0:T(8,128)(2,1)} fusion(bf16[2048,1024]{1,0:T(8,128)(2,1)} %get-tuple-element.204, bf16[1024,2048]{1,0:T(8,128)(2,1)} %all-gather.16.cloned.1.call-done), kind=kOutput, calls=%fused_computation.37 | convolution fusion | flops 8594128896 | bytes 16777216 | tf_op jit(solution)/shard_map/dot_general | solution.py:57
  692.2 12.9 %fusion.95 = f32[1024,2048]{1,0:T(8,128)S(1)} fusion(bf16[2048,1024]{1,0:T(8,128)(2,1)} %get-tuple-element.204, bf16[2048,2048]{1,0:T(8,128)(2,1)} %all-gather.8.cloned.1.call-done), kind=kOutput, calls=%fused_computation.179 | convolution fusion | flops 8589934592 | bytes 20971520 | tf_op jit(solution)/shard_map/dot_general | solution.py:61
  705.0 13.0 %add_convert_fusion.2 = bf16[1024,2048]{1,0:T(8,128)(2,1)} fusion(f32[1024,2048]{1,0:T(8,128)S(1)} %fusion.95, bf16[2048,1024]{1,0:T(8,128)(2,1)S(1)} %copy-done.86, bf16[2048,2048]{1,0:T(8,128)(2,1)} %all-gather.10.cloned.1.call-done), kind=kOutput, calls=%fused_computation.22 | convolution fusion | flops 8594128896 | bytes 25165824 | tf_op jit(solution)/shard_map/dot_general | solution.py:61
  718.0 15.3 %add_convert_fusion.4 = bf16[2048,1024]{1,0:T(8,128)(2,1)} fusion(f32[2048,1024]{1,0:T(8,128)} %fusion.93, bf16[2048,2048]{1,0:T(8,128)(2,1)} %all-gather.20.cloned.1.call-done, bf16[2048,1024]{1,0:T(8,128)(2,1)} %get-tuple-element.203), kind=kOutput, calls=%fused_computation.26 | convolution fusion | flops 8594128896 | bytes 25165824 | tf_op jit(solution)/shard_map/dot_general | solution.py:61
  733.4 18.9 %add_convert_fusion.3 = bf16[2048,1024]{1,0:T(8,128)(2,1)} fusion(f32[2048,1024]{1,0:T(8,128)} %fusion.94, bf16[2048,2048]{1,0:T(8,128)(2,1)} %all-gather.20.cloned.1.call-done, bf16[2048,1024]{1,0:T(8,128)(2,1)} %convolution_convert_fusion.2, f32[2048,1024]{1,0:T(8,128)} %fusion.91), kind=kOutput, calls=%fused_computation.25 | convolution fusion | flops 8608808960 | bytes 33554432 | tf_op jit(solution)/shard_map/dot_general | solution.py:61
  772.8 52.6 %all_to_all.20 = bf16[8,512,256]{1,2,0:T(8,128)(2,1)S(1)} all-to-all(bf16[8,512,256]{1,2,0:T(8,128)(2,1)} %convert_bitcast_fusion.2), channel_id=1, replica_groups=mesh['narrow'=4,'wide'=8] {'wide'}, dimensions={0} | all-to-all | bytes 4194304 | tf_op jit(solution)/shard_map/all_to_all | solution.py:425
  845.8 119.2 %attend_back.1 = bf16[4096,384]{1,0:T(8,128)(2,1)} custom-call(bf16[4096,384]{1,0:T(8,128)(2,1)} %bitcast.132, bf16[4096,256]{1,0:T(8,128)(2,1)} %get-tuple-element.208.g_ref, f32[4,4096]{1,0:T(4,128)} %bitcast.140), custom_call_target="tpu_custom_call" | custom-call | flops 85899345920 | bytes 18874368 | tf_op jit(solution)/shard_map/attend_back/pallas_call | solution.py:229
  973.7 71.2 %all-to-all-done.3 = bf16[8,512,384]{1,2,0:T(8,128)(2,1)S(1)} async-done(((bf16[8,512,384]{1,2,0:T(8,128)(2,1)}), bf16[8,512,384]{1,2,0:T(8,128)(2,1)S(1)}, u32[]{:S(2)}, u32[]{:S(2)}) %all-to-all-start.3) | async-done | bytes 3145760 | tf_op jit(solution)/shard_map/all_to_all | solution.py:425
  1064.3 10.9 convert_bitcast_fusion.1.out_ref
  1089.0 14.3 %fusion.26 = (f32[512]{0:T(512)S(1)}, f32[2048]{0:T(1024)S(1)}, f32[512,2048,1]{1,0,2:T(8,128)}) fusion(bf16[512,2048]{1,0:T(8,128)(2,1)S(1)} %copy-done.12, f32[2048]{0:T(1024)S(1)} %bitcast.142, f32[512]{0:T(512)S(1)} %copy-done.74, bf16[8,2048,640]{2,1,0:T(8,128)(2,1)} %gather_weights.1, bf16[8,512,64]{1,2,0:T(8,128)(2,1)S(1)} %get-tuple-element.214, ...), kind=kOutput, calls=%fused_computation.53 | convolution fusion | flops 6459225600 | bytes 22040576 | tf_op jit(solution)/shard_map/gtc,gdc->td/dot_general | solution.py:910
  1114.5 9.8 convert_bitcast_fusion.in_ref
  1124.3 110.4 %sum_weights.1 = (f32[512,640]{1,0:T(8,128)}, bf16[8,512,128]{2,1,0:T(8,128)(2,1)S(1)}, f32[40,128]{1,0:T(8,128)S(1)}) custom-call(bf16[8,2048,384]{2,1,0:T(8,128)(2,1)} %convert_bitcast_fusion.in_ref, bf16[8,2048,256]{2,1,0:T(8,128)(2,1)} %convert_bitcast_fusion.1.out_ref, f32[40,128]{1,0:T(8,128)S(1)} %pad_bitcast_fusion.gain_ref), custom_call_target="tpu_custom_call" | custom-call | bytes 314572800 | tf_op jit(solution)/shard_map/sum_weights/pallas_call | solution.py:693
  (328 shorter events, 203.7 us)
Async XLA Ops:
  7.2 190.8 %all-gather.10.cloned.1.call-start = ((), (), s32[]{:S(2)}) async-start(), calls=%async_computation.12 | async-start | bytes 9437184 | tf_op jit(solution)/shard_map/all_gather | solution.py:778
  10.5 192.8 %all-gather.8.cloned.1.call-start = ((), (), s32[]{:S(2)}) async-start(), calls=%async_computation.11 | async-start | bytes 9437184 | tf_op jit(solution)/shard_map/all_gather | solution.py:777
  11.2 339.8 %all-gather.12.cloned.1.call-start = ((), (), s32[]{:S(2)}) async-start(), calls=%async_computation.13 | async-start | bytes 5242880 | tf_op jit(solution)/shard_map/all_gather | solution.py:788
  168.2 182.9 %all-gather.14.cloned.1.call-start = ((), (), s32[]{:S(2)}) async-start(), calls=%async_computation.14 | async-start | bytes 5242880 | tf_op jit(solution)/shard_map/all_gather | solution.py:789
  168.8 239.1 %copy-start.54 = (f32[1,2048]{1,0:T(1,128)}, f32[1,2048]{1,0:T(1,128)S(1)}, u32[]{:S(2)}) copy-start(f32[1,2048]{1,0:T(1,128)S(1)} %get-tuple-element.225) | copy-start | bytes 24580
  203.2 75.1 %all-to-all-start = ((bf16[8,512,384]{1,2,0:T(8,128)(2,1)}), bf16[8,512,384]{1,2,0:T(8,128)(2,1)S(1)}, u32[]{:S(2)}, u32[]{:S(2)}) async-start(bf16[8,512,384]{1,2,0:T(8,128)(2,1)} %pad_maximum_fusion), calls=%async_computation | async-start | bytes 6291456 | tf_op jit(solution)/shard_map/all_to_all | solution.py:425
  206.9 159.9 %all-gather.16.cloned.1.call-start = ((), (), s32[]{:S(2)}) async-start(), calls=%async_computation.15 | async-start | bytes 5242880 | tf_op jit(solution)/shard_map/all_gather | solution.py:790
  342.5 57.6 %copy-start.11 = (bf16[512,2048]{1,0:T(8,128)(2,1)S(1)}, bf16[512,2048]{1,0:T(8,128)(2,1)}, u32[]{:S(2)}) copy-start(bf16[512,2048]{1,0:T(8,128)(2,1)} %param.30) | copy-start | bytes 6291460
  346.6 53.4 %all-to-all-start.1 = ((bf16[8,512,256]{1,2,0:T(8,128)(2,1)}), bf16[8,512,256]{1,2,0:T(8,128)(2,1)}, u32[]{:S(2)}, u32[]{:S(2)}) async-start(bf16[8,512,256]{1,2,0:T(8,128)(2,1)} %copy.85), calls=%async_computation.1 | async-start | bytes 4194304 | tf_op jit(solution)/shard_map/all_to_all | solution.py:425
  351.0 140.7 %all-gather.20.cloned.1.call-start = ((), (), s32[]{:S(2)}) async-start(), calls=%async_computation.18 | async-start | bytes 9437184 | tf_op jit(solution)/shard_map/all_gather | solution.py:421
  410.6 163.9 %all-gather.18.cloned.1.call-start = ((), (), s32[]{:S(2)}) async-start(), calls=%async_computation.16 | async-start | bytes 9437184 | tf_op jit(solution)/shard_map/all_gather | solution.py:421
  411.3 340.9 %reduce-scatter.10.cloned.1.call-start = ((), (), s32[]{:S(2)}) async-start(), calls=%async_computation.19 | async-start | bytes 9437184 | tf_op jit(solution)/shard_map/reduce_scatter | solution.py:432
  491.7 14.6 %copy-start.79 = (bf16[2048,2048]{1,0:T(8,128)(2,1)S(1)}, bf16[2048,2048]{1,0:T(8,128)(2,1)}, u32[]{:S(2)}) copy-start(bf16[2048,2048]{1,0:T(8,128)(2,1)} %all-gather.20.cloned.1.call-done) | copy-start | bytes 25165828
  506.3 17.3 %copy-start.81 = (bf16[2048,1024]{1,0:T(8,128)(2,1)S(1)}, bf16[2048,1024]{1,0:T(8,128)(2,1)}, u32[]{:S(2)}) copy-start(bf16[2048,1024]{1,0:T(8,128)(2,1)} %all-gather.12.cloned.1.call-done) | copy-start | bytes 12582916
  558.7 196.6 %reduce-scatter.8.cloned.1.call-start = ((), (), s32[]{:S(2)}) async-start(), calls=%async_computation.17 | async-start | bytes 9437184 | tf_op jit(solution)/shard_map/reduce_scatter | solution.py:432
  574.5 14.6 %copy-start.80 = (bf16[2048,2048]{1,0:T(8,128)(2,1)S(1)}, bf16[2048,2048]{1,0:T(8,128)(2,1)}, u32[]{:S(2)}) copy-start(bf16[2048,2048]{1,0:T(8,128)(2,1)} %all-gather.18.cloned.1.call-done) | copy-start | bytes 25165828
  589.1 18.4 %copy-start.82 = (bf16[2048,1024]{1,0:T(8,128)(2,1)S(1)}, bf16[2048,1024]{1,0:T(8,128)(2,1)}, u32[]{:S(2)}) copy-start(bf16[2048,1024]{1,0:T(8,128)(2,1)} %all-gather.12.cloned.1.call-done) | copy-start | bytes 12582916
  607.5 14.4 %copy-start.83 = (bf16[2048,1024]{1,0:T(8,128)(2,1)S(1)}, bf16[2048,1024]{1,0:T(8,128)(2,1)}, u32[]{:S(2)}) copy-start(bf16[2048,1024]{1,0:T(8,128)(2,1)} %all-gather.14.cloned.1.call-done) | copy-start | bytes 12582916
  638.0 189.8 %reduce-scatter.12.cloned.1.call-start = ((), (), s32[]{:S(2)}) async-start(), calls=%async_computation.20 | async-start | bytes 5242880 | tf_op jit(solution)/shard_map/reduce_scatter | solution.py:875
  638.0 15.3 %copy-start.87 = (bf16[2048,1024]{1,0:T(8,128)(2,1)S(1)}, bf16[2048,1024]{1,0:T(8,128)(2,1)}, u32[]{:S(2)}) copy-start(bf16[2048,1024]{1,0:T(8,128)(2,1)} %get-tuple-element.205) | copy-start | bytes 12582916
  653.3 13.7 %copy-start.84 = (bf16[1024,2048]{1,0:T(8,128)(2,1)S(1)}, bf16[1024,2048]{1,0:T(8,128)(2,1)}, u32[]{:S(2)}) copy-start(bf16[1024,2048]{1,0:T(8,128)(2,1)} %all-gather.16.cloned.1.call-done) | copy-start | bytes 12582916
  653.3 13.7 %copy-start.85 = (bf16[2048,1024]{1,0:T(8,128)(2,1)S(1)}, bf16[2048,1024]{1,0:T(8,128)(2,1)}, u32[]{:S(2)}) copy-start(bf16[2048,1024]{1,0:T(8,128)(2,1)} %get-tuple-element.202) | copy-start | bytes 12582916
  772.8 192.2 %reduce-scatter.14.cloned.1.call-start = ((), (), s32[]{:S(2)}) async-start(), calls=%async_computation.21 | async-start | bytes 9437184 | tf_op jit(solution)/shard_map/reduce_scatter | solution.py:880
  827.8 145.9 %reduce-scatter.16.cloned.1.call-start = ((), (), s32[]{:S(2)}) async-start(), calls=%async_computation.22 | async-start | bytes 5242880 | tf_op jit(solution)/shard_map/reduce_scatter | solution.py:881
  828.4 295.9 %reduce-scatter.18.cloned.1.call-start = ((), (), s32[]{:S(2)}) async-start(), calls=%async_computation.23 | async-start | bytes 5242880 | tf_op jit(solution)/shard_map/reduce_scatter | solution.py:887
  969.8 75.1 %all-to-all-start.3 = ((bf16[8,512,384]{1,2,0:T(8,128)(2,1)}), bf16[8,512,384]{1,2,0:T(8,128)(2,1)S(1)}, u32[]{:S(2)}, u32[]{:S(2)}) async-start(bf16[8,512,384]{1,2,0:T(8,128)(2,1)} %copy.90), calls=%async_computation.7 | async-start | bytes 6291456 | tf_op jit(solution)/shard_map/all_to_all | solution.py:425
  973.4 292.1 %reduce-scatter.20.cloned.1.call-start = ((), (), s32[]{:S(2)}) async-start(), calls=%async_computation.24 | async-start | bytes 9437184 | tf_op jit(solution)/shard_map/reduce_scatter | solution.py:892
  1088.5 14.8 %copy-start.31 = (bf16[8,512,4,64]{1,3,2,0:T(8,128)(2,1)}, bf16[8,512,4,64]{1,3,2,0:T(8,128)(2,1)S(1)}, u32[]{:S(2)}) copy-start(bf16[8,512,4,64]{1,3,2,0:T(8,128)(2,1)S(1)} %fusion.23) | copy-start | bytes 6291460
  1089.0 14.4 %copy-start.60 = (f32[2048]{0:T(1024)S(1)}, f32[2048]{0:T(1024)}, u32[]{:S(2)}) copy-start(f32[2048]{0:T(1024)} %get-tuple-element.167) | copy-start | bytes 24580
  1089.0 14.5 %copy-start.64 = (f32[512]{0:T(512)S(1)}, f32[512]{0:T(512)}, u32[]{:S(2)}) copy-start(f32[512]{0:T(512)} %copy-done.63) | copy-start | bytes 6148
  1089.0 14.5 %copy-start.7 = (f32[512,1024]{1,0:T(8,128)S(1)}, f32[512,1024]{1,0:T(8,128)}, u32[]{:S(2)}) copy-start(f32[512,1024]{1,0:T(8,128)} %param.45) | copy-start | bytes 6291460
  1089.0 14.5 %copy-start.39 = (bf16[512,1024]{1,0:T(8,128)(2,1)S(1)}, bf16[512,1024]{1,0:T(8,128)(2,1)}, u32[]{:S(2)}) copy-start(bf16[512,1024]{1,0:T(8,128)(2,1)} %reduce-scatter.16.cloned.1.call-done) | copy-start | bytes 3145732
  (80 other events, 383.2 us)
Sparse Core Ops, SparseCore 0:
  10.6 106.7 all-gather.9
  119.6 83.5 all-gather.7
  205.7 51.2 all-gather.11
  259.2 52.6 all-gather.13
  314.2 52.5 all-gather.15
  410.7 80.9 all-gather.19
  493.8 80.5 all-gather.17
  576.7 88.1 reduce-scatter.9
  667.2 87.9 reduce-scatter.7
  772.9 51.0 reduce-scatter.11
  827.9 88.4 reduce-scatter.13
  919.5 51.0 reduce-scatter.15
  973.6 52.6 reduce-scatter.17
  1045.0 90.9 reduce-scatter.19

commit v6 on v5

--- a/solution.py
+++ b/solution.py
@@ -725,6 +725,400 @@
         name="sum_weights",
     )(input_wgrad, output_wgrad, flat)
     return total, spread, flat.reshape(-1)[:size].reshape(gains.shape)
+
+
+def tell_wide():
+    narrow = lax.axis_index("narrow")
+    wide = lax.axis_index("wide")
+    barrier = pltpu.get_barrier_semaphore()
+    for step in range(1, 8):
+        pl.semaphore_signal(
+            barrier, inc=1, device_id=(narrow, (wide + step) % 8),
+            device_id_type=pl.DeviceIdType.MESH,
+        )
+    pl.semaphore_wait(barrier, 7)
+
+
+def attend_swap_kernel(
+    heads, src_ref, packed_ref, o_ref, s_ref, out_ref, kk_ref, va_ref, vb_ref, acc_ref, low_ref,
+    own_sem, send_sem, got_sem, out_send, out_got,
+):
+    narrow, wide, chip, core = place()
+    block = src_ref.shape[1]
+    base = 4 * (chip // 2)
+    away = 4 - base
+    low = low_lanes(block)
+    tell_wide()
+
+    def send(to):
+        return remote(
+            src_ref.at[to], packed_ref.at[wide], send_sem.at[to], got_sem.at[wide], (narrow, to)
+        )
+
+    def arrival(at):
+        target = packed_ref.at[at]
+        return remote(target, target, send_sem.at[at], got_sem.at[at], (narrow, at))
+
+    def send_out(to):
+        return remote(
+            low_ref.at[to], out_ref.at[wide], out_send.at[to], out_got.at[wide], (narrow, to)
+        )
+
+    own = pltpu.make_async_copy(src_ref.at[wide], packed_ref.at[wide], own_sem)
+    own.start()
+    for step in (1, 2, 3, 4, 5, 6, 7):
+        send((wide + step) % 8).start()
+
+    def prepare(j):
+        rows = pl.ds(pl.multiple_of(j * block, block), block)
+        kv = packed_ref[j, :, pl.ds(heads * 64, 128)]
+        vk = jnp.concatenate([kv[:, 64:], kv[:, :64]], axis=1)
+        one = jnp.ones_like(kv)
+        kk_ref[rows, :] = jnp.where(low, kv, vk)
+        va_ref[rows, :] = jnp.where(low, vk, one)
+        vb_ref[rows, :] = jnp.where(low, one, kv)
+
+    def await_blocks(start):
+        @pl.loop(start, start + 4)
+        def _(j):
+            @pl.when(j != wide)
+            def _():
+                arrival(j).wait_recv()
+
+            prepare(j)
+
+    causal = lax.broadcasted_iota(jnp.int32, (block, block), 0) >= lax.broadcasted_iota(
+        jnp.int32, (block, block), 1
+    )
+
+    def pairs(i, first, stop, diagonal):
+        for pair in range(heads // 2):
+            both = packed_ref[i, :, pl.ds(pair * 128, 128)]
+            zero = jnp.zeros_like(both)
+            sides = (jnp.where(low, both, zero), jnp.where(low, zero, both))
+
+            def step(j, masked, fresh):
+                keys = pl.ds(pl.multiple_of(j * block, block), block)
+                kk = kk_ref[keys, :]
+                for side in range(2):
+                    weights = jnp.exp2(nt(sides[side], kk))
+                    if masked:
+                        weights = jnp.where(causal, weights, 0.0)
+                    part = nn(weights.astype(jnp.bfloat16), (va_ref, vb_ref)[side][keys, :])
+                    if fresh:
+                        acc_ref[i, pair * 2 + side] = part
+                    else:
+                        acc_ref[i, pair * 2 + side] += part
+
+            if diagonal:
+                step(i, True, True)
+
+            @pl.loop(first, stop)
+            def _(j):
+                step(j, False, False)
+
+    def finish(i):
+        rows = pl.ds(pl.multiple_of(i * block, block), block)
+        for pair in range(heads // 2):
+            lanes = pl.ds(pair * 128, 128)
+            first, second = acc_ref[i, pair * 2], acc_ref[i, pair * 2 + 1]
+            summed = jnp.where(low, first, second)
+            sums = jnp.where(low, second, first)
+            sums = jnp.concatenate([sums[:, 64:], sums[:, :64]], axis=1)
+            result = summed / sums
+            o_ref[rows, lanes] = result
+            s_ref[rows, lanes] = sums
+            low_ref[i, :, lanes] = result.astype(jnp.bfloat16)
+
+        @pl.when(i != wide)
+        def _():
+            send_out(i).start()
+
+        @pl.when(i == wide)
+        def _():
+            out_ref[i] = low_ref[i]
+
+    own.wait()
+    await_blocks(base)
+
+    @pl.loop(base, base + 4)
+    def _(i):
+        pairs(i, base, i, True)
+
+        @pl.when(base == 0)
+        def _():
+            finish(i)
+
+    await_blocks(away)
+
+    @pl.loop(away, away + 4)
+    def _(i):
+        pairs(i, 0, i, True)
+        finish(i)
+
+    @pl.when(base > 0)
+    def _():
+        @pl.loop(4, 8)
+        def _(i):
+            pairs(i, 0, 4, False)
+            finish(i)
+
+    for step in range(1, 8):
+        to = (wide + step) % 8
+        target = out_ref.at[to]
+        remote(target, target, out_send.at[to], out_got.at[to], (narrow, to)).wait_recv()
+        send_out(to).wait_send()
+        send(to).wait_send()
+
+
+def attend_swap(src, heads):
+    if lax.axis_size("narrow") != 4 or lax.axis_size("wide") != 8:
+        packed = swap(src)
+        flat = packed.reshape(-1, src.shape[2])
+        attended, weight_sums, attended_low = attend(flat, heads)
+        return packed, attended, weight_sums, swap(attended_low.reshape(src.shape[0], -1, heads * 64))
+    count, block, lanes = src.shape
+    total = count * block
+    dma = pltpu.SemaphoreType.DMA
+    vmem = pltpu.VMEM
+    cost = heads * total * total // 2
+    return pl.pallas_call(
+        functools.partial(attend_swap_kernel, heads),
+        out_shape=[
+            jax.ShapeDtypeStruct(src.shape, jnp.bfloat16),
+            jax.ShapeDtypeStruct((total, heads * 64), jnp.float32),
+            jax.ShapeDtypeStruct((total, heads * 64), jnp.float32),
+            jax.ShapeDtypeStruct((count, block, heads * 64), jnp.bfloat16),
+        ],
+        in_specs=[pl.BlockSpec(memory_space=pl.ANY)],
+        out_specs=[pl.BlockSpec(memory_space=vmem)] * 4,
+        scratch_shapes=[vmem((total, 128), jnp.bfloat16)] * 3
+        + [
+            vmem((count, heads, block, 128), jnp.float32),
+            vmem((count, block, heads * 64), jnp.bfloat16),
+            dma, dma((8,)), dma((8,)), dma((8,)), dma((8,)),
+        ],
+        compiler_params=pltpu.CompilerParams(
+            collective_id=4, has_side_effects=True, vmem_limit_bytes=52 << 20
+        ),
+        cost_estimate=pl.CostEstimate(
+            flops=8 * cost * 256, bytes_accessed=12 * src.size, transcendentals=cost
+        ),
+        name="attend_swap",
+    )(src)
+
+
+def back_swap_kernel(
+    heads, packed_ref, g_ref, o_ref, s_ref, dq_out, dkv_out,
+    grad_ref, scaled_ref, dots_ref, dq_ref, dkv_ref, kk_ref, vv_ref, ka_ref, kb_ref,
+    low_q, low_kv, own_sem, send_sem, got_sem, q_send, q_got, kv_send, kv_got,
+):
+    narrow, wide, chip, core = place()
+    count, block, _ = packed_ref.shape
+    base = 4 * (chip // 2)
+    away = 4 - base
+    low = low_lanes(block)
+    tell_wide()
+
+    def send(to):
+        return remote(
+            g_ref.at[to], grad_ref.at[wide], send_sem.at[to], got_sem.at[wide], (narrow, to)
+        )
+
+    def send_q(to):
+        return remote(low_q.at[to], dq_out.at[wide], q_send.at[to], q_got.at[wide], (narrow, to))
+
+    def send_kv(to):
+        return remote(
+            low_kv.at[to], dkv_out.at[wide], kv_send.at[to], kv_got.at[wide], (narrow, to)
+        )
+
+    own = pltpu.make_async_copy(g_ref.at[wide], grad_ref.at[wide], own_sem)
+    own.start()
+    for step in range(1, 8):
+        send((wide + step) % 8).start()
+
+    @pl.loop(0, count)
+    def _(j):
+        rows = pl.ds(pl.multiple_of(j * block, block), block)
+        kv = packed_ref[j, :, pl.ds(heads * 64, 128)]
+        vk = jnp.concatenate([kv[:, 64:], kv[:, :64]], axis=1)
+        zero = jnp.zeros_like(kv)
+        kk_ref[rows, :] = jnp.where(low, kv, vk)
+        vv_ref[rows, :] = jnp.where(low, vk, kv)
+        ka_ref[rows, :] = jnp.where(low, kv, zero)
+        kb_ref[rows, :] = jnp.where(low, zero, vk)
+        dkv_ref[0, rows, :] = jnp.zeros((block, 128), jnp.float32)
+        dkv_ref[1, rows, :] = jnp.zeros((block, 128), jnp.float32)
+
+    causal = lax.broadcasted_iota(jnp.int32, (block, block), 0) <= lax.broadcasted_iota(
+        jnp.int32, (block, block), 1
+    )
+    first_lanes = lax.broadcasted_iota(jnp.int32, (8, 128), 1) < 64
+    picks = (
+        jnp.where(first_lanes, 1.0, 0.0).astype(jnp.bfloat16),
+        jnp.where(first_lanes, 0.0, 1.0).astype(jnp.bfloat16),
+    )
+
+    def rows_back(i):
+        rows = pl.ds(pl.multiple_of(i * block, block), block)
+        for pair in range(heads // 2):
+            lanes = pl.ds(pair * 128, 128)
+            grad = grad_ref[i, :, lanes].astype(jnp.float32) / s_ref[rows, lanes]
+            scaled_ref[...] = grad.astype(jnp.bfloat16)
+            product = grad * o_ref[rows, lanes]
+            high = product.astype(jnp.bfloat16)
+            rest = (product - high.astype(jnp.float32)).astype(jnp.bfloat16)
+            for side in range(2):
+                dots_ref[side] = nt(picks[side], high) + nt(picks[side], rest)
+            qboth = packed_ref[i, :, lanes]
+            gboth = scaled_ref[...]
+            zero = jnp.zeros_like(qboth)
+            qs = (jnp.where(low, qboth, zero), jnp.where(low, zero, qboth))
+            gs = (jnp.where(low, gboth, zero), jnp.where(low, zero, gboth))
+
+            def step(j, diagonal):
+                keys = pl.ds(pl.multiple_of(j * block, block), block)
+                kk = kk_ref[keys, :]
+                vv = vv_ref[keys, :]
+                for side in range(2):
+                    weights = jnp.exp2(nt(kk, qs[side]))
+                    if diagonal:
+                        weights = jnp.where(causal, weights, 0.0)
+                    dots = dots_ref[side, pl.ds(0, 1), :]
+                    grads = (weights * (nt(vv, gs[side]) - dots)).astype(jnp.bfloat16)
+                    dkv_ref[1, keys, :] += nn(weights.astype(jnp.bfloat16), gs[side])
+                    dkv_ref[0, keys, :] += nn(grads, qs[side])
+                    part = tn(grads, (ka_ref, kb_ref)[side][keys, :])
+                    if diagonal and side == 0:
+                        dq_ref[...] = part
+                    else:
+                        dq_ref[...] += part
+
+            step(i, True)
+
+            @pl.loop(0, i)
+            def _(j):
+                step(j, False)
+
+            low_q[i, :, lanes] = (dq_ref[...] * 0.125).astype(jnp.bfloat16)
+
+        @pl.when(i != wide)
+        def _():
+            send_q(i).start()
+
+        @pl.when(i == wide)
+        def _():
+            dq_out[i] = low_q[i]
+
+    def keys_back(j):
+        rows = pl.ds(pl.multiple_of(j * block, block), block)
+        keys = dkv_ref[0, rows, :] * (1.0 / LOG2E)
+        values = dkv_ref[1, rows, :]
+        keys = keys + jnp.concatenate([keys[:, 64:], keys[:, :64]], axis=1)
+        values = values + jnp.concatenate([values[:, 64:], values[:, :64]], axis=1)
+        low_kv[j] = jnp.where(low, keys, values).astype(jnp.bfloat16)
+
+        @pl.when(j != wide)
+        def _():
+            send_kv(j).start()
+
+        @pl.when(j == wide)
+        def _():
+            dkv_out[j] = low_kv[j]
+
+    own.wait()
+
+    @pl.loop(0, 4)
+    def _(k):
+        i = base + 3 - k
+
+        @pl.when(i != wide)
+        def _():
+            target = grad_ref.at[i]
+            remote(target, target, send_sem.at[i], got_sem.at[i], (narrow, i)).wait_recv()
+
+        rows_back(i)
+
+        @pl.when(base > 0)
+        def _():
+            keys_back(i)
+
+    @pl.loop(0, 4)
+    def _(k):
+        i = away + 3 - k
+        target = grad_ref.at[i]
+        remote(target, target, send_sem.at[i], got_sem.at[i], (narrow, i)).wait_recv()
+        rows_back(i)
+        keys_back(i)
+
+    @pl.when(base == 0)
+    def _():
+        @pl.loop(0, 4)
+        def _(k):
+            keys_back(3 - k)
+
+    for step in range(1, 8):
+        to = (wide + step) % 8
+        target = dq_out.at[to]
+        remote(target, target, q_send.at[to], q_got.at[to], (narrow, to)).wait_recv()
+        target = dkv_out.at[to]
+        remote(target, target, kv_send.at[to], kv_got.at[to], (narrow, to)).wait_recv()
+        send(to).wait_send()
+        send_q(to).wait_send()
+        send_kv(to).wait_send()
+
+
+def back_swap(packed, grad, attended, weight_sums, heads):
+    count, block, lanes = packed.shape
+    split = heads * 64
+    if lax.axis_size("narrow") != 4 or lax.axis_size("wide") != 8:
+        head_grad = swap(grad).reshape(-1, split).astype(jnp.float32) / weight_sums
+        dots = jnp.sum((head_grad * attended).reshape(-1, heads, 64), axis=-1).T
+        result = attend_back(
+            packed.reshape(-1, lanes), head_grad.astype(jnp.bfloat16), dots, heads
+        )
+        result = swap(result.reshape(packed.shape))
+        return result[:, :, :split], result[:, :, split:]
+    total = count * block
+    dma = pltpu.SemaphoreType.DMA
+    vmem = pltpu.VMEM
+    low = jnp.bfloat16
+    cost = heads * total * total // 2
+    return pl.pallas_call(
+        functools.partial(back_swap_kernel, heads),
+        out_shape=[
+            jax.ShapeDtypeStruct((count, block, split), low),
+            jax.ShapeDtypeStruct((count, block, 128), low),
+        ],
+        in_specs=[
+            pl.BlockSpec(memory_space=vmem),
+            pl.BlockSpec(memory_space=pl.ANY),
+            pl.BlockSpec(memory_space=vmem),
+            pl.BlockSpec(memory_space=vmem),
+        ],
+        out_specs=[pl.BlockSpec(memory_space=vmem)] * 2,
+        scratch_shapes=[
+            vmem((count, block, split), low),
+            vmem((block, 128), low),
+            vmem((2, 8, block), jnp.float32),
+            vmem((block, 128), jnp.float32),
+            vmem((2, total, 128), jnp.float32),
+        ]
+        + [vmem((total, 128), low)] * 4
+        + [
+            vmem((count, block, split), low),
+            vmem((count, block, 128), low),
+            dma, dma((8,)), dma((8,)), dma((8,)), dma((8,)), dma((8,)), dma((8,)),
+        ],
+        compiler_params=pltpu.CompilerParams(
+            collective_id=5, has_side_effects=True, vmem_limit_bytes=52 << 20
+        ),
+        cost_estimate=pl.CostEstimate(
+            flops=12 * cost * 256, bytes_accessed=12 * packed.size, transcendentals=cost
+        ),
+        name="back_swap",
+    )(packed, grad, attended, weight_sums)
 
 
 def shards(
@@ -824,10 +1218,7 @@
     )
     packed = jnp.concatenate([query_rot, key_rot.astype(jnp.bfloat16), value_rows], axis=2)
     packed, grad_halves = lax.optimization_barrier((packed, grad_halves))
-    packed = swap(packed)
-    packed = packed.reshape(wide_count * shard_rows, group_columns)
-    attended, weight_sums, attended_low = attend(packed, local_heads)
-    attended_low = swap(attended_low.reshape(wide_count, shard_rows, query_columns))
+    packed, attended, weight_sums, attended_low = attend_swap(packed, local_heads)
     attended_low, gate_local, up_local, down_local = lax.optimization_barrier(
         (attended_low, gate_local, up_local, down_local)
     )
@@ -839,8 +1230,9 @@
     block_parts = []
     mid_sums = []
     rows_halves = [gather_rows(mid_low[:half_rows]), gather_rows(mid_low[half_rows:])]
-    for rows_mid, grad_rows in zip(rows_halves, grad_halves):
-        hidden_grad = dot_back(grad_rows, down_local).astype(jnp.bfloat16)
+    hidden_grads = [dot_back(rows, down_local).astype(jnp.bfloat16) for rows in grad_halves]
+    rows_halves[0], hidden_grads = lax.optimization_barrier((rows_halves[0], hidden_grads))
+    for rows_mid, grad_rows, hidden_grad in zip(rows_halves, grad_halves, hidden_grads):
         gate_pre = dot_last(rows_mid, gate_local)
         up_pre = dot_last(rows_mid, up_local)
         hidden, hidden_back = jax.vjp(
@@ -873,34 +1265,32 @@
     )
     attended_grad, down_wgrad = lax.optimization_barrier((attended_grad, down_wgrad))
     down_total = lax.psum_scatter(down_wgrad, "narrow", scatter_dimension=1, tiled=True)
-    head_grad = swap(attended_grad).reshape(wide_count * shard_rows, query_columns)
-    head_grad, down_total, first_part, gate_wgrad = lax.optimization_barrier(
-        (head_grad, down_total, block_parts[0], gate_wgrad)
+    attended_grad, first_part, gate_wgrad = lax.optimization_barrier(
+        (attended_grad, block_parts[0], gate_wgrad)
     )
     first_sum = lax.psum_scatter(first_part, "wide", scatter_dimension=0, tiled=True)
     gate_total = lax.psum_scatter(gate_wgrad, "narrow", scatter_dimension=0, tiled=True)
-    head_grad = head_grad.astype(jnp.float32) / weight_sums
-    scaled_grad = head_grad.astype(jnp.bfloat16)
-    grad_dot = jnp.sum((head_grad * attended).reshape(-1, local_heads, head_dim), axis=-1).T
-    packed_grad = attend_back(packed, scaled_grad, grad_dot, local_heads)
-    packed_grad, up_wgrad, first_sum = lax.optimization_barrier((packed_grad, up_wgrad, first_sum))
+    query_rot_grad, key_value_grad = back_swap(
+        packed, attended_grad, attended, weight_sums, local_heads
+    )
+    query_rot_grad, first_sum, gate_total, down_total, up_wgrad, second_part = (
+        lax.optimization_barrier(
+            (query_rot_grad, first_sum, gate_total, down_total, up_wgrad, block_parts[1])
+        )
+    )
     up_total = lax.psum_scatter(up_wgrad, "narrow", scatter_dimension=0, tiled=True)
-    packed_grad = swap(packed_grad.reshape(wide_count, shard_rows, group_columns))
-    packed_grad, gate_total, second_part = lax.optimization_barrier(
-        (packed_grad, gate_total, block_parts[1])
-    )
     second_sum = lax.psum_scatter(second_part, "wide", scatter_dimension=0, tiled=True)
-    query_rot_grad = packed_grad[:, :, :query_columns].astype(jnp.float32).reshape(
+    query_rot_grad = query_rot_grad.astype(jnp.float32).reshape(
         wide_count, shard_rows, local_heads, head_dim
     )
-    key_rot_grad = packed_grad[:, :, query_columns : query_columns + head_dim]
+    key_rot_grad = key_value_grad[:, :, :head_dim]
     query_raw_grad, query_gain_grad = query_back(query_rot_grad)
     key_raw_grad, key_gain_grad = key_back(key_rot_grad.astype(jnp.float32))
     input_low = jnp.concatenate(
         [
             query_raw_grad.reshape(wide_count, shard_rows, query_columns).astype(jnp.bfloat16),
             key_raw_grad.astype(jnp.bfloat16),
-            packed_grad[:, :, query_columns + head_dim :],
+            key_value_grad[:, :, head_dim:],
         ],
         axis=2,
     )

time: 1290 us -> 1270 us (0.984)
  Pallas kernels: 438 us -> 623 us
  waiting for transfers between devices: 269 us -> 144 us
  blocking collectives: 52.6 us -> 0 us
    all_to_all x3 -> x0, waiting for transfers between devices: 175 us -> none  [swap(): return lax.all_to_all(blocks, 'wide', 0, 0)]
    pallas_call x2, Pallas kernels: 181 us -> 338 us  [the longest x1 239 us: back_swap(): pl.pallas_call(functools.partial(back_swap_kernel, heads), out_shape=[jax...]
    all_to_all x1 -> x0, blocking collectives: 52.6 us -> none  [swap(): return lax.all_to_all(blocks, 'wide', 0, 0)]
    all_gather x1, waiting for transfers between devices: 15.7 us -> 54.9 us  [shards(): down_local = lax.all_gather(down_own, 'narrow', axis=1, tiled=True)]
    pallas_call x1, Pallas kernels: 110 us -> 135 us  [sum_weights(): pl.pallas_call(scatter_kernel, out_shape=[jax.ShapeDtypeStruct((rows, col...]
    unnamed x207 -> x223, local copies, waits for them, and re-layouts: 50.7 us -> 45.1 us
  transfers between devices with their start and end apart: 17 -> 14, of which waited for: 8 -> 5; matrix products, arithmetic and copies ran while one was open for 34% -> 34% of each run, Pallas kernels for 34% -> 49%
where the time goes in v6:
time: 1270 us
  Pallas kernels  623 us (49%)
  matrix products  333 us (26%)
  waiting for transfers between devices  144 us (11%)
  other arithmetic  78.4 us (6%)
  local copies, waits for them, and re-layouts  72.5 us (6%)
  between operations  15.3 us (1%)
    pallas_call x1, Pallas kernels, back_swap(): pl.pallas_call(functools.partial(back_swap_kernel, heads), out_shape=[jax...  239 us
    pallas_call x1, Pallas kernels, gather_weights(): pl.pallas_call(gather_kernel, out_shape=jax.ShapeDtypeStruct((8, 4 * att....  150 us
    pallas_call x1, Pallas kernels, sum_weights(): pl.pallas_call(scatter_kernel, out_shape=[jax.ShapeDtypeStruct((rows, col...  135 us
    pallas_call x1, Pallas kernels, attend_swap(): pl.pallas_call(functools.partial(attend_swap_kernel, heads), out_shape=[j...  99.8 us
    dot_general x6, matrix products, dot_back(): lax.dot_general(left, right, (((1,), (1,)), ((), ())), preferred_element_...  92.6 us
    dot_general x6, matrix products, dot_last(): return jnp.dot(left, right, preferred_element_type=jnp.float32)  90.8 us
    dot_general x6, matrix products, dot_first(): lax.dot_general(left, right, (((0,), (0,)), ((), ())), preferred_element_...  89 us
    all_gather x2, waiting for transfers between devices, gather_rows(): return lax.all_gather(shard, 'wide', axis=0, tiled=True)  72.8 us
  transfers between devices with their start and end apart: 14, of which 5 were waited for; matrix products, arithmetic and copies ran while one was open for 34% of the time, Pallas kernels for 49%

profile of v6, /device:TPU:0, one launch (start us, length us, event | category | flops | bytes accessed | tf_op | source)
XLA Modules:
  0.0 1266.9 jit_solution(8082893030038496772)
XLA Ops:
  19.0 149.5 %gather_weights.1 = bf16[8,2048,640]{2,1,0:T(8,128)(2,1)} custom-call(bf16[512,640]{1,0:T(8,128)(2,1)} %pad_maximum_fusion.4.att_ref), custom_call_target="tpu_custom_call" | custom-call | bytes 314572800 | tf_op jit(solution)/shard_map/gather_weights/pallas_call | solution.py:406
  171.2 9.6 fusion.30
  209.0 99.8 %attend_swap.1 = (bf16[8,512,384]{2,1,0:T(8,128)(2,1)}, f32[4096,256]{1,0:T(8,128)}, f32[4096,256]{1,0:T(8,128)}, bf16[8,512,256]{2,1,0:T(8,128)(2,1)}) custom-call(bf16[8,512,384]{2,1,0:T(8,128)(2,1)} %pad_maximum_fusion.src_ref), custom_call_target="tpu_custom_call" | custom-call | flops 68719476736 | bytes 18874368 | tf_op jit(solution)/shard_map/attend_swap/pallas_call | solution.py:885
  314.9 54.9 %all-gather.16.cloned.1.call-done = bf16[1024,2048]{1,0:T(8,128)(2,1)} async-done(((bf16[1024,512]{1,0:T(8,128)(2,1)}), bf16[1024,2048]{1,0:T(8,128)(2,1)}) %all-gather.16.cloned.1.call-update) | async-done | bytes 4194320 | tf_op jit(solution)/shard_map/all_gather | solution.py:1184
  369.8 7.8 multiply_reduce_fusion.4
  381.0 15.3 %convolution_convert_fusion.2 = bf16[2048,1024]{1,0:T(8,128)(2,1)} fusion(bf16[2048,2048]{1,0:T(8,128)(2,1)} %all-gather.10.cloned.1.call-done, bf16[1024,2048]{1,0:T(8,128)(2,1)} %all-gather.16.cloned.1.call-done), kind=kOutput, calls=%fused_computation.67 | convolution fusion | flops 8592031744 | bytes 16777216 | tf_op jit(solution)/shard_map/dot_general | solution.py:67
  396.3 12.6 convolution_convert_fusion.3
  408.9 53.5 %all-gather.18.cloned.1.call-done = bf16[2048,2048]{1,0:T(8,128)(2,1)} async-done(((bf16[256,2048]{1,0:T(8,128)(2,1)}), bf16[2048,2048]{1,0:T(8,128)(2,1)}) %all-gather.18.cloned.1.call-update) | async-done | bytes 8388624 | tf_op jit(solution)/shard_map/all_gather | solution.py:421
  462.4 14.7 %fusion.87 = f32[2048,1024]{1,0:T(8,128)} fusion(bf16[2048,2048]{1,0:T(8,128)(2,1)} %all-gather.18.cloned.1.call-done, bf16[2048,1024]{1,0:T(8,128)(2,1)} %all-gather.12.cloned.1.call-done), kind=kOutput, calls=%fused_computation.169 | convolution fusion | flops 8589934592 | bytes 20971520 | tf_op jit(solution)/shard_map/dot_general | solution.py:57
  477.1 18.6 %multiply_convert_fusion.1 = (bf16[2048,1024]{1,0:T(8,128)(2,1)}, bf16[2048,1024]{1,0:T(8,128)(2,1)}, bf16[2048,1024]{1,0:T(8,128)(2,1)}) fusion(f32[2048,1024]{1,0:T(8,128)} %fusion.87, bf16[2048,1024]{1,0:T(8,128)(2,1)} %convolution_convert_fusion.3, bf16[2048,2048]{1,0:T(8,128)(2,1)S(1)} %copy-done.91, bf16[2048,1024]{1,0:T(8,128)(2,1)} %all-gather.14.cloned.1.call-done), kind=kOutput, calls=%fused_computation.24 | convolution fusion | flops 8625586176 | bytes 37748736 | tf_op jit(solution)/shard_map/dot_general | solution.py:57
  495.7 14.1 %fusion.88 = f32[2048,2048]{1,0:T(8,128)} fusion(bf16[2048,1024]{1,0:T(8,128)(2,1)} %get-tuple-element.244, bf16[2048,1024]{1,0:T(8,128)(2,1)S(1)} %copy-done.94), kind=kOutput, calls=%fused_computation.170 | convolution fusion | flops 8589934592 | bytes 25165824 | tf_op jit(solution)/shard_map/dot_general | solution.py:67
  509.8 16.1 %add_convert_fusion.1 = bf16[2048,2048]{1,0:T(8,128)(2,1)} fusion(f32[2048,2048]{1,0:T(8,128)} %fusion.88, bf16[2048,1024]{1,0:T(8,128)(2,1)} %get-tuple-element.245, bf16[2048,1024]{1,0:T(8,128)(2,1)S(1)} %copy-done.96), kind=kOutput, calls=%fused_computation.1 | convolution fusion | flops 8598323200 | bytes 33554432 | tf_op jit(solution)/shard_map/dot_general | solution.py:67
  525.9 19.3 %all-gather.20.cloned.1.call-done = bf16[2048,2048]{1,0:T(8,128)(2,1)} async-done(((bf16[256,2048]{1,0:T(8,128)(2,1)}), bf16[2048,2048]{1,0:T(8,128)(2,1)}) %all-gather.20.cloned.1.call-update) | async-done | bytes 8388624 | tf_op jit(solution)/shard_map/all_gather | solution.py:421
  545.2 15.0 %fusion.89 = f32[2048,1024]{1,0:T(8,128)} fusion(bf16[2048,2048]{1,0:T(8,128)(2,1)} %all-gather.20.cloned.1.call-done, bf16[2048,1024]{1,0:T(8,128)(2,1)} %all-gather.12.cloned.1.call-done), kind=kOutput, calls=%fused_computation.171 | convolution fusion | flops 8589934592 | bytes 20971520 | tf_op jit(solution)/shard_map/dot_general | solution.py:57
  560.3 17.3 %multiply_convert_fusion = (bf16[2048,1024]{1,0:T(8,128)(2,1)}, bf16[2048,1024]{1,0:T(8,128)(2,1)}) fusion(f32[2048,1024]{1,0:T(8,128)} %fusion.89, bf16[2048,1024]{1,0:T(8,128)(2,1)} %convolution_convert_fusion.2, bf16[2048,2048]{1,0:T(8,128)(2,1)S(1)} %copy-done.90, bf16[2048,1024]{1,0:T(8,128)(2,1)} %all-gather.14.cloned.1.call-done), kind=kOutput, calls=%fused_computation.23 | convolution fusion | flops 8621391872 | bytes 33554432 | tf_op jit(solution)/shard_map/dot_general | solution.py:57
  577.6 14.1 %fusion.90 = f32[2048,2048]{1,0:T(8,128)} fusion(bf16[2048,1024]{1,0:T(8,128)(2,1)} %get-tuple-element.242, bf16[2048,1024]{1,0:T(8,128)(2,1)S(1)} %copy-done.95), kind=kOutput, calls=%fused_computation.172 | convolution fusion | flops 8589934592 | bytes 25165824 | tf_op jit(solution)/shard_map/dot_general | solution.py:67
  591.7 20.5 %add_convert_fusion = bf16[2048,2048]{1,0:T(8,128)(2,1)} fusion(f32[2048,2048]{1,0:T(8,128)} %fusion.90, bf16[2048,1024]{1,0:T(8,128)(2,1)} %all-gather.14.cloned.1.call-done, bf16[2048,1024]{1,0:T(8,128)(2,1)} %convolution_convert_fusion.2, f32[2048,1024]{1,0:T(8,128)} %fusion.89), kind=kOutput, calls=%fused_computation | convolution fusion | flops 8613003264 | bytes 41943040 | tf_op jit(solution)/shard_map/dot_general | solution.py:67
  612.3 15.0 %fusion.91 = f32[2048,1024]{1,0:T(8,128)} fusion(bf16[2048,2048]{1,0:T(8,128)(2,1)} %all-gather.18.cloned.1.call-done, bf16[2048,1024]{1,0:T(8,128)(2,1)} %get-tuple-element.244), kind=kOutput, calls=%fused_computation.173 | convolution fusion | flops 8589934592 | bytes 20971520 | tf_op jit(solution)/shard_map/dot_general | solution.py:61
  627.3 13.7 %fusion.92 = f32[2048,1024]{1,0:T(8,128)} fusion(bf16[2048,2048]{1,0:T(8,128)(2,1)} %all-gather.18.cloned.1.call-done, bf16[2048,1024]{1,0:T(8,128)(2,1)S(1)} %copy-done.99), kind=kOutput, calls=%fused_computation.174 | convolution fusion | flops 8589934592 | bytes 20971520 | tf_op jit(solution)/shard_map/dot_general | solution.py:61
  641.0 10.9 convolution_convert_fusion.1
  651.9 14.2 %convolution_convert_fusion = bf16[2048,2048]{1,0:T(8,128)(2,1)} fusion(bf16[2048,1024]{1,0:T(8,128)(2,1)} %get-tuple-element.241, bf16[1024,2048]{1,0:T(8,128)(2,1)} %all-gather.16.cloned.1.call-done), kind=kOutput, calls=%fused_computation.36 | convolution fusion | flops 8594128896 | bytes 16777216 | tf_op jit(solution)/shard_map/dot_general | solution.py:57
  666.1 12.8 %fusion.93 = f32[1024,2048]{1,0:T(8,128)S(1)} fusion(bf16[2048,1024]{1,0:T(8,128)(2,1)} %get-tuple-element.243, bf16[2048,2048]{1,0:T(8,128)(2,1)} %all-gather.8.cloned.1.call-done), kind=kOutput, calls=%fused_computation.175 | convolution fusion | flops 8589934592 | bytes 20971520 | tf_op jit(solution)/shard_map/dot_general | solution.py:61
  679.0 13.3 %add_convert_fusion.2 = bf16[1024,2048]{1,0:T(8,128)(2,1)} fusion(f32[1024,2048]{1,0:T(8,128)S(1)} %fusion.93, bf16[2048,1024]{1,0:T(8,128)(2,1)S(1)} %copy-done.97, bf16[2048,2048]{1,0:T(8,128)(2,1)} %all-gather.10.cloned.1.call-done), kind=kOutput, calls=%fused_computation.22 | convolution fusion | flops 8594128896 | bytes 25165824 | tf_op jit(solution)/shard_map/dot_general | solution.py:61
  692.3 15.3 %add_convert_fusion.4 = bf16[2048,1024]{1,0:T(8,128)(2,1)} fusion(f32[2048,1024]{1,0:T(8,128)} %fusion.91, bf16[2048,2048]{1,0:T(8,128)(2,1)} %all-gather.20.cloned.1.call-done, bf16[2048,1024]{1,0:T(8,128)(2,1)} %get-tuple-element.242), kind=kOutput, calls=%fused_computation.26 | convolution fusion | flops 8594128896 | bytes 25165824 | tf_op jit(solution)/shard_map/dot_general | solution.py:61
  707.6 18.8 %add_convert_fusion.3 = bf16[2048,1024]{1,0:T(8,128)(2,1)} fusion(f32[2048,1024]{1,0:T(8,128)} %fusion.92, bf16[2048,2048]{1,0:T(8,128)(2,1)} %all-gather.20.cloned.1.call-done, bf16[2048,1024]{1,0:T(8,128)(2,1)} %convolution_convert_fusion.2, f32[2048,1024]{1,0:T(8,128)} %fusion.89), kind=kOutput, calls=%fused_computation.25 | convolution fusion | flops 8608808960 | bytes 33554432 | tf_op jit(solution)/shard_map/dot_general | solution.py:61
  736.2 9.0 convert_bitcast_fusion.2.g_ref
  746.6 238.7 %back_swap.1 = (bf16[8,512,256]{2,1,0:T(8,128)(2,1)}, bf16[8,512,128]{2,1,0:T(8,128)(2,1)S(1)}) custom-call(bf16[8,512,384]{2,1,0:T(8,128)(2,1)} %get-tuple-element.81.packed_ref, bf16[8,512,256]{2,1,0:T(8,128)(2,1)} %convert_bitcast_fusion.2.g_ref, f32[4096,256]{1,0:T(8,128)} %get-tuple-element.97.o_ref, f32[4096,256]{1,0:T(8,128)} %get-tuple-element.98.s_ref), custom_call_target="tpu_custom_call" | custom-call | flops 103079215104 | bytes 18874368 | tf_op jit(solution)/shard_map/back_swap/pallas_call | solution.py:1088
  1020.9 10.8 convert_bitcast_fusion.1.out_ref
  1042.4 14.1 %fusion.26 = (f32[512]{0:T(512)S(1)}, f32[2048]{0:T(1024)S(1)}, f32[512,2048,1]{1,0,2:T(8,128)}) fusion(bf16[512,2048]{1,0:T(8,128)(2,1)S(1)} %copy-done.16, f32[2048]{0:T(1024)S(1)} %bitcast.124, f32[512]{0:T(512)S(1)} %copy-done.83, bf16[8,2048,640]{2,1,0:T(8,128)(2,1)} %gather_weights.1, bf16[8,512,64]{1,2,0:T(8,128)(2,1)S(1)} %copy-done.56, ...), kind=kOutput, calls=%fused_computation.53 | convolution fusion | flops 6459225600 | bytes 22040576 | tf_op jit(solution)/shard_map/gtc,gdc->td/dot_general | solution.py:1300
  1072.9 9.7 convert_bitcast_fusion.in_ref
  1082.6 134.7 %sum_weights.1 = (f32[512,640]{1,0:T(8,128)}, bf16[8,512,128]{2,1,0:T(8,128)(2,1)S(1)}, f32[40,128]{1,0:T(8,128)S(1)}) custom-call(bf16[8,2048,384]{2,1,0:T(8,128)(2,1)} %convert_bitcast_fusion.in_ref, bf16[8,2048,256]{2,1,0:T(8,128)(2,1)} %convert_bitcast_fusion.1.out_ref, f32[40,128]{1,0:T(8,128)S(1)} %pad_bitcast_fusion.gain_ref), custom_call_target="tpu_custom_call" | custom-call | bytes 314572800 | tf_op jit(solution)/shard_map/sum_weights/pallas_call | solution.py:693
  1241.4 6.6 multiply_subtract_fusion.1
  (332 shorter events, 161.3 us)
Async XLA Ops:
  7.2 201.8 %all-gather.10.cloned.1.call-start = ((), (), s32[]{:S(2)}) async-start(), calls=%async_computation.8 | async-start | bytes 9437184 | tf_op jit(solution)/shard_map/all_gather | solution.py:1172
  10.6 198.5 %all-gather.8.cloned.1.call-start = ((), (), s32[]{:S(2)}) async-start(), calls=%async_computation.7 | async-start | bytes 9437184 | tf_op jit(solution)/shard_map/all_gather | solution.py:1171
  11.3 297.5 %all-gather.12.cloned.1.call-start = ((), (), s32[]{:S(2)}) async-start(), calls=%async_computation.9 | async-start | bytes 5242880 | tf_op jit(solution)/shard_map/all_gather | solution.py:1182
  168.6 146.3 %all-gather.14.cloned.1.call-start = ((), (), s32[]{:S(2)}) async-start(), calls=%async_computation.10 | async-start | bytes 5242880 | tf_op jit(solution)/shard_map/all_gather | solution.py:1183
  169.2 200.6 %all-gather.16.cloned.1.call-start = ((), (), s32[]{:S(2)}) async-start(), calls=%async_computation.11 | async-start | bytes 5242880 | tf_op jit(solution)/shard_map/all_gather | solution.py:1184
  169.8 292.7 %all-gather.18.cloned.1.call-start = ((), (), s32[]{:S(2)}) async-start(), calls=%async_computation.12 | async-start | bytes 9437184 | tf_op jit(solution)/shard_map/all_gather | solution.py:421
  170.7 206.9 %copy-start.65 = (f32[1,2048]{1,0:T(1,128)}, f32[1,2048]{1,0:T(1,128)S(1)}, u32[]{:S(2)}) copy-start(f32[1,2048]{1,0:T(1,128)S(1)} %get-tuple-element.262) | copy-start | bytes 24580
  185.9 16.2 %copy-start.84 = (f32[64]{0:T(128)}, f32[64]{0:T(128)S(1)}, u32[]{:S(2)}) copy-start(f32[64]{0:T(128)S(1)} %get-tuple-element.267) | copy-start | bytes 772
  187.2 17.0 %copy-start.28 = (f32[512,32]{1,0:T(8,128)}, f32[512,32]{1,0:T(8,128)S(1)}, u32[]{:S(2)}) copy-start(f32[512,32]{1,0:T(8,128)S(1)} %copy.122) | copy-start | bytes 196612
  188.0 14.1 %copy-start.61 = (f32[8,512]{1,0:T(8,128)}, f32[8,512]{1,0:T(8,128)S(1)}, u32[]{:S(2)}) copy-start(f32[8,512]{1,0:T(8,128)S(1)} %fusion.60) | copy-start | bytes 49156
  209.0 160.7 %copy-start.15 = (bf16[512,2048]{1,0:T(8,128)(2,1)S(1)}, bf16[512,2048]{1,0:T(8,128)(2,1)}, u32[]{:S(2)}) copy-start(bf16[512,2048]{1,0:T(8,128)(2,1)} %param.30) | copy-start | bytes 6291460
  380.2 165.0 %all-gather.20.cloned.1.call-start = ((), (), s32[]{:S(2)}) async-start(), calls=%async_computation.14 | async-start | bytes 9437184 | tf_op jit(solution)/shard_map/all_gather | solution.py:421
  381.0 345.4 %reduce-scatter.8.cloned.1.call-start = ((), (), s32[]{:S(2)}) async-start(), calls=%async_computation.13 | async-start | bytes 9437184 | tf_op jit(solution)/shard_map/reduce_scatter | solution.py:432
  381.0 15.3 %copy-start.92 = (bf16[1024,2048]{1,0:T(8,128)(2,1)S(1)}, bf16[1024,2048]{1,0:T(8,128)(2,1)}, u32[]{:S(2)}) copy-start(bf16[1024,2048]{1,0:T(8,128)(2,1)} %all-gather.16.cloned.1.call-done) | copy-start | bytes 12582916
  462.4 14.7 %copy-start.91 = (bf16[2048,2048]{1,0:T(8,128)(2,1)S(1)}, bf16[2048,2048]{1,0:T(8,128)(2,1)}, u32[]{:S(2)}) copy-start(bf16[2048,2048]{1,0:T(8,128)(2,1)} %all-gather.18.cloned.1.call-done) | copy-start | bytes 25165828
  477.1 18.6 %copy-start.94 = (bf16[2048,1024]{1,0:T(8,128)(2,1)S(1)}, bf16[2048,1024]{1,0:T(8,128)(2,1)}, u32[]{:S(2)}) copy-start(bf16[2048,1024]{1,0:T(8,128)(2,1)} %all-gather.12.cloned.1.call-done) | copy-start | bytes 12582916
  495.7 14.1 %copy-start.96 = (bf16[2048,1024]{1,0:T(8,128)(2,1)S(1)}, bf16[2048,1024]{1,0:T(8,128)(2,1)}, u32[]{:S(2)}) copy-start(bf16[2048,1024]{1,0:T(8,128)(2,1)} %all-gather.14.cloned.1.call-done) | copy-start | bytes 12582916
  525.9 202.0 %reduce-scatter.10.cloned.1.call-start = ((), (), s32[]{:S(2)}) async-start(), calls=%async_computation.15 | async-start | bytes 9437184 | tf_op jit(solution)/shard_map/reduce_scatter | solution.py:432
  545.2 15.0 %copy-start.90 = (bf16[2048,2048]{1,0:T(8,128)(2,1)S(1)}, bf16[2048,2048]{1,0:T(8,128)(2,1)}, u32[]{:S(2)}) copy-start(bf16[2048,2048]{1,0:T(8,128)(2,1)} %all-gather.20.cloned.1.call-done) | copy-start | bytes 25165828
  560.3 17.3 %copy-start.95 = (bf16[2048,1024]{1,0:T(8,128)(2,1)S(1)}, bf16[2048,1024]{1,0:T(8,128)(2,1)}, u32[]{:S(2)}) copy-start(bf16[2048,1024]{1,0:T(8,128)(2,1)} %all-gather.12.cloned.1.call-done) | copy-start | bytes 12582916
  612.2 373.1 %reduce-scatter.14.cloned.1.call-start = ((), (), s32[]{:S(2)}) async-start(), calls=%async_computation.17 | async-start | bytes 5242880 | tf_op jit(solution)/shard_map/reduce_scatter | solution.py:1272
  612.3 15.0 %copy-start.99 = (bf16[2048,1024]{1,0:T(8,128)(2,1)S(1)}, bf16[2048,1024]{1,0:T(8,128)(2,1)}, u32[]{:S(2)}) copy-start(bf16[2048,1024]{1,0:T(8,128)(2,1)} %get-tuple-element.245) | copy-start | bytes 12582916
  627.3 13.7 %copy-start.98 = (bf16[2048,1024]{1,0:T(8,128)(2,1)S(1)}, bf16[2048,1024]{1,0:T(8,128)(2,1)}, u32[]{:S(2)}) copy-start(bf16[2048,1024]{1,0:T(8,128)(2,1)} %get-tuple-element.243) | copy-start | bytes 12582916
  745.3 240.1 %reduce-scatter.16.cloned.1.call-start = ((), (), s32[]{:S(2)}) async-start(), calls=%async_computation.18 | async-start | bytes 5242880 | tf_op jit(solution)/shard_map/reduce_scatter | solution.py:1267
  746.0 245.3 %reduce-scatter.12.cloned.1.call-start = ((), (), s32[]{:S(2)}) async-start(), calls=%async_computation.16 | async-start | bytes 9437184 | tf_op jit(solution)/shard_map/reduce_scatter | solution.py:1271
  746.6 336.0 %reduce-scatter.18.cloned.1.call-start = ((), (), s32[]{:S(2)}) async-start(), calls=%async_computation.19 | async-start | bytes 5242880 | tf_op jit(solution)/shard_map/reduce_scatter | solution.py:1281
  991.4 256.7 %reduce-scatter.20.cloned.1.call-start = ((), (), s32[]{:S(2)}) async-start(), calls=%async_computation.20 | async-start | bytes 9437184 | tf_op jit(solution)/shard_map/reduce_scatter | solution.py:1282
  1041.6 14.9 %copy-start.37 = (bf16[8,512,4,64]{1,3,2,0:T(8,128)(2,1)}, bf16[8,512,4,64]{1,3,2,0:T(8,128)(2,1)S(1)}, u32[]{:S(2)}) copy-start(bf16[8,512,4,64]{1,3,2,0:T(8,128)(2,1)S(1)} %fusion.23) | copy-start | bytes 6291460
  1042.3 14.2 %copy-start.71 = (f32[2048]{0:T(1024)S(1)}, f32[2048]{0:T(1024)}, u32[]{:S(2)}) copy-start(f32[2048]{0:T(1024)} %get-tuple-element.208) | copy-start | bytes 24580
  1042.3 14.3 %copy-start.75 = (f32[512]{0:T(512)S(1)}, f32[512]{0:T(512)}, u32[]{:S(2)}) copy-start(f32[512]{0:T(512)} %copy-done.74) | copy-start | bytes 6148
  1042.3 14.3 %copy-start.8 = (f32[512,1024]{1,0:T(8,128)S(1)}, f32[512,1024]{1,0:T(8,128)}, u32[]{:S(2)}) copy-start(f32[512,1024]{1,0:T(8,128)} %param.45) | copy-start | bytes 6291460
  1042.4 14.3 %copy-start.50 = (bf16[512,1024]{1,0:T(8,128)(2,1)S(1)}, bf16[512,1024]{1,0:T(8,128)(2,1)}, u32[]{:S(2)}) copy-start(bf16[512,1024]{1,0:T(8,128)(2,1)} %reduce-scatter.14.cloned.1.call-done) | copy-start | bytes 3145732
  (84 other events, 407.9 us)
Sparse Core Ops, SparseCore 0:
  10.7 111.8 all-gather.9
  124.7 81.2 all-gather.7
  208.5 51.2 all-gather.11
  262.0 52.8 all-gather.13
  317.2 52.5 all-gather.15
  380.3 82.0 all-gather.17
  464.6 80.5 all-gather.19
  547.5 88.1 reduce-scatter.7
  638.0 87.9 reduce-scatter.9
  745.4 51.2 reduce-scatter.13
  800.0 52.6 reduce-scatter.15
  854.8 136.4 reduce-scatter.11
  994.3 61.0 reduce-scatter.17
  1057.7 106.2 reduce-scatter.19

commit v7 on v6

--- a/solution.py
+++ b/solution.py
@@ -727,6 +727,23 @@
     return total, spread, flat.reshape(-1)[:size].reshape(gains.shape)
 
 
+def tell_all():
+    narrow = lax.axis_index("narrow")
+    wide = lax.axis_index("wide")
+    barrier = pltpu.get_barrier_semaphore()
+    for step in range(1, 8):
+        pl.semaphore_signal(
+            barrier, inc=1, device_id=(narrow, (wide + step) % 8),
+            device_id_type=pl.DeviceIdType.MESH,
+        )
+    for step in range(1, 4):
+        pl.semaphore_signal(
+            barrier, inc=1, device_id=((narrow + step) % 4, wide),
+            device_id_type=pl.DeviceIdType.MESH,
+        )
+    pl.semaphore_wait(barrier, 10)
+
+
 def tell_wide():
     narrow = lax.axis_index("narrow")
     wide = lax.axis_index("wide")
@@ -740,15 +757,34 @@
 
 
 def attend_swap_kernel(
-    heads, src_ref, packed_ref, o_ref, s_ref, out_ref, kk_ref, va_ref, vb_ref, acc_ref, low_ref,
-    own_sem, send_sem, got_sem, out_send, out_got,
+    heads, src_ref, up_ref, down_ref, packed_ref, o_ref, s_ref, out_ref, up_all, down_all,
+    kk_ref, va_ref, vb_ref, acc_ref, low_ref,
+    own_sem, send_sem, got_sem, out_send, out_got, ffn_own, ffn_send, ffn_got,
 ):
     narrow, wide, chip, core = place()
     block = src_ref.shape[1]
     base = 4 * (chip // 2)
     away = 4 - base
     low = low_lanes(block)
-    tell_wide()
+    columns = down_ref.shape[1]
+    tell_all()
+
+    def ffn_slot(k, who):
+        if k:
+            return down_all.at[:, pl.ds(pl.multiple_of(who * columns, columns), columns)]
+        return up_all.at[who]
+
+    def ffn(k, step):
+        return remote(
+            (up_ref, down_ref)[k], ffn_slot(k, narrow), ffn_send.at[k, step],
+            ffn_got.at[k, step], ((narrow + step) % 4, wide),
+        )
+
+    def ffn_arrival(k, step):
+        target = ffn_slot(k, (narrow + 4 - step) % 4)
+        return remote(
+            target, target, ffn_send.at[k, step], ffn_got.at[k, step], ((narrow + step) % 4, wide)
+        )
 
     def send(to):
         return remote(
@@ -766,8 +802,16 @@
 
     own = pltpu.make_async_copy(src_ref.at[wide], packed_ref.at[wide], own_sem)
     own.start()
-    for step in (1, 2, 3, 4, 5, 6, 7):
+    for step in range(1, 8):
         send((wide + step) % 8).start()
+    keep = [
+        pltpu.make_async_copy((up_ref, down_ref)[k], ffn_slot(k, narrow), ffn_own.at[k])
+        for k in range(2)
+    ]
+    for k in (1, 0):
+        keep[k].start()
+        for step in range(1, 4):
+            ffn(k, step).start()
 
     def prepare(j):
         rows = pl.ds(pl.multiple_of(j * block, block), block)
@@ -869,34 +913,44 @@
         remote(target, target, out_send.at[to], out_got.at[to], (narrow, to)).wait_recv()
         send_out(to).wait_send()
         send(to).wait_send()
-
-
-def attend_swap(src, heads):
+    for k in range(2):
+        keep[k].wait()
+        for step in range(1, 4):
+            ffn_arrival(k, step).wait_recv()
+            ffn(k, step).wait_send()
+
+
+def attend_swap(src, up, down, heads):
     if lax.axis_size("narrow") != 4 or lax.axis_size("wide") != 8:
         packed = swap(src)
         flat = packed.reshape(-1, src.shape[2])
         attended, weight_sums, attended_low = attend(flat, heads)
-        return packed, attended, weight_sums, swap(attended_low.reshape(src.shape[0], -1, heads * 64))
+        attended_low = swap(attended_low.reshape(src.shape[0], -1, heads * 64))
+        up_all = lax.all_gather(up, "narrow", axis=0, tiled=True)
+        down_all = lax.all_gather(down, "narrow", axis=1, tiled=True)
+        return packed, attended, weight_sums, attended_low, up_all, down_all
     count, block, lanes = src.shape
     total = count * block
     dma = pltpu.SemaphoreType.DMA
     vmem = pltpu.VMEM
     cost = heads * total * total // 2
-    return pl.pallas_call(
+    *results, up_all, down_all = pl.pallas_call(
         functools.partial(attend_swap_kernel, heads),
         out_shape=[
             jax.ShapeDtypeStruct(src.shape, jnp.bfloat16),
             jax.ShapeDtypeStruct((total, heads * 64), jnp.float32),
             jax.ShapeDtypeStruct((total, heads * 64), jnp.float32),
             jax.ShapeDtypeStruct((count, block, heads * 64), jnp.bfloat16),
+            jax.ShapeDtypeStruct((4,) + up.shape, jnp.bfloat16),
+            jax.ShapeDtypeStruct((down.shape[0], 4 * down.shape[1]), jnp.bfloat16),
         ],
-        in_specs=[pl.BlockSpec(memory_space=pl.ANY)],
-        out_specs=[pl.BlockSpec(memory_space=vmem)] * 4,
+        in_specs=[pl.BlockSpec(memory_space=pl.ANY)] * 3,
+        out_specs=[pl.BlockSpec(memory_space=vmem)] * 4 + [pl.BlockSpec(memory_space=pl.ANY)] * 2,
         scratch_shapes=[vmem((total, 128), jnp.bfloat16)] * 3
         + [
             vmem((count, heads, block, 128), jnp.float32),
             vmem((count, block, heads * 64), jnp.bfloat16),
-            dma, dma((8,)), dma((8,)), dma((8,)), dma((8,)),
+            dma, dma((8,)), dma((8,)), dma((8,)), dma((8,)), dma((2,)), dma((2, 4)), dma((2, 4)),
         ],
         compiler_params=pltpu.CompilerParams(
             collective_id=4, has_side_effects=True, vmem_limit_bytes=52 << 20
@@ -905,7 +959,8 @@
             flops=8 * cost * 256, bytes_accessed=12 * src.size, transcendentals=cost
         ),
         name="attend_swap",
-    )(src)
+    )(src, up, down)
+    return *results, up_all.reshape(-1, up.shape[1]), down_all
 
 
 def back_swap_kernel(
@@ -1171,17 +1226,10 @@
         lax.all_gather(out_grad[:half_rows], "wide", axis=0, tiled=True),
         lax.all_gather(out_grad[half_rows:], "wide", axis=0, tiled=True),
     ]
-    att_full, gate_own, up_own, down_own = lax.optimization_barrier(
-        (
-            gather_weights(att_own.astype(jnp.bfloat16)),
-            gate_weight.astype(jnp.bfloat16),
-            up_weight.astype(jnp.bfloat16),
-            down_weight.astype(jnp.bfloat16),
-        )
+    att_full, gate_own = lax.optimization_barrier(
+        (gather_weights(att_own.astype(jnp.bfloat16)), gate_weight.astype(jnp.bfloat16))
     )
     gate_local = lax.all_gather(gate_own, "narrow", axis=0, tiled=True)
-    up_local = lax.all_gather(up_own, "narrow", axis=0, tiled=True)
-    down_local = lax.all_gather(down_own, "narrow", axis=1, tiled=True)
     group_columns = query_columns + 2 * head_dim
     input_full = att_full[:, :, :group_columns]
     output_full = att_full[:, :, group_columns:]
@@ -1217,10 +1265,12 @@
         .astype(jnp.bfloat16)
     )
     packed = jnp.concatenate([query_rot, key_rot.astype(jnp.bfloat16), value_rows], axis=2)
-    packed, grad_halves = lax.optimization_barrier((packed, grad_halves))
-    packed, attended, weight_sums, attended_low = attend_swap(packed, local_heads)
-    attended_low, gate_local, up_local, down_local = lax.optimization_barrier(
-        (attended_low, gate_local, up_local, down_local)
+    packed, grad_halves[0] = lax.optimization_barrier((packed, grad_halves[0]))
+    packed, attended, weight_sums, attended_low, up_local, down_local = attend_swap(
+        packed, up_weight.astype(jnp.bfloat16), down_weight.astype(jnp.bfloat16), local_heads
+    )
+    attended_low, gate_local, grad_halves[1] = lax.optimization_barrier(
+        (attended_low, gate_local, grad_halves[1])
     )
     branch = jnp.einsum("gth,gdh->td", attended_low, output_full, preferred_element_type=jnp.float32)
     middle = residual + branch
@@ -1265,20 +1315,20 @@
     )
     attended_grad, down_wgrad = lax.optimization_barrier((attended_grad, down_wgrad))
     down_total = lax.psum_scatter(down_wgrad, "narrow", scatter_dimension=1, tiled=True)
-    attended_grad, first_part, gate_wgrad = lax.optimization_barrier(
-        (attended_grad, block_parts[0], gate_wgrad)
-    )
-    first_sum = lax.psum_scatter(first_part, "wide", scatter_dimension=0, tiled=True)
+    attended_grad, up_wgrad, gate_wgrad = lax.optimization_barrier(
+        (attended_grad, up_wgrad, gate_wgrad)
+    )
+    up_total = lax.psum_scatter(up_wgrad, "narrow", scatter_dimension=0, tiled=True)
     gate_total = lax.psum_scatter(gate_wgrad, "narrow", scatter_dimension=0, tiled=True)
     query_rot_grad, key_value_grad = back_swap(
         packed, attended_grad, attended, weight_sums, local_heads
     )
-    query_rot_grad, first_sum, gate_total, down_total, up_wgrad, second_part = (
+    query_rot_grad, gate_total, down_total, up_total, first_part, second_part = (
         lax.optimization_barrier(
-            (query_rot_grad, first_sum, gate_total, down_total, up_wgrad, block_parts[1])
-        )
-    )
-    up_total = lax.psum_scatter(up_wgrad, "narrow", scatter_dimension=0, tiled=True)
+            (query_rot_grad, gate_total, down_total, up_total, block_parts[0], block_parts[1])
+        )
+    )
+    first_sum = lax.psum_scatter(first_part, "wide", scatter_dimension=0, tiled=True)
     second_sum = lax.psum_scatter(second_part, "wide", scatter_dimension=0, tiled=True)
     query_rot_grad = query_rot_grad.astype(jnp.float32).reshape(
         wide_count, shard_rows, local_heads, head_dim
@@ -1302,7 +1352,7 @@
     input_grad = middle_grad + input_part
     gain_stack = jnp.stack([in_gain_grad, mid_gain_grad])
     head_stack = jnp.stack([query_gain_grad, key_gain_grad])
-    input_wgrad, up_total = lax.optimization_barrier((input_wgrad, up_total))
+    input_wgrad, first_sum = lax.optimization_barrier((input_wgrad, first_sum))
     input_total, spread, gains = sum_weights(
         input_wgrad,
         output_wgrad.astype(jnp.bfloat16),
@@ -1313,7 +1363,7 @@
     block_out = (middle + block_sum).astype(jnp.bfloat16)
     gain_total = gains[:, :model_width]
     head_total = gains[:, model_width:]
-    output_total = input_total[:, group_columns:].T
+    output_total = lax.optimization_barrier(input_total[:, group_columns:].T)
     query_total = input_total[:, :query_columns]
     spread = jnp.sum(
         spread.reshape(key_heads, copies, -1, 2, head_dim).astype(jnp.float32), axis=1

time: 1270 us -> 1240 us (0.976)
  waiting for transfers between devices: 144 us -> 91.8 us
    pallas_call x1, Pallas kernels: 99.8 us -> 172 us  [attend_swap(): pl.pallas_call(functools.partial(attend_swap_kernel, heads), out_shape=[j...]
    pallas_call x1, Pallas kernels: 239 us -> 178 us  [back_swap(): pl.pallas_call(functools.partial(back_swap_kernel, heads), out_shape=[jax...]
    all_gather x2 -> x0, waiting for transfers between devices: 60.9 us -> none  [the longest x1 54.9 us: shards(): down_local = lax.all_gather(down_own, 'narrow', axis=1, tiled=True)]
    all_gather x2, waiting for transfers between devices: 72.8 us -> 89 us  [gather_rows(): return lax.all_gather(shard, 'wide', axis=0, tiled=True)]
    unnamed x223 -> x233, local copies, waits for them, and re-layouts: 45.1 us -> 45.7 us
  transfers between devices with their start and end apart: 14 -> 12, of which waited for: 5 -> 2; matrix products, arithmetic and copies ran while one was open for 34% -> 33% of each run, Pallas kernels for 49% -> 52%
where the time goes in v7:
time: 1240 us; the launch traced here: 1220 us
  Pallas kernels  634 us (51%)
  matrix products  334 us (27%)
  waiting for transfers between devices  91.8 us (7%)
  local copies, waits for them, and re-layouts  74.3 us (6%)
  other arithmetic  74.3 us (6%)
  between operations  15.9 us (1%)
    pallas_call x1, Pallas kernels, back_swap(): pl.pallas_call(functools.partial(back_swap_kernel, heads), out_shape=[jax...  178 us
    pallas_call x1, Pallas kernels, attend_swap(): pl.pallas_call(functools.partial(attend_swap_kernel, heads), out_shape=[j...  172 us
    pallas_call x1, Pallas kernels, gather_weights(): pl.pallas_call(gather_kernel, out_shape=jax.ShapeDtypeStruct((8, 4 * att....  147 us
    pallas_call x1, Pallas kernels, sum_weights(): pl.pallas_call(scatter_kernel, out_shape=[jax.ShapeDtypeStruct((rows, col...  136 us
    dot_general x6, matrix products, dot_back(): lax.dot_general(left, right, (((1,), (1,)), ((), ())), preferred_element_...  92.5 us
    dot_general x6, matrix products, dot_last(): return jnp.dot(left, right, preferred_element_type=jnp.float32)  90.7 us
    all_gather x2, waiting for transfers between devices, gather_rows(): return lax.all_gather(shard, 'wide', axis=0, tiled=True)  89 us
    dot_general x6, matrix products, dot_first(): lax.dot_general(left, right, (((0,), (0,)), ((), ())), preferred_element_...  88.9 us
  transfers between devices with their start and end apart: 12, of which 2 were waited for; matrix products, arithmetic and copies ran while one was open for 33% of the time, Pallas kernels for 52%

profile of v7, /device:TPU:0, one launch (start us, length us, event | category | flops | bytes accessed | tf_op | source)
XLA Modules:
  0.0 1224.7 jit_solution(13172794769153552996)
XLA Ops:
  14.2 147.5 %gather_weights.1 = bf16[8,2048,640]{2,1,0:T(8,128)(2,1)} custom-call(bf16[512,640]{1,0:T(8,128)(2,1)} %pad_maximum_fusion.4.att_ref), custom_call_target="tpu_custom_call" | custom-call | bytes 314572800 | tf_op jit(solution)/shard_map/gather_weights/pallas_call | solution.py:406
  163.7 9.5 fusion.30
  183.4 5.4 copy.121
  207.1 172.4 %attend_swap.1 = (bf16[8,512,384]{2,1,0:T(8,128)(2,1)}, f32[4096,256]{1,0:T(8,128)}, f32[4096,256]{1,0:T(8,128)}, bf16[8,512,256]{2,1,0:T(8,128)(2,1)}, bf16[4,5...) custom-call(bf16[8,512,384]{2,1,0:T(8,128)(2,1)} %pad_maximum_fusion.src_ref, ...), custom_call_target="tpu_custom_call" | custom-call | flops 68719476736 | bytes 18874368 | tf_op jit(solution)/shard_map/attend_swap/pallas_call | solution.py:937
  379.5 7.8 multiply_reduce_fusion.4
  390.6 15.2 %convolution_convert_fusion.2 = bf16[2048,1024]{1,0:T(8,128)(2,1)} fusion(bf16[2048,2048]{1,0:T(8,128)(2,1)} %all-gather.10.cloned.1.call-done, bf16[1024,2048]{1,0:T(8,128)(2,1)} %get-tuple-element.79), kind=kOutput, calls=%fused_computation.67 | convolution fusion | flops 8592031744 | bytes 16777216 | tf_op jit(solution)/shard_map/dot_general | solution.py:67
  405.8 12.6 %convolution_convert_fusion.3 = bf16[2048,1024]{1,0:T(8,128)(2,1)} fusion(bf16[2048,2048]{1,0:T(8,128)(2,1)} %all-gather.6.cloned.1.call-done, bf16[1024,2048]{1,0:T(8,128)(2,1)S(1)} %copy-done.103), kind=kOutput, calls=%fused_computation.68 | convolution fusion | flops 8592031744 | bytes 16777216 | tf_op jit(solution)/shard_map/dot_general | solution.py:67
  418.4 69.8 %all-gather.12.cloned.1.call-done = bf16[2048,2048]{1,0:T(8,128)(2,1)} async-done(((bf16[256,2048]{1,0:T(8,128)(2,1)}), bf16[2048,2048]{1,0:T(8,128)(2,1)}) %all-gather.12.cloned.1.call-update) | async-done | bytes 8388624 | tf_op jit(solution)/shard_map/all_gather | solution.py:421
  488.2 14.6 %fusion.85 = f32[2048,1024]{1,0:T(8,128)} fusion(bf16[2048,2048]{1,0:T(8,128)(2,1)} %all-gather.12.cloned.1.call-done, bf16[2048,1024]{1,0:T(8,128)(2,1)} %all-gather.8.cloned.1.call-done), kind=kOutput, calls=%fused_computation.169 | convolution fusion | flops 8589934592 | bytes 20971520 | tf_op jit(solution)/shard_map/dot_general | solution.py:57
  502.7 18.6 %multiply_convert_fusion.1 = (bf16[2048,1024]{1,0:T(8,128)(2,1)}, bf16[2048,1024]{1,0:T(8,128)(2,1)}, bf16[2048,1024]{1,0:T(8,128)(2,1)}) fusion(f32[2048,1024]{1,0:T(8,128)} %fusion.85, bf16[2048,1024]{1,0:T(8,128)(2,1)} %convolution_convert_fusion.3, bf16[2048,2048]{1,0:T(8,128)(2,1)S(1)} %copy-done.96, bf16[2048,1024]{1,0:T(8,128)(2,1)} %bitcast.127), kind=kOutput, calls=%fused_computation.24 | convolution fusion | flops 8625586176 | bytes 37748736 | tf_op jit(solution)/shard_map/dot_general | solution.py:57
  521.3 14.1 %fusion.86 = f32[2048,2048]{1,0:T(8,128)} fusion(bf16[2048,1024]{1,0:T(8,128)(2,1)} %get-tuple-element.240, bf16[2048,1024]{1,0:T(8,128)(2,1)S(1)} %copy-done.97), kind=kOutput, calls=%fused_computation.170 | convolution fusion | flops 8589934592 | bytes 25165824 | tf_op jit(solution)/shard_map/dot_general | solution.py:67
  535.4 16.0 %add_convert_fusion.1 = bf16[2048,2048]{1,0:T(8,128)(2,1)} fusion(f32[2048,2048]{1,0:T(8,128)} %fusion.86, bf16[2048,1024]{1,0:T(8,128)(2,1)} %get-tuple-element.241, bf16[2048,1024]{1,0:T(8,128)(2,1)S(1)} %bitcast.130), kind=kOutput, calls=%fused_computation.1 | convolution fusion | flops 8598323200 | bytes 33554432 | tf_op jit(solution)/shard_map/dot_general | solution.py:67
  551.6 19.2 %all-gather.14.cloned.1.call-done = bf16[2048,2048]{1,0:T(8,128)(2,1)} async-done(((bf16[256,2048]{1,0:T(8,128)(2,1)}), bf16[2048,2048]{1,0:T(8,128)(2,1)}) %all-gather.14.cloned.1.call-update) | async-done | bytes 8388624 | tf_op jit(solution)/shard_map/all_gather | solution.py:421
  570.8 15.0 %fusion.87 = f32[2048,1024]{1,0:T(8,128)} fusion(bf16[2048,2048]{1,0:T(8,128)(2,1)} %all-gather.14.cloned.1.call-done, bf16[2048,1024]{1,0:T(8,128)(2,1)} %all-gather.8.cloned.1.call-done), kind=kOutput, calls=%fused_computation.171 | convolution fusion | flops 8589934592 | bytes 20971520 | tf_op jit(solution)/shard_map/dot_general | solution.py:57
  585.9 17.3 %multiply_convert_fusion = (bf16[2048,1024]{1,0:T(8,128)(2,1)}, bf16[2048,1024]{1,0:T(8,128)(2,1)}) fusion(f32[2048,1024]{1,0:T(8,128)} %fusion.87, bf16[2048,1024]{1,0:T(8,128)(2,1)} %convolution_convert_fusion.2, bf16[2048,2048]{1,0:T(8,128)(2,1)S(1)} %copy-done.95, bf16[2048,1024]{1,0:T(8,128)(2,1)} %bitcast.128), kind=kOutput, calls=%fused_computation.23 | convolution fusion | flops 8621391872 | bytes 33554432 | tf_op jit(solution)/shard_map/dot_general | solution.py:57
  603.2 14.1 %fusion.88 = f32[2048,2048]{1,0:T(8,128)} fusion(bf16[2048,1024]{1,0:T(8,128)(2,1)} %get-tuple-element.238, bf16[2048,1024]{1,0:T(8,128)(2,1)S(1)} %copy-done.98), kind=kOutput, calls=%fused_computation.172 | convolution fusion | flops 8589934592 | bytes 25165824 | tf_op jit(solution)/shard_map/dot_general | solution.py:67
  617.3 20.5 %add_convert_fusion = bf16[2048,2048]{1,0:T(8,128)(2,1)} fusion(f32[2048,2048]{1,0:T(8,128)} %fusion.88, bf16[2048,1024]{1,0:T(8,128)(2,1)} %bitcast.129, bf16[2048,1024]{1,0:T(8,128)(2,1)} %convolution_convert_fusion.2, f32[2048,1024]{1,0:T(8,128)} %fusion.87), kind=kOutput, calls=%fused_computation | convolution fusion | flops 8613003264 | bytes 41943040 | tf_op jit(solution)/shard_map/dot_general | solution.py:67
  637.9 15.0 %fusion.89 = f32[2048,1024]{1,0:T(8,128)} fusion(bf16[2048,2048]{1,0:T(8,128)(2,1)} %all-gather.12.cloned.1.call-done, bf16[2048,1024]{1,0:T(8,128)(2,1)} %get-tuple-element.240), kind=kOutput, calls=%fused_computation.173 | convolution fusion | flops 8589934592 | bytes 20971520 | tf_op jit(solution)/shard_map/dot_general | solution.py:61
  652.9 13.7 %fusion.90 = f32[2048,1024]{1,0:T(8,128)} fusion(bf16[2048,2048]{1,0:T(8,128)(2,1)} %all-gather.12.cloned.1.call-done, bf16[2048,1024]{1,0:T(8,128)(2,1)S(1)} %copy-done.102), kind=kOutput, calls=%fused_computation.174 | convolution fusion | flops 8589934592 | bytes 20971520 | tf_op jit(solution)/shard_map/dot_general | solution.py:61
  666.6 10.9 convolution_convert_fusion.1
  677.5 14.2 %convolution_convert_fusion = bf16[2048,2048]{1,0:T(8,128)(2,1)} fusion(bf16[2048,1024]{1,0:T(8,128)(2,1)} %get-tuple-element.237, bf16[1024,2048]{1,0:T(8,128)(2,1)} %get-tuple-element.79), kind=kOutput, calls=%fused_computation.36 | convolution fusion | flops 8594128896 | bytes 16777216 | tf_op jit(solution)/shard_map/dot_general | solution.py:57
  691.8 12.8 %fusion.91 = f32[1024,2048]{1,0:T(8,128)S(1)} fusion(bf16[2048,1024]{1,0:T(8,128)(2,1)} %get-tuple-element.239, bf16[2048,2048]{1,0:T(8,128)(2,1)} %all-gather.6.cloned.1.call-done), kind=kOutput, calls=%fused_computation.175 | convolution fusion | flops 8589934592 | bytes 20971520 | tf_op jit(solution)/shard_map/dot_general | solution.py:61
  704.6 13.3 %add_convert_fusion.2 = bf16[1024,2048]{1,0:T(8,128)(2,1)} fusion(f32[1024,2048]{1,0:T(8,128)S(1)} %fusion.91, bf16[2048,1024]{1,0:T(8,128)(2,1)S(1)} %copy-done.100, bf16[2048,2048]{1,0:T(8,128)(2,1)} %all-gather.10.cloned.1.call-done), kind=kOutput, calls=%fused_computation.22 | convolution fusion | flops 8594128896 | bytes 25165824 | tf_op jit(solution)/shard_map/dot_general | solution.py:61
  717.9 15.3 %add_convert_fusion.4 = bf16[2048,1024]{1,0:T(8,128)(2,1)} fusion(f32[2048,1024]{1,0:T(8,128)} %fusion.89, bf16[2048,2048]{1,0:T(8,128)(2,1)} %all-gather.14.cloned.1.call-done, bf16[2048,1024]{1,0:T(8,128)(2,1)} %get-tuple-element.238), kind=kOutput, calls=%fused_computation.26 | convolution fusion | flops 8594128896 | bytes 25165824 | tf_op jit(solution)/shard_map/dot_general | solution.py:61
  733.2 18.8 %add_convert_fusion.3 = bf16[2048,1024]{1,0:T(8,128)(2,1)} fusion(f32[2048,1024]{1,0:T(8,128)} %fusion.90, bf16[2048,2048]{1,0:T(8,128)(2,1)} %all-gather.14.cloned.1.call-done, bf16[2048,1024]{1,0:T(8,128)(2,1)} %convolution_convert_fusion.2, f32[2048,1024]{1,0:T(8,128)} %fusion.87), kind=kOutput, calls=%fused_computation.25 | convolution fusion | flops 8608808960 | bytes 33554432 | tf_op jit(solution)/shard_map/dot_general | solution.py:61
  761.8 9.0 convert_bitcast_fusion.2.g_ref
  772.2 177.6 %back_swap.1 = (bf16[8,512,256]{2,1,0:T(8,128)(2,1)}, bf16[8,512,128]{2,1,0:T(8,128)(2,1)S(1)}) custom-call(bf16[8,512,384]{2,1,0:T(8,128)(2,1)} %get-tuple-element.77.packed_ref, bf16[8,512,256]{2,1,0:T(8,128)(2,1)} %convert_bitcast_fusion.2.g_ref, f32[4096,256]{1,0:T(8,128)} %get-tuple-element.93.o_ref, f32[4096,256]{1,0:T(8,128)} %get-tuple-element.94.s_ref), custom_call_target="tpu_custom_call" | custom-call | flops 103079215104 | bytes 18874368 | tf_op jit(solution)/shard_map/back_swap/pallas_call | solution.py:1143
  979.8 10.8 convert_bitcast_fusion.1.out_ref
  1000.9 14.6 %fusion.26 = (f32[512]{0:T(512)S(1)}, f32[2048]{0:T(1024)S(1)}, f32[512,2048,1]{1,0,2:T(8,128)}) fusion(bf16[512,2048]{1,0:T(8,128)(2,1)S(1)} %copy-done.17, f32[2048]{0:T(1024)S(1)} %bitcast.120, f32[512]{0:T(512)S(1)} %copy-done.88, bf16[8,2048,640]{2,1,0:T(8,128)(2,1)} %gather_weights.1, bf16[8,512,64]{1,2,0:T(8,128)(2,1)S(1)} %copy-done.61, ...), kind=kOutput, calls=%fused_computation.53 | convolution fusion | flops 6459225600 | bytes 22040576 | tf_op jit(solution)/shard_map/gtc,gdc->td/dot_general | solution.py:1350
  1015.7 6.6 multiply_subtract_fusion.2
  1037.1 9.7 convert_bitcast_fusion.in_ref
  1046.8 136.4 %sum_weights.1 = (f32[512,640]{1,0:T(8,128)}, bf16[8,512,128]{2,1,0:T(8,128)(2,1)S(1)}, f32[40,128]{1,0:T(8,128)S(1)}) custom-call(bf16[8,2048,384]{2,1,0:T(8,128)(2,1)} %convert_bitcast_fusion.in_ref, bf16[8,2048,256]{2,1,0:T(8,128)(2,1)} %convert_bitcast_fusion.1.out_ref, f32[40,128]{1,0:T(8,128)S(1)} %pad_bitcast_fusion.gain_ref), custom_call_target="tpu_custom_call" | custom-call | bytes 314572800 | tf_op jit(solution)/shard_map/sum_weights/pallas_call | solution.py:693
  (336 shorter events, 140.4 us)
Async XLA Ops:
  7.2 199.8 %all-gather.6.cloned.1.call-start = ((), (), s32[]{:S(2)}) async-start(), calls=%async_computation.7 | async-start | bytes 9437184 | tf_op jit(solution)/shard_map/all_gather | solution.py:1226
  10.6 368.9 %all-gather.8.cloned.1.call-start = ((), (), s32[]{:S(2)}) async-start(), calls=%async_computation.8 | async-start | bytes 5242880 | tf_op jit(solution)/shard_map/all_gather | solution.py:1232
  10.9 150.8 %copy-start.19 = (f32[256,512]{0,1:T(8,128)}, f32[256,512]{0,1:T(8,128)S(1)}, u32[]{:S(2)}) copy-start(f32[256,512]{0,1:T(8,128)S(1)} %copy.118) | copy-start | bytes 1572868
  14.2 148.3 %copy-start.15 = (bf16[512,2048]{1,0:T(8,128)(2,1)S(1)}, bf16[512,2048]{1,0:T(8,128)(2,1)}, u32[]{:S(2)}) copy-start(bf16[512,2048]{1,0:T(8,128)(2,1)} %param.30) | copy-start | bytes 6291460
  161.8 217.7 %all-gather.10.cloned.1.call-start = ((), (), s32[]{:S(2)}) async-start(), calls=%async_computation.9 | async-start | bytes 9437184 | tf_op jit(solution)/shard_map/all_gather | solution.py:1227
  162.5 325.7 %all-gather.12.cloned.1.call-start = ((), (), s32[]{:S(2)}) async-start(), calls=%async_computation.10 | async-start | bytes 9437184 | tf_op jit(solution)/shard_map/all_gather | solution.py:421
  163.7 223.7 %copy-start.70 = (f32[1,2048]{1,0:T(1,128)}, f32[1,2048]{1,0:T(1,128)S(1)}, u32[]{:S(2)}) copy-start(f32[1,2048]{1,0:T(1,128)S(1)} %get-tuple-element.259) | copy-start | bytes 24580
  179.7 13.9 %copy-start.49 = (f32[512,32]{0,1:T(8,128)}, f32[512,32]{0,1:T(8,128)S(1)}, u32[]{:S(2)}) copy-start(f32[512,32]{0,1:T(8,128)S(1)} %get-tuple-element.261) | copy-start | bytes 196612
  179.7 13.9 %copy-start.51 = (f32[512,32]{0,1:T(8,128)}, f32[512,32]{0,1:T(8,128)S(1)}, u32[]{:S(2)}) copy-start(f32[512,32]{0,1:T(8,128)S(1)} %get-tuple-element.262) | copy-start | bytes 196612
  179.8 22.0 %copy-start.31 = (f32[512,32]{1,0:T(8,128)}, f32[512,32]{1,0:T(8,128)S(1)}, u32[]{:S(2)}) copy-start(f32[512,32]{1,0:T(8,128)S(1)} %copy.122) | copy-start | bytes 196612
  207.1 172.4 %copy-start.16 = (bf16[512,2048]{1,0:T(8,128)(2,1)S(1)}, bf16[512,2048]{1,0:T(8,128)(2,1)}, u32[]{:S(2)}) copy-start(bf16[512,2048]{1,0:T(8,128)(2,1)} %param.30) | copy-start | bytes 6291460
  390.0 180.8 %all-gather.14.cloned.1.call-start = ((), (), s32[]{:S(2)}) async-start(), calls=%async_computation.12 | async-start | bytes 9437184 | tf_op jit(solution)/shard_map/all_gather | solution.py:421
  390.6 361.4 %reduce-scatter.8.cloned.1.call-start = ((), (), s32[]{:S(2)}) async-start(), calls=%async_computation.11 | async-start | bytes 9437184 | tf_op jit(solution)/shard_map/reduce_scatter | solution.py:432
  390.6 15.2 %copy-start.103 = (bf16[1024,2048]{1,0:T(8,128)(2,1)S(1)}, bf16[1024,2048]{1,0:T(8,128)(2,1)}, u32[]{:S(2)}) copy-start(bf16[1024,2048]{1,0:T(8,128)(2,1)} %get-tuple-element.79) | copy-start | bytes 12582916
  488.1 14.6 %copy-start.96 = (bf16[2048,2048]{1,0:T(8,128)(2,1)S(1)}, bf16[2048,2048]{1,0:T(8,128)(2,1)}, u32[]{:S(2)}) copy-start(bf16[2048,2048]{1,0:T(8,128)(2,1)} %all-gather.12.cloned.1.call-done) | copy-start | bytes 25165828
  502.7 18.6 %copy-start.97 = (bf16[2048,1024]{1,0:T(8,128)(2,1)S(1)}, bf16[2048,1024]{1,0:T(8,128)(2,1)}, u32[]{:S(2)}) copy-start(bf16[2048,1024]{1,0:T(8,128)(2,1)} %all-gather.8.cloned.1.call-done) | copy-start | bytes 12582916
  521.3 14.1 %copy-start.99 = (bf16[4,512,1024]{2,1,0:T(8,128)(2,1)S(1)}, bf16[4,512,1024]{2,1,0:T(8,128)(2,1)}, u32[]{:S(2)}) copy-start(bf16[4,512,1024]{2,1,0:T(8,128)(2,1)} %get-tuple-element.83) | copy-start | bytes 12582916
  551.5 201.9 %reduce-scatter.10.cloned.1.call-start = ((), (), s32[]{:S(2)}) async-start(), calls=%async_computation.13 | async-start | bytes 9437184 | tf_op jit(solution)/shard_map/reduce_scatter | solution.py:432
  570.8 15.1 %copy-start.95 = (bf16[2048,2048]{1,0:T(8,128)(2,1)S(1)}, bf16[2048,2048]{1,0:T(8,128)(2,1)}, u32[]{:S(2)}) copy-start(bf16[2048,2048]{1,0:T(8,128)(2,1)} %all-gather.14.cloned.1.call-done) | copy-start | bytes 25165828
  585.8 17.3 %copy-start.98 = (bf16[2048,1024]{1,0:T(8,128)(2,1)S(1)}, bf16[2048,1024]{1,0:T(8,128)(2,1)}, u32[]{:S(2)}) copy-start(bf16[2048,1024]{1,0:T(8,128)(2,1)} %all-gather.8.cloned.1.call-done) | copy-start | bytes 12582916
  637.8 312.1 %reduce-scatter.12.cloned.1.call-start = ((), (), s32[]{:S(2)}) async-start(), calls=%async_computation.14 | async-start | bytes 5242880 | tf_op jit(solution)/shard_map/reduce_scatter | solution.py:1322
  637.9 15.0 %copy-start.102 = (bf16[2048,1024]{1,0:T(8,128)(2,1)S(1)}, bf16[2048,1024]{1,0:T(8,128)(2,1)}, u32[]{:S(2)}) copy-start(bf16[2048,1024]{1,0:T(8,128)(2,1)} %get-tuple-element.241) | copy-start | bytes 12582916
  652.9 13.7 %copy-start.104 = (bf16[1024,2048]{1,0:T(8,128)(2,1)S(1)}, bf16[1024,2048]{1,0:T(8,128)(2,1)}, u32[]{:S(2)}) copy-start(bf16[1024,2048]{1,0:T(8,128)(2,1)} %get-tuple-element.79) | copy-start | bytes 12582916
  770.9 179.0 %reduce-scatter.16.cloned.1.call-start = ((), (), s32[]{:S(2)}) async-start(), calls=%async_computation.16 | async-start | bytes 5242880 | tf_op jit(solution)/shard_map/reduce_scatter | solution.py:1321
  771.6 178.3 %reduce-scatter.14.cloned.1.call-start = ((), (), s32[]{:S(2)}) async-start(), calls=%async_computation.15 | async-start | bytes 5242880 | tf_op jit(solution)/shard_map/reduce_scatter | solution.py:1317
  772.2 274.6 %reduce-scatter.18.cloned.1.call-start = ((), (), s32[]{:S(2)}) async-start(), calls=%async_computation.17 | async-start | bytes 9437184 | tf_op jit(solution)/shard_map/reduce_scatter | solution.py:1331
  950.0 233.3 %reduce-scatter.20.cloned.1.call-start = ((), (), s32[]{:S(2)}) async-start(), calls=%async_computation.18 | async-start | bytes 9437184 | tf_op jit(solution)/shard_map/reduce_scatter | solution.py:1332
  1000.5 15.0 %copy-start.43 = (bf16[8,512,4,64]{1,3,2,0:T(8,128)(2,1)}, bf16[8,512,4,64]{1,3,2,0:T(8,128)(2,1)S(1)}, u32[]{:S(2)}) copy-start(bf16[8,512,4,64]{1,3,2,0:T(8,128)(2,1)S(1)} %fusion.23) | copy-start | bytes 6291460
  1000.8 14.6 %copy-start.76 = (f32[2048]{0:T(1024)S(1)}, f32[2048]{0:T(1024)}, u32[]{:S(2)}) copy-start(f32[2048]{0:T(1024)} %get-tuple-element.204) | copy-start | bytes 24580
  1000.8 14.8 %copy-start.80 = (f32[512]{0:T(512)S(1)}, f32[512]{0:T(512)}, u32[]{:S(2)}) copy-start(f32[512]{0:T(512)} %copy-done.79) | copy-start | bytes 6148
  1000.8 14.8 %copy-start.8 = (f32[512,1024]{1,0:T(8,128)S(1)}, f32[512,1024]{1,0:T(8,128)}, u32[]{:S(2)}) copy-start(f32[512,1024]{1,0:T(8,128)} %param.45) | copy-start | bytes 6291460
  1000.8 14.8 %copy-start.56 = (bf16[512,1024]{1,0:T(8,128)(2,1)S(1)}, bf16[512,1024]{1,0:T(8,128)(2,1)}, u32[]{:S(2)}) copy-start(bf16[512,1024]{1,0:T(8,128)(2,1)} %reduce-scatter.12.cloned.1.call-done) | copy-start | bytes 3145732
  (87 other events, 372.2 us)
Sparse Core Ops, SparseCore 0:
  10.7 107.0 all-gather.5
  161.9 55.1 all-gather.7
  219.3 159.0 all-gather.9
  390.1 98.0 all-gather.11
  490.2 80.5 all-gather.13
  572.9 88.1 reduce-scatter.7
  663.4 87.9 reduce-scatter.9
  771.0 51.3 reduce-scatter.11
  825.6 52.6 reduce-scatter.15
  881.1 52.6 reduce-scatter.13
  950.1 87.5 reduce-scatter.17
  1039.9 131.1 reduce-scatter.19

commit v8 on v7

--- a/solution.py
+++ b/solution.py
@@ -744,18 +744,6 @@
     pl.semaphore_wait(barrier, 10)
 
 
-def tell_wide():
-    narrow = lax.axis_index("narrow")
-    wide = lax.axis_index("wide")
-    barrier = pltpu.get_barrier_semaphore()
-    for step in range(1, 8):
-        pl.semaphore_signal(
-            barrier, inc=1, device_id=(narrow, (wide + step) % 8),
-            device_id_type=pl.DeviceIdType.MESH,
-        )
-    pl.semaphore_wait(barrier, 7)
-
-
 def attend_swap_kernel(
     heads, src_ref, up_ref, down_ref, packed_ref, o_ref, s_ref, out_ref, up_all, down_all,
     kk_ref, va_ref, vb_ref, acc_ref, low_ref,
@@ -964,16 +952,32 @@
 
 
 def back_swap_kernel(
-    heads, packed_ref, g_ref, o_ref, s_ref, dq_out, dkv_out,
+    heads, packed_ref, g_ref, o_ref, s_ref, gate_ref, up_ref, down_ref,
+    dq_out, dkv_out, gate_out, up_out, down_out,
     grad_ref, scaled_ref, dots_ref, dq_ref, dkv_ref, kk_ref, vv_ref, ka_ref, kb_ref,
     low_q, low_kv, own_sem, send_sem, got_sem, q_send, q_got, kv_send, kv_got,
+    ffn_own, ffn_send, ffn_got,
 ):
     narrow, wide, chip, core = place()
     count, block, _ = packed_ref.shape
     base = 4 * (chip // 2)
     away = 4 - base
     low = low_lanes(block)
-    tell_wide()
+    rows_out = gate_out.shape[1]
+    columns = down_out.shape[2]
+    tell_all()
+
+    def share(k, who):
+        if k == 2:
+            return down_ref.at[:, pl.ds(pl.multiple_of(who * columns, columns), columns)]
+        return (gate_ref, up_ref)[k].at[pl.ds(pl.multiple_of(who * rows_out, rows_out), rows_out), :]
+
+    def ffn(k, step):
+        to = (narrow + step) % 4
+        return remote(
+            share(k, to), (gate_out, up_out, down_out)[k].at[step], ffn_send.at[k, step],
+            ffn_got.at[k, step], (to, wide),
+        )
 
     def send(to):
         return remote(
@@ -992,6 +996,16 @@
     own.start()
     for step in range(1, 8):
         send((wide + step) % 8).start()
+    keep = [
+        pltpu.make_async_copy(
+            share(k, narrow), (gate_out, up_out, down_out)[k].at[0], ffn_own.at[k]
+        )
+        for k in range(3)
+    ]
+    for k in range(3):
+        keep[k].start()
+        for step in range(1, 4):
+            ffn(k, step).start()
 
     @pl.loop(0, count)
     def _(j):
@@ -1122,9 +1136,13 @@
         send(to).wait_send()
         send_q(to).wait_send()
         send_kv(to).wait_send()
-
-
-def back_swap(packed, grad, attended, weight_sums, heads):
+    for k in range(3):
+        keep[k].wait()
+        for step in range(1, 4):
+            ffn(k, step).wait()
+
+
+def back_swap(packed, grad, attended, weight_sums, gate, up, down, heads):
     count, block, lanes = packed.shape
     split = heads * 64
     if lax.axis_size("narrow") != 4 or lax.axis_size("wide") != 8:
@@ -1134,7 +1152,13 @@
             packed.reshape(-1, lanes), head_grad.astype(jnp.bfloat16), dots, heads
         )
         result = swap(result.reshape(packed.shape))
-        return result[:, :, :split], result[:, :, split:]
+        return (
+            result[:, :, :split],
+            result[:, :, split:],
+            lax.psum_scatter(gate, "narrow", scatter_dimension=0, tiled=True)[None],
+            lax.psum_scatter(up, "narrow", scatter_dimension=0, tiled=True)[None],
+            lax.psum_scatter(down, "narrow", scatter_dimension=1, tiled=True)[None],
+        )
     total = count * block
     dma = pltpu.SemaphoreType.DMA
     vmem = pltpu.VMEM
@@ -1145,14 +1169,18 @@
         out_shape=[
             jax.ShapeDtypeStruct((count, block, split), low),
             jax.ShapeDtypeStruct((count, block, 128), low),
+            jax.ShapeDtypeStruct((4, gate.shape[0] // 4, gate.shape[1]), low),
+            jax.ShapeDtypeStruct((4, up.shape[0] // 4, up.shape[1]), low),
+            jax.ShapeDtypeStruct((4, down.shape[0], down.shape[1] // 4), low),
         ],
         in_specs=[
             pl.BlockSpec(memory_space=vmem),
             pl.BlockSpec(memory_space=pl.ANY),
             pl.BlockSpec(memory_space=vmem),
             pl.BlockSpec(memory_space=vmem),
-        ],
-        out_specs=[pl.BlockSpec(memory_space=vmem)] * 2,
+        ]
+        + [pl.BlockSpec(memory_space=pl.ANY)] * 3,
+        out_specs=[pl.BlockSpec(memory_space=vmem)] * 2 + [pl.BlockSpec(memory_space=pl.ANY)] * 3,
         scratch_shapes=[
             vmem((count, block, split), low),
             vmem((block, 128), low),
@@ -1165,6 +1193,7 @@
             vmem((count, block, split), low),
             vmem((count, block, 128), low),
             dma, dma((8,)), dma((8,)), dma((8,)), dma((8,)), dma((8,)), dma((8,)),
+            dma((3,)), dma((3, 4)), dma((3, 4)),
         ],
         compiler_params=pltpu.CompilerParams(
             collective_id=5, has_side_effects=True, vmem_limit_bytes=52 << 20
@@ -1173,7 +1202,7 @@
             flops=12 * cost * 256, bytes_accessed=12 * packed.size, transcendentals=cost
         ),
         name="back_swap",
-    )(packed, grad, attended, weight_sums)
+    )(packed, grad, attended, weight_sums, gate, up, down)
 
 
 def shards(
@@ -1265,13 +1294,11 @@
         .astype(jnp.bfloat16)
     )
     packed = jnp.concatenate([query_rot, key_rot.astype(jnp.bfloat16), value_rows], axis=2)
-    packed, grad_halves[0] = lax.optimization_barrier((packed, grad_halves[0]))
+    packed, grad_halves = lax.optimization_barrier((packed, grad_halves))
     packed, attended, weight_sums, attended_low, up_local, down_local = attend_swap(
         packed, up_weight.astype(jnp.bfloat16), down_weight.astype(jnp.bfloat16), local_heads
     )
-    attended_low, gate_local, grad_halves[1] = lax.optimization_barrier(
-        (attended_low, gate_local, grad_halves[1])
-    )
+    attended_low, gate_local = lax.optimization_barrier((attended_low, gate_local))
     branch = jnp.einsum("gth,gdh->td", attended_low, output_full, preferred_element_type=jnp.float32)
     middle = residual + branch
     normed_mid, norm_mid_back = jax.vjp(rms_scale, middle, norm_gains[1])
@@ -1313,22 +1340,14 @@
     output_wgrad = jnp.einsum(
         "td,gth->gdh", branch_grad, attended_low, preferred_element_type=jnp.float32
     )
-    attended_grad, down_wgrad = lax.optimization_barrier((attended_grad, down_wgrad))
-    down_total = lax.psum_scatter(down_wgrad, "narrow", scatter_dimension=1, tiled=True)
-    attended_grad, up_wgrad, gate_wgrad = lax.optimization_barrier(
-        (attended_grad, up_wgrad, gate_wgrad)
-    )
-    up_total = lax.psum_scatter(up_wgrad, "narrow", scatter_dimension=0, tiled=True)
-    gate_total = lax.psum_scatter(gate_wgrad, "narrow", scatter_dimension=0, tiled=True)
-    query_rot_grad, key_value_grad = back_swap(
-        packed, attended_grad, attended, weight_sums, local_heads
-    )
-    query_rot_grad, gate_total, down_total, up_total, first_part, second_part = (
-        lax.optimization_barrier(
-            (query_rot_grad, gate_total, down_total, up_total, block_parts[0], block_parts[1])
-        )
-    )
+    attended_grad, first_part = lax.optimization_barrier((attended_grad, block_parts[0]))
     first_sum = lax.psum_scatter(first_part, "wide", scatter_dimension=0, tiled=True)
+    query_rot_grad, key_value_grad, gate_shares, up_shares, down_shares = back_swap(
+        packed, attended_grad, attended, weight_sums, gate_wgrad, up_wgrad, down_wgrad, local_heads
+    )
+    query_rot_grad, first_sum, second_part = lax.optimization_barrier(
+        (query_rot_grad, first_sum, block_parts[1])
+    )
     second_sum = lax.psum_scatter(second_part, "wide", scatter_dimension=0, tiled=True)
     query_rot_grad = query_rot_grad.astype(jnp.float32).reshape(
         wide_count, shard_rows, local_heads, head_dim
@@ -1352,13 +1371,12 @@
     input_grad = middle_grad + input_part
     gain_stack = jnp.stack([in_gain_grad, mid_gain_grad])
     head_stack = jnp.stack([query_gain_grad, key_gain_grad])
-    input_wgrad, first_sum = lax.optimization_barrier((input_wgrad, first_sum))
+    input_wgrad, second_sum = lax.optimization_barrier((input_wgrad, second_sum))
     input_total, spread, gains = sum_weights(
         input_wgrad,
         output_wgrad.astype(jnp.bfloat16),
         jnp.concatenate([gain_stack, head_stack], axis=1),
     )
-    input_total, second_sum = lax.optimization_barrier((input_total, second_sum))
     block_sum = jnp.concatenate([first_sum, second_sum], axis=0).astype(jnp.float32)
     block_out = (middle + block_sum).astype(jnp.bfloat16)
     gain_total = gains[:, :model_width]
@@ -1371,9 +1389,9 @@
     key_total = spread[0].reshape(key_weight.shape)
     value_total = spread[1].reshape(value_weight.shape)
     gate_total, up_total, down_total = (
-        gate_total.astype(jnp.float32),
-        up_total.astype(jnp.float32),
-        down_total.astype(jnp.float32),
+        jnp.sum(gate_shares.astype(jnp.float32), axis=0),
+        jnp.sum(up_shares.astype(jnp.float32), axis=0),
+        jnp.sum(down_shares.astype(jnp.float32), axis=0),
     )
     wide_rate = D ** (-0.5)
     query_new = adam_update(

time: 1240 us -> 1190 us (0.960)
  Pallas kernels: 634 us -> 607 us
  waiting for transfers between devices: 91.8 us -> 73.2 us
    pallas_call x1, Pallas kernels: 172 us -> 135 us  [attend_swap(): pl.pallas_call(functools.partial(attend_swap_kernel, heads), out_shape=[j...]
    pallas_call x1, Pallas kernels: 178 us -> 214 us  [back_swap(): pl.pallas_call(functools.partial(back_swap_kernel, heads), out_shape=[jax...]
    pallas_call x1, Pallas kernels: 136 us -> 110 us  [sum_weights(): pl.pallas_call(scatter_kernel, out_shape=[jax.ShapeDtypeStruct((rows, col...]
    all_gather x2, waiting for transfers between devices: 89 us -> 71 us  [gather_rows(): return lax.all_gather(shard, 'wide', axis=0, tiled=True)]
    unnamed x233 -> x235, local copies, waits for them, and re-layouts: 45.7 us -> 45.9 us
  transfers between devices with their start and end apart: 12 -> 9, of which waited for: 2 -> 3; matrix products, arithmetic and copies ran while one was open for 33% -> 35% of each run, Pallas kernels for 52% -> 42%
where the time goes in v8:
time: 1190 us; the launch traced here: 1180 us
  Pallas kernels  607 us (51%)
  matrix products  327 us (27%)
  other arithmetic  83.3 us (7%)
  local copies, waits for them, and re-layouts  76 us (6%)
  waiting for transfers between devices  73.2 us (6%)
  between operations  15.2 us (1%)
    pallas_call x1, Pallas kernels, back_swap(): pl.pallas_call(functools.partial(back_swap_kernel, heads), out_shape=[jax...  214 us
    pallas_call x1, Pallas kernels, gather_weights(): pl.pallas_call(gather_kernel, out_shape=jax.ShapeDtypeStruct((8, 4 * att....  148 us
    pallas_call x1, Pallas kernels, attend_swap(): pl.pallas_call(functools.partial(attend_swap_kernel, heads), out_shape=[j...  135 us
    pallas_call x1, Pallas kernels, sum_weights(): pl.pallas_call(scatter_kernel, out_shape=[jax.ShapeDtypeStruct((rows, col...  110 us
    dot_general x6, matrix products, dot_back(): lax.dot_general(left, right, (((1,), (1,)), ((), ())), preferred_element_...  92.3 us
    dot_general x6, matrix products, dot_last(): return jnp.dot(left, right, preferred_element_type=jnp.float32)  91 us
    dot_general x6, matrix products, dot_first(): lax.dot_general(left, right, (((0,), (0,)), ((), ())), preferred_element_...  86.2 us
    all_gather x2, waiting for transfers between devices, gather_rows(): return lax.all_gather(shard, 'wide', axis=0, tiled=True)  71 us
  transfers between devices with their start and end apart: 9, of which 3 were waited for; matrix products, arithmetic and copies ran while one was open for 35% of the time, Pallas kernels for 42%

profile of v8, /device:TPU:0, one launch (start us, length us, event | category | flops | bytes accessed | tf_op | source)
XLA Modules:
  0.0 1182.3 jit_solution(15437410279289097227)
XLA Ops:
  15.0 147.6 %gather_weights.1 = bf16[8,2048,640]{2,1,0:T(8,128)(2,1)} custom-call(bf16[512,640]{1,0:T(8,128)(2,1)} %pad_maximum_fusion.4.att_ref), custom_call_target="tpu_custom_call" | custom-call | bytes 314572800 | tf_op jit(solution)/shard_map/gather_weights/pallas_call | solution.py:406
  164.4 9.4 fusion.30
  185.4 5.4 copy.121
  206.5 135.0 %attend_swap.1 = (bf16[8,512,384]{2,1,0:T(8,128)(2,1)}, f32[4096,256]{1,0:T(8,128)}, f32[4096,256]{1,0:T(8,128)}, bf16[8,512,256]{2,1,0:T(8,128)(2,1)}, bf16[4,5...) custom-call(bf16[8,512,384]{2,1,0:T(8,128)(2,1)} %pad_maximum_fusion.src_ref, ...), custom_call_target="tpu_custom_call" | custom-call | flops 68719476736 | bytes 18874368 | tf_op jit(solution)/shard_map/attend_swap/pallas_call | solution.py:925
  341.6 7.8 multiply_reduce_fusion.4
  352.8 15.0 %convolution_convert_fusion.2 = bf16[2048,1024]{1,0:T(8,128)(2,1)} fusion(bf16[2048,2048]{1,0:T(8,128)(2,1)} %all-gather.8.cloned.1.call-done, bf16[1024,2048]{1,0:T(8,128)(2,1)} %get-tuple-element.74), kind=kOutput, calls=%fused_computation.70 | convolution fusion | flops 8592031744 | bytes 16777216 | tf_op jit(solution)/shard_map/dot_general | solution.py:67
  367.8 12.6 %convolution_convert_fusion.3 = bf16[2048,1024]{1,0:T(8,128)(2,1)} fusion(bf16[2048,2048]{1,0:T(8,128)(2,1)} %all-gather.6.cloned.1.call-done, bf16[1024,2048]{1,0:T(8,128)(2,1)S(1)} %copy-done.102), kind=kOutput, calls=%fused_computation.71 | convolution fusion | flops 8592031744 | bytes 16777216 | tf_op jit(solution)/shard_map/dot_general | solution.py:67
  380.4 52.1 %all-gather.12.cloned.1.call-done = bf16[2048,2048]{1,0:T(8,128)(2,1)} async-done(((bf16[256,2048]{1,0:T(8,128)(2,1)}), bf16[2048,2048]{1,0:T(8,128)(2,1)}) %all-gather.12.cloned.1.call-update) | async-done | bytes 8388624 | tf_op jit(solution)/shard_map/all_gather | solution.py:421
  432.5 14.7 %fusion.79 = f32[2048,1024]{1,0:T(8,128)} fusion(bf16[2048,2048]{1,0:T(8,128)(2,1)} %all-gather.12.cloned.1.call-done, bf16[2048,1024]{1,0:T(8,128)(2,1)} %all-gather.10.cloned.1.call-done), kind=kOutput, calls=%fused_computation.169 | convolution fusion | flops 8589934592 | bytes 20971520 | tf_op jit(solution)/shard_map/dot_general | solution.py:57
  447.2 18.9 %multiply_convert_fusion.1 = (bf16[2048,1024]{1,0:T(8,128)(2,1)}, bf16[2048,1024]{1,0:T(8,128)(2,1)}, bf16[2048,1024]{1,0:T(8,128)(2,1)}) fusion(f32[2048,1024]{1,0:T(8,128)} %fusion.79, bf16[2048,1024]{1,0:T(8,128)(2,1)} %convolution_convert_fusion.3, bf16[2048,2048]{1,0:T(8,128)(2,1)S(1)} %copy-done.93, bf16[2048,1024]{1,0:T(8,128)(2,1)} %bitcast.129), kind=kOutput, calls=%fused_computation.27 | convolution fusion | flops 8625586176 | bytes 37748736 | tf_op jit(solution)/shard_map/dot_general | solution.py:57
  466.1 14.0 %fusion.80 = f32[2048,2048]{1,0:T(8,128)} fusion(bf16[2048,1024]{1,0:T(8,128)(2,1)} %get-tuple-element.230, bf16[2048,1024]{1,0:T(8,128)(2,1)S(1)} %copy-done.94), kind=kOutput, calls=%fused_computation.170 | convolution fusion | flops 8589934592 | bytes 25165824 | tf_op jit(solution)/shard_map/dot_general | solution.py:67
  480.1 16.1 %add_convert_fusion.1 = bf16[2048,2048]{1,0:T(8,128)(2,1)} fusion(f32[2048,2048]{1,0:T(8,128)} %fusion.80, bf16[2048,1024]{1,0:T(8,128)(2,1)} %get-tuple-element.231, bf16[2048,1024]{1,0:T(8,128)(2,1)S(1)} %bitcast.132), kind=kOutput, calls=%fused_computation.1 | convolution fusion | flops 8598323200 | bytes 33554432 | tf_op jit(solution)/shard_map/dot_general | solution.py:67
  496.3 18.9 %all-gather.14.cloned.1.call-done = bf16[2048,2048]{1,0:T(8,128)(2,1)} async-done(((bf16[256,2048]{1,0:T(8,128)(2,1)}), bf16[2048,2048]{1,0:T(8,128)(2,1)}) %all-gather.14.cloned.1.call-update) | async-done | bytes 8388624 | tf_op jit(solution)/shard_map/all_gather | solution.py:421
  515.2 14.8 %fusion.81 = f32[2048,1024]{1,0:T(8,128)} fusion(bf16[2048,2048]{1,0:T(8,128)(2,1)} %all-gather.14.cloned.1.call-done, bf16[2048,1024]{1,0:T(8,128)(2,1)} %all-gather.10.cloned.1.call-done), kind=kOutput, calls=%fused_computation.171 | convolution fusion | flops 8589934592 | bytes 20971520 | tf_op jit(solution)/shard_map/dot_general | solution.py:57
  530.0 17.3 %multiply_convert_fusion = (bf16[2048,1024]{1,0:T(8,128)(2,1)}, bf16[2048,1024]{1,0:T(8,128)(2,1)}) fusion(f32[2048,1024]{1,0:T(8,128)} %fusion.81, bf16[2048,1024]{1,0:T(8,128)(2,1)} %convolution_convert_fusion.2, bf16[2048,2048]{1,0:T(8,128)(2,1)S(1)} %copy-done.92, bf16[2048,1024]{1,0:T(8,128)(2,1)} %bitcast.130), kind=kOutput, calls=%fused_computation.26 | convolution fusion | flops 8621391872 | bytes 33554432 | tf_op jit(solution)/shard_map/dot_general | solution.py:57
  547.3 14.1 %fusion.82 = f32[2048,2048]{1,0:T(8,128)} fusion(bf16[2048,1024]{1,0:T(8,128)(2,1)} %get-tuple-element.228, bf16[2048,1024]{1,0:T(8,128)(2,1)S(1)} %copy-done.95), kind=kOutput, calls=%fused_computation.172 | convolution fusion | flops 8589934592 | bytes 25165824 | tf_op jit(solution)/shard_map/dot_general | solution.py:67
  561.4 20.5 %add_convert_fusion = bf16[2048,2048]{1,0:T(8,128)(2,1)} fusion(f32[2048,2048]{1,0:T(8,128)} %fusion.82, bf16[2048,1024]{1,0:T(8,128)(2,1)} %bitcast.131, bf16[2048,1024]{1,0:T(8,128)(2,1)} %convolution_convert_fusion.2, f32[2048,1024]{1,0:T(8,128)} %fusion.81), kind=kOutput, calls=%fused_computation | convolution fusion | flops 8613003264 | bytes 41943040 | tf_op jit(solution)/shard_map/dot_general | solution.py:67
  581.9 15.1 %fusion.83 = f32[2048,1024]{1,0:T(8,128)} fusion(bf16[2048,2048]{1,0:T(8,128)(2,1)} %all-gather.12.cloned.1.call-done, bf16[2048,1024]{1,0:T(8,128)(2,1)} %get-tuple-element.230), kind=kOutput, calls=%fused_computation.173 | convolution fusion | flops 8589934592 | bytes 20971520 | tf_op jit(solution)/shard_map/dot_general | solution.py:61
  597.0 13.7 %fusion.84 = f32[2048,1024]{1,0:T(8,128)} fusion(bf16[2048,2048]{1,0:T(8,128)(2,1)} %all-gather.12.cloned.1.call-done, bf16[2048,1024]{1,0:T(8,128)(2,1)S(1)} %copy-done.101), kind=kOutput, calls=%fused_computation.174 | convolution fusion | flops 8589934592 | bytes 20971520 | tf_op jit(solution)/shard_map/dot_general | solution.py:61
  610.7 10.9 convolution_convert_fusion.1
  621.6 14.4 %convolution_convert_fusion = bf16[2048,2048]{1,0:T(8,128)(2,1)} fusion(bf16[2048,1024]{1,0:T(8,128)(2,1)} %get-tuple-element.227, bf16[1024,2048]{1,0:T(8,128)(2,1)} %get-tuple-element.74), kind=kOutput, calls=%fused_computation.39 | convolution fusion | flops 8594128896 | bytes 16777216 | tf_op jit(solution)/shard_map/dot_general | solution.py:57
  636.0 12.8 %fusion.85 = f32[1024,2048]{1,0:T(8,128)S(1)} fusion(bf16[2048,1024]{1,0:T(8,128)(2,1)} %get-tuple-element.229, bf16[2048,2048]{1,0:T(8,128)(2,1)} %all-gather.6.cloned.1.call-done), kind=kOutput, calls=%fused_computation.175 | convolution fusion | flops 8589934592 | bytes 20971520 | tf_op jit(solution)/shard_map/dot_general | solution.py:61
  648.9 13.2 %add_convert_fusion.2.down_ref = bf16[1024,2048]{1,0:T(8,128)(2,1)} fusion(f32[1024,2048]{1,0:T(8,128)S(1)} %fusion.85, bf16[2048,1024]{1,0:T(8,128)(2,1)S(1)} %copy-done.97, bf16[2048,2048]{1,0:T(8,128)(2,1)} %all-gather.8.cloned.1.call-done), kind=kOutput, calls=%fused_computation.25 | convolution fusion | flops 8594128896 | bytes 25165824 | tf_op jit(solution)/shard_map/dot_general | solution.py:61
  662.1 15.4 %add_convert_fusion.4.gate_ref = bf16[2048,1024]{1,0:T(8,128)(2,1)} fusion(f32[2048,1024]{1,0:T(8,128)} %fusion.83, bf16[2048,2048]{1,0:T(8,128)(2,1)} %all-gather.14.cloned.1.call-done, bf16[2048,1024]{1,0:T(8,128)(2,1)} %get-tuple-element.228), kind=kOutput, calls=%fused_computation.29 | convolution fusion | flops 8594128896 | bytes 25165824 | tf_op jit(solution)/shard_map/dot_general | solution.py:61
  677.6 15.9 %add_convert_fusion.3.up_ref = bf16[2048,1024]{1,0:T(8,128)(2,1)} fusion(f32[2048,1024]{1,0:T(8,128)} %fusion.84, bf16[2048,2048]{1,0:T(8,128)(2,1)S(1)} %bitcast.128, bf16[2048,1024]{1,0:T(8,128)(2,1)S(1)} %copy-done.100, f32[2048,1024]{1,0:T(8,128)} %fusion.81), kind=kOutput, calls=%fused_computation.28 | convolution fusion | flops 8608808960 | bytes 33554432 | tf_op jit(solution)/shard_map/dot_general | solution.py:61
  704.1 9.0 convert_bitcast_fusion.2.g_ref
  713.2 214.3 %back_swap.1 = (bf16[8,512,256]{2,1,0:T(8,128)(2,1)}, bf16[8,512,128]{2,1,0:T(8,128)(2,1)S(1)}, bf16[4,512,1024]{2,1,0:T(8,128)(2,1)}, bf16[4,512,1024]{2,1,0:T(8,128)(2,1)}, bf16[4,1024,512]{2,1,0:T(8,128)(2,1)}) custom-call(bf16[8,512,384]{2,1,0:T(8,128)(2,1)} %get-tuple-element.72.packed_ref, bf16[8,512,256]{2,1,0:T(8,128)(2,1)} %convert_bitcast_fusion.2.g_ref, ...), custom_call_target="tpu_custom_call" | custom-call | flops 103079215104 | bytes 18874368 | tf_op jit(solution)/shard_map/back_swap/pallas_call | solution.py:1167
  980.6 6.9 convert_bitcast_fusion.1.out_ref
  998.0 14.6 %fusion.21 = (f32[2048]{0:T(1024)S(1)}, f32[512]{0:T(512)S(1)}, f32[512,2048,1]{1,0,2:T(8,128)}) fusion(bf16[512,2048]{1,0:T(8,128)(2,1)S(1)} %copy-done.16, f32[512]{0:T(512)S(1)} %copy-done.85, f32[2048]{0:T(1024)S(1)} %bitcast.120, bf16[8,2048,640]{2,1,0:T(8,128)(2,1)} %gather_weights.1, bf16[8,512,64]{1,2,0:T(8,128)(2,1)S(1)} %copy-done.61, ...), kind=kOutput, calls=%fused_computation.51 | convolution fusion | flops 6459225600 | bytes 22040576 | tf_op jit(solution)/shard_map/gtc,gdc->td/dot_general | solution.py:1369
  1012.8 6.9 fusion.24
  1019.7 9.8 convert_bitcast_fusion.in_ref
  1029.5 110.4 %sum_weights.1 = (f32[512,640]{1,0:T(8,128)}, bf16[8,512,128]{2,1,0:T(8,128)(2,1)S(1)}, f32[40,128]{1,0:T(8,128)S(1)}) custom-call(bf16[8,2048,384]{2,1,0:T(8,128)(2,1)} %convert_bitcast_fusion.in_ref, bf16[8,2048,256]{2,1,0:T(8,128)(2,1)} %convert_bitcast_fusion.1.out_ref, f32[40,128]{1,0:T(8,128)S(1)} %pad_bitcast_fusion.gain_ref), custom_call_target="tpu_custom_call" | custom-call | bytes 314572800 | tf_op jit(solution)/shard_map/sum_weights/pallas_call | solution.py:693
  (333 shorter events, 149.6 us)
Async XLA Ops:
  7.2 199.3 %all-gather.8.cloned.1.call-start = ((), (), s32[]{:S(2)}) async-start(), calls=%async_computation.5 | async-start | bytes 9437184 | tf_op jit(solution)/shard_map/all_gather | solution.py:1256
  10.6 195.9 %all-gather.6.cloned.1.call-start = ((), (), s32[]{:S(2)}) async-start(), calls=%async_computation.4 | async-start | bytes 9437184 | tf_op jit(solution)/shard_map/all_gather | solution.py:1255
  11.3 330.3 %all-gather.10.cloned.1.call-start = ((), (), s32[]{:S(2)}) async-start(), calls=%async_computation.6 | async-start | bytes 5242880 | tf_op jit(solution)/shard_map/all_gather | solution.py:1261
  11.6 151.0 %copy-start.17 = (f32[256,512]{0,1:T(8,128)}, f32[256,512]{0,1:T(8,128)S(1)}, u32[]{:S(2)}) copy-start(f32[256,512]{0,1:T(8,128)S(1)} %copy.118) | copy-start | bytes 1572868
  15.0 147.7 %copy-start.14 = (bf16[512,2048]{1,0:T(8,128)(2,1)S(1)}, bf16[512,2048]{1,0:T(8,128)(2,1)}, u32[]{:S(2)}) copy-start(bf16[512,2048]{1,0:T(8,128)(2,1)} %param.30) | copy-start | bytes 6291460
  15.0 148.8 %copy-start.69 = (f32[2,2048]{1,0:T(2,128)S(1)}, f32[2,2048]{1,0:T(2,128)}, u32[]{:S(2)}) copy-start(f32[2,2048]{1,0:T(2,128)} %param.54) | copy-start | bytes 49156
  162.7 269.8 %all-gather.12.cloned.1.call-start = ((), (), s32[]{:S(2)}) async-start(), calls=%async_computation.7 | async-start | bytes 9437184 | tf_op jit(solution)/shard_map/all_gather | solution.py:421
  180.8 14.4 %copy-start.51 = (f32[512,32]{0,1:T(8,128)}, f32[512,32]{0,1:T(8,128)S(1)}, u32[]{:S(2)}) copy-start(f32[512,32]{0,1:T(8,128)S(1)} %get-tuple-element.251) | copy-start | bytes 196612
  180.8 14.4 %copy-start.53 = (f32[512,32]{0,1:T(8,128)}, f32[512,32]{0,1:T(8,128)S(1)}, u32[]{:S(2)}) copy-start(f32[512,32]{0,1:T(8,128)S(1)} %get-tuple-element.252) | copy-start | bytes 196612
  181.0 20.3 %copy-start.31 = (f32[512,32]{1,0:T(8,128)}, f32[512,32]{1,0:T(8,128)S(1)}, u32[]{:S(2)}) copy-start(f32[512,32]{1,0:T(8,128)S(1)} %copy.122) | copy-start | bytes 196612
  185.4 13.8 %copy-start.64 = (f32[8,512]{1,0:T(8,128)}, f32[8,512]{1,0:T(8,128)S(1)}, u32[]{:S(2)}) copy-start(f32[8,512]{1,0:T(8,128)S(1)} %fusion.56) | copy-start | bytes 49156
  206.5 135.1 %copy-start.15 = (bf16[512,2048]{1,0:T(8,128)(2,1)S(1)}, bf16[512,2048]{1,0:T(8,128)(2,1)}, u32[]{:S(2)}) copy-start(bf16[512,2048]{1,0:T(8,128)(2,1)} %param.30) | copy-start | bytes 6291460
  352.1 163.0 %all-gather.14.cloned.1.call-start = ((), (), s32[]{:S(2)}) async-start(), calls=%async_computation.9 | async-start | bytes 9437184 | tf_op jit(solution)/shard_map/all_gather | solution.py:421
  352.7 340.8 %reduce-scatter.5.cloned.1.call-start = ((), (), s32[]{:S(2)}) async-start(), calls=%async_computation.8 | async-start | bytes 9437184 | tf_op jit(solution)/shard_map/reduce_scatter | solution.py:432
  352.7 15.0 %copy-start.102 = (bf16[1024,2048]{1,0:T(8,128)(2,1)S(1)}, bf16[1024,2048]{1,0:T(8,128)(2,1)}, u32[]{:S(2)}) copy-start(bf16[1024,2048]{1,0:T(8,128)(2,1)} %get-tuple-element.74) | copy-start | bytes 12582916
  432.5 14.7 %copy-start.93 = (bf16[2048,2048]{1,0:T(8,128)(2,1)S(1)}, bf16[2048,2048]{1,0:T(8,128)(2,1)}, u32[]{:S(2)}) copy-start(bf16[2048,2048]{1,0:T(8,128)(2,1)} %all-gather.12.cloned.1.call-done) | copy-start | bytes 25165828
  447.2 18.9 %copy-start.94 = (bf16[2048,1024]{1,0:T(8,128)(2,1)S(1)}, bf16[2048,1024]{1,0:T(8,128)(2,1)}, u32[]{:S(2)}) copy-start(bf16[2048,1024]{1,0:T(8,128)(2,1)} %all-gather.10.cloned.1.call-done) | copy-start | bytes 12582916
  466.1 14.0 %copy-start.96 = (bf16[4,512,1024]{2,1,0:T(8,128)(2,1)S(1)}, bf16[4,512,1024]{2,1,0:T(8,128)(2,1)}, u32[]{:S(2)}) copy-start(bf16[4,512,1024]{2,1,0:T(8,128)(2,1)} %get-tuple-element.78) | copy-start | bytes 12582916
  496.2 199.5 %reduce-scatter.7.cloned.1.call-start = ((), (), s32[]{:S(2)}) async-start(), calls=%async_computation.10 | async-start | bytes 9437184 | tf_op jit(solution)/shard_map/reduce_scatter | solution.py:432
  515.2 14.8 %copy-start.92 = (bf16[2048,2048]{1,0:T(8,128)(2,1)S(1)}, bf16[2048,2048]{1,0:T(8,128)(2,1)}, u32[]{:S(2)}) copy-start(bf16[2048,2048]{1,0:T(8,128)(2,1)} %all-gather.14.cloned.1.call-done) | copy-start | bytes 25165828
  529.9 17.3 %copy-start.95 = (bf16[2048,1024]{1,0:T(8,128)(2,1)S(1)}, bf16[2048,1024]{1,0:T(8,128)(2,1)}, u32[]{:S(2)}) copy-start(bf16[2048,1024]{1,0:T(8,128)(2,1)} %all-gather.10.cloned.1.call-done) | copy-start | bytes 12582916
  581.9 345.6 %reduce-scatter.9.cloned.1.call-start = ((), (), s32[]{:S(2)}) async-start(), calls=%async_computation.11 | async-start | bytes 9437184 | tf_op jit(solution)/shard_map/reduce_scatter | solution.py:1344
  581.9 15.1 %copy-start.101 = (bf16[2048,1024]{1,0:T(8,128)(2,1)S(1)}, bf16[2048,1024]{1,0:T(8,128)(2,1)}, u32[]{:S(2)}) copy-start(bf16[2048,1024]{1,0:T(8,128)(2,1)} %get-tuple-element.231) | copy-start | bytes 12582916
  597.0 13.7 %copy-start.103 = (bf16[1024,2048]{1,0:T(8,128)(2,1)S(1)}, bf16[1024,2048]{1,0:T(8,128)(2,1)}, u32[]{:S(2)}) copy-start(bf16[1024,2048]{1,0:T(8,128)(2,1)} %get-tuple-element.74) | copy-start | bytes 12582916
  648.9 28.7 %slice-start.2 = ((s8[8388608]{0:T(1024)(128)(4,1)}), s8[4194304]{0:T(1024)(128)(4,1)S(1)}, s32[]{:S(2)}) async-start(s8[8388608]{0:T(1024)(128)(4,1)} %bitcast.127), calls=%async_computation.15 | async-start | bytes 8388608
  662.1 15.4 %slice-start.3 = ((s8[8388608]{0:T(1024)(128)(4,1)}), s8[4194304]{0:T(1024)(128)(4,1)S(1)}, s32[]{:S(2)}) async-start(s8[8388608]{0:T(1024)(128)(4,1)} %bitcast.127), calls=%async_computation.16 | async-start | bytes 8388608
  662.1 15.4 %copy-start.100 = (bf16[2048,1024]{1,0:T(8,128)(2,1)S(1)}, bf16[2048,1024]{1,0:T(8,128)(2,1)}, u32[]{:S(2)}) copy-start(bf16[2048,1024]{1,0:T(8,128)(2,1)} %convolution_convert_fusion.2) | copy-start | bytes 12582916
  713.1 316.3 %reduce-scatter.11.cloned.1.call-start = ((), (), s32[]{:S(2)}) async-start(), calls=%async_computation.12 | async-start | bytes 9437184 | tf_op jit(solution)/shard_map/reduce_scatter | solution.py:1351
  997.7 14.9 %copy-start.45 = (bf16[8,512,4,64]{1,3,2,0:T(8,128)(2,1)}, bf16[8,512,4,64]{1,3,2,0:T(8,128)(2,1)S(1)}, u32[]{:S(2)}) copy-start(bf16[8,512,4,64]{1,3,2,0:T(8,128)(2,1)S(1)} %fusion.23) | copy-start | bytes 6291460
  998.0 14.6 %copy-start.73 = (f32[2048]{0:T(1024)S(1)}, f32[2048]{0:T(1024)}, u32[]{:S(2)}) copy-start(f32[2048]{0:T(1024)} %get-tuple-element.194) | copy-start | bytes 24580
  998.0 14.7 %copy-start.77 = (f32[512]{0:T(512)S(1)}, f32[512]{0:T(512)}, u32[]{:S(2)}) copy-start(f32[512]{0:T(512)} %copy-done.76) | copy-start | bytes 6148
  1029.5 110.6 %copy-start.42 = (f32[512,256]{1,0:T(8,128)S(1)}, f32[512,256]{1,0:T(8,128)}, u32[]{:S(2)}) copy-start(f32[512,256]{1,0:T(8,128)} %param.33) | copy-start | bytes 1572868
  (85 other events, 335.2 us)
Sparse Core Ops, SparseCore 0:
  10.7 107.7 all-gather.7
  120.7 81.7 all-gather.5
  204.9 126.2 all-gather.9
  352.2 80.2 all-gather.11
  434.5 80.5 all-gather.13
  517.3 88.1 reduce-scatter.4
  607.7 87.9 reduce-scatter.6
  713.3 169.7 reduce-scatter.8
  927.7 87.7 reduce-scatter.10

commit v9 on v8

--- a/solution.py
+++ b/solution.py
@@ -435,8 +435,9 @@
 
 
 def scatter_kernel(
-    in_ref, out_ref, gain_ref, sum_ref, spread_ref, gain_sum_ref,
-    own, other, halves, wholes, from_left, from_right, low, wide_gains, mid_gain, narrow_gains,
+    in_ref, out_ref, gain_ref, query_sum, output_sum, key_sum, value_sum, gain_sum_ref,
+    own, other, halves, wholes, from_left, from_right, spread_ref, low, wide_gains, mid_gain,
+    narrow_gains,
     load_sem, core_send, core_got, half_send, half_got, whole_send, whole_got,
     line_send, left_got, right_got, spread_send, spread_got, pass_send, pass_got,
     wide_send, wide_got, narrow_send, narrow_got,
@@ -445,7 +446,7 @@
     beside = narrow + 1 - 2 * (narrow % 2)
     across = (narrow + 2) % 4
     corner = (beside + 2) % 4
-    rows = sum_ref.shape[0]
+    rows = query_sum.shape[0]
     half_rows = rows // 2
     split = in_ref.shape[2]
     twin = (narrow, 2 * chip + 1 - core)
@@ -616,13 +617,12 @@
         add(target, from_right.at[chip], rows)
 
     lanes = pl.ds(split - 128, 128)
-
-    @pl.loop(0, rows // 64)
-    def _(i):
-        piece = pl.ds(pl.multiple_of(i * 64, 64), 64)
-        value = target[piece, :]
-        sum_ref[piece, :] = value.astype(f32)
-        low[piece, :] = target[piece, lanes]
+    for i in range(rows // 128):
+        piece = pl.ds(pl.multiple_of(narrow * rows + i * 128, 128), 128)
+        here = pl.ds(i * 128, 128)
+        query_sum[here, :] = own[chip, piece, pl.ds(0, split - 128)].astype(f32)
+        output_sum[:, here] = own[chip, piece, pl.ds(split, out_ref.shape[2])].astype(f32).T
+        low[here, :] = own[chip, piece, lanes]
 
     spread_ref[wide] = low[...]
 
@@ -660,6 +660,13 @@
         pass_on(step).wait_send()
     for step in (1, 2, 3):
         spread(step).wait_send()
+    first = low_lanes(rows)
+    for at in range(4):
+        even = spread_ref[2 * at].astype(f32)
+        odd = spread_ref[2 * at + 1].astype(f32)
+        here = pl.ds(at * 128, 128)
+        key_sum[:, here] = jnp.where(first, even, pltpu.roll(odd, 64, 1))
+        value_sum[:, here] = jnp.where(first, pltpu.roll(even, 64, 1), odd)
     for at in range(4):
         for k in range(2):
             exchange(at, k).wait_send()
@@ -671,17 +678,21 @@
             to_right(at).wait_send()
 
 
-def sum_weights(input_wgrad, output_wgrad, gains):
+def sum_weights(input_wgrad, output_wgrad, gains, key_heads):
     narrow_count = lax.axis_size("narrow")
     wide_count = lax.axis_size("wide")
     split = input_wgrad.shape[2]
-    if narrow_count != 4 or wide_count != 8:
+    if narrow_count != 4 or wide_count != 8 or key_heads != 8:
         total = jnp.concatenate([input_wgrad, output_wgrad], axis=2)
         total = lax.psum_scatter(total, "narrow", scatter_dimension=1, tiled=True)
         total = lax.psum_scatter(total, "wide", scatter_dimension=0)
         spread = lax.all_gather(total[:, split - 128 : split], "wide", axis=0)
+        spread = spread.reshape(key_heads, wide_count // key_heads, -1, 2, 64)
+        spread = jnp.sum(spread.astype(jnp.float32), axis=1).transpose(2, 1, 0, 3)
+        spread = spread.reshape(2, -1, key_heads * 64)
         gains = jnp.sum(lax.all_gather(gains, ("narrow", "wide"), axis=0), axis=0)
-        return total.astype(jnp.float32), spread, gains
+        total = total.astype(jnp.float32)
+        return total[:, : split - 128], total[:, split:].T, spread[0], spread[1], gains
     low = jnp.bfloat16
     rows = input_wgrad.shape[1] // 4
     columns = split + output_wgrad.shape[2]
@@ -690,11 +701,13 @@
     flat = jnp.pad(gains.reshape(-1), (0, gain_rows * 128 - size)).reshape(gain_rows, 128)
     dma = pltpu.SemaphoreType.DMA
     vmem = pltpu.VMEM
-    total, spread, flat = pl.pallas_call(
+    *sums, flat = pl.pallas_call(
         scatter_kernel,
         out_shape=[
-            jax.ShapeDtypeStruct((rows, columns), jnp.float32),
-            jax.ShapeDtypeStruct((8, rows, 128), low),
+            jax.ShapeDtypeStruct((rows, split - 128), jnp.float32),
+            jax.ShapeDtypeStruct((columns - split, rows), jnp.float32),
+            jax.ShapeDtypeStruct((rows, 512), jnp.float32),
+            jax.ShapeDtypeStruct((rows, 512), jnp.float32),
             jax.ShapeDtypeStruct(flat.shape, jnp.float32),
         ],
         in_specs=[
@@ -702,7 +715,7 @@
             pl.BlockSpec(memory_space=pl.ANY),
             pl.BlockSpec(memory_space=vmem),
         ],
-        out_specs=[pl.BlockSpec(memory_space=vmem)] * 3,
+        out_specs=[pl.BlockSpec(memory_space=vmem)] * 5,
         scratch_shapes=[
             vmem((4, 4 * rows, columns), low),
             vmem((4, 4 * rows, columns), low),
@@ -710,6 +723,7 @@
             vmem((4, 2, rows, columns), low),
             vmem((4, rows, columns), low),
             vmem((4, rows, columns), low),
+            vmem((8, rows, 128), low),
             vmem((rows, 128), low),
             vmem((7, gain_rows, 128), jnp.float32),
             vmem((gain_rows, 128), jnp.float32),
@@ -721,10 +735,10 @@
         compiler_params=pltpu.CompilerParams(
             collective_id=3, has_side_effects=True, vmem_limit_bytes=52 << 20
         ),
-        cost_estimate=pl.CostEstimate(flops=0, bytes_accessed=300 << 20, transcendentals=0),
+        cost_estimate=pl.CostEstimate(flops=0, bytes_accessed=1 << 20, transcendentals=0),
         name="sum_weights",
     )(input_wgrad, output_wgrad, flat)
-    return total, spread, flat.reshape(-1)[:size].reshape(gains.shape)
+    return *sums, flat.reshape(-1)[:size].reshape(gains.shape)
 
 
 def tell_all():
@@ -1203,6 +1217,164 @@
         ),
         name="back_swap",
     )(packed, grad, attended, weight_sums, gate, up, down)
+
+
+def swap_halves(values):
+    lane = lax.broadcasted_iota(jnp.int32, values.shape, 1)
+    return jnp.where(lane % 64 < 32, pltpu.roll(values, 96, 1), pltpu.roll(values, 32, 1))
+
+
+def head_mean(values):
+    row = lax.broadcasted_iota(jnp.int32, (128, 128), 0) < 64
+    lane = lax.broadcasted_iota(jnp.int32, (128, 128), 1) < 64
+    same = jnp.logical_or(
+        jnp.logical_and(row, lane),
+        jnp.logical_and(jnp.logical_not(row), jnp.logical_not(lane)),
+    )
+    spread = jnp.where(same, 1.0 / 64.0, 0.0).astype(jnp.bfloat16)
+    high = values.astype(jnp.bfloat16)
+    rest = (values - high.astype(jnp.float32)).astype(jnp.bfloat16)
+    return nn(high, spread) + nn(rest, spread)
+
+
+def project_kernel(pairs, rows_ref, weight_ref, cos_ref, sin_ref, gain_ref, src_ref, raw_ref):
+    low = low_lanes(rows_ref.shape[0])
+    raw_ref[0] = nn(rows_ref[...], weight_ref[0])
+    for pair in range(pairs + 1):
+        lanes = pl.ds(pair * 128, 128)
+        raw = raw_ref[0, :, lanes]
+        which = 0 if pair < pairs else 1
+        scaled = raw * lax.rsqrt(head_mean(raw * raw) + EPSILON) * gain_ref[which : which + 1, :]
+        turned = scaled * cos_ref[...] + swap_halves(scaled) * sin_ref[...]
+        if pair < pairs:
+            result = turned * (0.125 * LOG2E)
+        else:
+            result = jnp.where(low, turned, raw)
+        src_ref[0, :, lanes] = result.astype(jnp.bfloat16)
+
+
+def project(rows, weights, cosine, sine_part, gains, heads):
+    count, width, _ = weights.shape
+    length = rows.shape[0]
+    lanes = heads * 64 + 128
+    whole = lambda g: (0, 0)
+    group = lambda g: (g, 0, 0)
+    return pl.pallas_call(
+        functools.partial(project_kernel, heads // 2),
+        grid=(count,),
+        out_shape=[
+            jax.ShapeDtypeStruct((count, length, lanes), jnp.bfloat16),
+            jax.ShapeDtypeStruct((count, length, lanes), jnp.float32),
+        ],
+        in_specs=[
+            pl.BlockSpec((length, width), whole),
+            pl.BlockSpec((1, width, lanes), group),
+            pl.BlockSpec((length, 128), whole),
+            pl.BlockSpec((length, 128), whole),
+            pl.BlockSpec((2, 128), whole),
+        ],
+        out_specs=[pl.BlockSpec((1, length, lanes), group)] * 2,
+        compiler_params=pltpu.CompilerParams(vmem_limit_bytes=48 << 20),
+        cost_estimate=pl.CostEstimate(
+            flops=2 * count * length * width * lanes,
+            bytes_accessed=2 * count * width * lanes + 8 * count * length * lanes,
+            transcendentals=0,
+        ),
+        name="project",
+    )(rows, weights, cosine, sine_part, gains)
+
+
+def project_back_kernel(
+    pairs, dq_ref, dkv_ref, raw_ref, cos_ref, sin_ref, gain_ref, rows_ref, weight_ref,
+    branch_ref, att_ref, in_ref, out_ref, back_ref, gain_out, low_ref, rows_turned, branch_turned,
+):
+    length, width = rows_ref.shape
+    low = low_lanes(length)
+    step = 512
+
+    @pl.when(pl.program_id(0) == 0)
+    def _():
+        back_ref[...] = jnp.zeros_like(back_ref)
+        gain_out[...] = jnp.zeros_like(gain_out)
+
+        @pl.loop(0, width // step)
+        def _(i):
+            piece = pl.ds(pl.multiple_of(i * step, step), step)
+            rows_turned[piece, :] = rows_ref[:, piece].T
+            branch_turned[piece, :] = branch_ref[:, piece].T
+
+    for pair in range(pairs + 1):
+        lanes = pl.ds(pair * 128, 128)
+        last = pair == pairs
+        which = 1 if last else 0
+        turned = (dkv_ref[0] if last else dq_ref[0, :, lanes]).astype(jnp.float32)
+        raw = raw_ref[0, :, lanes]
+        inverse = lax.rsqrt(head_mean(raw * raw) + EPSILON)
+        unit = raw * inverse
+        scaled = turned * cos_ref[...] + swap_halves(turned * sin_ref[...])
+        part = jnp.sum(scaled * unit, axis=0, keepdims=True)
+        scaled = scaled * gain_ref[which : which + 1, :]
+        result = inverse * (scaled - unit * inverse * head_mean(scaled * raw))
+        if last:
+            result = jnp.where(low, result, turned)
+        gain_out[which : which + 1, :] += part
+        low_ref[:, lanes] = result.astype(jnp.bfloat16)
+
+    @pl.loop(0, width // step)
+    def _(i):
+        piece = pl.ds(pl.multiple_of(i * step, step), step)
+        in_ref[0, piece, :] = nn(rows_turned[piece, :], low_ref[...]).astype(jnp.bfloat16)
+        out_ref[0, piece, :] = nn(branch_turned[piece, :], att_ref[0]).astype(jnp.bfloat16)
+        back_ref[:, piece] += nt(low_ref[...], weight_ref[0, piece, :])
+
+
+def project_back(dq, dkv, raw, cosine, sine_part, gains, rows, weights, branch, attended, heads):
+    count, length, lanes = raw.shape
+    width = rows.shape[1]
+    split = heads * 64
+    low = jnp.bfloat16
+    whole = lambda g: (0, 0)
+    group = lambda g: (g, 0, 0)
+    return pl.pallas_call(
+        functools.partial(project_back_kernel, heads // 2),
+        grid=(count,),
+        out_shape=[
+            jax.ShapeDtypeStruct((count, width, lanes), low),
+            jax.ShapeDtypeStruct((count, width, split), low),
+            jax.ShapeDtypeStruct((length, width), jnp.float32),
+            jax.ShapeDtypeStruct((8, 128), jnp.float32),
+        ],
+        in_specs=[
+            pl.BlockSpec((1, length, split), group),
+            pl.BlockSpec((1, length, 128), group),
+            pl.BlockSpec((1, length, lanes), group),
+            pl.BlockSpec((length, 128), whole),
+            pl.BlockSpec((length, 128), whole),
+            pl.BlockSpec((2, 128), whole),
+            pl.BlockSpec((length, width), whole),
+            pl.BlockSpec((1, width, lanes), group),
+            pl.BlockSpec((length, width), whole),
+            pl.BlockSpec((1, length, split), group),
+        ],
+        out_specs=[
+            pl.BlockSpec((1, width, lanes), group),
+            pl.BlockSpec((1, width, split), group),
+            pl.BlockSpec((length, width), whole),
+            pl.BlockSpec((8, 128), whole),
+        ],
+        scratch_shapes=[
+            pltpu.VMEM((length, lanes), low),
+            pltpu.VMEM((width, length), low),
+            pltpu.VMEM((width, length), low),
+        ],
+        compiler_params=pltpu.CompilerParams(vmem_limit_bytes=48 << 20),
+        cost_estimate=pl.CostEstimate(
+            flops=2 * count * length * width * (2 * lanes + split),
+            bytes_accessed=count * width * (4 * lanes + 2 * split) + 8 * count * length * lanes,
+            transcendentals=0,
+        ),
+        name="project_back",
+    )(dq, dkv, raw, cosine, sine_part, gains, rows, weights, branch, attended)
 
 
 def shards(
@@ -1260,40 +1432,19 @@
     )
     gate_local = lax.all_gather(gate_own, "narrow", axis=0, tiled=True)
     group_columns = query_columns + 2 * head_dim
-    input_full = att_full[:, :, :group_columns]
     output_full = att_full[:, :, group_columns:]
     inverse = jnp.power(ROTARY_BASE, -2.0 * jnp.arange(head_dim // 2, dtype=jnp.float32) / head_dim)
     own_positions = lax.dynamic_slice_in_dim(positions, wide_rank * shard_rows, shard_rows, 0)
     angles = own_positions.astype(jnp.float32)[:, None] * inverse[None, :]
     cosine = jnp.cos(angles)
     sine_part = jnp.sin(angles)
+    cosine = jnp.concatenate([cosine] * 4, axis=1)
+    sine_part = jnp.concatenate([-sine_part, sine_part] * 2, axis=1)
+    lane_gains = jnp.concatenate([head_gains, head_gains], axis=1)
     residual = tokens_in.astype(jnp.float32)
     normed_in, norm_in_back = jax.vjp(rms_scale, residual, norm_gains[0])
     rows_in = normed_in.astype(jnp.bfloat16)
-    input_raw = jnp.einsum("td,gdc->gtc", rows_in, input_full, preferred_element_type=jnp.float32)
-    query_raw = input_raw[:, :, :query_columns].reshape(
-        wide_count, shard_rows, local_heads, head_dim
-    )
-    key_raw = input_raw[:, :, query_columns : query_columns + head_dim]
-    value_rows = input_raw[:, :, query_columns + head_dim :].astype(jnp.bfloat16)
-
-    def query_turn(raw_heads, gain):
-        return rotate(
-            rms_scale(raw_heads, gain), cosine[None, :, None, :], sine_part[None, :, None, :]
-        )
-
-    def key_turn(raw_heads, gain):
-        return rotate(rms_scale(raw_heads, gain), cosine[None], sine_part[None])
-
-    query_rot, query_back = jax.vjp(query_turn, query_raw, head_gains[0])
-    key_rot, key_back = jax.vjp(key_turn, key_raw, head_gains[1])
-    score_scale = head_dim ** (-0.5)
-    query_rot = (
-        (query_rot * (score_scale * LOG2E))
-        .reshape(wide_count, shard_rows, query_columns)
-        .astype(jnp.bfloat16)
-    )
-    packed = jnp.concatenate([query_rot, key_rot.astype(jnp.bfloat16), value_rows], axis=2)
+    packed, input_raw = project(rows_in, att_full, cosine, sine_part, lane_gains, local_heads)
     packed, grad_halves = lax.optimization_barrier((packed, grad_halves))
     packed, attended, weight_sums, attended_low, up_local, down_local = attend_swap(
         packed, up_weight.astype(jnp.bfloat16), down_weight.astype(jnp.bfloat16), local_heads
@@ -1337,9 +1488,6 @@
     attended_grad = jnp.einsum(
         "td,gdh->gth", branch_grad, output_full, preferred_element_type=jnp.float32
     ).astype(jnp.bfloat16)
-    output_wgrad = jnp.einsum(
-        "td,gth->gdh", branch_grad, attended_low, preferred_element_type=jnp.float32
-    )
     attended_grad, first_part = lax.optimization_barrier((attended_grad, block_parts[0]))
     first_sum = lax.psum_scatter(first_part, "wide", scatter_dimension=0, tiled=True)
     query_rot_grad, key_value_grad, gate_shares, up_shares, down_shares = back_swap(
@@ -1349,45 +1497,27 @@
         (query_rot_grad, first_sum, block_parts[1])
     )
     second_sum = lax.psum_scatter(second_part, "wide", scatter_dimension=0, tiled=True)
-    query_rot_grad = query_rot_grad.astype(jnp.float32).reshape(
-        wide_count, shard_rows, local_heads, head_dim
-    )
-    key_rot_grad = key_value_grad[:, :, :head_dim]
-    query_raw_grad, query_gain_grad = query_back(query_rot_grad)
-    key_raw_grad, key_gain_grad = key_back(key_rot_grad.astype(jnp.float32))
-    input_low = jnp.concatenate(
-        [
-            query_raw_grad.reshape(wide_count, shard_rows, query_columns).astype(jnp.bfloat16),
-            key_raw_grad.astype(jnp.bfloat16),
-            key_value_grad[:, :, head_dim:],
-        ],
-        axis=2,
-    )
-    input_wgrad = jnp.einsum(
-        "td,gtc->gdc", rows_in, input_low, preferred_element_type=jnp.float32
-    ).astype(jnp.bfloat16)
-    input_back = jnp.einsum("gtc,gdc->td", input_low, input_full, preferred_element_type=jnp.float32)
+    input_wgrad, output_wgrad, input_back, head_sums = project_back(
+        query_rot_grad, key_value_grad, input_raw, cosine, sine_part, lane_gains, rows_in,
+        att_full, branch_grad, attended_low, local_heads,
+    )
     input_part, in_gain_grad = norm_in_back(input_back)
     input_grad = middle_grad + input_part
     gain_stack = jnp.stack([in_gain_grad, mid_gain_grad])
-    head_stack = jnp.stack([query_gain_grad, key_gain_grad])
-    input_wgrad, second_sum = lax.optimization_barrier((input_wgrad, second_sum))
-    input_total, spread, gains = sum_weights(
+    head_stack = jnp.stack(
+        [head_sums[0, :head_dim] + head_sums[0, head_dim:], head_sums[1, :head_dim]]
+    )
+    query_total, output_total, key_total, value_total, gains = sum_weights(
         input_wgrad,
-        output_wgrad.astype(jnp.bfloat16),
+        output_wgrad,
         jnp.concatenate([gain_stack, head_stack], axis=1),
-    )
+        key_heads,
+    )
+    query_total, second_sum = lax.optimization_barrier((query_total, second_sum))
     block_sum = jnp.concatenate([first_sum, second_sum], axis=0).astype(jnp.float32)
     block_out = (middle + block_sum).astype(jnp.bfloat16)
     gain_total = gains[:, :model_width]
     head_total = gains[:, model_width:]
-    output_total = lax.optimization_barrier(input_total[:, group_columns:].T)
-    query_total = input_total[:, :query_columns]
-    spread = jnp.sum(
-        spread.reshape(key_heads, copies, -1, 2, head_dim).astype(jnp.float32), axis=1
-    ).transpose(2, 1, 0, 3)
-    key_total = spread[0].reshape(key_weight.shape)
-    value_total = spread[1].reshape(value_weight.shape)
     gate_total, up_total, down_total = (
         jnp.sum(gate_shares.astype(jnp.float32), axis=0),
         jnp.sum(up_shares.astype(jnp.float32), axis=0),

time: 1190 us -> 1150 us (0.966)
  Pallas kernels: 607 us -> 667 us
  local copies, waits for them, and re-layouts: 76 us -> 21.9 us
  matrix products: 327 us -> 287 us
  other arithmetic: 83.3 us -> 56.6 us
  waiting for transfers between devices: 73.2 us -> 85.8 us
    pallas_call x1 -> x3, Pallas kernels: 110 us -> 171 us  [the longest x1 112 us: sum_weights(): pl.pallas_call(scatter_kernel, out_shape=[jax.ShapeDtypeStruct((rows, spl...]
    dot_general x4 -> x0, matrix products: 40.6 us -> none  [the longest x1 14.6 us: shards(): jnp.einsum('gtc,gdc->td', input_low, input_full, preferred_element_type=j...]
    unnamed x235 -> x158, local copies, waits for them, and re-layouts: 45.9 us -> 15.2 us
    slice x5 -> x0, local copies, waits for them, and re-layouts: 12.7 us -> none  [the longest x2 7.77 us: shards(): input_raw[:, :, :query_columns]]
  transfers between devices with their start and end apart: 9 -> 9, of which waited for: 3 -> 3; matrix products, arithmetic and copies ran while one was open for 35% -> 28% of each run, Pallas kernels for 42% -> 59%
where the time goes in v9:
time: 1150 us; the launch traced here: 1130 us
  Pallas kernels  667 us (58%)
  matrix products  287 us (25%)
  waiting for transfers between devices  85.8 us (7%)
  other arithmetic  56.6 us (5%)
  local copies, waits for them, and re-layouts  21.9 us (2%)
  between operations  15 us (1%)
    pallas_call x1, Pallas kernels, back_swap(): pl.pallas_call(functools.partial(back_swap_kernel, heads), out_shape=[jax...  215 us
    pallas_call x1, Pallas kernels, gather_weights(): pl.pallas_call(gather_kernel, out_shape=jax.ShapeDtypeStruct((8, 4 * att....  148 us
    pallas_call x1, Pallas kernels, attend_swap(): pl.pallas_call(functools.partial(attend_swap_kernel, heads), out_shape=[j...  133 us
    pallas_call x1, Pallas kernels, sum_weights(): pl.pallas_call(scatter_kernel, out_shape=[jax.ShapeDtypeStruct((rows, spl...  112 us
    dot_general x6, matrix products, dot_back(): lax.dot_general(left, right, (((1,), (1,)), ((), ())), preferred_element_...  91.2 us
    dot_general x6, matrix products, dot_last(): return jnp.dot(left, right, preferred_element_type=jnp.float32)  91.1 us
    dot_general x6, matrix products, dot_first(): lax.dot_general(left, right, (((0,), (0,)), ((), ())), preferred_element_...  87.6 us
    all_gather x2, waiting for transfers between devices, gather_rows(): return lax.all_gather(shard, 'wide', axis=0, tiled=True)  73 us
  transfers between devices with their start and end apart: 9, of which 3 were waited for; matrix products, arithmetic and copies ran while one was open for 28% of the time, Pallas kernels for 59%

profile of v9, /device:TPU:0, one launch (start us, length us, event | category | flops | bytes accessed | tf_op | source)
XLA Modules:
  0.0 1133.1 jit_solution(15211476732555531179)
XLA Ops:
  14.9 147.6 %gather_weights.1.weight_ref = bf16[8,2048,640]{2,1,0:T(8,128)(2,1)} custom-call(bf16[512,640]{1,0:T(8,128)(2,1)} %pad_maximum_fusion.att_ref), custom_call_target="tpu_custom_call" | custom-call | bytes 314572800 | tf_op jit(solution)/shard_map/gather_weights/pallas_call | solution.py:406
  169.5 16.9 %project.1 = (bf16[8,512,384]{2,1,0:T(8,128)(2,1)S(1)}, f32[8,512,384]{2,1,0:T(8,128)}) custom-call(bf16[512,2048]{1,0:T(8,128)(2,1)S(1)} %fusion.16.rows_ref, bf16[8,2048,640]{2,1,0:T(8,128)(2,1)} %gather_weights.1.weight_ref, f32[512,128]{1,0:T(8,128)S(1)} %get-tuple-element.174.cos_ref, f32[512,128]{1,0:T(8,128)S(1)} %get-tuple-element.175.sin_ref, ...), custom_call_target="tpu_custom_call" | custom-call | flops 6442450944 | bytes 25165824 | tf_op jit(solution)/shard_map/project/pallas_call | solution.py:1262
  190.9 11.5 %all-gather.6.cloned.1.call-done = bf16[2048,2048]{1,0:T(8,128)(2,1)} async-done(((bf16[256,2048]{1,0:T(8,128)(2,1)}), bf16[2048,2048]{1,0:T(8,128)(2,1)}) %all-gather.6.cloned.1.call-update) | async-done | bytes 8388624 | tf_op jit(solution)/shard_map/all_gather | solution.py:1427
  202.3 133.2 %attend_swap.1 = (bf16[8,512,384]{2,1,0:T(8,128)(2,1)}, f32[4096,256]{1,0:T(8,128)}, f32[4096,256]{1,0:T(8,128)}, bf16[8,512,256]{2,1,0:T(8,128)(2,1)}, bf16[4,5...) custom-call(bf16[8,512,384]{2,1,0:T(8,128)(2,1)} %copy-done.6, bf16[512,1024]{1,0:T(8,128)(2,1)S(1)} %convert_element_type.112.up_ref, ...), custom_call_target="tpu_custom_call" | custom-call | flops 68719476736 | bytes 18874368 | tf_op jit(solution)/shard_map/attend_swap/pallas_call | solution.py:939
  335.5 7.8 multiply_reduce_fusion.2
  346.7 14.0 %convolution_convert_fusion.2 = bf16[2048,1024]{1,0:T(8,128)(2,1)} fusion(bf16[2048,2048]{1,0:T(8,128)(2,1)} %all-gather.8.cloned.1.call-done, bf16[1024,2048]{1,0:T(8,128)(2,1)} %get-tuple-element.83), kind=kOutput, calls=%fused_computation.54 | convolution fusion | flops 8592031744 | bytes 16777216 | tf_op jit(solution)/shard_map/dot_general | solution.py:67
  360.7 12.7 %convolution_convert_fusion.3 = bf16[2048,1024]{1,0:T(8,128)(2,1)} fusion(bf16[2048,2048]{1,0:T(8,128)(2,1)} %all-gather.6.cloned.1.call-done, bf16[1024,2048]{1,0:T(8,128)(2,1)S(1)} %copy-done.74), kind=kOutput, calls=%fused_computation.55 | convolution fusion | flops 8592031744 | bytes 16777216 | tf_op jit(solution)/shard_map/dot_general | solution.py:67
  373.4 54.0 %all-gather.12.cloned.1.call-done = bf16[2048,2048]{1,0:T(8,128)(2,1)} async-done(((bf16[256,2048]{1,0:T(8,128)(2,1)}), bf16[2048,2048]{1,0:T(8,128)(2,1)}) %all-gather.12.cloned.1.call-update) | async-done | bytes 8388624 | tf_op jit(solution)/shard_map/all_gather | solution.py:421
  427.5 14.6 %fusion.56 = f32[2048,1024]{1,0:T(8,128)} fusion(bf16[2048,2048]{1,0:T(8,128)(2,1)} %all-gather.12.cloned.1.call-done, bf16[2048,1024]{1,0:T(8,128)(2,1)} %all-gather.10.cloned.1.call-done), kind=kOutput, calls=%fused_computation.121 | convolution fusion | flops 8589934592 | bytes 20971520 | tf_op jit(solution)/shard_map/dot_general | solution.py:57
  442.0 19.0 %multiply_convert_fusion.1 = (bf16[2048,1024]{1,0:T(8,128)(2,1)}, bf16[2048,1024]{1,0:T(8,128)(2,1)}, bf16[2048,1024]{1,0:T(8,128)(2,1)}) fusion(f32[2048,1024]{1,0:T(8,128)} %fusion.56, bf16[2048,1024]{1,0:T(8,128)(2,1)} %convolution_convert_fusion.3, bf16[2048,2048]{1,0:T(8,128)(2,1)S(1)} %copy-done.66, bf16[2048,1024]{1,0:T(8,128)(2,1)} %bitcast.68), kind=kOutput, calls=%fused_computation.21 | convolution fusion | flops 8625586176 | bytes 37748736 | tf_op jit(solution)/shard_map/dot_general | solution.py:57
  461.1 14.1 %fusion.57 = f32[2048,2048]{1,0:T(8,128)} fusion(bf16[2048,1024]{1,0:T(8,128)(2,1)} %get-tuple-element.155, bf16[2048,1024]{1,0:T(8,128)(2,1)S(1)} %copy-done.67), kind=kOutput, calls=%fused_computation.122 | convolution fusion | flops 8589934592 | bytes 25165824 | tf_op jit(solution)/shard_map/dot_general | solution.py:67
  475.2 15.9 %add_convert_fusion.1 = bf16[2048,2048]{1,0:T(8,128)(2,1)} fusion(f32[2048,2048]{1,0:T(8,128)} %fusion.57, bf16[2048,1024]{1,0:T(8,128)(2,1)} %get-tuple-element.156, bf16[2048,1024]{1,0:T(8,128)(2,1)S(1)} %bitcast.71), kind=kOutput, calls=%fused_computation.1 | convolution fusion | flops 8598323200 | bytes 33554432 | tf_op jit(solution)/shard_map/dot_general | solution.py:67
  491.2 18.9 %all-gather.14.cloned.1.call-done = bf16[2048,2048]{1,0:T(8,128)(2,1)} async-done(((bf16[256,2048]{1,0:T(8,128)(2,1)}), bf16[2048,2048]{1,0:T(8,128)(2,1)}) %all-gather.14.cloned.1.call-update) | async-done | bytes 8388624 | tf_op jit(solution)/shard_map/all_gather | solution.py:421
  510.1 14.8 %fusion.58 = f32[2048,1024]{1,0:T(8,128)} fusion(bf16[2048,2048]{1,0:T(8,128)(2,1)} %all-gather.14.cloned.1.call-done, bf16[2048,1024]{1,0:T(8,128)(2,1)} %all-gather.10.cloned.1.call-done), kind=kOutput, calls=%fused_computation.123 | convolution fusion | flops 8589934592 | bytes 20971520 | tf_op jit(solution)/shard_map/dot_general | solution.py:57
  524.9 17.4 %multiply_convert_fusion = (bf16[2048,1024]{1,0:T(8,128)(2,1)}, bf16[2048,1024]{1,0:T(8,128)(2,1)}) fusion(f32[2048,1024]{1,0:T(8,128)} %fusion.58, bf16[2048,1024]{1,0:T(8,128)(2,1)} %convolution_convert_fusion.2, bf16[2048,2048]{1,0:T(8,128)(2,1)S(1)} %copy-done.65, bf16[2048,1024]{1,0:T(8,128)(2,1)} %bitcast.69), kind=kOutput, calls=%fused_computation.20 | convolution fusion | flops 8621391872 | bytes 33554432 | tf_op jit(solution)/shard_map/dot_general | solution.py:57
  542.3 14.0 %fusion.59 = f32[2048,2048]{1,0:T(8,128)} fusion(bf16[2048,1024]{1,0:T(8,128)(2,1)} %get-tuple-element.153, bf16[2048,1024]{1,0:T(8,128)(2,1)S(1)} %copy-done.68), kind=kOutput, calls=%fused_computation.124 | convolution fusion | flops 8589934592 | bytes 25165824 | tf_op jit(solution)/shard_map/dot_general | solution.py:67
  556.2 20.4 %add_convert_fusion = bf16[2048,2048]{1,0:T(8,128)(2,1)} fusion(f32[2048,2048]{1,0:T(8,128)} %fusion.59, bf16[2048,1024]{1,0:T(8,128)(2,1)} %bitcast.70, bf16[2048,1024]{1,0:T(8,128)(2,1)} %convolution_convert_fusion.2, f32[2048,1024]{1,0:T(8,128)} %fusion.58), kind=kOutput, calls=%fused_computation | convolution fusion | flops 8613003264 | bytes 41943040 | tf_op jit(solution)/shard_map/dot_general | solution.py:67
  576.8 15.1 %fusion.60 = f32[2048,1024]{1,0:T(8,128)} fusion(bf16[2048,2048]{1,0:T(8,128)(2,1)} %all-gather.12.cloned.1.call-done, bf16[2048,1024]{1,0:T(8,128)(2,1)} %get-tuple-element.155), kind=kOutput, calls=%fused_computation.125 | convolution fusion | flops 8589934592 | bytes 20971520 | tf_op jit(solution)/shard_map/dot_general | solution.py:61
  591.8 13.7 %fusion.61 = f32[2048,1024]{1,0:T(8,128)} fusion(bf16[2048,2048]{1,0:T(8,128)(2,1)} %all-gather.12.cloned.1.call-done, bf16[2048,1024]{1,0:T(8,128)(2,1)S(1)} %copy-done.73), kind=kOutput, calls=%fused_computation.126 | convolution fusion | flops 8589934592 | bytes 20971520 | tf_op jit(solution)/shard_map/dot_general | solution.py:61
  605.5 10.9 convolution_convert_fusion.1
  616.4 14.4 %convolution_convert_fusion = bf16[2048,2048]{1,0:T(8,128)(2,1)} fusion(bf16[2048,1024]{1,0:T(8,128)(2,1)} %get-tuple-element.152, bf16[1024,2048]{1,0:T(8,128)(2,1)} %get-tuple-element.83), kind=kOutput, calls=%fused_computation.33 | convolution fusion | flops 8594128896 | bytes 16777216 | tf_op jit(solution)/shard_map/dot_general | solution.py:57
  630.8 13.3 %fusion.62 = f32[1024,2048]{1,0:T(8,128)S(1)} fusion(bf16[2048,1024]{1,0:T(8,128)(2,1)} %get-tuple-element.154, bf16[2048,2048]{1,0:T(8,128)(2,1)} %all-gather.6.cloned.1.call-done), kind=kOutput, calls=%fused_computation.127 | convolution fusion | flops 8589934592 | bytes 20971520 | tf_op jit(solution)/shard_map/dot_general | solution.py:61
  644.1 13.8 %add_convert_fusion.2.down_ref = bf16[1024,2048]{1,0:T(8,128)(2,1)} fusion(f32[1024,2048]{1,0:T(8,128)S(1)} %fusion.62, bf16[2048,1024]{1,0:T(8,128)(2,1)S(1)} %copy-done.70, bf16[2048,2048]{1,0:T(8,128)(2,1)} %all-gather.8.cloned.1.call-done), kind=kOutput, calls=%fused_computation.19 | convolution fusion | flops 8594128896 | bytes 25165824 | tf_op jit(solution)/shard_map/dot_general | solution.py:61
  657.9 15.4 %add_convert_fusion.4.gate_ref = bf16[2048,1024]{1,0:T(8,128)(2,1)} fusion(f32[2048,1024]{1,0:T(8,128)} %fusion.60, bf16[2048,2048]{1,0:T(8,128)(2,1)} %all-gather.14.cloned.1.call-done, bf16[2048,1024]{1,0:T(8,128)(2,1)} %get-tuple-element.153), kind=kOutput, calls=%fused_computation.23 | convolution fusion | flops 8594128896 | bytes 25165824 | tf_op jit(solution)/shard_map/dot_general | solution.py:61
  673.4 16.3 %add_convert_fusion.3.up_ref = bf16[2048,1024]{1,0:T(8,128)(2,1)} fusion(f32[2048,1024]{1,0:T(8,128)} %fusion.61, bf16[2048,2048]{1,0:T(8,128)(2,1)S(1)} %bitcast.67, bf16[2048,1024]{1,0:T(8,128)(2,1)S(1)} %copy-done.72, f32[2048,1024]{1,0:T(8,128)} %fusion.58), kind=kOutput, calls=%fused_computation.22 | convolution fusion | flops 8608808960 | bytes 33554432 | tf_op jit(solution)/shard_map/dot_general | solution.py:61
  700.5 9.1 convert_bitcast_fusion.g_ref
  709.7 215.4 %back_swap.1 = (bf16[8,512,256]{2,1,0:T(8,128)(2,1)}, bf16[8,512,128]{2,1,0:T(8,128)(2,1)S(1)}, bf16[4,512,1024]{2,1,0:T(8,128)(2,1)}, bf16[4,512,1024]{2,1,0:T(8,128)(2,1)}, bf16[4,1024,512]{2,1,0:T(8,128)(2,1)}) custom-call(bf16[8,512,384]{2,1,0:T(8,128)(2,1)} %get-tuple-element.81.packed_ref, bf16[8,512,256]{2,1,0:T(8,128)(2,1)} %convert_bitcast_fusion.g_ref, ...), custom_call_target="tpu_custom_call" | custom-call | flops 103079215104 | bytes 18874368 | tf_op jit(solution)/shard_map/back_swap/pallas_call | solution.py:1181
  938.6 4.2 multiply_subtract_fusion.1
  943.4 4.2 multiply_subtract_fusion.2
  947.6 42.0 %project_back.1 = (bf16[8,2048,384]{2,1,0:T(8,128)(2,1)}, bf16[8,2048,256]{2,1,0:T(8,128)(2,1)}, f32[512,2048]{1,0:T(8,128)}, f32[8,128]{1,0:T(8,128)S(1)}) custom-call(bf16[8,512,256]{2,1,0:T(8,128)(2,1)S(1)} %copy-done.7, bf16[8,512,128]{2,1,0:T(8,128)(2,1)S(1)} %get-tuple-element.104.dkv_ref, f32[8,512,384]{2,1,0:T(8,128)} %get-tuple-element.105.raw_ref, ...), custom_call_target="tpu_custom_call" | custom-call | flops 17179869184 | bytes 46137344 | tf_op jit(solution)/shard_map/project_back/pallas_call | solution.py:1338
  993.5 111.6 %sum_weights.1 = (f32[512,256]{1,0:T(8,128)S(1)}, f32[256,512]{1,0:T(8,128)S(1)}, f32[512,512]{1,0:T(8,128)}, f32[512,512]{1,0:T(8,128)}, f32[40,128]{1,0:T(8,128)S(1)}) custom-call(bf16[8,2048,384]{2,1,0:T(8,128)(2,1)} %get-tuple-element.106.in_ref, bf16[8,2048,256]{2,1,0:T(8,128)(2,1)} %get-tuple-element.107.out_ref, f32[40,128]{1,0:T(8,128)S(1)} %pad_bitcast_fusion.gain_ref), custom_call_target="tpu_custom_call" | custom-call | bytes 1048576 | tf_op jit(solution)/shard_map/sum_weights/pallas_call | solution.py:704
  1115.7 9.2 fusion.19
  (225 shorter events, 62.7 us)
Async XLA Ops:
  7.2 183.6 %all-gather.8.cloned.1.call-start = ((), (), s32[]{:S(2)}) async-start(), calls=%async_computation.5 | async-start | bytes 9437184 | tf_op jit(solution)/shard_map/all_gather | solution.py:1428
  10.6 191.8 %all-gather.6.cloned.1.call-start = ((), (), s32[]{:S(2)}) async-start(), calls=%async_computation.4 | async-start | bytes 9437184 | tf_op jit(solution)/shard_map/all_gather | solution.py:1427
  11.3 324.2 %all-gather.10.cloned.1.call-start = ((), (), s32[]{:S(2)}) async-start(), calls=%async_computation.6 | async-start | bytes 5242880 | tf_op jit(solution)/shard_map/all_gather | solution.py:1433
  14.9 147.7 %copy-start.61 = (f32[2,64]{1,0:T(2,128)S(1)}, f32[2,64]{1,0:T(2,128)}, u32[]{:S(2)}) copy-start(f32[2,64]{1,0:T(2,128)} %param.57) | copy-start | bytes 1540
  14.9 147.8 %copy-start.11 = (bf16[512,2048]{1,0:T(8,128)(2,1)S(1)}, bf16[512,2048]{1,0:T(8,128)(2,1)}, u32[]{:S(2)}) copy-start(bf16[512,2048]{1,0:T(8,128)(2,1)} %param.30) | copy-start | bytes 6291460
  14.9 148.9 %copy-start.45 = (f32[2,2048]{1,0:T(2,128)S(1)}, f32[2,2048]{1,0:T(2,128)}, u32[]{:S(2)}) copy-start(f32[2,2048]{1,0:T(2,128)} %param.54) | copy-start | bytes 49156
  162.6 264.9 %all-gather.12.cloned.1.call-start = ((), (), s32[]{:S(2)}) async-start(), calls=%async_computation.7 | async-start | bytes 9437184 | tf_op jit(solution)/shard_map/all_gather | solution.py:421
  163.8 179.6 %copy-start.40 = (f32[1,2048]{1,0:T(1,128)}, f32[1,2048]{1,0:T(1,128)S(1)}, u32[]{:S(2)}) copy-start(f32[1,2048]{1,0:T(1,128)S(1)} %get-tuple-element.163) | copy-start | bytes 24580
  346.0 164.1 %all-gather.14.cloned.1.call-start = ((), (), s32[]{:S(2)}) async-start(), calls=%async_computation.9 | async-start | bytes 9437184 | tf_op jit(solution)/shard_map/all_gather | solution.py:421
  346.6 343.1 %reduce-scatter.5.cloned.1.call-start = ((), (), s32[]{:S(2)}) async-start(), calls=%async_computation.8 | async-start | bytes 9437184 | tf_op jit(solution)/shard_map/reduce_scatter | solution.py:432
  346.7 14.1 %copy-start.74 = (bf16[1024,2048]{1,0:T(8,128)(2,1)S(1)}, bf16[1024,2048]{1,0:T(8,128)(2,1)}, u32[]{:S(2)}) copy-start(bf16[1024,2048]{1,0:T(8,128)(2,1)} %get-tuple-element.83) | copy-start | bytes 12582916
  427.5 14.6 %copy-start.66 = (bf16[2048,2048]{1,0:T(8,128)(2,1)S(1)}, bf16[2048,2048]{1,0:T(8,128)(2,1)}, u32[]{:S(2)}) copy-start(bf16[2048,2048]{1,0:T(8,128)(2,1)} %all-gather.12.cloned.1.call-done) | copy-start | bytes 25165828
  442.0 19.0 %copy-start.67 = (bf16[2048,1024]{1,0:T(8,128)(2,1)S(1)}, bf16[2048,1024]{1,0:T(8,128)(2,1)}, u32[]{:S(2)}) copy-start(bf16[2048,1024]{1,0:T(8,128)(2,1)} %all-gather.10.cloned.1.call-done) | copy-start | bytes 12582916
  461.1 14.1 %copy-start.69 = (bf16[4,512,1024]{2,1,0:T(8,128)(2,1)S(1)}, bf16[4,512,1024]{2,1,0:T(8,128)(2,1)}, u32[]{:S(2)}) copy-start(bf16[4,512,1024]{2,1,0:T(8,128)(2,1)} %get-tuple-element.87) | copy-start | bytes 12582916
  491.1 200.1 %reduce-scatter.7.cloned.1.call-start = ((), (), s32[]{:S(2)}) async-start(), calls=%async_computation.10 | async-start | bytes 9437184 | tf_op jit(solution)/shard_map/reduce_scatter | solution.py:432
  510.1 14.8 %copy-start.65 = (bf16[2048,2048]{1,0:T(8,128)(2,1)S(1)}, bf16[2048,2048]{1,0:T(8,128)(2,1)}, u32[]{:S(2)}) copy-start(bf16[2048,2048]{1,0:T(8,128)(2,1)} %all-gather.14.cloned.1.call-done) | copy-start | bytes 25165828
  524.9 17.4 %copy-start.68 = (bf16[2048,1024]{1,0:T(8,128)(2,1)S(1)}, bf16[2048,1024]{1,0:T(8,128)(2,1)}, u32[]{:S(2)}) copy-start(bf16[2048,1024]{1,0:T(8,128)(2,1)} %all-gather.10.cloned.1.call-done) | copy-start | bytes 12582916
  576.7 348.4 %reduce-scatter.9.cloned.1.call-start = ((), (), s32[]{:S(2)}) async-start(), calls=%async_computation.11 | async-start | bytes 9437184 | tf_op jit(solution)/shard_map/reduce_scatter | solution.py:1492
  576.8 15.1 %copy-start.73 = (bf16[2048,1024]{1,0:T(8,128)(2,1)S(1)}, bf16[2048,1024]{1,0:T(8,128)(2,1)}, u32[]{:S(2)}) copy-start(bf16[2048,1024]{1,0:T(8,128)(2,1)} %get-tuple-element.156) | copy-start | bytes 12582916
  591.8 13.7 %copy-start.71 = (bf16[2048,1024]{1,0:T(8,128)(2,1)S(1)}, bf16[2048,1024]{1,0:T(8,128)(2,1)}, u32[]{:S(2)}) copy-start(bf16[2048,1024]{1,0:T(8,128)(2,1)} %get-tuple-element.154) | copy-start | bytes 12582916
  591.8 13.7 %copy-start.75 = (bf16[1024,2048]{1,0:T(8,128)(2,1)S(1)}, bf16[1024,2048]{1,0:T(8,128)(2,1)}, u32[]{:S(2)}) copy-start(bf16[1024,2048]{1,0:T(8,128)(2,1)} %get-tuple-element.83) | copy-start | bytes 12582916
  644.1 29.2 %slice-start = ((s8[8388608]{0:T(1024)(128)(4,1)}), s8[4194304]{0:T(1024)(128)(4,1)S(1)}, s32[]{:S(2)}) async-start(s8[8388608]{0:T(1024)(128)(4,1)} %bitcast.66), calls=%async_computation.13 | async-start | bytes 8388608
  657.9 15.4 %slice-start.1 = ((s8[8388608]{0:T(1024)(128)(4,1)}), s8[4194304]{0:T(1024)(128)(4,1)S(1)}, s32[]{:S(2)}) async-start(s8[8388608]{0:T(1024)(128)(4,1)} %bitcast.66), calls=%async_computation.14 | async-start | bytes 8388608
  657.9 15.4 %copy-start.72 = (bf16[2048,1024]{1,0:T(8,128)(2,1)S(1)}, bf16[2048,1024]{1,0:T(8,128)(2,1)}, u32[]{:S(2)}) copy-start(bf16[2048,1024]{1,0:T(8,128)(2,1)} %convolution_convert_fusion.2) | copy-start | bytes 12582916
  709.6 406.0 %reduce-scatter.11.cloned.1.call-start = ((), (), s32[]{:S(2)}) async-start(), calls=%async_computation.12 | async-start | bytes 9437184 | tf_op jit(solution)/shard_map/reduce_scatter | solution.py:1499
  947.6 42.1 %copy-start.12 = (bf16[512,2048]{1,0:T(8,128)(2,1)S(1)}, bf16[512,2048]{1,0:T(8,128)(2,1)}, u32[]{:S(2)}) copy-start(bf16[512,2048]{1,0:T(8,128)(2,1)} %param.30) | copy-start | bytes 6291460
  947.6 42.1 %copy-start.44 = (f32[1,2048]{1,0:T(1,128)S(1)}, f32[1,2048]{1,0:T(1,128)}, u32[]{:S(2)}) copy-start(f32[1,2048]{1,0:T(1,128)} %copy-done.43) | copy-start | bytes 24580
  947.6 42.1 %copy-start.51 = (f32[512]{0:T(512)S(1)}, f32[512]{0:T(512)}, u32[]{:S(2)}) copy-start(f32[512]{0:T(512)} %copy-done.50) | copy-start | bytes 6148
  993.4 111.8 %copy-start.56 = (f32[512]{0:T(512)S(1)}, f32[512]{0:T(512)}, u32[]{:S(2)}) copy-start(f32[512]{0:T(512)} %copy-done.55) | copy-start | bytes 6148
  993.4 111.8 %copy-start.62 = (f32[2,64]{1,0:T(2,128)S(1)}, f32[2,64]{1,0:T(2,128)}, u32[]{:S(2)}) copy-start(f32[2,64]{1,0:T(2,128)} %param.57) | copy-start | bytes 1540
  993.4 111.8 %copy-start.63 = (f32[2,64]{1,0:T(2,128)S(1)}, f32[2,64]{1,0:T(2,128)}, u32[]{:S(2)}) copy-start(f32[2,64]{1,0:T(2,128)} %param.58) | copy-start | bytes 1540
  993.5 111.8 %copy-start.64 = (f32[2,64]{1,0:T(2,128)S(1)}, f32[2,64]{1,0:T(2,128)}, u32[]{:S(2)}) copy-start(f32[2,64]{1,0:T(2,128)} %param.59) | copy-start | bytes 1540
  (55 other events, 200.7 us)
Sparse Core Ops, SparseCore 0:
  10.7 107.6 all-gather.7
  120.6 81.7 all-gather.5
  204.7 121.3 all-gather.9
  346.1 81.2 all-gather.11
  429.5 80.5 all-gather.13
  512.2 88.1 reduce-scatter.4
  602.7 87.9 reduce-scatter.6
  709.7 170.1 reduce-scatter.8
  925.2 90.4 reduce-scatter.10

commit v10 on v9

--- a/solution.py
+++ b/solution.py
@@ -776,17 +776,37 @@
             return down_all.at[:, pl.ds(pl.multiple_of(who * columns, columns), columns)]
         return up_all.at[who]
 
-    def ffn(k, step):
+    beside = narrow + 1 - 2 * (narrow % 2)
+    across = (narrow + 2) % 4
+    corner = (beside + 2) % 4
+    near = (beside, across)
+    sides = ((beside, wide), (across, wide))
+
+    def ffn_half(k, who, half):
+        size = (up_ref, down_ref)[k].shape[0] // 2
+        if k:
+            return down_all.at[
+                pl.ds(half * size, size), pl.ds(pl.multiple_of(who * columns, columns), columns)
+            ]
+        return up_all.at[who, pl.ds(half * size, size), :]
+
+    def ffn(k, j):
         return remote(
-            (up_ref, down_ref)[k], ffn_slot(k, narrow), ffn_send.at[k, step],
-            ffn_got.at[k, step], ((narrow + step) % 4, wide),
-        )
-
-    def ffn_arrival(k, step):
-        target = ffn_slot(k, (narrow + 4 - step) % 4)
-        return remote(
-            target, target, ffn_send.at[k, step], ffn_got.at[k, step], ((narrow + step) % 4, wide)
-        )
+            (up_ref, down_ref)[k], ffn_slot(k, narrow), ffn_send.at[k, j], ffn_got.at[k, j],
+            sides[j],
+        )
+
+    def ffn_arrival(k, j):
+        target = ffn_slot(k, near[j])
+        return remote(target, target, ffn_send.at[k, j], ffn_got.at[k, j], sides[j])
+
+    def ffn_forward(k, j):
+        piece = ffn_half(k, near[j], j)
+        return remote(piece, piece, ffn_send.at[k, 2 + j], ffn_got.at[k, 2 + j], sides[1 - j])
+
+    def ffn_corner(k, j):
+        piece = ffn_half(k, corner, j)
+        return remote(piece, piece, ffn_send.at[k, 2 + j], ffn_got.at[k, 2 + j], sides[1 - j])
 
     def send(to):
         return remote(
@@ -812,8 +832,8 @@
     ]
     for k in (1, 0):
         keep[k].start()
-        for step in range(1, 4):
-            ffn(k, step).start()
+        for j in range(2):
+            ffn(k, j).start()
 
     def prepare(j):
         rows = pl.ds(pl.multiple_of(j * block, block), block)
@@ -896,6 +916,10 @@
             finish(i)
 
     await_blocks(away)
+    for k in (1, 0):
+        for j in range(2):
+            ffn_arrival(k, j).wait_recv()
+            ffn_forward(k, j).start()
 
     @pl.loop(away, away + 4)
     def _(i):
@@ -917,9 +941,10 @@
         send(to).wait_send()
     for k in range(2):
         keep[k].wait()
-        for step in range(1, 4):
-            ffn_arrival(k, step).wait_recv()
-            ffn(k, step).wait_send()
+        for j in range(2):
+            ffn_corner(k, j).wait_recv()
+            ffn_forward(k, j).wait_send()
+            ffn(k, j).wait_send()
 
 
 def attend_swap(src, up, down, heads):
@@ -1488,14 +1513,13 @@
     attended_grad = jnp.einsum(
         "td,gdh->gth", branch_grad, output_full, preferred_element_type=jnp.float32
     ).astype(jnp.bfloat16)
-    attended_grad, first_part = lax.optimization_barrier((attended_grad, block_parts[0]))
-    first_sum = lax.psum_scatter(first_part, "wide", scatter_dimension=0, tiled=True)
     query_rot_grad, key_value_grad, gate_shares, up_shares, down_shares = back_swap(
         packed, attended_grad, attended, weight_sums, gate_wgrad, up_wgrad, down_wgrad, local_heads
     )
-    query_rot_grad, first_sum, second_part = lax.optimization_barrier(
-        (query_rot_grad, first_sum, block_parts[1])
-    )
+    query_rot_grad, first_part, second_part = lax.optimization_barrier(
+        (query_rot_grad, block_parts[0], block_parts[1])
+    )
+    first_sum = lax.psum_scatter(first_part, "wide", scatter_dimension=0, tiled=True)
     second_sum = lax.psum_scatter(second_part, "wide", scatter_dimension=0, tiled=True)
     input_wgrad, output_wgrad, input_back, head_sums = project_back(
         query_rot_grad, key_value_grad, input_raw, cosine, sine_part, lane_gains, rows_in,
@@ -1513,7 +1537,9 @@
         jnp.concatenate([gain_stack, head_stack], axis=1),
         key_heads,
     )
-    query_total, second_sum = lax.optimization_barrier((query_total, second_sum))
+    query_total, first_sum, second_sum = lax.optimization_barrier(
+        (query_total, first_sum, second_sum)
+    )
     block_sum = jnp.concatenate([first_sum, second_sum], axis=0).astype(jnp.float32)
     block_out = (middle + block_sum).astype(jnp.bfloat16)
     gain_total = gains[:, :model_width]

time: 1150 us -> 1160 us (level)
  waiting for transfers between devices: 85.8 us -> 108 us
  Pallas kernels: 667 us -> 650 us
    pallas_call x1, Pallas kernels: 215 us -> 178 us  [back_swap(): pl.pallas_call(functools.partial(back_swap_kernel, heads), out_shape=[jax...]
    pallas_call x1, Pallas kernels: 112 us -> 139 us  [sum_weights(): pl.pallas_call(scatter_kernel, out_shape=[jax.ShapeDtypeStruct((rows, spl...]
    all_gather x2, waiting for transfers between devices: 73 us -> 90.7 us  [gather_rows(): return lax.all_gather(shard, 'wide', axis=0, tiled=True)]
  transfers between devices with their start and end apart: 9 -> 9, of which waited for: 3 -> 5; matrix products, arithmetic and copies ran while one was open for 28% -> 27% of each run, Pallas kernels for 59% -> 41%
where the time goes in v10:
time: 1160 us; the launch traced here: 1140 us
  Pallas kernels  650 us (56%)
  matrix products  286 us (25%)
  waiting for transfers between devices  108 us (9%)
  other arithmetic  52.8 us (5%)
  local copies, waits for them, and re-layouts  26.2 us (2%)
  between operations  15 us (1%)
    pallas_call x1, Pallas kernels, back_swap(): pl.pallas_call(functools.partial(back_swap_kernel, heads), out_shape=[jax...  178 us
    pallas_call x1, Pallas kernels, gather_weights(): pl.pallas_call(gather_kernel, out_shape=jax.ShapeDtypeStruct((8, 4 * att....  148 us
    pallas_call x1, Pallas kernels, sum_weights(): pl.pallas_call(scatter_kernel, out_shape=[jax.ShapeDtypeStruct((rows, spl...  139 us
    pallas_call x1, Pallas kernels, attend_swap(): pl.pallas_call(functools.partial(attend_swap_kernel, heads), out_shape=[j...  128 us
    dot_general x6, matrix products, dot_back(): lax.dot_general(left, right, (((1,), (1,)), ((), ())), preferred_element_...  91.2 us
    dot_general x6, matrix products, dot_last(): return jnp.dot(left, right, preferred_element_type=jnp.float32)  90.9 us
    all_gather x2, waiting for transfers between devices, gather_rows(): return lax.all_gather(shard, 'wide', axis=0, tiled=True)  90.7 us
    dot_general x6, matrix products, dot_first(): lax.dot_general(left, right, (((0,), (0,)), ((), ())), preferred_element_...  86.2 us
  transfers between devices with their start and end apart: 9, of which 5 were waited for; matrix products, arithmetic and copies ran while one was open for 27% of the time, Pallas kernels for 41%

profile of v10, /device:TPU:0, one launch (start us, length us, event | category | flops | bytes accessed | tf_op | source)
XLA Modules:
  0.0 1138.9 jit_solution(16386715680969691928)
XLA Ops:
  14.9 147.6 %gather_weights.1.weight_ref = bf16[8,2048,640]{2,1,0:T(8,128)(2,1)} custom-call(bf16[512,640]{1,0:T(8,128)(2,1)} %pad_maximum_fusion.att_ref), custom_call_target="tpu_custom_call" | custom-call | bytes 314572800 | tf_op jit(solution)/shard_map/gather_weights/pallas_call | solution.py:406
  169.6 16.7 %project.1 = (bf16[8,512,384]{2,1,0:T(8,128)(2,1)S(1)}, f32[8,512,384]{2,1,0:T(8,128)}) custom-call(bf16[512,2048]{1,0:T(8,128)(2,1)S(1)} %fusion.16.rows_ref, bf16[8,2048,640]{2,1,0:T(8,128)(2,1)} %gather_weights.1.weight_ref, f32[512,128]{1,0:T(8,128)S(1)} %get-tuple-element.172.cos_ref, f32[512,128]{1,0:T(8,128)S(1)} %get-tuple-element.173.sin_ref, ...), custom_call_target="tpu_custom_call" | custom-call | flops 6442450944 | bytes 25165824 | tf_op jit(solution)/shard_map/project/pallas_call | solution.py:1287
  190.6 11.7 %all-gather.6.cloned.1.call-done = bf16[2048,2048]{1,0:T(8,128)(2,1)} async-done(((bf16[256,2048]{1,0:T(8,128)(2,1)}), bf16[2048,2048]{1,0:T(8,128)(2,1)}) %all-gather.6.cloned.1.call-update) | async-done | bytes 8388624 | tf_op jit(solution)/shard_map/all_gather | solution.py:1452
  202.3 127.9 %attend_swap.1 = (bf16[8,512,384]{2,1,0:T(8,128)(2,1)}, f32[4096,256]{1,0:T(8,128)}, f32[4096,256]{1,0:T(8,128)}, bf16[8,512,256]{2,1,0:T(8,128)(2,1)}, bf16[4,5...) custom-call(bf16[8,512,384]{2,1,0:T(8,128)(2,1)} %copy-done.8, bf16[512,1024]{1,0:T(8,128)(2,1)S(1)} %convert_element_type.111.up_ref, ...), custom_call_target="tpu_custom_call" | custom-call | flops 68719476736 | bytes 18874368 | tf_op jit(solution)/shard_map/attend_swap/pallas_call | solution.py:964
  330.2 7.8 multiply_reduce_fusion.2
  341.4 14.0 %convolution_convert_fusion.2 = bf16[2048,1024]{1,0:T(8,128)(2,1)} fusion(bf16[2048,2048]{1,0:T(8,128)(2,1)} %all-gather.8.cloned.1.call-done, bf16[1024,2048]{1,0:T(8,128)(2,1)} %get-tuple-element.82), kind=kOutput, calls=%fused_computation.54 | convolution fusion | flops 8592031744 | bytes 16777216 | tf_op jit(solution)/shard_map/dot_general | solution.py:67
  355.4 12.6 %convolution_convert_fusion.3 = bf16[2048,1024]{1,0:T(8,128)(2,1)} fusion(bf16[2048,2048]{1,0:T(8,128)(2,1)} %all-gather.6.cloned.1.call-done, bf16[1024,2048]{1,0:T(8,128)(2,1)S(1)} %copy-done.82), kind=kOutput, calls=%fused_computation.55 | convolution fusion | flops 8592031744 | bytes 16777216 | tf_op jit(solution)/shard_map/dot_general | solution.py:67
  368.0 71.7 %all-gather.12.cloned.1.call-done = bf16[2048,2048]{1,0:T(8,128)(2,1)} async-done(((bf16[256,2048]{1,0:T(8,128)(2,1)}), bf16[2048,2048]{1,0:T(8,128)(2,1)}) %all-gather.12.cloned.1.call-update) | async-done | bytes 8388624 | tf_op jit(solution)/shard_map/all_gather | solution.py:421
  439.8 14.6 %fusion.56 = f32[2048,1024]{1,0:T(8,128)} fusion(bf16[2048,2048]{1,0:T(8,128)(2,1)} %all-gather.12.cloned.1.call-done, bf16[2048,1024]{1,0:T(8,128)(2,1)} %all-gather.10.cloned.1.call-done), kind=kOutput, calls=%fused_computation.121 | convolution fusion | flops 8589934592 | bytes 20971520 | tf_op jit(solution)/shard_map/dot_general | solution.py:57
  454.3 18.9 %multiply_convert_fusion.1 = (bf16[2048,1024]{1,0:T(8,128)(2,1)}, bf16[2048,1024]{1,0:T(8,128)(2,1)}, bf16[2048,1024]{1,0:T(8,128)(2,1)}) fusion(f32[2048,1024]{1,0:T(8,128)} %fusion.56, bf16[2048,1024]{1,0:T(8,128)(2,1)} %convolution_convert_fusion.3, bf16[2048,2048]{1,0:T(8,128)(2,1)S(1)} %copy-done.74, bf16[2048,1024]{1,0:T(8,128)(2,1)} %bitcast.68), kind=kOutput, calls=%fused_computation.21 | convolution fusion | flops 8625586176 | bytes 37748736 | tf_op jit(solution)/shard_map/dot_general | solution.py:57
  473.2 14.1 %fusion.57 = f32[2048,2048]{1,0:T(8,128)} fusion(bf16[2048,1024]{1,0:T(8,128)(2,1)} %get-tuple-element.153, bf16[2048,1024]{1,0:T(8,128)(2,1)S(1)} %copy-done.75), kind=kOutput, calls=%fused_computation.122 | convolution fusion | flops 8589934592 | bytes 25165824 | tf_op jit(solution)/shard_map/dot_general | solution.py:67
  487.3 16.1 %add_convert_fusion.1 = bf16[2048,2048]{1,0:T(8,128)(2,1)} fusion(f32[2048,2048]{1,0:T(8,128)} %fusion.57, bf16[2048,1024]{1,0:T(8,128)(2,1)} %get-tuple-element.154, bf16[2048,1024]{1,0:T(8,128)(2,1)S(1)} %bitcast.71), kind=kOutput, calls=%fused_computation.1 | convolution fusion | flops 8598323200 | bytes 33554432 | tf_op jit(solution)/shard_map/dot_general | solution.py:67
  503.5 18.9 %all-gather.14.cloned.1.call-done = bf16[2048,2048]{1,0:T(8,128)(2,1)} async-done(((bf16[256,2048]{1,0:T(8,128)(2,1)}), bf16[2048,2048]{1,0:T(8,128)(2,1)}) %all-gather.14.cloned.1.call-update) | async-done | bytes 8388624 | tf_op jit(solution)/shard_map/all_gather | solution.py:421
  522.4 14.7 %fusion.58 = f32[2048,1024]{1,0:T(8,128)} fusion(bf16[2048,2048]{1,0:T(8,128)(2,1)} %all-gather.14.cloned.1.call-done, bf16[2048,1024]{1,0:T(8,128)(2,1)} %all-gather.10.cloned.1.call-done), kind=kOutput, calls=%fused_computation.123 | convolution fusion | flops 8589934592 | bytes 20971520 | tf_op jit(solution)/shard_map/dot_general | solution.py:57
  537.1 17.4 %multiply_convert_fusion = (bf16[2048,1024]{1,0:T(8,128)(2,1)}, bf16[2048,1024]{1,0:T(8,128)(2,1)}) fusion(f32[2048,1024]{1,0:T(8,128)} %fusion.58, bf16[2048,1024]{1,0:T(8,128)(2,1)} %convolution_convert_fusion.2, bf16[2048,2048]{1,0:T(8,128)(2,1)S(1)} %copy-done.73, bf16[2048,1024]{1,0:T(8,128)(2,1)} %bitcast.69), kind=kOutput, calls=%fused_computation.20 | convolution fusion | flops 8621391872 | bytes 33554432 | tf_op jit(solution)/shard_map/dot_general | solution.py:57
  554.5 14.0 %fusion.59 = f32[2048,2048]{1,0:T(8,128)} fusion(bf16[2048,1024]{1,0:T(8,128)(2,1)} %get-tuple-element.151, bf16[2048,1024]{1,0:T(8,128)(2,1)S(1)} %copy-done.76), kind=kOutput, calls=%fused_computation.124 | convolution fusion | flops 8589934592 | bytes 25165824 | tf_op jit(solution)/shard_map/dot_general | solution.py:67
  568.5 20.5 %add_convert_fusion = bf16[2048,2048]{1,0:T(8,128)(2,1)} fusion(f32[2048,2048]{1,0:T(8,128)} %fusion.59, bf16[2048,1024]{1,0:T(8,128)(2,1)} %bitcast.70, bf16[2048,1024]{1,0:T(8,128)(2,1)} %convolution_convert_fusion.2, f32[2048,1024]{1,0:T(8,128)} %fusion.58), kind=kOutput, calls=%fused_computation | convolution fusion | flops 8613003264 | bytes 41943040 | tf_op jit(solution)/shard_map/dot_general | solution.py:67
  589.0 15.1 %fusion.60 = f32[2048,1024]{1,0:T(8,128)} fusion(bf16[2048,2048]{1,0:T(8,128)(2,1)} %all-gather.12.cloned.1.call-done, bf16[2048,1024]{1,0:T(8,128)(2,1)} %get-tuple-element.153), kind=kOutput, calls=%fused_computation.125 | convolution fusion | flops 8589934592 | bytes 20971520 | tf_op jit(solution)/shard_map/dot_general | solution.py:61
  604.1 13.7 %fusion.61 = f32[2048,1024]{1,0:T(8,128)} fusion(bf16[2048,2048]{1,0:T(8,128)(2,1)} %all-gather.12.cloned.1.call-done, bf16[2048,1024]{1,0:T(8,128)(2,1)S(1)} %copy-done.81), kind=kOutput, calls=%fused_computation.126 | convolution fusion | flops 8589934592 | bytes 20971520 | tf_op jit(solution)/shard_map/dot_general | solution.py:61
  617.8 10.9 convolution_convert_fusion.1
  628.8 14.4 %convolution_convert_fusion = bf16[2048,2048]{1,0:T(8,128)(2,1)} fusion(bf16[2048,1024]{1,0:T(8,128)(2,1)} %get-tuple-element.150, bf16[1024,2048]{1,0:T(8,128)(2,1)} %get-tuple-element.82), kind=kOutput, calls=%fused_computation.33 | convolution fusion | flops 8594128896 | bytes 16777216 | tf_op jit(solution)/shard_map/dot_general | solution.py:57
  643.2 12.8 %fusion.62 = f32[1024,2048]{1,0:T(8,128)S(1)} fusion(bf16[2048,1024]{1,0:T(8,128)(2,1)} %get-tuple-element.152, bf16[2048,2048]{1,0:T(8,128)(2,1)} %all-gather.6.cloned.1.call-done), kind=kOutput, calls=%fused_computation.127 | convolution fusion | flops 8589934592 | bytes 20971520 | tf_op jit(solution)/shard_map/dot_general | solution.py:61
  656.0 13.2 %add_convert_fusion.2.down_ref = bf16[1024,2048]{1,0:T(8,128)(2,1)} fusion(f32[1024,2048]{1,0:T(8,128)S(1)} %fusion.62, bf16[2048,1024]{1,0:T(8,128)(2,1)S(1)} %copy-done.78, bf16[2048,2048]{1,0:T(8,128)(2,1)} %all-gather.8.cloned.1.call-done), kind=kOutput, calls=%fused_computation.19 | convolution fusion | flops 8594128896 | bytes 25165824 | tf_op jit(solution)/shard_map/dot_general | solution.py:61
  669.2 15.4 %add_convert_fusion.4.gate_ref = bf16[2048,1024]{1,0:T(8,128)(2,1)} fusion(f32[2048,1024]{1,0:T(8,128)} %fusion.60, bf16[2048,2048]{1,0:T(8,128)(2,1)} %all-gather.14.cloned.1.call-done, bf16[2048,1024]{1,0:T(8,128)(2,1)} %get-tuple-element.151), kind=kOutput, calls=%fused_computation.23 | convolution fusion | flops 8594128896 | bytes 25165824 | tf_op jit(solution)/shard_map/dot_general | solution.py:61
  684.7 16.0 %add_convert_fusion.3.up_ref = bf16[2048,1024]{1,0:T(8,128)(2,1)} fusion(f32[2048,1024]{1,0:T(8,128)} %fusion.61, bf16[2048,2048]{1,0:T(8,128)(2,1)S(1)} %bitcast.67, bf16[2048,1024]{1,0:T(8,128)(2,1)S(1)} %copy-done.80, f32[2048,1024]{1,0:T(8,128)} %fusion.58), kind=kOutput, calls=%fused_computation.22 | convolution fusion | flops 8608808960 | bytes 33554432 | tf_op jit(solution)/shard_map/dot_general | solution.py:61
  711.0 9.8 convert_bitcast_fusion.g_ref
  720.8 177.7 %back_swap.1 = (bf16[8,512,256]{2,1,0:T(8,128)(2,1)}, bf16[8,512,128]{2,1,0:T(8,128)(2,1)S(1)}, bf16[4,512,1024]{2,1,0:T(8,128)(2,1)}, bf16[4,512,1024]{2,1,0:T(8,128)(2,1)}, bf16[4,1024,512]{2,1,0:T(8,128)(2,1)}) custom-call(bf16[8,512,384]{2,1,0:T(8,128)(2,1)} %get-tuple-element.80.packed_ref, bf16[8,512,256]{2,1,0:T(8,128)(2,1)} %convert_bitcast_fusion.g_ref, ...), custom_call_target="tpu_custom_call" | custom-call | flops 103079215104 | bytes 18874368 | tf_op jit(solution)/shard_map/back_swap/pallas_call | solution.py:1206
  904.3 41.5 %project_back.1 = (bf16[8,2048,384]{2,1,0:T(8,128)(2,1)}, bf16[8,2048,256]{2,1,0:T(8,128)(2,1)}, f32[512,2048]{1,0:T(8,128)}, f32[8,128]{1,0:T(8,128)S(1)}) custom-call(bf16[8,512,256]{2,1,0:T(8,128)(2,1)S(1)} %copy-done.9, bf16[8,512,128]{2,1,0:T(8,128)(2,1)S(1)} %copy-done.11, f32[8,512,384]{2,1,0:T(8,128)} %get-tuple-element.101.raw_ref, ...), custom_call_target="tpu_custom_call" | custom-call | flops 17179869184 | bytes 46137344 | tf_op jit(solution)/shard_map/project_back/pallas_call | solution.py:1363
  949.5 138.9 %sum_weights.1 = (f32[512,256]{1,0:T(8,128)S(1)}, f32[256,512]{1,0:T(8,128)S(1)}, f32[512,512]{1,0:T(8,128)}, f32[512,512]{1,0:T(8,128)}, f32[40,128]{1,0:T(8,128)S(1)}) custom-call(bf16[8,2048,384]{2,1,0:T(8,128)(2,1)} %get-tuple-element.102.in_ref, bf16[8,2048,256]{2,1,0:T(8,128)(2,1)} %get-tuple-element.103.out_ref, f32[40,128]{1,0:T(8,128)S(1)} %pad_bitcast_fusion.gain_ref), custom_call_target="tpu_custom_call" | custom-call | bytes 1048576 | tf_op jit(solution)/shard_map/sum_weights/pallas_call | solution.py:704
  1109.3 4.1 multiply_subtract_fusion.1
  1114.1 4.3 multiply_subtract_fusion.2
  1121.5 9.2 fusion.19
  (241 shorter events, 67.6 us)
Async XLA Ops:
  7.2 183.4 %all-gather.8.cloned.1.call-start = ((), (), s32[]{:S(2)}) async-start(), calls=%async_computation.5 | async-start | bytes 9437184 | tf_op jit(solution)/shard_map/all_gather | solution.py:1453
  10.6 191.8 %all-gather.6.cloned.1.call-start = ((), (), s32[]{:S(2)}) async-start(), calls=%async_computation.4 | async-start | bytes 9437184 | tf_op jit(solution)/shard_map/all_gather | solution.py:1452
  11.3 318.9 %all-gather.10.cloned.1.call-start = ((), (), s32[]{:S(2)}) async-start(), calls=%async_computation.6 | async-start | bytes 5242880 | tf_op jit(solution)/shard_map/all_gather | solution.py:1458
  14.9 147.7 %copy-start.69 = (f32[2,64]{1,0:T(2,128)S(1)}, f32[2,64]{1,0:T(2,128)}, u32[]{:S(2)}) copy-start(f32[2,64]{1,0:T(2,128)} %param.57) | copy-start | bytes 1540
  14.9 147.8 %copy-start.15 = (bf16[512,2048]{1,0:T(8,128)(2,1)S(1)}, bf16[512,2048]{1,0:T(8,128)(2,1)}, u32[]{:S(2)}) copy-start(bf16[512,2048]{1,0:T(8,128)(2,1)} %param.30) | copy-start | bytes 6291460
  14.9 148.9 %copy-start.54 = (f32[2,2048]{1,0:T(2,128)S(1)}, f32[2,2048]{1,0:T(2,128)}, u32[]{:S(2)}) copy-start(f32[2,2048]{1,0:T(2,128)} %param.54) | copy-start | bytes 49156
  162.6 277.2 %all-gather.12.cloned.1.call-start = ((), (), s32[]{:S(2)}) async-start(), calls=%async_computation.7 | async-start | bytes 9437184 | tf_op jit(solution)/shard_map/all_gather | solution.py:421
  163.8 174.3 %copy-start.49 = (f32[1,2048]{1,0:T(1,128)}, f32[1,2048]{1,0:T(1,128)S(1)}, u32[]{:S(2)}) copy-start(f32[1,2048]{1,0:T(1,128)S(1)} %get-tuple-element.161) | copy-start | bytes 24580
  340.8 181.6 %all-gather.14.cloned.1.call-start = ((), (), s32[]{:S(2)}) async-start(), calls=%async_computation.9 | async-start | bytes 9437184 | tf_op jit(solution)/shard_map/all_gather | solution.py:421
  341.3 359.3 %reduce-scatter.5.cloned.1.call-start = ((), (), s32[]{:S(2)}) async-start(), calls=%async_computation.8 | async-start | bytes 9437184 | tf_op jit(solution)/shard_map/reduce_scatter | solution.py:432
  439.8 14.6 %copy-start.74 = (bf16[2048,2048]{1,0:T(8,128)(2,1)S(1)}, bf16[2048,2048]{1,0:T(8,128)(2,1)}, u32[]{:S(2)}) copy-start(bf16[2048,2048]{1,0:T(8,128)(2,1)} %all-gather.12.cloned.1.call-done) | copy-start | bytes 25165828
  454.3 18.9 %copy-start.75 = (bf16[2048,1024]{1,0:T(8,128)(2,1)S(1)}, bf16[2048,1024]{1,0:T(8,128)(2,1)}, u32[]{:S(2)}) copy-start(bf16[2048,1024]{1,0:T(8,128)(2,1)} %all-gather.10.cloned.1.call-done) | copy-start | bytes 12582916
  473.2 14.1 %copy-start.77 = (bf16[4,512,1024]{2,1,0:T(8,128)(2,1)S(1)}, bf16[4,512,1024]{2,1,0:T(8,128)(2,1)}, u32[]{:S(2)}) copy-start(bf16[4,512,1024]{2,1,0:T(8,128)(2,1)} %get-tuple-element.86) | copy-start | bytes 12582916
  503.4 199.6 %reduce-scatter.7.cloned.1.call-start = ((), (), s32[]{:S(2)}) async-start(), calls=%async_computation.10 | async-start | bytes 9437184 | tf_op jit(solution)/shard_map/reduce_scatter | solution.py:432
  522.4 14.7 %copy-start.73 = (bf16[2048,2048]{1,0:T(8,128)(2,1)S(1)}, bf16[2048,2048]{1,0:T(8,128)(2,1)}, u32[]{:S(2)}) copy-start(bf16[2048,2048]{1,0:T(8,128)(2,1)} %all-gather.14.cloned.1.call-done) | copy-start | bytes 25165828
  537.1 17.4 %copy-start.76 = (bf16[2048,1024]{1,0:T(8,128)(2,1)S(1)}, bf16[2048,1024]{1,0:T(8,128)(2,1)}, u32[]{:S(2)}) copy-start(bf16[2048,1024]{1,0:T(8,128)(2,1)} %all-gather.10.cloned.1.call-done) | copy-start | bytes 12582916
  589.0 529.5 %reduce-scatter.9.cloned.1.call-start = ((), (), s32[]{:S(2)}) async-start(), calls=%async_computation.11 | async-start | bytes 9437184 | tf_op jit(solution)/shard_map/reduce_scatter | solution.py:1522
  589.0 15.1 %copy-start.81 = (bf16[2048,1024]{1,0:T(8,128)(2,1)S(1)}, bf16[2048,1024]{1,0:T(8,128)(2,1)}, u32[]{:S(2)}) copy-start(bf16[2048,1024]{1,0:T(8,128)(2,1)} %get-tuple-element.154) | copy-start | bytes 12582916
  656.0 28.6 %slice-start = ((s8[8388608]{0:T(1024)(128)(4,1)}), s8[4194304]{0:T(1024)(128)(4,1)S(1)}, s32[]{:S(2)}) async-start(s8[8388608]{0:T(1024)(128)(4,1)} %bitcast.66), calls=%async_computation.13 | async-start | bytes 8388608
  669.2 15.4 %slice-start.1 = ((s8[8388608]{0:T(1024)(128)(4,1)}), s8[4194304]{0:T(1024)(128)(4,1)S(1)}, s32[]{:S(2)}) async-start(s8[8388608]{0:T(1024)(128)(4,1)} %bitcast.66), calls=%async_computation.14 | async-start | bytes 8388608
  669.2 15.4 %copy-start.80 = (bf16[2048,1024]{1,0:T(8,128)(2,1)S(1)}, bf16[2048,1024]{1,0:T(8,128)(2,1)}, u32[]{:S(2)}) copy-start(bf16[2048,1024]{1,0:T(8,128)(2,1)} %convolution_convert_fusion.2) | copy-start | bytes 12582916
  899.6 221.9 %reduce-scatter.11.cloned.1.call-start = ((), (), s32[]{:S(2)}) async-start(), calls=%async_computation.12 | async-start | bytes 9437184 | tf_op jit(solution)/shard_map/reduce_scatter | solution.py:1523
  904.3 41.6 %copy-start.16 = (bf16[512,2048]{1,0:T(8,128)(2,1)S(1)}, bf16[512,2048]{1,0:T(8,128)(2,1)}, u32[]{:S(2)}) copy-start(bf16[512,2048]{1,0:T(8,128)(2,1)} %param.30) | copy-start | bytes 6291460
  904.3 41.6 %copy-start.53 = (f32[1,2048]{1,0:T(1,128)S(1)}, f32[1,2048]{1,0:T(1,128)}, u32[]{:S(2)}) copy-start(f32[1,2048]{1,0:T(1,128)} %copy-done.52) | copy-start | bytes 24580
  904.3 41.6 %copy-start.60 = (f32[512]{0:T(512)S(1)}, f32[512]{0:T(512)}, u32[]{:S(2)}) copy-start(f32[512]{0:T(512)} %copy-done.59) | copy-start | bytes 6148
  949.4 139.1 %copy-start.64 = (f32[512]{0:T(512)S(1)}, f32[512]{0:T(512)}, u32[]{:S(2)}) copy-start(f32[512]{0:T(512)} %copy-done.63) | copy-start | bytes 6148
  949.4 139.1 %copy-start.70 = (f32[2,64]{1,0:T(2,128)S(1)}, f32[2,64]{1,0:T(2,128)}, u32[]{:S(2)}) copy-start(f32[2,64]{1,0:T(2,128)} %param.57) | copy-start | bytes 1540
  949.4 139.1 %copy-start.71 = (f32[2,64]{1,0:T(2,128)S(1)}, f32[2,64]{1,0:T(2,128)}, u32[]{:S(2)}) copy-start(f32[2,64]{1,0:T(2,128)} %param.58) | copy-start | bytes 1540
  949.4 139.1 %copy-start.72 = (f32[2,64]{1,0:T(2,128)S(1)}, f32[2,64]{1,0:T(2,128)}, u32[]{:S(2)}) copy-start(f32[2,64]{1,0:T(2,128)} %param.59) | copy-start | bytes 1540
  949.4 139.6 %copy-start.34 = (f32[256,512]{1,0:T(8,128)S(1)}, f32[256,512]{1,0:T(8,128)}, u32[]{:S(2)}) copy-start(f32[256,512]{1,0:T(8,128)} %param.42) | copy-start | bytes 1572868
  949.4 139.6 %copy-start.45 = (f32[256,512]{1,0:T(8,128)S(1)}, f32[256,512]{1,0:T(8,128)}, u32[]{:S(2)}) copy-start(f32[256,512]{1,0:T(8,128)} %param.43) | copy-start | bytes 1572868
  949.5 139.6 %copy-start.46 = (f32[256,512]{1,0:T(8,128)S(1)}, f32[256,512]{1,0:T(8,128)}, u32[]{:S(2)}) copy-start(f32[256,512]{1,0:T(8,128)} %param.44) | copy-start | bytes 1572868
  (63 other events, 264.1 us)
Sparse Core Ops, SparseCore 0:
  10.7 107.6 all-gather.7
  120.6 81.7 all-gather.5
  204.7 85.1 all-gather.9
  340.9 98.8 all-gather.11
  441.8 80.5 all-gather.13
  524.5 88.1 reduce-scatter.4
  615.0 87.9 reduce-scatter.6
  899.6 90.3 reduce-scatter.8
  992.4 129.0 reduce-scatter.10

commit v11 on v9

--- a/solution.py
+++ b/solution.py
@@ -1471,7 +1471,16 @@
         gate_grad = gate_grad.astype(jnp.bfloat16)
         up_grad = up_grad.astype(jnp.bfloat16)
         mid_sums.append(sum_back(((gate_grad, gate_local), (up_grad, up_local))))
-        block_parts.append(dot_last(hidden_low, down_local).astype(jnp.bfloat16))
+        pieces = [hidden_low]
+        if not block_parts:
+            blocks = hidden_low.reshape(wide_count, half_rows, -1)
+            quarter = half_rows // 2
+            pieces = [
+                blocks[:, :quarter].reshape(wide_count * quarter, -1),
+                blocks[:, quarter:].reshape(wide_count * quarter, -1),
+            ]
+        for piece in pieces:
+            block_parts.append(dot_last(piece, down_local).astype(jnp.bfloat16))
         down_wgrad = down_wgrad + dot_first(hidden_low, grad_rows)
         gate_wgrad = gate_wgrad + dot_first(rows_mid, gate_grad)
         up_wgrad = up_wgrad + dot_first(rows_mid, up_grad)
@@ -1493,10 +1502,11 @@
     query_rot_grad, key_value_grad, gate_shares, up_shares, down_shares = back_swap(
         packed, attended_grad, attended, weight_sums, gate_wgrad, up_wgrad, down_wgrad, local_heads
     )
-    query_rot_grad, first_sum, second_part = lax.optimization_barrier(
-        (query_rot_grad, first_sum, block_parts[1])
+    query_rot_grad, first_sum, second_part, third_part = lax.optimization_barrier(
+        (query_rot_grad, first_sum, block_parts[1], block_parts[2])
     )
     second_sum = lax.psum_scatter(second_part, "wide", scatter_dimension=0, tiled=True)
+    third_sum = lax.psum_scatter(third_part, "wide", scatter_dimension=0, tiled=True)
     input_wgrad, output_wgrad, input_back, head_sums = project_back(
         query_rot_grad, key_value_grad, input_raw, cosine, sine_part, lane_gains, rows_in,
         att_full, branch_grad, attended_low, local_heads,
@@ -1513,8 +1523,10 @@
         jnp.concatenate([gain_stack, head_stack], axis=1),
         key_heads,
     )
-    query_total, second_sum = lax.optimization_barrier((query_total, second_sum))
-    block_sum = jnp.concatenate([first_sum, second_sum], axis=0).astype(jnp.float32)
+    query_total, second_sum, third_sum = lax.optimization_barrier(
+        (query_total, second_sum, third_sum)
+    )
+    block_sum = jnp.concatenate([first_sum, second_sum, third_sum], axis=0).astype(jnp.float32)
     block_out = (middle + block_sum).astype(jnp.bfloat16)
     gain_total = gains[:, :model_width]
     head_total = gains[:, model_width:]

time: 1150 us -> 1150 us (level)
    pallas_call x1, Pallas kernels: 215 us -> 200 us  [back_swap(): pl.pallas_call(functools.partial(back_swap_kernel, heads), out_shape=[jax...]
    pallas_call x1, Pallas kernels: 112 us -> 127 us  [sum_weights(): pl.pallas_call(scatter_kernel, out_shape=[jax.ShapeDtypeStruct((rows, spl...]
    dot_general x6 -> x7, matrix products: 91.1 us -> 94.3 us  [dot_last(): return jnp.dot(left, right, preferred_element_type=jnp.float32)]
  transfers between devices with their start and end apart: 9 -> 10, of which waited for: 3 -> 3; matrix products, arithmetic and copies ran while one was open for 28% -> 28% of each run, Pallas kernels for 59% -> 59%
where the time goes in v11:
time: 1150 us; the launch traced here: 1140 us
  Pallas kernels  667 us (58%)
  matrix products  290 us (25%)
  waiting for transfers between devices  82.5 us (7%)
  other arithmetic  58.2 us (5%)
  local copies, waits for them, and re-layouts  25.9 us (2%)
  between operations  15.5 us (1%)
    pallas_call x1, Pallas kernels, back_swap(): pl.pallas_call(functools.partial(back_swap_kernel, heads), out_shape=[jax...  200 us
    pallas_call x1, Pallas kernels, gather_weights(): pl.pallas_call(gather_kernel, out_shape=jax.ShapeDtypeStruct((8, 4 * att....  148 us
    pallas_call x1, Pallas kernels, attend_swap(): pl.pallas_call(functools.partial(attend_swap_kernel, heads), out_shape=[j...  133 us
    pallas_call x1, Pallas kernels, sum_weights(): pl.pallas_call(scatter_kernel, out_shape=[jax.ShapeDtypeStruct((rows, spl...  127 us
    dot_general x7, matrix products, dot_last(): return jnp.dot(left, right, preferred_element_type=jnp.float32)  94.3 us
    dot_general x6, matrix products, dot_back(): lax.dot_general(left, right, (((1,), (1,)), ((), ())), preferred_element_...  91.7 us
    dot_general x6, matrix products, dot_first(): lax.dot_general(left, right, (((0,), (0,)), ((), ())), preferred_element_...  87.5 us
    all_gather x2, waiting for transfers between devices, gather_rows(): return lax.all_gather(shard, 'wide', axis=0, tiled=True)  69.1 us
  transfers between devices with their start and end apart: 10, of which 3 were waited for; matrix products, arithmetic and copies ran while one was open for 28% of the time, Pallas kernels for 59%

profile of v11, /device:TPU:0, one launch (start us, length us, event | category | flops | bytes accessed | tf_op | source)
XLA Modules:
  0.0 1139.7 jit_solution(9491557553288170892)
XLA Ops:
  14.9 147.6 %gather_weights.1.weight_ref = bf16[8,2048,640]{2,1,0:T(8,128)(2,1)} custom-call(bf16[512,640]{1,0:T(8,128)(2,1)} %pad_maximum_fusion.att_ref), custom_call_target="tpu_custom_call" | custom-call | bytes 314572800 | tf_op jit(solution)/shard_map/gather_weights/pallas_call | solution.py:406
  169.5 16.9 %project.1 = (bf16[8,512,384]{2,1,0:T(8,128)(2,1)S(1)}, f32[8,512,384]{2,1,0:T(8,128)}) custom-call(bf16[512,2048]{1,0:T(8,128)(2,1)S(1)} %fusion.16.rows_ref, bf16[8,2048,640]{2,1,0:T(8,128)(2,1)} %gather_weights.1.weight_ref, f32[512,128]{1,0:T(8,128)S(1)} %get-tuple-element.182.cos_ref, f32[512,128]{1,0:T(8,128)S(1)} %get-tuple-element.183.sin_ref, ...), custom_call_target="tpu_custom_call" | custom-call | flops 6442450944 | bytes 25165824 | tf_op jit(solution)/shard_map/project/pallas_call | solution.py:1262
  190.9 11.4 %all-gather.6.cloned.1.call-done = bf16[2048,2048]{1,0:T(8,128)(2,1)} async-done(((bf16[256,2048]{1,0:T(8,128)(2,1)}), bf16[2048,2048]{1,0:T(8,128)(2,1)}) %all-gather.6.cloned.1.call-update) | async-done | bytes 8388624 | tf_op jit(solution)/shard_map/all_gather | solution.py:1427
  202.3 133.1 %attend_swap.1 = (bf16[8,512,384]{2,1,0:T(8,128)(2,1)}, f32[4096,256]{1,0:T(8,128)}, f32[4096,256]{1,0:T(8,128)}, bf16[8,512,256]{2,1,0:T(8,128)(2,1)}, bf16[4,5...) custom-call(bf16[8,512,384]{2,1,0:T(8,128)(2,1)} %copy-done.6, bf16[512,1024]{1,0:T(8,128)(2,1)S(1)} %convert_element_type.115.up_ref, ...), custom_call_target="tpu_custom_call" | custom-call | flops 68719476736 | bytes 18874368 | tf_op jit(solution)/shard_map/attend_swap/pallas_call | solution.py:939
  335.5 7.8 multiply_reduce_fusion.2
  346.6 13.9 %convolution_convert_fusion.1 = bf16[2048,1024]{1,0:T(8,128)(2,1)} fusion(bf16[2048,2048]{1,0:T(8,128)(2,1)} %all-gather.8.cloned.1.call-done, bf16[1024,2048]{1,0:T(8,128)(2,1)} %get-tuple-element.86), kind=kOutput, calls=%fused_computation.53 | convolution fusion | flops 8592031744 | bytes 16777216 | tf_op jit(solution)/shard_map/dot_general | solution.py:67
  360.6 12.6 %convolution_convert_fusion.2 = bf16[2048,1024]{1,0:T(8,128)(2,1)} fusion(bf16[2048,2048]{1,0:T(8,128)(2,1)} %all-gather.6.cloned.1.call-done, bf16[1024,2048]{1,0:T(8,128)(2,1)S(1)} %copy-done.72), kind=kOutput, calls=%fused_computation.54 | convolution fusion | flops 8592031744 | bytes 16777216 | tf_op jit(solution)/shard_map/dot_general | solution.py:67
  373.2 54.2 %all-gather.12.cloned.1.call-done = bf16[2048,2048]{1,0:T(8,128)(2,1)} async-done(((bf16[256,2048]{1,0:T(8,128)(2,1)}), bf16[2048,2048]{1,0:T(8,128)(2,1)}) %all-gather.12.cloned.1.call-update) | async-done | bytes 8388624 | tf_op jit(solution)/shard_map/all_gather | solution.py:421
  427.4 14.6 %fusion.57 = f32[2048,1024]{1,0:T(8,128)} fusion(bf16[2048,2048]{1,0:T(8,128)(2,1)} %all-gather.12.cloned.1.call-done, bf16[2048,1024]{1,0:T(8,128)(2,1)} %all-gather.10.cloned.1.call-done), kind=kOutput, calls=%fused_computation.123 | convolution fusion | flops 8589934592 | bytes 20971520 | tf_op jit(solution)/shard_map/dot_general | solution.py:57
  442.0 18.7 %multiply_convert_fusion.1 = (bf16[2048,1024]{1,0:T(8,128)(2,1)}, bf16[2048,1024]{1,0:T(8,128)(2,1)}, bf16[2048,1024]{1,0:T(8,128)(2,1)}) fusion(f32[2048,1024]{1,0:T(8,128)} %fusion.57, bf16[2048,1024]{1,0:T(8,128)(2,1)} %convolution_convert_fusion.2, bf16[2048,2048]{1,0:T(8,128)(2,1)S(1)} %copy-done.66, bf16[2048,1024]{1,0:T(8,128)(2,1)} %bitcast.76), kind=kOutput, calls=%fused_computation.21 | convolution fusion | flops 8625586176 | bytes 37748736 | tf_op jit(solution)/shard_map/dot_general | solution.py:57
  460.7 14.2 %fusion.58 = f32[2048,2048]{1,0:T(8,128)} fusion(bf16[2048,1024]{1,0:T(8,128)(2,1)} %get-tuple-element.161, bf16[2048,1024]{1,0:T(8,128)(2,1)S(1)} %copy-done.67), kind=kOutput, calls=%fused_computation.124 | convolution fusion | flops 8589934592 | bytes 25165824 | tf_op jit(solution)/shard_map/dot_general | solution.py:67
  474.9 16.0 %add_convert_fusion.1 = bf16[2048,2048]{1,0:T(8,128)(2,1)} fusion(f32[2048,2048]{1,0:T(8,128)} %fusion.58, bf16[2048,1024]{1,0:T(8,128)(2,1)} %get-tuple-element.162, bf16[2048,1024]{1,0:T(8,128)(2,1)S(1)} %bitcast.79), kind=kOutput, calls=%fused_computation.1 | convolution fusion | flops 8598323200 | bytes 33554432 | tf_op jit(solution)/shard_map/dot_general | solution.py:67
  495.2 14.9 %all-gather.14.cloned.1.call-done = bf16[2048,2048]{1,0:T(8,128)(2,1)} async-done(((bf16[256,2048]{1,0:T(8,128)(2,1)}), bf16[2048,2048]{1,0:T(8,128)(2,1)}) %all-gather.14.cloned.1.call-update) | async-done | bytes 8388624 | tf_op jit(solution)/shard_map/all_gather | solution.py:421
  510.1 14.8 %fusion.59 = f32[2048,1024]{1,0:T(8,128)} fusion(bf16[2048,2048]{1,0:T(8,128)(2,1)} %all-gather.14.cloned.1.call-done, bf16[2048,1024]{1,0:T(8,128)(2,1)} %all-gather.10.cloned.1.call-done), kind=kOutput, calls=%fused_computation.125 | convolution fusion | flops 8589934592 | bytes 20971520 | tf_op jit(solution)/shard_map/dot_general | solution.py:57
  524.9 17.4 %multiply_convert_fusion = (bf16[2048,1024]{1,0:T(8,128)(2,1)}, bf16[2048,1024]{1,0:T(8,128)(2,1)}) fusion(f32[2048,1024]{1,0:T(8,128)} %fusion.59, bf16[2048,1024]{1,0:T(8,128)(2,1)} %convolution_convert_fusion.1, bf16[2048,2048]{1,0:T(8,128)(2,1)S(1)} %copy-done.65, bf16[2048,1024]{1,0:T(8,128)(2,1)} %bitcast.77), kind=kOutput, calls=%fused_computation.20 | convolution fusion | flops 8621391872 | bytes 33554432 | tf_op jit(solution)/shard_map/dot_general | solution.py:57
  542.2 14.0 %fusion.60 = f32[2048,2048]{1,0:T(8,128)} fusion(bf16[2048,1024]{1,0:T(8,128)(2,1)} %get-tuple-element.159, bf16[2048,1024]{1,0:T(8,128)(2,1)S(1)} %copy-done.68), kind=kOutput, calls=%fused_computation.126 | convolution fusion | flops 8589934592 | bytes 25165824 | tf_op jit(solution)/shard_map/dot_general | solution.py:67
  556.3 20.9 %add_convert_fusion = bf16[2048,2048]{1,0:T(8,128)(2,1)} fusion(f32[2048,2048]{1,0:T(8,128)} %fusion.60, bf16[2048,1024]{1,0:T(8,128)(2,1)} %bitcast.78, bf16[2048,1024]{1,0:T(8,128)(2,1)} %convolution_convert_fusion.1, f32[2048,1024]{1,0:T(8,128)} %fusion.59), kind=kOutput, calls=%fused_computation | convolution fusion | flops 8613003264 | bytes 41943040 | tf_op jit(solution)/shard_map/dot_general | solution.py:67
  577.3 9.3 convolution_convert_fusion.4
  586.6 8.4 convolution_convert_fusion.3
  595.0 14.8 %fusion.61 = f32[2048,1024]{1,0:T(8,128)} fusion(bf16[2048,2048]{1,0:T(8,128)(2,1)} %all-gather.12.cloned.1.call-done, bf16[2048,1024]{1,0:T(8,128)(2,1)} %get-tuple-element.161), kind=kOutput, calls=%fused_computation.127 | convolution fusion | flops 8589934592 | bytes 20971520 | tf_op jit(solution)/shard_map/dot_general | solution.py:61
  609.8 13.7 %fusion.62 = f32[2048,1024]{1,0:T(8,128)} fusion(bf16[2048,2048]{1,0:T(8,128)(2,1)} %all-gather.12.cloned.1.call-done, bf16[2048,1024]{1,0:T(8,128)(2,1)S(1)} %copy-done.75), kind=kOutput, calls=%fused_computation.128 | convolution fusion | flops 8589934592 | bytes 20971520 | tf_op jit(solution)/shard_map/dot_general | solution.py:61
  623.6 11.1 convolution_convert_fusion
  634.7 13.3 %fusion.63 = f32[1024,2048]{1,0:T(8,128)S(1)} fusion(bf16[2048,1024]{1,0:T(8,128)(2,1)} %get-tuple-element.160, bf16[2048,2048]{1,0:T(8,128)(2,1)} %all-gather.6.cloned.1.call-done), kind=kOutput, calls=%fused_computation.129 | convolution fusion | flops 8589934592 | bytes 20971520 | tf_op jit(solution)/shard_map/dot_general | solution.py:61
  648.0 13.5 %add_convert_fusion.2.down_ref = bf16[1024,2048]{1,0:T(8,128)(2,1)} fusion(f32[1024,2048]{1,0:T(8,128)S(1)} %fusion.63, bf16[2048,1024]{1,0:T(8,128)(2,1)S(1)} %copy-done.71, bf16[2048,2048]{1,0:T(8,128)(2,1)} %all-gather.8.cloned.1.call-done), kind=kOutput, calls=%fused_computation.19 | convolution fusion | flops 8594128896 | bytes 25165824 | tf_op jit(solution)/shard_map/dot_general | solution.py:61
  661.5 16.1 %add_convert_fusion.4.gate_ref = bf16[2048,1024]{1,0:T(8,128)(2,1)} fusion(f32[2048,1024]{1,0:T(8,128)} %fusion.61, bf16[2048,2048]{1,0:T(8,128)(2,1)} %all-gather.14.cloned.1.call-done, bf16[2048,1024]{1,0:T(8,128)(2,1)} %get-tuple-element.159), kind=kOutput, calls=%fused_computation.23 | convolution fusion | flops 8594128896 | bytes 25165824 | tf_op jit(solution)/shard_map/dot_general | solution.py:61
  677.6 16.0 %add_convert_fusion.3.up_ref = bf16[2048,1024]{1,0:T(8,128)(2,1)} fusion(f32[2048,1024]{1,0:T(8,128)} %fusion.62, bf16[2048,2048]{1,0:T(8,128)(2,1)S(1)} %bitcast.75, bf16[2048,1024]{1,0:T(8,128)(2,1)S(1)} %copy-done.74, f32[2048,1024]{1,0:T(8,128)} %fusion.59), kind=kOutput, calls=%fused_computation.22 | convolution fusion | flops 8608808960 | bytes 33554432 | tf_op jit(solution)/shard_map/dot_general | solution.py:61
  704.5 9.1 convert_bitcast_fusion.g_ref
  713.7 200.3 %back_swap.1 = (bf16[8,512,256]{2,1,0:T(8,128)(2,1)}, bf16[8,512,128]{2,1,0:T(8,128)(2,1)S(1)}, bf16[4,512,1024]{2,1,0:T(8,128)(2,1)}, bf16[4,512,1024]{2,1,0:T(8,128)(2,1)}, bf16[4,1024,512]{2,1,0:T(8,128)(2,1)}) custom-call(bf16[8,512,384]{2,1,0:T(8,128)(2,1)} %get-tuple-element.84.packed_ref, bf16[8,512,256]{2,1,0:T(8,128)(2,1)} %convert_bitcast_fusion.g_ref, ...), custom_call_target="tpu_custom_call" | custom-call | flops 103079215104 | bytes 18874368 | tf_op jit(solution)/shard_map/back_swap/pallas_call | solution.py:1181
  927.7 4.2 multiply_subtract_fusion.1
  937.0 42.1 %project_back.1 = (bf16[8,2048,384]{2,1,0:T(8,128)(2,1)}, bf16[8,2048,256]{2,1,0:T(8,128)(2,1)}, f32[512,2048]{1,0:T(8,128)}, f32[8,128]{1,0:T(8,128)S(1)}) custom-call(bf16[8,512,256]{2,1,0:T(8,128)(2,1)S(1)} %copy-done.7, bf16[8,512,128]{2,1,0:T(8,128)(2,1)S(1)} %get-tuple-element.108.dkv_ref, f32[8,512,384]{2,1,0:T(8,128)} %get-tuple-element.109.raw_ref, ...), custom_call_target="tpu_custom_call" | custom-call | flops 17179869184 | bytes 46137344 | tf_op jit(solution)/shard_map/project_back/pallas_call | solution.py:1338
  982.8 126.7 %sum_weights.1 = (f32[512,256]{1,0:T(8,128)S(1)}, f32[256,512]{1,0:T(8,128)S(1)}, f32[512,512]{1,0:T(8,128)}, f32[512,512]{1,0:T(8,128)}, f32[40,128]{1,0:T(8,128)S(1)}) custom-call(bf16[8,2048,384]{2,1,0:T(8,128)(2,1)} %get-tuple-element.110.in_ref, bf16[8,2048,256]{2,1,0:T(8,128)(2,1)} %get-tuple-element.111.out_ref, f32[40,128]{1,0:T(8,128)S(1)} %pad_bitcast_fusion.gain_ref), custom_call_target="tpu_custom_call" | custom-call | bytes 1048576 | tf_op jit(solution)/shard_map/sum_weights/pallas_call | solution.py:704
  1122.9 9.6 fusion.19
  (230 shorter events, 72.7 us)
Async XLA Ops:
  7.2 183.6 %all-gather.8.cloned.1.call-start = ((), (), s32[]{:S(2)}) async-start(), calls=%async_computation.6 | async-start | bytes 9437184 | tf_op jit(solution)/shard_map/all_gather | solution.py:1428
  10.6 191.8 %all-gather.6.cloned.1.call-start = ((), (), s32[]{:S(2)}) async-start(), calls=%async_computation.5 | async-start | bytes 9437184 | tf_op jit(solution)/shard_map/all_gather | solution.py:1427
  11.3 324.2 %all-gather.10.cloned.1.call-start = ((), (), s32[]{:S(2)}) async-start(), calls=%async_computation.7 | async-start | bytes 5242880 | tf_op jit(solution)/shard_map/all_gather | solution.py:1433
  14.9 147.7 %copy-start.61 = (f32[2,64]{1,0:T(2,128)S(1)}, f32[2,64]{1,0:T(2,128)}, u32[]{:S(2)}) copy-start(f32[2,64]{1,0:T(2,128)} %param.57) | copy-start | bytes 1540
  14.9 147.8 %copy-start.11 = (bf16[512,2048]{1,0:T(8,128)(2,1)S(1)}, bf16[512,2048]{1,0:T(8,128)(2,1)}, u32[]{:S(2)}) copy-start(bf16[512,2048]{1,0:T(8,128)(2,1)} %param.30) | copy-start | bytes 6291460
  14.9 148.9 %copy-start.45 = (f32[2,2048]{1,0:T(2,128)S(1)}, f32[2,2048]{1,0:T(2,128)}, u32[]{:S(2)}) copy-start(f32[2,2048]{1,0:T(2,128)} %param.54) | copy-start | bytes 49156
  162.6 264.9 %all-gather.12.cloned.1.call-start = ((), (), s32[]{:S(2)}) async-start(), calls=%async_computation.8 | async-start | bytes 9437184 | tf_op jit(solution)/shard_map/all_gather | solution.py:421
  163.8 179.5 %copy-start.40 = (f32[1,2048]{1,0:T(1,128)}, f32[1,2048]{1,0:T(1,128)S(1)}, u32[]{:S(2)}) copy-start(f32[1,2048]{1,0:T(1,128)S(1)} %get-tuple-element.171) | copy-start | bytes 24580
  346.0 164.1 %all-gather.14.cloned.1.call-start = ((), (), s32[]{:S(2)}) async-start(), calls=%async_computation.10 | async-start | bytes 9437184 | tf_op jit(solution)/shard_map/all_gather | solution.py:421
  346.6 347.1 %reduce-scatter.6.cloned.1.call-start = ((), (), s32[]{:S(2)}) async-start(), calls=%async_computation.9 | async-start | bytes 9437184 | tf_op jit(solution)/shard_map/reduce_scatter | solution.py:432
  346.6 14.0 %copy-start.72 = (bf16[1024,2048]{1,0:T(8,128)(2,1)S(1)}, bf16[1024,2048]{1,0:T(8,128)(2,1)}, u32[]{:S(2)}) copy-start(bf16[1024,2048]{1,0:T(8,128)(2,1)} %get-tuple-element.86) | copy-start | bytes 12582916
  427.4 14.6 %copy-start.66 = (bf16[2048,2048]{1,0:T(8,128)(2,1)S(1)}, bf16[2048,2048]{1,0:T(8,128)(2,1)}, u32[]{:S(2)}) copy-start(bf16[2048,2048]{1,0:T(8,128)(2,1)} %all-gather.12.cloned.1.call-done) | copy-start | bytes 25165828
  442.0 18.7 %copy-start.67 = (bf16[2048,1024]{1,0:T(8,128)(2,1)S(1)}, bf16[2048,1024]{1,0:T(8,128)(2,1)}, u32[]{:S(2)}) copy-start(bf16[2048,1024]{1,0:T(8,128)(2,1)} %all-gather.10.cloned.1.call-done) | copy-start | bytes 12582916
  460.7 14.2 %copy-start.69 = (bf16[4,512,1024]{2,1,0:T(8,128)(2,1)S(1)}, bf16[4,512,1024]{2,1,0:T(8,128)(2,1)}, u32[]{:S(2)}) copy-start(bf16[4,512,1024]{2,1,0:T(8,128)(2,1)} %get-tuple-element.90) | copy-start | bytes 12582916
  490.9 204.2 %reduce-scatter.8.cloned.1.call-start = ((), (), s32[]{:S(2)}) async-start(), calls=%async_computation.11 | async-start | bytes 9437184 | tf_op jit(solution)/shard_map/reduce_scatter | solution.py:432
  510.1 14.8 %copy-start.65 = (bf16[2048,2048]{1,0:T(8,128)(2,1)S(1)}, bf16[2048,2048]{1,0:T(8,128)(2,1)}, u32[]{:S(2)}) copy-start(bf16[2048,2048]{1,0:T(8,128)(2,1)} %all-gather.14.cloned.1.call-done) | copy-start | bytes 25165828
  524.9 17.4 %copy-start.68 = (bf16[2048,1024]{1,0:T(8,128)(2,1)S(1)}, bf16[2048,1024]{1,0:T(8,128)(2,1)}, u32[]{:S(2)}) copy-start(bf16[2048,1024]{1,0:T(8,128)(2,1)} %all-gather.10.cloned.1.call-done) | copy-start | bytes 12582916
  577.2 336.8 %reduce-scatter.10.cloned.1.call-start = ((), (), s32[]{:S(2)}) async-start(), calls=%async_computation.12 | async-start | bytes 4718592 | tf_op jit(solution)/shard_map/reduce_scatter | solution.py:1501
  595.0 14.9 %copy-start.75 = (bf16[2048,1024]{1,0:T(8,128)(2,1)S(1)}, bf16[2048,1024]{1,0:T(8,128)(2,1)}, u32[]{:S(2)}) copy-start(bf16[2048,1024]{1,0:T(8,128)(2,1)} %get-tuple-element.162) | copy-start | bytes 12582916
  609.8 13.7 %copy-start.73 = (bf16[1024,2048]{1,0:T(8,128)(2,1)S(1)}, bf16[1024,2048]{1,0:T(8,128)(2,1)}, u32[]{:S(2)}) copy-start(bf16[1024,2048]{1,0:T(8,128)(2,1)} %get-tuple-element.86) | copy-start | bytes 12582916
  648.0 29.7 %slice-start = ((s8[8388608]{0:T(1024)(128)(4,1)}), s8[4194304]{0:T(1024)(128)(4,1)S(1)}, s32[]{:S(2)}) async-start(s8[8388608]{0:T(1024)(128)(4,1)} %bitcast.74), calls=%async_computation.15 | async-start | bytes 8388608
  661.5 16.1 %slice-start.1 = ((s8[8388608]{0:T(1024)(128)(4,1)}), s8[4194304]{0:T(1024)(128)(4,1)S(1)}, s32[]{:S(2)}) async-start(s8[8388608]{0:T(1024)(128)(4,1)} %bitcast.74), calls=%async_computation.16 | async-start | bytes 8388608
  661.5 16.1 %copy-start.74 = (bf16[2048,1024]{1,0:T(8,128)(2,1)S(1)}, bf16[2048,1024]{1,0:T(8,128)(2,1)}, u32[]{:S(2)}) copy-start(bf16[2048,1024]{1,0:T(8,128)(2,1)} %convolution_convert_fusion.1) | copy-start | bytes 12582916
  713.6 406.4 %reduce-scatter.12.cloned.1.call-start = ((), (), s32[]{:S(2)}) async-start(), calls=%async_computation.13 | async-start | bytes 4718592 | tf_op jit(solution)/shard_map/reduce_scatter | solution.py:1508
  914.0 206.0 %reduce-scatter.14.cloned.1.call-start = ((), (), s32[]{:S(2)}) async-start(), calls=%async_computation.14 | async-start | bytes 9437184 | tf_op jit(solution)/shard_map/reduce_scatter | solution.py:1509
  936.9 42.2 %copy-start.12 = (bf16[512,2048]{1,0:T(8,128)(2,1)S(1)}, bf16[512,2048]{1,0:T(8,128)(2,1)}, u32[]{:S(2)}) copy-start(bf16[512,2048]{1,0:T(8,128)(2,1)} %param.30) | copy-start | bytes 6291460
  936.9 42.2 %copy-start.44 = (f32[1,2048]{1,0:T(1,128)S(1)}, f32[1,2048]{1,0:T(1,128)}, u32[]{:S(2)}) copy-start(f32[1,2048]{1,0:T(1,128)} %copy-done.43) | copy-start | bytes 24580
  936.9 42.2 %copy-start.51 = (f32[512]{0:T(512)S(1)}, f32[512]{0:T(512)}, u32[]{:S(2)}) copy-start(f32[512]{0:T(512)} %copy-done.50) | copy-start | bytes 6148
  982.8 126.9 %copy-start.56 = (f32[512]{0:T(512)S(1)}, f32[512]{0:T(512)}, u32[]{:S(2)}) copy-start(f32[512]{0:T(512)} %copy-done.55) | copy-start | bytes 6148
  982.8 126.9 %copy-start.62 = (f32[2,64]{1,0:T(2,128)S(1)}, f32[2,64]{1,0:T(2,128)}, u32[]{:S(2)}) copy-start(f32[2,64]{1,0:T(2,128)} %param.57) | copy-start | bytes 1540
  982.8 126.9 %copy-start.63 = (f32[2,64]{1,0:T(2,128)S(1)}, f32[2,64]{1,0:T(2,128)}, u32[]{:S(2)}) copy-start(f32[2,64]{1,0:T(2,128)} %param.58) | copy-start | bytes 1540
  982.8 126.9 %copy-start.64 = (f32[2,64]{1,0:T(2,128)S(1)}, f32[2,64]{1,0:T(2,128)}, u32[]{:S(2)}) copy-start(f32[2,64]{1,0:T(2,128)} %param.59) | copy-start | bytes 1540
  (56 other events, 202.1 us)
Sparse Core Ops, SparseCore 0:
  10.7 107.6 all-gather.7
  120.6 81.7 all-gather.5
  204.7 121.3 all-gather.9
  346.1 81.2 all-gather.11
  429.4 80.5 all-gather.13
  512.2 88.1 reduce-scatter.5
  602.7 87.9 reduce-scatter.7
  713.8 93.3 reduce-scatter.9
  914.1 47.9 reduce-scatter.11
  964.3 119.0 reduce-scatter.13
